TPU v7x, 32 devices: a whole 2x2x4 slice. The times are simulated.
32 devices in a mesh: groups: 2 (over y), seq: 16 (over z, x, core).
Axes of the slice: x: 2, y: 2, z: 4, core: 2. Of those that a mesh axis runs over, the one named last changes fastest.
Arguments:
- acts: bfloat16 [2, 8192, 8192], P(None, ('groups', 'seq')), parts along dimension 1, may hold values from -6 to 6
- cots: bfloat16 [2, 8192, 1024], P(None, ('groups', 'seq')), parts along dimension 1, may hold values from -0.29882812 to 0.29882812
- proj_in: bfloat16 [8192, 128], P('seq'), may hold values from -0.0625 to 0.0625
- proj_out: bfloat16 [1024, 128], replicated, may hold values from -0.1875 to 0.1875
- lengths: int32 [2, 32], P('groups'), parts along dimension 0, may hold values from 1 to 1024, 4096 in all within a row
- slots: int32 [64], P('groups'), parts along dimension 0, may hold values from 0 to 31, as said below
- pairs: int32 [3, 2], replicated, may hold values from 0 to 1
Outputs:
- logged: bfloat16 [64, 8192], P(('groups', 'seq')), parts along dimension 0
- covariance: float32 [6, 4096, 4096], P('groups', 'seq'), parts along dimension 0
There are 2 independent parts, one for each index of `groups`. A program takes and returns all parts, laid end to end along the dimension named above; an argument that names none is the same for every part. Nothing has to cross between parts.
Inputs may be any that keep to these rules, and one draw needn't show every extreme that they name: The slots are distinct, so no owner logs more than 2 sequences; in every draw some owner logs exactly 2.
All inputs are finite; a program needn't handle non-finite values.
Results may differ from a plain program's by a relative error of at most 0.0075.
Values may be sent and summed in bfloat16 or wider, within the bound.
No kernel may reach another device: no remote copies, remote signals or barrier semaphores. Data moves between devices by JAX's collectives and lax.ppermute only.
A program may use at most 128 MiB of HBM per device.

v0:
```python
import jax
import jax.numpy as jnp
from jax import lax
from jax.sharding import PartitionSpec as P

CAP = 2


def shards(acts, cots, proj_in, proj_out, lengths, slots, pairs):
    layers = acts.shape[0]
    tok_rows = acts.shape[1]
    width_k = proj_out.shape[1] // layers
    square = width_k * width_k
    devices = lax.axis_size("seq")
    here = lax.axis_index("seq")
    rows_all = lengths.shape[0]
    per_row = lengths.shape[1]
    row_len = tok_rows * devices // rows_all
    seq_count = slots.shape[0]
    npair = pairs.shape[0]
    piece = lax.all_gather(proj_in, "seq", axis=0, tiled=True)
    weights = piece.reshape(piece.shape[0], layers, width_k)
    projected = jnp.einsum("ltr,rlk->ltk", acts, weights, preferred_element_type=jnp.float32)
    px_half = projected.astype(jnp.bfloat16)
    pg_half = jnp.einsum(
        "ltd,dlk->ltk",
        cots,
        proj_out.reshape(proj_out.shape[0], layers, width_k),
        preferred_element_type=jnp.float32,
    ).astype(jnp.bfloat16)
    offset = here * tok_rows
    row_index = offset // row_len
    first = offset % row_len
    row_lengths = lax.dynamic_index_in_dim(lengths, row_index, 0, keepdims=False)
    ends = jnp.cumsum(row_lengths)
    starts = ends - row_lengths
    position = first + jnp.arange(tok_rows, dtype=jnp.int32)
    inside = (position[:, None] >= starts[None, :]) & (position[:, None] < ends[None, :])
    member = inside.astype(jnp.bfloat16)
    weighted = member[None, :, :, None] * pg_half[:, :, None, :]
    partial_value = jnp.einsum(
        "ltsa,ltb->slab", weighted, px_half, preferred_element_type=jnp.float32
    )
    partial_value = partial_value.reshape(per_row, layers * square)
    term = jnp.zeros((seq_count, layers * square), jnp.float32)
    term = lax.dynamic_update_slice_in_dim(term, partial_value, row_index * per_row, 0)
    totals = lax.psum(term, "seq")
    grads_half = totals.astype(jnp.bfloat16)
    own_slots = here * CAP + jnp.arange(CAP, dtype=jnp.int32)
    picker = (slots[None, :] == own_slots[:, None]).astype(jnp.bfloat16)
    logged = jnp.dot(picker, grads_half, preferred_element_type=jnp.float32).astype(jnp.bfloat16)
    by_layer = grads_half.reshape(seq_count, layers, square)
    band = square // devices
    base = here * band
    tiles = []
    for index in range(npair):
        left = lax.dynamic_index_in_dim(by_layer, pairs[index, 0], 1, keepdims=False)
        right = lax.dynamic_index_in_dim(by_layer, pairs[index, 1], 1, keepdims=False)
        left_band = lax.dynamic_slice_in_dim(left, base, band, 1)
        product = lax.dot_general(
            left_band, right, (((0,), (0,)), ((), ())), preferred_element_type=jnp.float32
        )
        tiles.append(product / jnp.float32(seq_count))
    covariance = jnp.stack(tiles)
    return (logged, covariance)


def solution(mesh):
    in_specs = (
        P(None, ("groups", "seq"), None),
        P(None, ("groups", "seq"), None),
        P("seq", None),
        P(),
        P("groups", None),
        P("groups"),
        P(),
    )
    out_specs = (P(("groups", "seq"), None), P("groups", "seq", None))
    return jax.shard_map(shards, mesh=mesh, in_specs=in_specs, out_specs=out_specs, check_vma=False)
```

profile of v0, /device:TPU:0, one launch (start us, length us, event | category | flops | bytes accessed | tf_op | source)
XLA Modules:
  0.0 165.2 jit_solution(8675637746422382729)
XLA Ops:
  7.2 0.0 copy-start
  7.2 0.0 all-gather.2.cloned.1.call-start
  7.2 1.7 %copy.10 = bf16[512,128]{0,1:T(8,128)(2,1)} copy(bf16[512,128]{1,0:T(8,128)(2,1)} %param.9) | data formatting | bytes 262144 | tf_op args[2]
  9.0 0.0 all-gather.2.cloned.1.call-update
  9.0 1.5 fusion.15
  19.7 0.7 copy.11
  20.5 0.1 reduce-window.4
  20.5 0.1 reduce
  20.7 1.1 copy.12
  23.6 0.7 fusion.12
  24.2 0.1 and_convert_fusion
  24.3 0.0 copy-done
  24.3 0.4 convolution_convert_fusion.1
  24.8 29.9 %all-gather.2.cloned.1.call-done = bf16[8192,128]{0,1:T(8,128)(2,1)} async-done(((bf16[512,128]{0,1:T(8,128)(2,1)}), bf16[8192,128]{0,1:T(8,128)(2,1)}) %all-gather.2.cloned.1.call-update) | async-done | bytes 2097168 | tf_op jit(solution)/shard_map/all_gather | solution.py:21
  54.7 9.0 %fusion.5 = f32[32,2,64,64]{2,3,0,1:T(8,128)} fusion(bf16[2,256,64]{1,2,0:T(8,128)(2,1)S(1)} %convolution_convert_fusion.1, bf16[256,32]{0,1:T(8,128)(2,1)S(1)} %and_convert_fusion, bf16[2,256,8192]{2,1,0:T(8,128)(2,1)} %param.7, bf16[8192,2,64]{0,2,1:T(8,128)(2,1)} %bitcast.65), kind=kOutput, calls=%fused_computation.10 | convolution fusion | flops 675315712 | bytes 11616256 | tf_op jit(solution)/shard_map/ltsa,ltb->slab/dot_general | solution.py:41
  63.7 0.0 copy-start.1
  63.7 1.9 %copy.13 = f32[32,2,64,64]{3,2,1,0:T(8,128)S(1)} copy(f32[32,2,64,64]{2,3,0,1:T(8,128)} %fusion.5) | data formatting | bytes 2097152 | tf_op jit(solution)/shard_map/ltsa,ltb->slab/transpose | solution.py:41
  65.6 1.6 reshape.108
  67.2 72.1 %all-reduce.1 = bf16[32,8192]{1,0:T(8,128)(2,1)S(1)} all-reduce(f32[32,8192]{1,0:T(8,128)} %reshape.108), channel_id=1, replica_groups=mesh['groups'=2,'seq'=16] {'seq'}, use_global_device_ids=true, to_apply=%region_1.2 | all-reduce | flops 262144 | bytes 1572864 | tf_op jit(solution)/shard_map/psum | solution.py:47
  139.3 0.4 reshape.109
  139.7 0.0 copy-done.1
  139.7 0.9 convolution_convert_fusion
  140.6 1.8 %constant_dynamic-slice_fusion.4 = (bf16[32,1,4096]{2,1,0:T(2,128)(2,1)S(1)}, bf16[32,1,4096]{2,1,0:T(2,128)(2,1)S(1)}, bf16[32,1,4096]{2,1,0:T(2,128)(2,1)S(1)}) fusion(bf16[32,2,4096]{2,1,0:T(2,128)(2,1)S(1)} %reshape.109, s32[]{:T(128)S(6)} %select_n.49, s32[]{:T(128)S(6)} %select_n.52, s32[]{:T(128)S(6)} %select_n.55), kind=kLoop, calls=%fused_computation.28 | loop fusion | bytes 1572876 | tf_op jit(solution)/shard_map/jit(dynamic_index_in_dim)/dynamic_slice | solution.py:58
  142.4 0.2 constant_dynamic-slice_fusion.5
  142.6 0.7 fusion.2
  143.4 2.7 %fusion.1 = f32[1,256,4096]{2,1,0:T(8,128)} fusion(bf16[32,1,4096]{2,1,0:T(2,128)(2,1)S(1)} %get-tuple-element.6, bf16[32,1,256]{2,1,0:T(2,128)(2,1)S(1)} %get-tuple-element.4), kind=kOutput, calls=%fused_computation.5 | convolution fusion | flops 68157440 | bytes 4472832 | tf_op jit(solution)/shard_map/dot_general | solution.py:60
  146.1 2.7 %fusion = f32[1,256,4096]{2,1,0:T(8,128)} fusion(bf16[32,1,4096]{2,1,0:T(2,128)(2,1)S(1)} %get-tuple-element.7, bf16[32,1,256]{2,1,0:T(2,128)(2,1)S(1)} %get-tuple-element.3), kind=kOutput, calls=%fused_computation.3 | convolution fusion | flops 68157440 | bytes 4472832 | tf_op jit(solution)/shard_map/dot_general | solution.py:60
  148.8 9.6 %pad_maximum_fusion = f32[3,256,4096]{2,1,0:T(8,128)} fusion(f32[1,256,4096]{2,1,0:T(8,128)} %fusion, f32[1,256,4096]{2,1,0:T(8,128)} %fusion.1, f32[1,256,4096]{2,1,0:T(8,128)S(1)} %fusion.2), kind=kLoop, calls=%fused_computation | loop fusion | flops 6291456 | bytes 25165824 | tf_op jit(solution)/shard_map/stack | solution.py:64
  (2 shorter events, 0.0 us)
Async XLA Ops:
  7.2 17.2 %copy-start = (bf16[2,256,1024]{2,1,0:T(8,128)(2,1)S(1)}, bf16[2,256,1024]{2,1,0:T(8,128)(2,1)}, u32[]{:S(2)}) copy-start(bf16[2,256,1024]{2,1,0:T(8,128)(2,1)} %param.8) | copy-start | bytes 3145732
  7.2 47.5 %all-gather.2.cloned.1.call-start = ((), (), s32[]{:S(2)}) async-start(), calls=%async_computation | async-start | bytes 2228224 | tf_op jit(solution)/shard_map/all_gather | solution.py:21
  63.7 76.0 %copy-start.1 = (s32[32]{0:T(128)S(1)}, s32[32]{0:T(128)}, u32[]{:S(2)}) copy-start(s32[32]{0:T(128)} %param.12) | copy-start | bytes 388
Sparse Core Ops, SparseCore 0:
  10.7 43.8 all-gather.1
where the time goes:
time: 166 us; the launch traced here: 165 us
  blocking collectives  72.1 us (43%)
  waiting for transfers between devices  29.9 us (18%)
  between operations  25.1 us (15%)
  matrix products  16.4 us (10%)
  local copies, waits for them, and re-layouts  11.1 us (7%)
  other arithmetic  10.5 us (6%)
    psum x1, blocking collectives, shards(): totals = lax.psum(term, 'seq')  72.1 us
    all_gather x1, waiting for transfers between devices, shards(): piece = lax.all_gather(proj_in, 'seq', axis=0, tiled=True)  29.9 us
    another operation x1, other arithmetic, shards(): covariance = jnp.stack(tiles)  9.56 us
    dot_general x1, matrix products, shards(): jnp.einsum('ltsa,ltb->slab', weighted, px_half, preferred_element_type=jn...  9.01 us
    dot_general x3, matrix products, shards(): lax.dot_general(left_band, right, (((0,), (0,)), ((), ())), preferred_ele...  6.13 us
  transfers between devices with their start and end apart: 1, of which 1 were waited for; matrix products, arithmetic and copies ran while one was open for 3% of the time, Pallas kernels for 0%

commit v1 on v0

v1 whole, which is shorter than its diff:
```python
import functools

import jax
import jax.numpy as jnp
from jax import lax
from jax.experimental import pallas as pl
from jax.experimental.pallas import tpu as pltpu
from jax.sharding import PartitionSpec as P

CAP = 2
MIB = 1 << 20


def digits_of(devices):
    if devices % 16 == 0 and devices >= 64:
        return ((8, devices // 8), (2, 4), (1, 2))
    if devices % 4 == 0 and devices > 4:
        return ((4, devices // 4), (2, 2), (1, 2))
    return ((1, devices),)


def shifted(index, digits, shift):
    out = index
    for (stride, size), step in zip(digits, shift):
        digit = (index // stride) % size
        out = out + ((digit + step) % size - digit) * stride
    return out


def send(value, devices, digits, shift):
    perm = [(i, shifted(i, digits, shift)) for i in range(devices)]
    return lax.ppermute(value, "seq", perm)


def gather(block, devices, digits):
    held = {(0,) * len(digits): block}
    for level, (_, size) in enumerate(digits):
        new = dict(held)
        for step in range(1, size):
            move = tuple(step if i == level else 0 for i in range(len(digits)))
            for key, value in held.items():
                new[tuple(a + b for a, b in zip(key, move))] = send(value, devices, digits, move)
        held = new
    return held


def back(me, digits, shift):
    out = me
    for (stride, size), step in zip(digits, shift):
        digit = (me // stride) % size
        out = out + ((digit + (size - step)) % size - digit) * stride
    return out


def grads_kernel(digits, shifts, per_part, rows_all, *refs):
    count = len(shifts)
    blocks = refs[:count]
    acts, cots, proj_out, lengths = refs[count:count + 4]
    outs = refs[count + 4:count + 4 + per_part]
    weights, held, sems = refs[count + 4 + per_part:]
    layers, rows, width = held.shape
    wide = proj_out.shape[1]
    width_k = wide // layers
    square = width_k * width_k
    lanes = square // per_part
    pieces = sems.shape[0]
    step = width // pieces
    me = lax.axis_index("seq")

    def copy(i):
        at = pl.ds(i * step, step)
        return pltpu.make_async_copy(acts.at[:, :, at], held.at[:, :, at], sems.at[i])

    for i in range(pieces):
        copy(i).start()
    tall = blocks[0].shape[0]
    for shift, block in zip(shifts, blocks):
        owner = back(me, digits, shift)
        weights[pl.ds(pl.multiple_of(owner * tall, tall), tall), :] = block[...]
    lane = lax.broadcasted_iota(jnp.int32, (rows, wide), 1)
    pg = [
        jnp.dot(cots[l], proj_out[...], preferred_element_type=jnp.float32).astype(jnp.bfloat16)
        for l in range(layers)
    ]
    total = [jnp.zeros((rows, wide), jnp.float32) for _ in range(layers)]
    for i in range(pieces):
        copy(i).wait()
        at = pl.ds(i * step, step)
        for l in range(layers):
            total[l] = total[l] + jnp.dot(held[l, :, at], weights[at, :], preferred_element_type=jnp.float32)
    repeat = lanes // width_k
    px = []
    for l in range(layers):
        own = total[l][:, l * width_k:(l + 1) * width_k].astype(jnp.bfloat16)
        px.append(jnp.concatenate([own] * repeat, axis=1))
    row = me // per_part
    first = (me % per_part) * rows
    sizes = lengths[pl.ds(row, 1), :]
    per_row = sizes.shape[1]
    upto = lax.broadcasted_iota(jnp.int32, (per_row, per_row), 1)
    which = lax.broadcasted_iota(jnp.int32, (per_row, per_row), 0)
    sizes = jnp.broadcast_to(sizes, (per_row, per_row))
    ends = jnp.sum(jnp.where(upto <= which, sizes, 0), axis=1, keepdims=True)
    starts = jnp.sum(jnp.where(upto < which, sizes, 0), axis=1, keepdims=True)
    position = first + lax.broadcasted_iota(jnp.int32, (per_row, rows), 1)
    member = ((position >= starts) & (position < ends)).astype(jnp.float32).astype(jnp.bfloat16)
    source = lax.broadcasted_iota(jnp.int32, (wide, lanes), 0)
    target = lax.broadcasted_iota(jnp.int32, (wide, lanes), 1) // width_k
    for k in range(per_part):
        part = (me + k) % per_part
        for l in range(layers):
            spread = (source == target + (l * width_k + part * repeat)).astype(jnp.float32).astype(jnp.bfloat16)
            left = jnp.dot(pg[l], spread, preferred_element_type=jnp.float32).astype(jnp.bfloat16)
            value = jnp.dot(member, left * px[l], preferred_element_type=jnp.float32)
            outs[k][:, l * lanes:(l + 1) * lanes] = value.astype(jnp.bfloat16)


def covariance_kernel(digits, shifts, per_part, band, *refs):
    count = len(shifts)
    blocks = refs[:count]
    slots, pairs = refs[count:count + 2]
    logged, out = refs[count + 2:count + 4]
    right = refs[count + 4]
    seqs, full = right.shape
    square = out.shape[2] * pl.num_programs(1)
    layers = full // square
    lanes = square // per_part
    per_row = blocks[0].shape[0]
    cols = out.shape[2]
    me = lax.axis_index("seq")

    @pl.when((pl.program_id(0) == 0) & (pl.program_id(1) == 0))
    def _():
        for shift, block in zip(shifts, blocks):
            owner = back(me, digits, shift)
            row = pl.ds(pl.multiple_of((owner // per_part) * per_row, per_row), per_row)
            for l in range(layers):
                at = pl.multiple_of(l * square + (owner % per_part) * lanes, lanes)
                right[row, pl.ds(at, lanes)] = block[:, l * lanes:(l + 1) * lanes]
        own = me * CAP + lax.broadcasted_iota(jnp.int32, (CAP, seqs), 0)
        picker = (jnp.broadcast_to(slots[...], (CAP, seqs)) == own).astype(jnp.float32).astype(jnp.bfloat16)
        logged[...] = jnp.dot(picker, right[...], preferred_element_type=jnp.float32).astype(jnp.bfloat16)

    pair = pl.program_id(0)
    if band % 128 == 0:
        at = pl.multiple_of(pairs[pair, 0] * square + me * band, band)
        left = right[:, pl.ds(at, band)]
    else:
        offset = me * band
        at = pl.multiple_of(pairs[pair, 0] * square + (offset // 128) * 128, 128)
        source = lax.broadcasted_iota(jnp.int32, (128, band), 0)
        target = lax.broadcasted_iota(jnp.int32, (128, band), 1)
        pick = (source == target + offset % 128).astype(jnp.float32).astype(jnp.bfloat16)
        left = jnp.dot(right[:, pl.ds(at, 128)], pick, preferred_element_type=jnp.float32).astype(jnp.bfloat16)
    at = pl.multiple_of(pairs[pair, 1] * square + pl.program_id(1) * cols, cols)
    product = lax.dot_general(
        left, right[:, pl.ds(at, cols)], (((0,), (0,)), ((), ())), preferred_element_type=jnp.float32
    )
    out[0] = product / jnp.float32(seqs)


def shards(acts, cots, proj_in, proj_out, lengths, slots, pairs):
    layers, rows, width = acts.shape
    wide = proj_out.shape[1]
    square = (wide // layers) ** 2
    devices = lax.axis_size("seq")
    rows_all, per_row = lengths.shape
    seqs = slots.shape[0]
    npair = pairs.shape[0]
    per_part = devices // rows_all
    lanes = square // per_part
    band = square // devices
    digits = digits_of(devices)
    vmem = pl.BlockSpec(memory_space=pltpu.VMEM)
    smem = pl.BlockSpec(memory_space=pltpu.SMEM)

    held = gather(proj_in, devices, digits)
    shifts = tuple(held)
    pieces = 16
    parts = pl.pallas_call(
        functools.partial(grads_kernel, digits, shifts, per_part, rows_all),
        out_shape=[jax.ShapeDtypeStruct((per_row, layers * lanes), jnp.bfloat16)] * per_part,
        in_specs=[vmem] * len(shifts) + [pl.BlockSpec(memory_space=pl.ANY), vmem, vmem, vmem],
        out_specs=[vmem] * per_part,
        scratch_shapes=[
            pltpu.VMEM((width, wide), jnp.bfloat16),
            pltpu.VMEM((layers, rows, width), jnp.bfloat16),
            pltpu.SemaphoreType.DMA((pieces,)),
        ],
        compiler_params=pltpu.CompilerParams(vmem_limit_bytes=40 * MIB),
        name="grads",
    )(*held.values(), acts, cots, proj_out, lengths)

    total = parts[0].astype(jnp.float32)
    for k in range(1, per_part):
        perm = [(i, i - i % per_part + (i + k) % per_part) for i in range(devices)]
        total = total + lax.ppermute(parts[k], "seq", perm).astype(jnp.float32)
    summed = gather(total.astype(jnp.bfloat16), devices, digits)
    shifts = tuple(summed)
    cols = 1024
    return pl.pallas_call(
        functools.partial(covariance_kernel, digits, shifts, per_part, band),
        grid=(npair, square // cols),
        out_shape=[
            jax.ShapeDtypeStruct((CAP, layers * square), jnp.bfloat16),
            jax.ShapeDtypeStruct((npair, band, square), jnp.float32),
        ],
        in_specs=[vmem] * len(shifts) + [vmem, smem],
        out_specs=[
            pl.BlockSpec((CAP, layers * square), lambda p, q: (0, 0)),
            pl.BlockSpec((1, band, cols), lambda p, q: (p, 0, q)),
        ],
        scratch_shapes=[pltpu.VMEM((seqs, layers * square), jnp.bfloat16)],
        compiler_params=pltpu.CompilerParams(vmem_limit_bytes=40 * MIB),
        name="covariance",
    )(*summed.values(), slots.reshape(1, seqs), pairs)


def solution(mesh):
    in_specs = (
        P(None, ("groups", "seq"), None),
        P(None, ("groups", "seq"), None),
        P("seq", None),
        P(),
        P("groups", None),
        P("groups"),
        P(),
    )
    out_specs = (P(("groups", "seq"), None), P("groups", "seq", None))
    return jax.shard_map(shards, mesh=mesh, in_specs=in_specs, out_specs=out_specs, check_vma=False)
```

time: 166 us -> 99.4 us (0.60)
  blocking collectives: 72.1 us -> 0 us
  starting transfers between devices: 0.04 us -> 35.7 us
  between operations: 25.1 us -> 0.73 us
  Pallas kernels: 0 us -> 22.8 us
  matrix products: 16.4 us -> 0 us
  other arithmetic: 10.5 us -> 0.08 us
  local copies, waits for them, and re-layouts: 11.1 us -> 8.53 us
    psum x1 -> x0, blocking collectives: 72.1 us -> none  [shards(): totals = lax.psum(term, 'seq')]
    ppermute x0 -> x45, starting transfers between devices: none -> 35.7 us  [the longest x30 19.4 us: send(): return lax.ppermute(value, 'seq', perm)]
    ppermute x0 -> x45, waiting for transfers between devices: none -> 31.2 us  [the longest x30 25.6 us: send(): return lax.ppermute(value, 'seq', perm)]
    all_gather x1 -> x0, waiting for transfers between devices: 29.9 us -> none  [shards(): piece = lax.all_gather(proj_in, 'seq', axis=0, tiled=True)]
    pallas_call x0 -> x2, Pallas kernels: none -> 22.8 us  [the longest x1 13.6 us: shards(): pl.pallas_call(functools.partial(grads_kernel, digits, shifts, per_part,...]
    dot_general x6 -> x0, matrix products: 16.4 us -> none  [the longest x1 9.01 us: shards(): jnp.einsum('ltsa,ltb->slab', weighted, px_half, preferred_element_type=jn...]
    another operation x3 -> x0, other arithmetic: 9.73 us -> none  [the longest x1 9.56 us: shards(): covariance = jnp.stack(tiles)]
    unnamed x6 -> x13, local copies, waits for them, and re-layouts: 2.85 us -> 8.53 us
  transfers between devices with their start and end apart: 1 -> 45, of which waited for: 1 -> 16; matrix products, arithmetic and copies ran while one was open for 3% -> 1% of each run, Pallas kernels for 0% -> 0%
where the time goes in v1:
time: 99.4 us; the launch traced here: 99.1 us
  starting transfers between devices  35.7 us (36%)
  waiting for transfers between devices  31.2 us (31%)
  Pallas kernels  22.8 us (23%)
  local copies, waits for them, and re-layouts  8.53 us (9%)
    ppermute x30, waiting for transfers between devices, send(): return lax.ppermute(value, 'seq', perm)  25.6 us
    ppermute x30, starting transfers between devices, send(): return lax.ppermute(value, 'seq', perm)  19.4 us
    ppermute x15, starting transfers between devices, shards(): total = total + lax.ppermute(parts[k], 'seq', perm).astype(jnp.float32)  16.4 us
    pallas_call x1, Pallas kernels, shards(): pl.pallas_call(functools.partial(grads_kernel, digits, shifts, per_part,...  13.6 us
    pallas_call x1, Pallas kernels, shards(): pl.pallas_call(functools.partial(covariance_kernel, digits, shifts, per_p...  9.2 us
    unnamed x13, local copies, waits for them, and re-layouts  8.53 us
    ppermute x15, waiting for transfers between devices, shards(): total = total + lax.ppermute(parts[k], 'seq', perm).astype(jnp.float32)  5.66 us
  transfers between devices with their start and end apart: 45, of which 16 were waited for; matrix products, arithmetic and copies ran while one was open for 1% of the time, Pallas kernels for 0%

profile of v1, /device:TPU:0, one launch (start us, length us, event | category | flops | bytes accessed | tf_op | source)
XLA Modules:
  0.0 99.1 jit_solution(225197702273396493)
XLA Ops:
  0.6 3.0 %collective-permute-start.3 = (bf16[512,128]{1,0:T(8,128)(2,1)}, bf16[512,128]{1,0:T(8,128)(2,1)S(1)}, u32[]{:S(2)}, u32[]{:S(2)}) collective-permute-start(bf16[512,128]{1,0:T(8,128)(2,1)} %refs_0_.1), channel_id=1, source_target_pairs={{0,2},{1,3},{2,0},{3,1},{4,6},{5,7},{6,4},{7,5},{8,10},{9,11},{10,... | collective-permute-start | bytes 393224 | tf_op jit(solution)/shard_map/ppermute | solution.py:32
  3.6 3.6 %collective-permute-start.2 = (bf16[512,128]{1,0:T(8,128)(2,1)}, bf16[512,128]{1,0:T(8,128)(2,1)S(1)}, u32[]{:S(2)}, u32[]{:S(2)}) collective-permute-start(bf16[512,128]{1,0:T(8,128)(2,1)} %refs_0_.1), channel_id=1, source_target_pairs={{0,12},{1,13},{2,14},{3,15},{4,0},{5,1},{6,2},{7,3},{8,4},{9,5},{1... | collective-permute-start | bytes 393224 | tf_op jit(solution)/shard_map/ppermute | solution.py:32
  7.2 1.0 %collective-permute-start = (bf16[512,128]{1,0:T(8,128)(2,1)}, bf16[512,128]{1,0:T(8,128)(2,1)S(1)}, u32[]{:S(2)}, u32[]{:S(2)}) collective-permute-start(bf16[512,128]{1,0:T(8,128)(2,1)} %refs_0_.1), channel_id=1, source_target_pairs={{0,4},{1,5},{2,6},{3,7},{4,8},{5,9},{6,10},{7,11},{8,12},{9,13},{1... | collective-permute-start | bytes 393224 | tf_op jit(solution)/shard_map/ppermute | solution.py:32
  8.8 2.7 %collective-permute-done.2.refs_3_ = bf16[512,128]{1,0:T(8,128)(2,1)S(1)} collective-permute-done((bf16[512,128]{1,0:T(8,128)(2,1)}, bf16[512,128]{1,0:T(8,128)(2,1)S(1)}, u32[]{:S(2)}, u32[]{:S(2)}) %collective-permute-start.2) | collective-permute-done | bytes 131104 | tf_op jit(solution)/shard_map/ppermute | solution.py:32
  11.5 6.8 %collective-permute-done.1.refs_2_ = bf16[512,128]{1,0:T(8,128)(2,1)S(1)} collective-permute-done((bf16[512,128]{1,0:T(8,128)(2,1)}, bf16[512,128]{1,0:T(8,128)(2,1)S(1)}, u32[]{:S(2)}, u32[]{:S(2)}) %collective-permute-start.1) | collective-permute-done | bytes 131104 | tf_op jit(solution)/shard_map/ppermute | solution.py:32
  18.8 1.5 %collective-permute-start.5 = (bf16[512,128]{1,0:T(8,128)(2,1)S(1)}, bf16[512,128]{1,0:T(8,128)(2,1)S(1)}, u32[]{:S(2)}, u32[]{:S(2)}) collective-permute-start(bf16[512,128]{1,0:T(8,128)(2,1)S(1)} %collective-permute-done.1.refs_2_), channel_id=1, source_target_pairs={{0,2},{1,3},{2,0},{3,1},{4,6},{5,7},{6,4},{7,5},{8,10},{9,11},{10,... | collective-permute-start | bytes 393224 | tf_op jit(solution)/shard_map/ppermute | solution.py:32
  21.3 3.3 %collective-permute-done.6.refs_7_ = bf16[512,128]{1,0:T(8,128)(2,1)S(1)} collective-permute-done((bf16[512,128]{1,0:T(8,128)(2,1)S(1)}, bf16[512,128]{1,0:T(8,128)(2,1)S(1)}, u32[]{:S(2)}, u32[]{:S(2)}) %collective-permute-start.6) | collective-permute-done | bytes 131104 | tf_op jit(solution)/shard_map/ppermute | solution.py:32
  24.7 2.4 %collective-permute-done.5.refs_6_ = bf16[512,128]{1,0:T(8,128)(2,1)S(1)} collective-permute-done((bf16[512,128]{1,0:T(8,128)(2,1)S(1)}, bf16[512,128]{1,0:T(8,128)(2,1)S(1)}, u32[]{:S(2)}, u32[]{:S(2)}) %collective-permute-start.5) | collective-permute-done | bytes 131104 | tf_op jit(solution)/shard_map/ppermute | solution.py:32
  27.1 1.4 %collective-permute-done.4.refs_5_ = bf16[512,128]{1,0:T(8,128)(2,1)S(1)} collective-permute-done((bf16[512,128]{1,0:T(8,128)(2,1)S(1)}, bf16[512,128]{1,0:T(8,128)(2,1)S(1)}, u32[]{:S(2)}, u32[]{:S(2)}) %collective-permute-start.4) | collective-permute-done | bytes 131104 | tf_op jit(solution)/shard_map/ppermute | solution.py:32
  28.5 1.3 %collective-permute-done.12.refs_13_ = bf16[512,128]{1,0:T(8,128)(2,1)S(1)} collective-permute-done((bf16[512,128]{1,0:T(8,128)(2,1)S(1)}, bf16[512,128]{1,0:T(8,128)(2,1)S(1)}, u32[]{:S(2)}, u32[]{:S(2)}) %collective-permute-start.12) | collective-permute-done | bytes 131104 | tf_op jit(solution)/shard_map/ppermute | solution.py:32
  29.9 3.4 %copy-done = bf16[2,256,8192]{2,1,0:T(8,128)(2,1)S(1)} copy-done((bf16[2,256,8192]{2,1,0:T(8,128)(2,1)S(1)}, bf16[2,256,8192]{2,1,0:T(8,128)(2,1)}, u32[]{:S(2)}) %copy-start) | copy-done | bytes 8388632
  33.2 1.2 %copy-done.1 = bf16[2,256,1024]{2,1,0:T(8,128)(2,1)S(1)} copy-done((bf16[2,256,1024]{2,1,0:T(8,128)(2,1)S(1)}, bf16[2,256,1024]{2,1,0:T(8,128)(2,1)}, u32[]{:S(2)}) %copy-start.1) | copy-done | bytes 1048600
  34.5 0.9 copy-done.2
  37.0 13.6 %grads.1 = (bf16[32,512]{1,0:T(8,128)(2,1)S(1)}, bf16[32,512]{1,0:T(8,128)(2,1)S(1)}, bf16[32,512]{1,0:T(8,128)(2,1)S(1)}, bf16[32,512]{1,0:T(8,128)(2,1)S(1)}, ...) custom-call(bf16[512,128]{1,0:T(8,128)(2,1)S(1)} %copy-done.3, ...), custom_call_target="tpu_custom_call" | custom-call | tf_op jit(solution)/shard_map/grads/pallas_call | solution.py:180
  51.4 1.2 %collective-permute-start.18 = (bf16[32,512]{1,0:T(8,128)(2,1)S(1)}, bf16[32,512]{1,0:T(8,128)(2,1)S(1)}, u32[]{:S(2)}, u32[]{:S(2)}) collective-permute-start(bf16[32,512]{1,0:T(8,128)(2,1)S(1)} %get-tuple-element.22), channel_id=1, source_target_pairs={{0,4},{1,5},{2,6},{3,7},{4,8},{5,9},{6,10},{7,11},{8,12},{9,13},{1... | collective-permute-start | bytes 98312 | tf_op jit(solution)/shard_map/ppermute | solution.py:197
  52.9 3.7 %collective-permute-done.15 = bf16[32,512]{1,0:T(8,128)(2,1)S(1)} collective-permute-done((bf16[32,512]{1,0:T(8,128)(2,1)S(1)}, bf16[32,512]{1,0:T(8,128)(2,1)S(1)}, u32[]{:S(2)}, u32[]{:S(2)}) %collective-permute-start.15) | collective-permute-done | bytes 32800 | tf_op jit(solution)/shard_map/ppermute | solution.py:197
  57.7 1.1 %collective-permute-start.21 = (bf16[32,512]{1,0:T(8,128)(2,1)S(1)}, bf16[32,512]{1,0:T(8,128)(2,1)S(1)}, u32[]{:S(2)}, u32[]{:S(2)}) collective-permute-start(bf16[32,512]{1,0:T(8,128)(2,1)S(1)} %get-tuple-element.25), channel_id=1, source_target_pairs={{0,7},{1,8},{2,9},{3,10},{4,11},{5,12},{6,13},{7,14},{8,15},{9,0},... | collective-permute-start | bytes 98312 | tf_op jit(solution)/shard_map/ppermute | solution.py:197
  58.8 1.8 %collective-permute-start.22 = (bf16[32,512]{1,0:T(8,128)(2,1)S(1)}, bf16[32,512]{1,0:T(8,128)(2,1)S(1)}, u32[]{:S(2)}, u32[]{:S(2)}) collective-permute-start(bf16[32,512]{1,0:T(8,128)(2,1)S(1)} %get-tuple-element.26), channel_id=1, source_target_pairs={{0,8},{1,9},{2,10},{3,11},{4,12},{5,13},{6,14},{7,15},{8,0},{9,1},... | collective-permute-start | bytes 98312 | tf_op jit(solution)/shard_map/ppermute | solution.py:197
  60.7 2.7 %collective-permute-start.24 = (bf16[32,512]{1,0:T(8,128)(2,1)S(1)}, bf16[32,512]{1,0:T(8,128)(2,1)S(1)}, u32[]{:S(2)}, u32[]{:S(2)}) collective-permute-start(bf16[32,512]{1,0:T(8,128)(2,1)S(1)} %get-tuple-element.28), channel_id=1, source_target_pairs={{0,10},{1,11},{2,12},{3,13},{4,14},{5,15},{6,0},{7,1},{8,2},{9,3},... | collective-permute-start | bytes 98312 | tf_op jit(solution)/shard_map/ppermute | solution.py:197
  63.4 3.5 %collective-permute-start.25 = (bf16[32,512]{1,0:T(8,128)(2,1)S(1)}, bf16[32,512]{1,0:T(8,128)(2,1)S(1)}, u32[]{:S(2)}, u32[]{:S(2)}) collective-permute-start(bf16[32,512]{1,0:T(8,128)(2,1)S(1)} %get-tuple-element.29), channel_id=1, source_target_pairs={{0,11},{1,12},{2,13},{3,14},{4,15},{5,0},{6,1},{7,2},{8,3},{9,4},{... | collective-permute-start | bytes 98312 | tf_op jit(solution)/shard_map/ppermute | solution.py:197
  66.9 1.2 %collective-permute-start.27 = (bf16[32,512]{1,0:T(8,128)(2,1)S(1)}, bf16[32,512]{1,0:T(8,128)(2,1)S(1)}, u32[]{:S(2)}, u32[]{:S(2)}) collective-permute-start(bf16[32,512]{1,0:T(8,128)(2,1)S(1)} %get-tuple-element.31), channel_id=1, source_target_pairs={{0,13},{1,14},{2,15},{3,0},{4,1},{5,2},{6,3},{7,4},{8,5},{9,6},{10... | collective-permute-start | bytes 98312 | tf_op jit(solution)/shard_map/ppermute | solution.py:197
  68.1 1.5 %collective-permute-start.28 = (bf16[32,512]{1,0:T(8,128)(2,1)S(1)}, bf16[32,512]{1,0:T(8,128)(2,1)S(1)}, u32[]{:S(2)}, u32[]{:S(2)}) collective-permute-start(bf16[32,512]{1,0:T(8,128)(2,1)S(1)} %get-tuple-element.32), channel_id=1, source_target_pairs={{0,14},{1,15},{2,0},{3,1},{4,2},{5,3},{6,4},{7,5},{8,6},{9,7},{10,... | collective-permute-start | bytes 98312 | tf_op jit(solution)/shard_map/ppermute | solution.py:197
  69.6 1.4 %collective-permute-start.29 = (bf16[32,512]{1,0:T(8,128)(2,1)S(1)}, bf16[32,512]{1,0:T(8,128)(2,1)S(1)}, u32[]{:S(2)}, u32[]{:S(2)}) collective-permute-start(bf16[32,512]{1,0:T(8,128)(2,1)S(1)} %get-tuple-element.33), channel_id=1, source_target_pairs={{0,15},{1,0},{2,1},{3,2},{4,3},{5,4},{6,5},{7,6},{8,7},{9,8},{10,9... | collective-permute-start | bytes 98312 | tf_op jit(solution)/shard_map/ppermute | solution.py:197
  71.0 1.0 %collective-permute-done.28 = bf16[32,512]{1,0:T(8,128)(2,1)S(1)} collective-permute-done((bf16[32,512]{1,0:T(8,128)(2,1)S(1)}, bf16[32,512]{1,0:T(8,128)(2,1)S(1)}, u32[]{:S(2)}, u32[]{:S(2)}) %collective-permute-start.28) | collective-permute-done | bytes 32800 | tf_op jit(solution)/shard_map/ppermute | solution.py:197
  72.7 2.2 %collective-permute-start.33 = (bf16[32,512]{1,0:T(8,128)(2,1)S(1)}, bf16[32,512]{1,0:T(8,128)(2,1)S(1)}, u32[]{:S(2)}, u32[]{:S(2)}) collective-permute-start(bf16[32,512]{1,0:T(8,128)(2,1)S(1)} %add_convert_fusion.refs_0_), channel_id=1, source_target_pairs={{0,2},{1,3},{2,0},{3,1},{4,6},{5,7},{6,4},{7,5},{8,10},{9,11},{10,... | collective-permute-start | bytes 98312 | tf_op jit(solution)/shard_map/ppermute | solution.py:32
  74.9 2.1 %collective-permute-start.32 = (bf16[32,512]{1,0:T(8,128)(2,1)S(1)}, bf16[32,512]{1,0:T(8,128)(2,1)S(1)}, u32[]{:S(2)}, u32[]{:S(2)}) collective-permute-start(bf16[32,512]{1,0:T(8,128)(2,1)S(1)} %add_convert_fusion.refs_0_), channel_id=1, source_target_pairs={{0,12},{1,13},{2,14},{3,15},{4,0},{5,1},{6,2},{7,3},{8,4},{9,5},{1... | collective-permute-start | bytes 98312 | tf_op jit(solution)/shard_map/ppermute | solution.py:32
  79.0 1.0 collective-permute-start.36
  79.9 2.5 %collective-permute-done.31.refs_2_ = bf16[32,512]{1,0:T(8,128)(2,1)S(1)} collective-permute-done((bf16[32,512]{1,0:T(8,128)(2,1)S(1)}, bf16[32,512]{1,0:T(8,128)(2,1)S(1)}, u32[]{:S(2)}, u32[]{:S(2)}) %collective-permute-start.31) | collective-permute-done | bytes 32800 | tf_op jit(solution)/shard_map/ppermute | solution.py:32
  82.8 1.4 %collective-permute-done.30.refs_1_ = bf16[32,512]{1,0:T(8,128)(2,1)S(1)} collective-permute-done((bf16[32,512]{1,0:T(8,128)(2,1)S(1)}, bf16[32,512]{1,0:T(8,128)(2,1)S(1)}, u32[]{:S(2)}, u32[]{:S(2)}) %collective-permute-start.30) | collective-permute-done | bytes 32800 | tf_op jit(solution)/shard_map/ppermute | solution.py:32
  85.0 1.3 %collective-permute-done.35.refs_6_ = bf16[32,512]{1,0:T(8,128)(2,1)S(1)} collective-permute-done((bf16[32,512]{1,0:T(8,128)(2,1)S(1)}, bf16[32,512]{1,0:T(8,128)(2,1)S(1)}, u32[]{:S(2)}, u32[]{:S(2)}) %collective-permute-start.35) | collective-permute-done | bytes 32800 | tf_op jit(solution)/shard_map/ppermute | solution.py:32
  86.3 1.7 %collective-permute-done.34.refs_5_ = bf16[32,512]{1,0:T(8,128)(2,1)S(1)} collective-permute-done((bf16[32,512]{1,0:T(8,128)(2,1)S(1)}, bf16[32,512]{1,0:T(8,128)(2,1)S(1)}, u32[]{:S(2)}, u32[]{:S(2)}) %collective-permute-start.34) | collective-permute-done | bytes 32800 | tf_op jit(solution)/shard_map/ppermute | solution.py:32
  89.9 9.2 %covariance.1 = (bf16[2,8192]{1,0:T(2,128)(2,1)}, f32[3,256,4096]{2,1,0:T(8,128)}) custom-call(bf16[32,512]{1,0:T(8,128)(2,1)S(1)} %add_convert_fusion.refs_0_, bf16[32,512]{1,0:T(8,128)(2,1)S(1)} %collective-permute-done.30.refs_1_, bf16[32,512]{1,0:T(8,128)(2,1)S(1)} %collective-permute-done.31.refs_2_, ...), custom_call_target="tpu_custom_call" | custom-call | tf_op jit(solution)/shard_map/covariance/pallas_call | solution.py:201
  (74 shorter events, 11.7 us)
Async XLA Ops:
  0.6 7.6 %collective-permute-start.3 = (bf16[512,128]{1,0:T(8,128)(2,1)}, bf16[512,128]{1,0:T(8,128)(2,1)S(1)}, u32[]{:S(2)}, u32[]{:S(2)}) collective-permute-start(bf16[512,128]{1,0:T(8,128)(2,1)} %refs_0_.1), channel_id=1, source_target_pairs={{0,2},{1,3},{2,0},{3,1},{4,6},{5,7},{6,4},{7,5},{8,10},{9,11},{10,... | collective-permute-start | bytes 393224 | tf_op jit(solution)/shard_map/ppermute | solution.py:32
  3.6 7.9 %collective-permute-start.2 = (bf16[512,128]{1,0:T(8,128)(2,1)}, bf16[512,128]{1,0:T(8,128)(2,1)S(1)}, u32[]{:S(2)}, u32[]{:S(2)}) collective-permute-start(bf16[512,128]{1,0:T(8,128)(2,1)} %refs_0_.1), channel_id=1, source_target_pairs={{0,12},{1,13},{2,14},{3,15},{4,0},{5,1},{6,2},{7,3},{8,4},{9,5},{1... | collective-permute-start | bytes 393224 | tf_op jit(solution)/shard_map/ppermute | solution.py:32
  7.2 11.0 %collective-permute-start.1 = (bf16[512,128]{1,0:T(8,128)(2,1)}, bf16[512,128]{1,0:T(8,128)(2,1)S(1)}, u32[]{:S(2)}, u32[]{:S(2)}) collective-permute-start(bf16[512,128]{1,0:T(8,128)(2,1)} %refs_0_.1), channel_id=1, source_target_pairs={{0,8},{1,9},{2,10},{3,11},{4,12},{5,13},{6,14},{7,15},{8,0},{9,1},... | collective-permute-start | bytes 393224 | tf_op jit(solution)/shard_map/ppermute | solution.py:32
  7.2 11.6 %collective-permute-start = (bf16[512,128]{1,0:T(8,128)(2,1)}, bf16[512,128]{1,0:T(8,128)(2,1)S(1)}, u32[]{:S(2)}, u32[]{:S(2)}) collective-permute-start(bf16[512,128]{1,0:T(8,128)(2,1)} %refs_0_.1), channel_id=1, source_target_pairs={{0,4},{1,5},{2,6},{3,7},{4,8},{5,9},{6,10},{7,11},{8,12},{9,13},{1... | collective-permute-start | bytes 393224 | tf_op jit(solution)/shard_map/ppermute | solution.py:32
  8.3 12.0 %collective-permute-start.7 = (bf16[512,128]{1,0:T(8,128)(2,1)}, bf16[512,128]{1,0:T(8,128)(2,1)S(1)}, u32[]{:S(2)}, u32[]{:S(2)}) collective-permute-start(bf16[512,128]{1,0:T(8,128)(2,1)} %refs_0_.1), channel_id=1, source_target_pairs={{0,1},{1,0},{2,3},{3,2},{4,5},{5,4},{6,7},{7,6},{8,9},{9,8},{10,11... | collective-permute-start | bytes 393224 | tf_op jit(solution)/shard_map/ppermute | solution.py:32
  8.3 12.6 %collective-permute-start.11 = (bf16[512,128]{1,0:T(8,128)(2,1)S(1)}, bf16[512,128]{1,0:T(8,128)(2,1)S(1)}, u32[]{:S(2)}, u32[]{:S(2)}) collective-permute-start(bf16[512,128]{1,0:T(8,128)(2,1)S(1)} %collective-permute-done.3.refs_4_), channel_id=1, source_target_pairs={{0,1},{1,0},{2,3},{3,2},{4,5},{5,4},{6,7},{7,6},{8,9},{9,8},{10,11... | collective-permute-start | bytes 393224 | tf_op jit(solution)/shard_map/ppermute | solution.py:32
  11.5 9.3 %collective-permute-start.10 = (bf16[512,128]{1,0:T(8,128)(2,1)S(1)}, bf16[512,128]{1,0:T(8,128)(2,1)S(1)}, u32[]{:S(2)}, u32[]{:S(2)}) collective-permute-start(bf16[512,128]{1,0:T(8,128)(2,1)S(1)} %collective-permute-done.2.refs_3_), channel_id=1, source_target_pairs={{0,1},{1,0},{2,3},{3,2},{4,5},{5,4},{6,7},{7,6},{8,9},{9,8},{10,11... | collective-permute-start | bytes 393224 | tf_op jit(solution)/shard_map/ppermute | solution.py:32
  18.3 6.4 %collective-permute-start.6 = (bf16[512,128]{1,0:T(8,128)(2,1)S(1)}, bf16[512,128]{1,0:T(8,128)(2,1)S(1)}, u32[]{:S(2)}, u32[]{:S(2)}) collective-permute-start(bf16[512,128]{1,0:T(8,128)(2,1)S(1)} %collective-permute-done.2.refs_3_), channel_id=1, source_target_pairs={{0,2},{1,3},{2,0},{3,1},{4,6},{5,7},{6,4},{7,5},{8,10},{9,11},{10,... | collective-permute-start | bytes 393224 | tf_op jit(solution)/shard_map/ppermute | solution.py:32
  18.8 8.3 %collective-permute-start.5 = (bf16[512,128]{1,0:T(8,128)(2,1)S(1)}, bf16[512,128]{1,0:T(8,128)(2,1)S(1)}, u32[]{:S(2)}, u32[]{:S(2)}) collective-permute-start(bf16[512,128]{1,0:T(8,128)(2,1)S(1)} %collective-permute-done.1.refs_2_), channel_id=1, source_target_pairs={{0,2},{1,3},{2,0},{3,1},{4,6},{5,7},{6,4},{7,5},{8,10},{9,11},{10,... | collective-permute-start | bytes 393224 | tf_op jit(solution)/shard_map/ppermute | solution.py:32
  20.3 8.2 %collective-permute-start.4 = (bf16[512,128]{1,0:T(8,128)(2,1)S(1)}, bf16[512,128]{1,0:T(8,128)(2,1)S(1)}, u32[]{:S(2)}, u32[]{:S(2)}) collective-permute-start(bf16[512,128]{1,0:T(8,128)(2,1)S(1)} %collective-permute-done.refs_1_), channel_id=1, source_target_pairs={{0,2},{1,3},{2,0},{3,1},{4,6},{5,7},{6,4},{7,5},{8,10},{9,11},{10,... | collective-permute-start | bytes 393224 | tf_op jit(solution)/shard_map/ppermute | solution.py:32
  20.8 7.7 %collective-permute-start.9 = (bf16[512,128]{1,0:T(8,128)(2,1)S(1)}, bf16[512,128]{1,0:T(8,128)(2,1)S(1)}, u32[]{:S(2)}, u32[]{:S(2)}) collective-permute-start(bf16[512,128]{1,0:T(8,128)(2,1)S(1)} %collective-permute-done.1.refs_2_), channel_id=1, source_target_pairs={{0,1},{1,0},{2,3},{3,2},{4,5},{5,4},{6,7},{7,6},{8,9},{9,8},{10,11... | collective-permute-start | bytes 393224 | tf_op jit(solution)/shard_map/ppermute | solution.py:32
  20.8 7.7 %collective-permute-start.8 = (bf16[512,128]{1,0:T(8,128)(2,1)S(1)}, bf16[512,128]{1,0:T(8,128)(2,1)S(1)}, u32[]{:S(2)}, u32[]{:S(2)}) collective-permute-start(bf16[512,128]{1,0:T(8,128)(2,1)S(1)} %collective-permute-done.refs_1_), channel_id=1, source_target_pairs={{0,1},{1,0},{2,3},{3,2},{4,5},{5,4},{6,7},{7,6},{8,9},{9,8},{10,11... | collective-permute-start | bytes 393224 | tf_op jit(solution)/shard_map/ppermute | solution.py:32
  50.6 6.1 %collective-permute-start.15 = (bf16[32,512]{1,0:T(8,128)(2,1)S(1)}, bf16[32,512]{1,0:T(8,128)(2,1)S(1)}, u32[]{:S(2)}, u32[]{:S(2)}) collective-permute-start(bf16[32,512]{1,0:T(8,128)(2,1)S(1)} %get-tuple-element.19), channel_id=1, source_target_pairs={{0,1},{1,2},{2,3},{3,4},{4,5},{5,6},{6,7},{7,8},{8,9},{9,10},{10,1... | collective-permute-start | bytes 98312 | tf_op jit(solution)/shard_map/ppermute | solution.py:197
  50.8 6.9 %collective-permute-start.16 = (bf16[32,512]{1,0:T(8,128)(2,1)S(1)}, bf16[32,512]{1,0:T(8,128)(2,1)S(1)}, u32[]{:S(2)}, u32[]{:S(2)}) collective-permute-start(bf16[32,512]{1,0:T(8,128)(2,1)S(1)} %get-tuple-element.20), channel_id=1, source_target_pairs={{0,2},{1,3},{2,4},{3,5},{4,6},{5,7},{6,8},{7,9},{8,10},{9,11},{10,... | collective-permute-start | bytes 98312 | tf_op jit(solution)/shard_map/ppermute | solution.py:197
  51.3 7.5 %collective-permute-start.17 = (bf16[32,512]{1,0:T(8,128)(2,1)S(1)}, bf16[32,512]{1,0:T(8,128)(2,1)S(1)}, u32[]{:S(2)}, u32[]{:S(2)}) collective-permute-start(bf16[32,512]{1,0:T(8,128)(2,1)S(1)} %get-tuple-element.21), channel_id=1, source_target_pairs={{0,3},{1,4},{2,5},{3,6},{4,7},{5,8},{6,9},{7,10},{8,11},{9,12},{10... | collective-permute-start | bytes 98312 | tf_op jit(solution)/shard_map/ppermute | solution.py:197
  51.4 9.3 %collective-permute-start.18 = (bf16[32,512]{1,0:T(8,128)(2,1)S(1)}, bf16[32,512]{1,0:T(8,128)(2,1)S(1)}, u32[]{:S(2)}, u32[]{:S(2)}) collective-permute-start(bf16[32,512]{1,0:T(8,128)(2,1)S(1)} %get-tuple-element.22), channel_id=1, source_target_pairs={{0,4},{1,5},{2,6},{3,7},{4,8},{5,9},{6,10},{7,11},{8,12},{9,13},{1... | collective-permute-start | bytes 98312 | tf_op jit(solution)/shard_map/ppermute | solution.py:197
  52.6 8.1 %collective-permute-start.19 = (bf16[32,512]{1,0:T(8,128)(2,1)S(1)}, bf16[32,512]{1,0:T(8,128)(2,1)S(1)}, u32[]{:S(2)}, u32[]{:S(2)}) collective-permute-start(bf16[32,512]{1,0:T(8,128)(2,1)S(1)} %get-tuple-element.23), channel_id=1, source_target_pairs={{0,5},{1,6},{2,7},{3,8},{4,9},{5,10},{6,11},{7,12},{8,13},{9,14},{... | collective-permute-start | bytes 98312 | tf_op jit(solution)/shard_map/ppermute | solution.py:197
  56.7 6.7 %collective-permute-start.20 = (bf16[32,512]{1,0:T(8,128)(2,1)S(1)}, bf16[32,512]{1,0:T(8,128)(2,1)S(1)}, u32[]{:S(2)}, u32[]{:S(2)}) collective-permute-start(bf16[32,512]{1,0:T(8,128)(2,1)S(1)} %get-tuple-element.24), channel_id=1, source_target_pairs={{0,6},{1,7},{2,8},{3,9},{4,10},{5,11},{6,12},{7,13},{8,14},{9,15},... | collective-permute-start | bytes 98312 | tf_op jit(solution)/shard_map/ppermute | solution.py:197
  57.7 9.1 %collective-permute-start.21 = (bf16[32,512]{1,0:T(8,128)(2,1)S(1)}, bf16[32,512]{1,0:T(8,128)(2,1)S(1)}, u32[]{:S(2)}, u32[]{:S(2)}) collective-permute-start(bf16[32,512]{1,0:T(8,128)(2,1)S(1)} %get-tuple-element.25), channel_id=1, source_target_pairs={{0,7},{1,8},{2,9},{3,10},{4,11},{5,12},{6,13},{7,14},{8,15},{9,0},... | collective-permute-start | bytes 98312 | tf_op jit(solution)/shard_map/ppermute | solution.py:197
  58.8 8.0 %collective-permute-start.22 = (bf16[32,512]{1,0:T(8,128)(2,1)S(1)}, bf16[32,512]{1,0:T(8,128)(2,1)S(1)}, u32[]{:S(2)}, u32[]{:S(2)}) collective-permute-start(bf16[32,512]{1,0:T(8,128)(2,1)S(1)} %get-tuple-element.26), channel_id=1, source_target_pairs={{0,8},{1,9},{2,10},{3,11},{4,12},{5,13},{6,14},{7,15},{8,0},{9,1},... | collective-permute-start | bytes 98312 | tf_op jit(solution)/shard_map/ppermute | solution.py:197
  60.7 7.4 %collective-permute-start.23 = (bf16[32,512]{1,0:T(8,128)(2,1)S(1)}, bf16[32,512]{1,0:T(8,128)(2,1)S(1)}, u32[]{:S(2)}, u32[]{:S(2)}) collective-permute-start(bf16[32,512]{1,0:T(8,128)(2,1)S(1)} %get-tuple-element.27), channel_id=1, source_target_pairs={{0,9},{1,10},{2,11},{3,12},{4,13},{5,14},{6,15},{7,0},{8,1},{9,2},... | collective-permute-start | bytes 98312 | tf_op jit(solution)/shard_map/ppermute | solution.py:197
  60.7 9.0 %collective-permute-start.24 = (bf16[32,512]{1,0:T(8,128)(2,1)S(1)}, bf16[32,512]{1,0:T(8,128)(2,1)S(1)}, u32[]{:S(2)}, u32[]{:S(2)}) collective-permute-start(bf16[32,512]{1,0:T(8,128)(2,1)S(1)} %get-tuple-element.28), channel_id=1, source_target_pairs={{0,10},{1,11},{2,12},{3,13},{4,14},{5,15},{6,0},{7,1},{8,2},{9,3},... | collective-permute-start | bytes 98312 | tf_op jit(solution)/shard_map/ppermute | solution.py:197
  63.4 7.7 %collective-permute-start.25 = (bf16[32,512]{1,0:T(8,128)(2,1)S(1)}, bf16[32,512]{1,0:T(8,128)(2,1)S(1)}, u32[]{:S(2)}, u32[]{:S(2)}) collective-permute-start(bf16[32,512]{1,0:T(8,128)(2,1)S(1)} %get-tuple-element.29), channel_id=1, source_target_pairs={{0,11},{1,12},{2,13},{3,14},{4,15},{5,0},{6,1},{7,2},{8,3},{9,4},{... | collective-permute-start | bytes 98312 | tf_op jit(solution)/shard_map/ppermute | solution.py:197
  66.9 4.2 %collective-permute-start.26 = (bf16[32,512]{1,0:T(8,128)(2,1)S(1)}, bf16[32,512]{1,0:T(8,128)(2,1)S(1)}, u32[]{:S(2)}, u32[]{:S(2)}) collective-permute-start(bf16[32,512]{1,0:T(8,128)(2,1)S(1)} %get-tuple-element.30), channel_id=1, source_target_pairs={{0,12},{1,13},{2,14},{3,15},{4,0},{5,1},{6,2},{7,3},{8,4},{9,5},{1... | collective-permute-start | bytes 98312 | tf_op jit(solution)/shard_map/ppermute | solution.py:197
  72.7 5.8 %collective-permute-start.33 = (bf16[32,512]{1,0:T(8,128)(2,1)S(1)}, bf16[32,512]{1,0:T(8,128)(2,1)S(1)}, u32[]{:S(2)}, u32[]{:S(2)}) collective-permute-start(bf16[32,512]{1,0:T(8,128)(2,1)S(1)} %add_convert_fusion.refs_0_), channel_id=1, source_target_pairs={{0,2},{1,3},{2,0},{3,1},{4,6},{5,7},{6,4},{7,5},{8,10},{9,11},{10,... | collective-permute-start | bytes 98312 | tf_op jit(solution)/shard_map/ppermute | solution.py:32
  77.6 4.8 %collective-permute-start.31 = (bf16[32,512]{1,0:T(8,128)(2,1)S(1)}, bf16[32,512]{1,0:T(8,128)(2,1)S(1)}, u32[]{:S(2)}, u32[]{:S(2)}) collective-permute-start(bf16[32,512]{1,0:T(8,128)(2,1)S(1)} %add_convert_fusion.refs_0_), channel_id=1, source_target_pairs={{0,8},{1,9},{2,10},{3,11},{4,12},{5,13},{6,14},{7,15},{8,0},{9,1},... | collective-permute-start | bytes 98312 | tf_op jit(solution)/shard_map/ppermute | solution.py:32
  78.4 5.7 %collective-permute-start.30 = (bf16[32,512]{1,0:T(8,128)(2,1)S(1)}, bf16[32,512]{1,0:T(8,128)(2,1)S(1)}, u32[]{:S(2)}, u32[]{:S(2)}) collective-permute-start(bf16[32,512]{1,0:T(8,128)(2,1)S(1)} %add_convert_fusion.refs_0_), channel_id=1, source_target_pairs={{0,4},{1,5},{2,6},{3,7},{4,8},{5,9},{6,10},{7,11},{8,12},{9,13},{1... | collective-permute-start | bytes 98312 | tf_op jit(solution)/shard_map/ppermute | solution.py:32
  78.5 6.0 %collective-permute-start.41 = (bf16[32,512]{1,0:T(8,128)(2,1)S(1)}, bf16[32,512]{1,0:T(8,128)(2,1)S(1)}, u32[]{:S(2)}, u32[]{:S(2)}) collective-permute-start(bf16[32,512]{1,0:T(8,128)(2,1)S(1)} %collective-permute-done.33.refs_4_), channel_id=1, source_target_pairs={{0,1},{1,0},{2,3},{3,2},{4,5},{5,4},{6,7},{7,6},{8,9},{9,8},{10,11... | collective-permute-start | bytes 98312 | tf_op jit(solution)/shard_map/ppermute | solution.py:32
  78.8 5.7 %collective-permute-start.40 = (bf16[32,512]{1,0:T(8,128)(2,1)S(1)}, bf16[32,512]{1,0:T(8,128)(2,1)S(1)}, u32[]{:S(2)}, u32[]{:S(2)}) collective-permute-start(bf16[32,512]{1,0:T(8,128)(2,1)S(1)} %collective-permute-done.32.refs_3_), channel_id=1, source_target_pairs={{0,1},{1,0},{2,3},{3,2},{4,5},{5,4},{6,7},{7,6},{8,9},{9,8},{10,11... | collective-permute-start | bytes 98312 | tf_op jit(solution)/shard_map/ppermute | solution.py:32
  79.0 6.0 %collective-permute-start.36 = (bf16[32,512]{1,0:T(8,128)(2,1)S(1)}, bf16[32,512]{1,0:T(8,128)(2,1)S(1)}, u32[]{:S(2)}, u32[]{:S(2)}) collective-permute-start(bf16[32,512]{1,0:T(8,128)(2,1)S(1)} %collective-permute-done.32.refs_3_), channel_id=1, source_target_pairs={{0,2},{1,3},{2,0},{3,1},{4,6},{5,7},{6,4},{7,5},{8,10},{9,11},{10,... | collective-permute-start | bytes 98312 | tf_op jit(solution)/shard_map/ppermute | solution.py:32
  84.5 4.3 %collective-permute-start.39 = (bf16[32,512]{1,0:T(8,128)(2,1)S(1)}, bf16[32,512]{1,0:T(8,128)(2,1)S(1)}, u32[]{:S(2)}, u32[]{:S(2)}) collective-permute-start(bf16[32,512]{1,0:T(8,128)(2,1)S(1)} %collective-permute-done.31.refs_2_), channel_id=1, source_target_pairs={{0,1},{1,0},{2,3},{3,2},{4,5},{5,4},{6,7},{7,6},{8,9},{9,8},{10,11... | collective-permute-start | bytes 98312 | tf_op jit(solution)/shard_map/ppermute | solution.py:32
  84.5 4.3 %collective-permute-start.38 = (bf16[32,512]{1,0:T(8,128)(2,1)S(1)}, bf16[32,512]{1,0:T(8,128)(2,1)S(1)}, u32[]{:S(2)}, u32[]{:S(2)}) collective-permute-start(bf16[32,512]{1,0:T(8,128)(2,1)S(1)} %collective-permute-done.30.refs_1_), channel_id=1, source_target_pairs={{0,1},{1,0},{2,3},{3,2},{4,5},{5,4},{6,7},{7,6},{8,9},{9,8},{10,11... | collective-permute-start | bytes 98312 | tf_op jit(solution)/shard_map/ppermute | solution.py:32
  (19 other events, 46.7 us)

commit v2 on v0

v2 whole, which is shorter than its diff:
```python
import functools

import jax
import jax.numpy as jnp
from jax import lax
from jax.experimental import pallas as pl
from jax.experimental.pallas import tpu as pltpu
from jax.sharding import PartitionSpec as P

CAP = 2
MIB = 1 << 20
VMEM = pl.BlockSpec(memory_space=pltpu.VMEM)
SMEM = pl.BlockSpec(memory_space=pltpu.SMEM)
ANY = pl.BlockSpec(memory_space=pl.ANY)


def levels(devices):
    cores = 2 if devices % 2 == 0 else 1
    wide = 4 if devices >= 64 and devices % 8 == 0 else 2 if devices % 4 == 0 else 1
    return devices // (cores * wide), wide, cores


def owners(me, devices, shift):
    deep, wide, cores = levels(devices)
    x = ((me // cores) % wide + wide - shift[0]) % wide
    core = (me % cores + cores - shift[1]) % cores
    return [z * (wide * cores) + x * cores + core for z in range(deep)]


def pg_kernel(cots, proj_out, out):
    layers = cots.shape[0]
    width_k = proj_out.shape[1] // layers
    for l in range(layers):
        pg = jnp.dot(cots[l], proj_out[...], preferred_element_type=jnp.float32)
        pg = pg.astype(jnp.bfloat16).astype(jnp.float32)
        out[l * width_k:(l + 1) * width_k, :] = pg.T[l * width_k:(l + 1) * width_k, :]


def accumulate(acts, block, held, sems, devices, shift, start):
    layers, rows, _ = acts.shape
    me = lax.axis_index("seq")
    own = owners(me, devices, shift)
    tall = block.shape[0] // len(own)
    copies = []
    for i, owner in enumerate(own):
        at = pl.ds(pl.multiple_of(owner * tall, tall), tall)
        copies.append(pltpu.make_async_copy(acts.at[:, :, at], held.at[i], sems.at[i]))
        copies[-1].start()
    total = list(start)
    for i, copy in enumerate(copies):
        copy.wait()
        part = block[i * tall:(i + 1) * tall, :]
        for l in range(layers):
            total[l] = total[l] + jnp.dot(held[i, l], part, preferred_element_type=jnp.float32)
    return total


def first_kernel(devices, shift, acts, block, out, held, sems):
    zero = jnp.zeros(out.shape[1:], jnp.float32)
    total = accumulate(acts, block, held, sems, devices, shift, [zero] * out.shape[0])
    for l, value in enumerate(total):
        out[l] = value


def next_kernel(devices, shift, acts, block, before, out, held, sems):
    total = accumulate(acts, block, held, sems, devices, shift, [before[l] for l in range(out.shape[0])])
    for l, value in enumerate(total):
        out[l] = value


def whole_kernel(devices, shifts, acts, *refs):
    count = len(shifts)
    blocks, (out, weights) = refs[:count], refs[count:]
    me = lax.axis_index("seq")
    for shift, block in zip(shifts, blocks):
        own = owners(me, devices, shift)
        tall = block.shape[0] // len(own)
        for i, owner in enumerate(own):
            weights[pl.ds(pl.multiple_of(owner * tall, tall), tall), :] = block[i * tall:(i + 1) * tall, :]
    for l in range(out.shape[0]):
        out[l] = jnp.dot(acts[l], weights[...], preferred_element_type=jnp.float32)


def grads_kernel(per_part, projected, pg_t, lengths, out):
    layers, rows, wide = projected.shape
    width_k = wide // layers
    lanes = width_k * width_k // per_part
    repeat = lanes // width_k
    me = lax.axis_index("seq")
    sizes = lengths[pl.ds(me // per_part, 1), :]
    per_row = sizes.shape[1]
    upto = lax.broadcasted_iota(jnp.int32, (per_row, per_row), 1)
    which = lax.broadcasted_iota(jnp.int32, (per_row, per_row), 0)
    sizes = jnp.broadcast_to(sizes, (per_row, per_row))
    ends = jnp.sum(jnp.where(upto <= which, sizes, 0), axis=1, keepdims=True)
    starts = jnp.sum(jnp.where(upto < which, sizes, 0), axis=1, keepdims=True)
    position = (me % per_part) * rows + lax.broadcasted_iota(jnp.int32, (per_row, rows), 1)
    member = ((position >= starts) & (position < ends)).astype(jnp.float32)
    low = lax.broadcasted_iota(jnp.int32, (per_row, 2 * width_k), 1) < width_k
    for l in range(layers):
        own = projected[l][:, l * width_k:(l + 1) * width_k].astype(jnp.bfloat16)
        px = jnp.concatenate([own, own], axis=1)
        for part in range(per_part):
            first = l * width_k + part * repeat
            terms = [(member * pg_t[first + i:first + i + 1, :]).astype(jnp.bfloat16) for i in range(repeat)]
            sums = jnp.dot(jnp.concatenate(terms, axis=0), px, preferred_element_type=jnp.float32)
            for i in range(0, repeat, 2):
                even = sums[i * per_row:(i + 1) * per_row]
                odd = sums[(i + 1) * per_row:(i + 2) * per_row]
                at = l * lanes + i * width_k
                out[part * per_row:(part + 1) * per_row, at:at + 2 * width_k] = jnp.where(low, even, odd).astype(jnp.bfloat16)


def total_kernel(parts, terms, out):
    tall = terms.shape[0] // parts
    total = terms[:tall].astype(jnp.float32)
    for i in range(1, parts):
        total = total + terms[i * tall:(i + 1) * tall].astype(jnp.float32)
    total = total.astype(jnp.bfloat16)
    for i in range(out.shape[0] // tall):
        out[i * tall:(i + 1) * tall] = total


def covariance_kernel(per_part, blocks, slots, pairs, logged, out, right, held, sems):
    npair, band, square = held.shape
    seqs, full = right.shape
    layers = full // square
    lanes = square // per_part
    me = lax.axis_index("seq")
    devices = square // band
    tall = blocks.shape[0] // devices
    for i in range(devices):
        row = (i // per_part) * tall
        for l in range(layers):
            at = l * square + (i % per_part) * lanes
            right[row:row + tall, at:at + lanes] = blocks[i * tall:(i + 1) * tall, l * lanes:(l + 1) * lanes]
    scale = jnp.float32(1.0 / seqs)
    cols = min(1024, square)
    chunks = square // cols
    copies = []
    for p in range(npair):
        if band % 128 == 0:
            at = pl.multiple_of(pairs[p, 0] * square + me * band, band)
            left = right[:, pl.ds(at, band)]
        else:
            offset = me * band
            at = pl.multiple_of(pairs[p, 0] * square + (offset // 128) * 128, 128)
            source = lax.broadcasted_iota(jnp.int32, (128, band), 0)
            target = lax.broadcasted_iota(jnp.int32, (128, band), 1)
            pick = (source == target + offset % 128).astype(jnp.float32).astype(jnp.bfloat16)
            left = jnp.dot(right[:, pl.ds(at, 128)], pick, preferred_element_type=jnp.float32).astype(jnp.bfloat16)
        for q in range(chunks):
            at = pl.multiple_of(pairs[p, 1] * square + q * cols, cols)
            product = lax.dot_general(
                left, right[:, pl.ds(at, cols)], (((0,), (0,)), ((), ())), preferred_element_type=jnp.float32
            )
            held[p, :, q * cols:(q + 1) * cols] = product * scale
            where = (p, slice(None), pl.ds(q * cols, cols))
            copy = pltpu.make_async_copy(held.at[where], out.at[where], sems.at[p * chunks + q])
            copy.start()
            copies.append(copy)
    own = me * CAP + lax.broadcasted_iota(jnp.int32, (CAP, seqs), 0)
    picker = (jnp.broadcast_to(slots[...], (CAP, seqs)) == own).astype(jnp.float32).astype(jnp.bfloat16)
    logged[...] = jnp.dot(picker, right[...], preferred_element_type=jnp.float32).astype(jnp.bfloat16)
    for copy in copies:
        copy.wait()


def shards(acts, cots, proj_in, proj_out, lengths, slots, pairs):
    layers, rows, width = acts.shape
    wide = proj_out.shape[1]
    width_k = wide // layers
    square = width_k * width_k
    devices = lax.axis_size("seq")
    rows_all, per_row = lengths.shape
    seqs = slots.shape[0]
    npair = pairs.shape[0]
    per_part = devices // rows_all
    lanes = square // per_part
    band = square // devices
    deep, across, cores = levels(devices)
    tall = proj_in.shape[0]
    params = pltpu.CompilerParams(vmem_limit_bytes=52 * MIB)

    pg_t = pl.pallas_call(
        pg_kernel,
        out_shape=jax.ShapeDtypeStruct((wide, rows), jnp.float32),
        in_specs=[VMEM, VMEM],
        out_specs=VMEM,
        compiler_params=params,
        cost_estimate=pl.CostEstimate(flops=8 << 27, bytes_accessed=cots.size * 2, transcendentals=0),
        name="pg",
    )(cots, proj_out)

    line = across * cores
    groups = [[z * line + i for z in range(deep)] for i in range(line)]
    column = lax.all_to_all(jnp.tile(proj_in, (deep, 1)), "seq", 0, 0, axis_index_groups=groups, tiled=True)
    blocks = {(0, 0): column}
    for step in range(1, across):
        perm = [(i, i + ((i // cores + step) % across - i // cores % across) * cores) for i in range(devices)]
        blocks[step, 0] = lax.ppermute(column, "seq", perm)
    for step in range(1, cores):
        perm = [(i, i + (i + step) % cores - i % cores) for i in range(devices)]
        for x in range(across):
            blocks[x, step] = lax.ppermute(blocks[x, 0], "seq", perm)
    partial_type = jax.ShapeDtypeStruct((layers, rows, wide), jnp.float32)
    if tall % 128 == 0:
        order = sorted(blocks, key=lambda shift: (shift[0], shift[1]))
        projected = None
        for shift in order:
            before = () if projected is None else (projected,)
            projected = pl.pallas_call(
                functools.partial(next_kernel if before else first_kernel, devices, shift),
                out_shape=partial_type,
                in_specs=[ANY] + [VMEM] * (1 + len(before)),
                out_specs=VMEM,
                scratch_shapes=[
                    pltpu.VMEM((deep, layers, rows, tall), jnp.bfloat16),
                    pltpu.SemaphoreType.DMA((deep,)),
                ],
                compiler_params=params,
                cost_estimate=pl.CostEstimate(flops=8 << 27, bytes_accessed=acts.size * 2 // len(order), transcendentals=0),
                name="px",
            )(acts, blocks[shift], *before)
    else:
        projected = pl.pallas_call(
            functools.partial(whole_kernel, devices, tuple(blocks)),
            out_shape=partial_type,
            in_specs=[VMEM] * (1 + len(blocks)),
            out_specs=VMEM,
            scratch_shapes=[pltpu.VMEM((width, wide), jnp.bfloat16)],
            compiler_params=params,
            name="px",
        )(acts, *blocks.values())

    parts = pl.pallas_call(
        functools.partial(grads_kernel, per_part),
        out_shape=jax.ShapeDtypeStruct((per_part * per_row, layers * lanes), jnp.bfloat16),
        in_specs=[VMEM] * 3,
        out_specs=VMEM,
        compiler_params=params,
        name="grads",
    )(projected, pg_t, lengths)
    rings = [[r * per_part + i for i in range(per_part)] for r in range(rows_all)]
    terms = lax.all_to_all(parts, "seq", 0, 0, axis_index_groups=rings, tiled=True)
    total = pl.pallas_call(
        functools.partial(total_kernel, per_part),
        out_shape=jax.ShapeDtypeStruct((devices * per_row, layers * lanes), jnp.bfloat16),
        in_specs=[VMEM],
        out_specs=VMEM,
        compiler_params=params,
        name="total",
    )(terms)
    summed = lax.all_to_all(total, "seq", 0, 0, tiled=True)
    return pl.pallas_call(
        functools.partial(covariance_kernel, per_part),
        out_shape=[
            jax.ShapeDtypeStruct((CAP, layers * square), jnp.bfloat16),
            jax.ShapeDtypeStruct((npair, band, square), jnp.float32),
        ],
        in_specs=[VMEM, VMEM, SMEM],
        out_specs=[VMEM, ANY],
        scratch_shapes=[
            pltpu.VMEM((seqs, layers * square), jnp.bfloat16),
            pltpu.VMEM((npair, band, square), jnp.float32),
            pltpu.SemaphoreType.DMA((npair * (square // min(1024, square)),)),
        ],
        compiler_params=params,
        name="covariance",
    )(summed, slots.reshape(1, seqs), pairs)


def solution(mesh):
    in_specs = (
        P(None, ("groups", "seq"), None),
        P(None, ("groups", "seq"), None),
        P("seq", None),
        P(),
        P("groups", None),
        P("groups"),
        P(),
    )
    out_specs = (P(("groups", "seq"), None), P("groups", "seq", None))
    return jax.shard_map(shards, mesh=mesh, in_specs=in_specs, out_specs=out_specs, check_vma=False)
```

time: 166 us -> 92.4 us (0.56)
  blocking collectives: 72.1 us -> 39.4 us
  between operations: 25.1 us -> 0.75 us
  Pallas kernels: 0 us -> 17.5 us
  matrix products: 16.4 us -> 0 us
  other arithmetic: 10.5 us -> 0 us
  local copies, waits for them, and re-layouts: 11.1 us -> 3.26 us
  starting transfers between devices: 0.04 us -> 5.59 us
  waiting for transfers between devices: 29.9 us -> 25.4 us
    psum x1 -> x0, blocking collectives: 72.1 us -> none  [shards(): totals = lax.psum(term, 'seq')]
    all_to_all x0 -> x2, blocking collectives: none -> 39.4 us  [the longest x1 20.6 us: shards(): lax.all_to_all(jnp.tile(proj_in, (deep, 1)), 'seq', 0, 0, axis_index_grou...]
    all_gather x1 -> x0, waiting for transfers between devices: 29.9 us -> none  [shards(): piece = lax.all_gather(proj_in, 'seq', axis=0, tiled=True)]
    pallas_call x0 -> x8, Pallas kernels: none -> 17.5 us  [the longest x4 9.01 us: shards(): pl.pallas_call(functools.partial(next_kernel if before else first_kernel,...]
    dot_general x6 -> x0, matrix products: 16.4 us -> none  [the longest x1 9.01 us: shards(): jnp.einsum('ltsa,ltb->slab', weighted, px_half, preferred_element_type=jn...]
    all_to_all x0 -> x1, waiting for transfers between devices: none -> 14.4 us  [shards(): summed = lax.all_to_all(total, 'seq', 0, 0, tiled=True)]
    ppermute x0 -> x3, waiting for transfers between devices: none -> 11 us  [the longest x1 11 us: shards(): blocks[step, 0] = lax.ppermute(column, 'seq', perm)]
    another operation x3 -> x0, other arithmetic: 9.73 us -> none  [the longest x1 9.56 us: shards(): covariance = jnp.stack(tiles)]
  transfers between devices with their start and end apart: 1 -> 4, of which waited for: 1 -> 2; matrix products, arithmetic and copies ran while one was open for 3% -> 0% of each run, Pallas kernels for 0% -> 8%
where the time goes in v2:
time: 92.4 us; the launch traced here: 91.9 us
  blocking collectives  39.4 us (43%)
  waiting for transfers between devices  25.4 us (27%)
  Pallas kernels  17.5 us (19%)
  starting transfers between devices  5.59 us (6%)
  local copies, waits for them, and re-layouts  3.26 us (4%)
    all_to_all x1, blocking collectives, shards(): lax.all_to_all(jnp.tile(proj_in, (deep, 1)), 'seq', 0, 0, axis_index_grou...  20.6 us
    all_to_all x1, blocking collectives, shards(): lax.all_to_all(parts, 'seq', 0, 0, axis_index_groups=rings, tiled=True)  18.8 us
    all_to_all x1, waiting for transfers between devices, shards(): summed = lax.all_to_all(total, 'seq', 0, 0, tiled=True)  14.4 us
    ppermute x1, waiting for transfers between devices, shards(): blocks[step, 0] = lax.ppermute(column, 'seq', perm)  11 us
    pallas_call x4, Pallas kernels, shards(): pl.pallas_call(functools.partial(next_kernel if before else first_kernel,...  9.01 us
    pallas_call x1, Pallas kernels, shards(): pl.pallas_call(functools.partial(covariance_kernel, per_part), out_shape=...  6.2 us
    all_to_all x1, starting transfers between devices, shards(): summed = lax.all_to_all(total, 'seq', 0, 0, tiled=True)  4.1 us
    unnamed x11, local copies, waits for them, and re-layouts  2.29 us
  transfers between devices with their start and end apart: 4, of which 2 were waited for; matrix products, arithmetic and copies ran while one was open for 0% of the time, Pallas kernels for 8%

profile of v2, /device:TPU:0, one launch (start us, length us, event | category | flops | bytes accessed | tf_op | source)
XLA Modules:
  0.0 91.9 jit_solution(8075988366326611251)
XLA Ops:
  0.6 1.0 %tile.2 = bf16[4,512,128]{2,1,0:T(8,128)(2,1)S(1)} broadcast(bf16[512,128]{1,0:T(8,128)(2,1)} %param.9), dimensions={1,2} | broadcast | bytes 655360 | tf_op jit(solution)/shard_map/tile | solution.py:197
  1.6 20.6 %all_to_all.30 = bf16[4,512,128]{2,1,0:T(8,128)(2,1)S(1)} all-to-all(bf16[4,512,128]{2,1,0:T(8,128)(2,1)S(1)} %tile.2), channel_id=1, replica_groups={{0,4,8,12},{1,5,9,13},{2,6,10,14},{3,7,11,15},{16,20,24,28},{17,21,25,2..., dimensions={0} | all-to-all | bytes 1048576 | tf_op jit(solution)/shard_map/all_to_all | solution.py:197
  22.2 1.5 %collective-permute-start = (bf16[2048,128]{1,0:T(8,128)(2,1)S(1)}, bf16[2048,128]{1,0:T(8,128)(2,1)S(1)}, u32[]{:S(2)}, u32[]{:S(2)}) collective-permute-start(bf16[2048,128]{1,0:T(8,128)(2,1)S(1)} %bitcast.6), channel_id=1, source_target_pairs={{0,2},{1,3},{2,0},{3,1},{4,6},{5,7},{6,4},{7,5},{8,10},{9,11},{10,... | collective-permute-start | bytes 1572872 | tf_op jit(solution)/shard_map/ppermute | solution.py:201
  23.7 0.0 collective-permute-start.2
  23.7 11.0 %collective-permute-done.block = bf16[2048,128]{1,0:T(8,128)(2,1)S(1)} collective-permute-done((bf16[2048,128]{1,0:T(8,128)(2,1)S(1)}, bf16[2048,128]{1,0:T(8,128)(2,1)S(1)}, u32[]{:S(2)}, u32[]{:S(2)}) %collective-permute-start) | collective-permute-done | bytes 524320 | tf_op jit(solution)/shard_map/ppermute | solution.py:201
  34.7 0.0 collective-permute-start.1
  34.7 0.0 copy-start.2
  34.8 1.2 %copy-done.2 = bf16[2,256,1024]{2,1,0:T(8,128)(2,1)S(1)} copy-done((bf16[2,256,1024]{2,1,0:T(8,128)(2,1)S(1)}, bf16[2,256,1024]{2,1,0:T(8,128)(2,1)}, u32[]{:S(2)}) %copy-start.2) | copy-done | bytes 1048600
  36.0 0.0 copy-start.3
  36.0 0.9 %copy-done.3 = bf16[1024,128]{1,0:T(8,128)(2,1)S(1)} copy-done((bf16[1024,128]{1,0:T(8,128)(2,1)S(1)}, bf16[1024,128]{1,0:T(8,128)(2,1)}, u32[]{:S(2)}) %copy-start.3) | copy-done | bytes 262168
  36.9 0.5 pg.1.pg_t
  37.4 2.3 %px.4.before = f32[2,256,128]{2,1,0:T(8,128)S(1)} custom-call(bf16[2,256,8192]{2,1,0:T(8,128)(2,1)} %acts.7, bf16[2048,128]{1,0:T(8,128)(2,1)S(1)} %bitcast.8), custom_call_target="tpu_custom_call" | custom-call | flops 1073741824 | bytes 2097152 | tf_op jit(solution)/shard_map/px/pallas_call | solution.py:212
  39.7 0.0 copy-start
  39.7 0.0 collective-permute-done.2.block
  39.7 2.2 %px.5.before = f32[2,256,128]{2,1,0:T(8,128)S(1)} custom-call(bf16[2,256,8192]{2,1,0:T(8,128)(2,1)} %acts.7, bf16[2048,128]{1,0:T(8,128)(2,1)S(1)} %collective-permute-done.2.block, f32[2,256,128]{2,1,0:T(8,128)S(1)} %px.4.before), custom_call_target="tpu_custom_call" | custom-call | flops 1073741824 | bytes 2097152 | tf_op jit(solution)/shard_map/px/pallas_call | solution.py:212
  42.0 0.0 copy-start.4
  42.0 0.0 copy-start.1
  42.0 2.2 %px.6.before = f32[2,256,128]{2,1,0:T(8,128)S(1)} custom-call(bf16[2,256,8192]{2,1,0:T(8,128)(2,1)} %acts.7, bf16[2048,128]{1,0:T(8,128)(2,1)S(1)} %collective-permute-done.block, f32[2,256,128]{2,1,0:T(8,128)S(1)} %px.5.before), custom_call_target="tpu_custom_call" | custom-call | flops 1073741824 | bytes 2097152 | tf_op jit(solution)/shard_map/px/pallas_call | solution.py:212
  44.2 0.0 collective-permute-done.1.block
  44.3 2.2 %px.7.projected = f32[2,256,128]{2,1,0:T(8,128)S(1)} custom-call(bf16[2,256,8192]{2,1,0:T(8,128)(2,1)} %acts.7, bf16[2048,128]{1,0:T(8,128)(2,1)S(1)} %collective-permute-done.1.block, f32[2,256,128]{2,1,0:T(8,128)S(1)} %px.6.before), custom_call_target="tpu_custom_call" | custom-call | flops 1073741824 | bytes 2097152 | tf_op jit(solution)/shard_map/px/pallas_call | solution.py:212
  46.5 0.0 copy-done
  46.5 0.9 grads.1
  47.4 18.8 %all_to_all.31 = bf16[16,32,512]{2,1,0:T(8,128)(2,1)S(1)} all-to-all(bf16[16,32,512]{2,1,0:T(8,128)(2,1)S(1)} %bitcast.10), channel_id=1, replica_groups={{0,1,2,3,4,5,6,7,8,9,10,11,12,13,14,15},{16,17,18,19,20,21,22,23,24,25,..., dimensions={0} | all-to-all | bytes 1048576 | tf_op jit(solution)/shard_map/all_to_all | solution.py:245
  66.2 0.9 total.1
  67.1 4.1 %all-to-all-start.2 = ((bf16[16,32,512]{2,1,0:T(8,128)(2,1)}), bf16[16,32,512]{2,1,0:T(8,128)(2,1)S(1)}, u32[]{:S(2)}, u32[]{:S(2)}) async-start(bf16[16,32,512]{2,1,0:T(8,128)(2,1)} %bitcast.3), calls=%async_computation.2 | async-start | bytes 1048576 | tf_op jit(solution)/shard_map/all_to_all | solution.py:254
  71.2 0.0 copy-done.4
  71.2 0.1 copy.9.pairs
  71.3 14.4 %all-to-all-done.2 = bf16[16,32,512]{2,1,0:T(8,128)(2,1)S(1)} async-done(((bf16[16,32,512]{2,1,0:T(8,128)(2,1)}), bf16[16,32,512]{2,1,0:T(8,128)(2,1)S(1)}, u32[]{:S(2)}, u32[]{:S(2)}) %all-to-all-start.2) | async-done | bytes 524320 | tf_op jit(solution)/shard_map/all_to_all | solution.py:254
  85.7 0.0 copy-done.1
  85.7 6.2 %covariance.1 = (bf16[2,8192]{1,0:T(2,128)(2,1)}, f32[3,256,4096]{2,1,0:T(8,128)}) custom-call(bf16[512,512]{1,0:T(8,128)(2,1)S(1)} %bitcast.9, s32[1,32]{1,0:T(1,128)S(1)} %bitcast.12, s32[3,2]{1,0:T(4,128)S(1)} %copy.9.pairs), custom_call_target="tpu_custom_call" | custom-call | tf_op jit(solution)/shard_map/covariance/pallas_call | solution.py:255
Async XLA Ops:
  22.2 12.5 %collective-permute-start = (bf16[2048,128]{1,0:T(8,128)(2,1)S(1)}, bf16[2048,128]{1,0:T(8,128)(2,1)S(1)}, u32[]{:S(2)}, u32[]{:S(2)}) collective-permute-start(bf16[2048,128]{1,0:T(8,128)(2,1)S(1)} %bitcast.6), channel_id=1, source_target_pairs={{0,2},{1,3},{2,0},{3,1},{4,6},{5,7},{6,4},{7,5},{8,10},{9,11},{10,... | collective-permute-start | bytes 1572872 | tf_op jit(solution)/shard_map/ppermute | solution.py:201
  23.7 16.0 %collective-permute-start.2 = (bf16[2048,128]{1,0:T(8,128)(2,1)S(1)}, bf16[2048,128]{1,0:T(8,128)(2,1)S(1)}, u32[]{:S(2)}, u32[]{:S(2)}) collective-permute-start(bf16[2048,128]{1,0:T(8,128)(2,1)S(1)} %bitcast.7), channel_id=1, source_target_pairs={{0,1},{1,0},{2,3},{3,2},{4,5},{5,4},{6,7},{7,6},{8,9},{9,8},{10,11... | collective-permute-start | bytes 1572872 | tf_op jit(solution)/shard_map/ppermute | solution.py:205
  34.7 9.5 %collective-permute-start.1 = (bf16[2048,128]{1,0:T(8,128)(2,1)S(1)}, bf16[2048,128]{1,0:T(8,128)(2,1)S(1)}, u32[]{:S(2)}, u32[]{:S(2)}) collective-permute-start(bf16[2048,128]{1,0:T(8,128)(2,1)S(1)} %collective-permute-done.block), channel_id=1, source_target_pairs={{0,1},{1,0},{2,3},{3,2},{4,5},{5,4},{6,7},{7,6},{8,9},{9,8},{10,11... | collective-permute-start | bytes 1572872 | tf_op jit(solution)/shard_map/ppermute | solution.py:205
  34.7 1.2 %copy-start.2 = (bf16[2,256,1024]{2,1,0:T(8,128)(2,1)S(1)}, bf16[2,256,1024]{2,1,0:T(8,128)(2,1)}, u32[]{:S(2)}) copy-start(bf16[2,256,1024]{2,1,0:T(8,128)(2,1)} %cots.1) | copy-start | bytes 3145732
  36.0 0.9 %copy-start.3 = (bf16[1024,128]{1,0:T(8,128)(2,1)S(1)}, bf16[1024,128]{1,0:T(8,128)(2,1)}, u32[]{:S(2)}) copy-start(bf16[1024,128]{1,0:T(8,128)(2,1)} %proj_out.1) | copy-start | bytes 786436
  39.7 6.8 %copy-start = (s32[1,32]{1,0:T(1,128)S(1)}, s32[1,32]{1,0:T(1,128)}, u32[]{:S(2)}) copy-start(s32[1,32]{1,0:T(1,128)} %lengths.1) | copy-start | bytes 388
  42.0 29.3 %copy-start.4 = (s32[3,2]{0,1:T(2,128)S(1)}, s32[3,2]{0,1:T(2,128)}, u32[]{:S(2)}) copy-start(s32[3,2]{0,1:T(2,128)} %param.13) | copy-start | bytes 76
  42.0 43.7 %copy-start.1 = (s32[32]{0:T(128)S(1)}, s32[32]{0:T(128)}, u32[]{:S(2)}) copy-start(s32[32]{0:T(128)} %param.12) | copy-start | bytes 388
  67.1 18.6 %all-to-all-start.2 = ((bf16[16,32,512]{2,1,0:T(8,128)(2,1)}), bf16[16,32,512]{2,1,0:T(8,128)(2,1)S(1)}, u32[]{:S(2)}, u32[]{:S(2)}) async-start(bf16[16,32,512]{2,1,0:T(8,128)(2,1)} %bitcast.3), calls=%async_computation.2 | async-start | bytes 1048576 | tf_op jit(solution)/shard_map/all_to_all | solution.py:254

commit v3 on v2

v3 whole, which is shorter than its diff:
```python
import functools

import jax
import jax.numpy as jnp
from jax import lax
from jax.experimental import pallas as pl
from jax.experimental.pallas import tpu as pltpu
from jax.sharding import PartitionSpec as P

CAP = 2
MIB = 1 << 20
VMEM = pl.BlockSpec(memory_space=pltpu.VMEM)
SMEM = pl.BlockSpec(memory_space=pltpu.SMEM)
ANY = pl.BlockSpec(memory_space=pl.ANY)


def levels(devices):
    cores = 2 if devices % 2 == 0 else 1
    wide = 4 if devices >= 64 and devices % 8 == 0 else 2 if devices % 4 == 0 else 1
    return devices // (cores * wide), wide, cores


def place(index, devices):
    _, wide, cores = levels(devices)
    return index // (wide * cores), index // cores % wide, index % cores


def owner(me, devices, shift):
    deep, wide, cores = levels(devices)
    z, x, core = place(me, devices)
    z = (z + (deep - shift[0])) % deep
    x = (x + (wide - shift[1])) % wide
    core = (core + (cores - shift[2])) % cores
    return (z * wide + x) * cores + core


def send(value, devices, shift):
    deep, wide, cores = levels(devices)
    perm = []
    for i in range(devices):
        z, x, core = place(i, devices)
        z, x, core = (z + shift[0]) % deep, (x + shift[1]) % wide, (core + shift[2]) % cores
        perm.append((i, (z * wide + x) * cores + core))
    return lax.ppermute(value, "seq", perm)


def chunks(spot, devices, square):
    deep, wide, cores = levels(devices)
    line = wide * cores
    band = square // devices
    if band % 128:
        return [(0, spot * (square // line), square // line)]
    return [(z * band, (z * line + spot) * band, band) for z in range(deep)]


def pg_kernel(cots, proj_out, out, held, weights, sems):
    layers = cots.shape[0]
    width_k = proj_out.shape[1] // layers
    copies = [pltpu.make_async_copy(proj_out, weights, sems.at[layers])]
    copies += [pltpu.make_async_copy(cots.at[l], held.at[l], sems.at[l]) for l in range(layers)]
    for copy in copies:
        copy.start()
    copies[0].wait()
    for l in range(layers):
        copies[1 + l].wait()
        pg = jnp.dot(held[l], weights[...], preferred_element_type=jnp.float32)
        out[l * width_k:(l + 1) * width_k, :] = pg.T[l * width_k:(l + 1) * width_k, :].astype(jnp.bfloat16)


def px_kernel(devices, shifts, begin, end, acts, *refs):
    count = len(shifts)
    blocks, refs = refs[:count], refs[count:]
    out, held, sems = refs[-3:]
    layers, rows, _ = acts.shape
    tall, wide = blocks[0].shape
    me = lax.axis_index("seq")
    copies = []
    for i, shift in enumerate(shifts):
        at = pl.ds(pl.multiple_of(owner(me, devices, shift) * tall, tall), tall)
        copies.append(pltpu.make_async_copy(acts.at[:, :, at], held.at[i], sems.at[i]))
        copies[-1].start()
    total = [jnp.zeros((rows, wide), jnp.float32) if begin else refs[0][l] for l in range(layers)]
    for i, copy in enumerate(copies):
        copy.wait()
        for l in range(layers):
            total[l] = total[l] + jnp.dot(held[i, l], blocks[i][...], preferred_element_type=jnp.float32)
    if end:
        pack(total, refs[-4], out)
    else:
        for l in range(layers):
            out[l] = total[l]


def pack(total, pg_t, out):
    layers = len(total)
    rows, wide = total[0].shape
    width_k = wide // layers
    for l in range(layers):
        at = slice(l * width_k, (l + 1) * width_k)
        out[:rows, at] = total[l][:, at].astype(jnp.bfloat16)
    for i in range(rows // wide):
        out[rows + i * wide:rows + (i + 1) * wide, :] = pg_t[:, i * wide:(i + 1) * wide]


def whole_kernel(devices, acts, *refs):
    blocks, (pg_t, out, weights) = refs[:-3], refs[-3:]
    deep, wide, cores = levels(devices)
    me = lax.axis_index("seq")
    tall = blocks[0].shape[0] // deep
    for i, block in enumerate(blocks):
        for z in range(deep):
            at = owner(me, devices, (0, i // cores, i % cores)) % (wide * cores) + z * wide * cores
            weights[pl.ds(pl.multiple_of(at * tall, tall), tall), :] = block[z * tall:(z + 1) * tall, :]
    pack([jnp.dot(acts[l], weights[...], preferred_element_type=jnp.float32) for l in range(acts.shape[0])], pg_t, out)


def grads_kernel(devices, per_part, layers, rows, shifts, *refs):
    count = len(shifts)
    feats, (lengths, out, spread) = refs[:count], refs[count:]
    wide = feats[0].shape[1]
    runs = rows // wide
    width_k = wide // layers
    square = width_k * width_k
    _, across, cores = levels(devices)
    me = lax.axis_index("seq")
    sizes = lengths[pl.ds(me // per_part, 1), :]
    per_row = sizes.shape[1]
    upto = lax.broadcasted_iota(jnp.int32, (per_row, per_row), 1)
    which = lax.broadcasted_iota(jnp.int32, (per_row, per_row), 0)
    sizes = jnp.broadcast_to(sizes, (per_row, per_row))
    ends = jnp.sum(jnp.where(upto <= which, sizes, 0), axis=1, keepdims=True)
    starts = jnp.sum(jnp.where(upto < which, sizes, 0), axis=1, keepdims=True)
    member = []
    for shift in shifts:
        first = (owner(me, devices, shift) % per_part) * rows
        position = first + lax.broadcasted_iota(jnp.int32, (per_row, wide), 1)
        for i in range(runs):
            now = position + i * wide
            member.append(((now >= starts) & (now < ends)).astype(jnp.float32))
    member = jnp.concatenate(member, axis=1)
    for f, feat in enumerate(feats):
        for i in range(runs):
            at = (f * runs + i) * wide
            spread[:, at:at + wide] = feat[rows + i * wide:rows + (i + 1) * wide, :].astype(jnp.float32)
    low = lax.broadcasted_iota(jnp.int32, (per_row, 2 * width_k), 1) < width_k
    lanes = square // (across * cores)
    spot = me % (across * cores)
    for l in range(layers):
        px = []
        for feat in feats:
            own = feat[:rows, l * width_k:(l + 1) * width_k]
            px.append(jnp.concatenate([own, own], axis=1))
        px = jnp.concatenate(px, axis=0)
        for here, there, size in chunks(spot, devices, square):
            terms = []
            for i in range(size // width_k):
                row = l * width_k + there // width_k + i
                terms.append((member * spread[pl.ds(row, 1), :]).astype(jnp.bfloat16))
            sums = jnp.dot(jnp.concatenate(terms, axis=0), px, preferred_element_type=jnp.float32)
            for i in range(0, size // width_k, 2):
                even = sums[i * per_row:(i + 1) * per_row]
                odd = sums[(i + 1) * per_row:(i + 2) * per_row]
                at = l * lanes + here + i * width_k
                out[:, at:at + 2 * width_k] = jnp.where(low, even, odd).astype(jnp.bfloat16)


def total_kernel(devices, per_part, *refs):
    terms, out = refs[:-1], refs[-1]
    deep, across, cores = levels(devices)
    tall = terms[0].shape[0]
    if out.shape[0] == tall:
        total = terms[0][...].astype(jnp.float32)
        for term in terms[1:]:
            total = total + term[...].astype(jnp.float32)
        out[...] = total.astype(jnp.bfloat16)
        return
    me = lax.axis_index("seq")
    owned = [owner(me, devices, (shift, 0, 0)) // per_part for shift in range(deep)]
    for row in range(out.shape[0] // tall):
        total = jnp.zeros(terms[0].shape, jnp.float32)
        for home, term in zip(owned, terms):
            total = total + jnp.where(home == row, term[...].astype(jnp.float32), 0.0)
        out[row * tall:(row + 1) * tall, :] = total.astype(jnp.bfloat16)


def covariance_kernel(devices, shifts, *refs):
    count = len(shifts)
    blocks, (slots, pairs, logged, out, right, held, sems) = refs[:count], refs[count:]
    npair, band, square = held.shape
    seqs, full = right.shape
    layers = full // square
    _, across, cores = levels(devices)
    lanes = square // (across * cores)
    me = lax.axis_index("seq")
    for shift, block in zip(shifts, blocks):
        spot = owner(me, devices, shift) % (across * cores)
        for here, there, size in chunks(spot, devices, square):
            for l in range(layers):
                at = pl.multiple_of(l * square + there, size)
                right[:, pl.ds(at, size)] = block[:, l * lanes + here:l * lanes + here + size]
    scale = jnp.float32(1.0 / seqs)
    cols = min(1024, square)
    steps = square // cols
    copies = []
    for p in range(npair):
        if band % 128 == 0:
            at = pl.multiple_of(pairs[p, 0] * square + me * band, band)
            left = right[:, pl.ds(at, band)]
        else:
            offset = me * band
            at = pl.multiple_of(pairs[p, 0] * square + (offset // 128) * 128, 128)
            source = lax.broadcasted_iota(jnp.int32, (128, band), 0)
            target = lax.broadcasted_iota(jnp.int32, (128, band), 1)
            pick = (source == target + offset % 128).astype(jnp.float32).astype(jnp.bfloat16)
            left = jnp.dot(right[:, pl.ds(at, 128)], pick, preferred_element_type=jnp.float32).astype(jnp.bfloat16)
        for q in range(steps):
            at = pl.multiple_of(pairs[p, 1] * square + q * cols, cols)
            product = lax.dot_general(
                left, right[:, pl.ds(at, cols)], (((0,), (0,)), ((), ())), preferred_element_type=jnp.float32
            )
            held[p, :, q * cols:(q + 1) * cols] = product * scale
            where = (p, slice(None), pl.ds(q * cols, cols))
            copy = pltpu.make_async_copy(held.at[where], out.at[where], sems.at[p * steps + q])
            copy.start()
            copies.append(copy)
    own = me * CAP + lax.broadcasted_iota(jnp.int32, (CAP, seqs), 0)
    picker = (jnp.broadcast_to(slots[...], (CAP, seqs)) == own).astype(jnp.float32).astype(jnp.bfloat16)
    logged[...] = jnp.dot(picker, right[...], preferred_element_type=jnp.float32).astype(jnp.bfloat16)
    for copy in copies:
        copy.wait()


def shards(acts, cots, proj_in, proj_out, lengths, slots, pairs):
    layers, rows, width = acts.shape
    wide = proj_out.shape[1]
    width_k = wide // layers
    square = width_k * width_k
    devices = lax.axis_size("seq")
    rows_all, per_row = lengths.shape
    seqs = slots.shape[0]
    npair = pairs.shape[0]
    per_part = devices // rows_all
    band = square // devices
    deep, across, cores = levels(devices)
    line = across * cores
    tall = proj_in.shape[0]
    params = pltpu.CompilerParams(vmem_limit_bytes=52 * MIB)

    pg_t = pl.pallas_call(
        pg_kernel,
        out_shape=jax.ShapeDtypeStruct((wide, rows), jnp.bfloat16),
        in_specs=[ANY, ANY],
        out_specs=VMEM,
        scratch_shapes=[
            pltpu.VMEM(cots.shape, jnp.bfloat16),
            pltpu.VMEM(proj_out.shape, jnp.bfloat16),
            pltpu.SemaphoreType.DMA((layers + 1,)),
        ],
        compiler_params=params,
        cost_estimate=pl.CostEstimate(flops=1 << 27, bytes_accessed=cots.size * 2, transcendentals=0),
        name="pg",
    )(cots, proj_out)

    feat_type = jax.ShapeDtypeStruct((2 * rows, wide), jnp.bfloat16)
    if tall % 128 == 0:
        spins = sorted(range(deep), key=lambda z: min(z, deep - z))
        column = {(z, 0, 0): send(proj_in, devices, (z, 0, 0)) if z else proj_in for z in spins}
        beside = {(k[0], x, 0): send(v, devices, (0, x, 0)) for x in range(1, across) for k, v in column.items()}
        twin = {(*k[:2], c): send(v, devices, (0, 0, c)) for c in range(1, cores) for k, v in column.items()}
        last = {(*k[:2], c): send(v, devices, (0, 0, c)) for c in range(1, cores) for k, v in beside.items()}
        stages = [stage for stage in (column, {**beside, **twin}, last) if stage]
        value = None
        for i, stage in enumerate(stages):
            begin, end = i == 0, i == len(stages) - 1
            more = (() if begin else (value,)) + ((pg_t,) if end else ())
            value = pl.pallas_call(
                functools.partial(px_kernel, devices, tuple(stage), begin, end),
                out_shape=feat_type if end else jax.ShapeDtypeStruct((layers, rows, wide), jnp.float32),
                in_specs=[ANY] + [VMEM] * (len(stage) + len(more)),
                out_specs=VMEM,
                scratch_shapes=[
                    pltpu.VMEM((len(stage), layers, rows, tall), jnp.bfloat16),
                    pltpu.SemaphoreType.DMA((len(stage),)),
                ],
                compiler_params=params,
                cost_estimate=pl.CostEstimate(
                    flops=2 * acts.size * wide * len(stage) // devices,
                    bytes_accessed=2 * acts.size * len(stage) // devices,
                    transcendentals=0,
                ),
                name="px",
            )(acts, *stage.values(), *more)
    else:
        groups = [[z * line + i for z in range(deep)] for i in range(line)]
        column = lax.all_to_all(jnp.tile(proj_in, (deep, 1)), "seq", 0, 0, axis_index_groups=groups, tiled=True)
        blocks = [column] + [send(column, devices, (0, x, 0)) for x in range(1, across)]
        blocks = [block if c == 0 else send(block, devices, (0, 0, c)) for block in blocks for c in range(cores)]
        value = pl.pallas_call(
            functools.partial(whole_kernel, devices),
            out_shape=feat_type,
            in_specs=[VMEM] * (2 + len(blocks)),
            out_specs=VMEM,
            scratch_shapes=[pltpu.VMEM((width, wide), jnp.bfloat16)],
            compiler_params=params,
            name="px",
        )(acts, *blocks, pg_t)

    def plane(block):
        held = {(0, x, 0): send(block, devices, (0, x, 0)) if x else block for x in range(across)}
        return {(*k[:2], c): send(v, devices, (0, 0, c)) if c else v for c in range(cores) for k, v in held.items()}

    feats = plane(value)
    lanes = layers * square // line
    sums = pl.pallas_call(
        functools.partial(grads_kernel, devices, per_part, layers, rows, tuple(feats)),
        out_shape=jax.ShapeDtypeStruct((per_row, lanes), jnp.bfloat16),
        in_specs=[VMEM] * (len(feats) + 1),
        out_specs=VMEM,
        scratch_shapes=[pltpu.VMEM((wide, rows * line), jnp.float32)],
        compiler_params=params,
        name="grads",
    )(*feats.values(), lengths)
    terms = [send(sums, devices, (z, 0, 0)) if z else sums for z in range(deep)]
    total = pl.pallas_call(
        functools.partial(total_kernel, devices, per_part),
        out_shape=jax.ShapeDtypeStruct((seqs, lanes), jnp.bfloat16),
        in_specs=[VMEM] * deep,
        out_specs=VMEM,
        compiler_params=params,
        name="total",
    )(*terms)
    full = plane(total)
    return pl.pallas_call(
        functools.partial(covariance_kernel, devices, tuple(full)),
        out_shape=[
            jax.ShapeDtypeStruct((CAP, layers * square), jnp.bfloat16),
            jax.ShapeDtypeStruct((npair, band, square), jnp.float32),
        ],
        in_specs=[VMEM] * (len(full) + 1) + [SMEM],
        out_specs=[VMEM, ANY],
        scratch_shapes=[
            pltpu.VMEM((seqs, layers * square), jnp.bfloat16),
            pltpu.VMEM((npair, band, square), jnp.float32),
            pltpu.SemaphoreType.DMA((npair * (square // min(1024, square)),)),
        ],
        compiler_params=params,
        name="covariance",
    )(*full.values(), slots.reshape(1, seqs), pairs)


def solution(mesh):
    in_specs = (
        P(None, ("groups", "seq"), None),
        P(None, ("groups", "seq"), None),
        P("seq", None),
        P(),
        P("groups", None),
        P("groups"),
        P(),
    )
    out_specs = (P(("groups", "seq"), None), P("groups", "seq", None))
    return jax.shard_map(shards, mesh=mesh, in_specs=in_specs, out_specs=out_specs, check_vma=False)
```

time: 92.4 us -> 74.9 us (0.81)
  blocking collectives: 39.4 us -> 0 us
  starting transfers between devices: 5.59 us -> 21.5 us
  waiting for transfers between devices: 25.4 us -> 33.1 us
  Pallas kernels: 17.5 us -> 16 us
    all_to_all x2 -> x0, blocking collectives: 39.4 us -> none  [the longest x1 20.6 us: shards(): lax.all_to_all(jnp.tile(proj_in, (deep, 1)), 'seq', 0, 0, axis_index_grou...]
    ppermute x3 -> x24, waiting for transfers between devices: 11 us -> 33.1 us  [send(): return lax.ppermute(value, 'seq', perm)]
    ppermute x3 -> x24, starting transfers between devices: 1.5 us -> 21.5 us  [send(): return lax.ppermute(value, 'seq', perm)]
    all_to_all x1 -> x0, waiting for transfers between devices: 14.4 us -> none  [shards(): summed = lax.all_to_all(total, 'seq', 0, 0, tiled=True)]
    all_to_all x1 -> x0, starting transfers between devices: 4.1 us -> none  [shards(): summed = lax.all_to_all(total, 'seq', 0, 0, tiled=True)]
    pallas_call x7 -> x6, Pallas kernels: 17 us -> 15.2 us  [the longest x3 7.99 us: shards(): pl.pallas_call(functools.partial(px_kernel, devices, tuple(stage), begin,...]
    another operation x1 -> x0, local copies, waits for them, and re-layouts: 0.97 us -> none  [shards(): jnp.tile(proj_in, (deep, 1))]
    unnamed x11 -> x13, local copies, waits for them, and re-layouts: 2.29 us -> 3.18 us
  transfers between devices with their start and end apart: 4 -> 24, of which waited for: 2 -> 11; matrix products, arithmetic and copies ran while one was open for 0% -> 0% of each run, Pallas kernels for 8% -> 9%
where the time goes in v3:
time: 74.9 us; the launch traced here: 74.6 us
  waiting for transfers between devices  33.1 us (44%)
  starting transfers between devices  21.5 us (29%)
  Pallas kernels  16 us (21%)
  local copies, waits for them, and re-layouts  3.18 us (4%)
  between operations  0.76 us (1%)
    ppermute x24, waiting for transfers between devices, send(): return lax.ppermute(value, 'seq', perm)  33.1 us
    ppermute x24, starting transfers between devices, send(): return lax.ppermute(value, 'seq', perm)  21.5 us
    pallas_call x3, Pallas kernels, shards(): pl.pallas_call(functools.partial(px_kernel, devices, tuple(stage), begin,...  7.99 us
    pallas_call x1, Pallas kernels, shards(): pl.pallas_call(functools.partial(covariance_kernel, devices, tuple(full))...  6.26 us
    unnamed x13, local copies, waits for them, and re-layouts  3.18 us
  transfers between devices with their start and end apart: 24, of which 11 were waited for; matrix products, arithmetic and copies ran while one was open for 0% of the time, Pallas kernels for 9%

profile of v3, /device:TPU:0, one launch (start us, length us, event | category | flops | bytes accessed | tf_op | source)
XLA Modules:
  0.0 74.6 jit_solution(11763100600789580909)
XLA Ops:
  0.6 4.1 %collective-permute-start.8 = (bf16[512,128]{1,0:T(8,128)(2,1)}, bf16[512,128]{1,0:T(8,128)(2,1)S(1)}, u32[]{:S(2)}, u32[]{:S(2)}) collective-permute-start(bf16[512,128]{1,0:T(8,128)(2,1)} %refs_0_.1), channel_id=1, source_target_pairs={{0,8},{1,9},{2,10},{3,11},{4,12},{5,13},{6,14},{7,15},{8,0},{9,1},... | collective-permute-start | bytes 393224 | tf_op jit(solution)/shard_map/ppermute | solution.py:44
  4.7 1.3 %collective-permute-start.5 = (bf16[512,128]{1,0:T(8,128)(2,1)}, bf16[512,128]{1,0:T(8,128)(2,1)S(1)}, u32[]{:S(2)}, u32[]{:S(2)}) collective-permute-start(bf16[512,128]{1,0:T(8,128)(2,1)} %refs_0_.1), channel_id=1, source_target_pairs={{0,12},{1,13},{2,14},{3,15},{4,0},{5,1},{6,2},{7,3},{8,4},{9,5},{1... | collective-permute-start | bytes 393224 | tf_op jit(solution)/shard_map/ppermute | solution.py:44
  6.1 0.7 collective-permute-start.2
  6.8 1.5 %collective-permute-start = (bf16[512,128]{1,0:T(8,128)(2,1)}, bf16[512,128]{1,0:T(8,128)(2,1)S(1)}, u32[]{:S(2)}, u32[]{:S(2)}) collective-permute-start(bf16[512,128]{1,0:T(8,128)(2,1)} %refs_0_.1), channel_id=1, source_target_pairs={{0,2},{1,3},{2,0},{3,1},{4,6},{5,7},{6,4},{7,5},{8,10},{9,11},{10,... | collective-permute-start | bytes 393224 | tf_op jit(solution)/shard_map/ppermute | solution.py:44
  8.3 4.6 %collective-permute-done.8.refs_3_ = bf16[512,128]{1,0:T(8,128)(2,1)S(1)} collective-permute-done((bf16[512,128]{1,0:T(8,128)(2,1)}, bf16[512,128]{1,0:T(8,128)(2,1)S(1)}, u32[]{:S(2)}, u32[]{:S(2)}) %collective-permute-start.8) | collective-permute-done | bytes 131104 | tf_op jit(solution)/shard_map/ppermute | solution.py:44
  12.9 2.1 %collective-permute-start.9 = (bf16[512,128]{1,0:T(8,128)(2,1)S(1)}, bf16[512,128]{1,0:T(8,128)(2,1)S(1)}, u32[]{:S(2)}, u32[]{:S(2)}) collective-permute-start(bf16[512,128]{1,0:T(8,128)(2,1)S(1)} %collective-permute-done.8.refs_3_), channel_id=1, source_target_pairs={{0,2},{1,3},{2,0},{3,1},{4,6},{5,7},{6,4},{7,5},{8,10},{9,11},{10,... | collective-permute-start | bytes 393224 | tf_op jit(solution)/shard_map/ppermute | solution.py:44
  15.0 0.2 collective-permute-done.2.refs_1_
  15.3 1.5 %collective-permute-start.6 = (bf16[512,128]{1,0:T(8,128)(2,1)S(1)}, bf16[512,128]{1,0:T(8,128)(2,1)S(1)}, u32[]{:S(2)}, u32[]{:S(2)}) collective-permute-start(bf16[512,128]{1,0:T(8,128)(2,1)S(1)} %collective-permute-done.5.refs_2_), channel_id=1, source_target_pairs={{0,2},{1,3},{2,0},{3,1},{4,6},{5,7},{6,4},{7,5},{8,10},{9,11},{10,... | collective-permute-start | bytes 393224 | tf_op jit(solution)/shard_map/ppermute | solution.py:44
  16.8 0.5 collective-permute-start.3
  17.3 2.1 %collective-permute-done.9.refs_3_ = bf16[512,128]{1,0:T(8,128)(2,1)S(1)} collective-permute-done((bf16[512,128]{1,0:T(8,128)(2,1)S(1)}, bf16[512,128]{1,0:T(8,128)(2,1)S(1)}, u32[]{:S(2)}, u32[]{:S(2)}) %collective-permute-start.9) | collective-permute-done | bytes 131104 | tf_op jit(solution)/shard_map/ppermute | solution.py:44
  19.4 0.5 collective-permute-start.10
  19.9 2.3 %collective-permute-done.6.refs_2_ = bf16[512,128]{1,0:T(8,128)(2,1)S(1)} collective-permute-done((bf16[512,128]{1,0:T(8,128)(2,1)S(1)}, bf16[512,128]{1,0:T(8,128)(2,1)S(1)}, u32[]{:S(2)}, u32[]{:S(2)}) %collective-permute-start.6) | collective-permute-done | bytes 131104 | tf_op jit(solution)/shard_map/ppermute | solution.py:44
  22.2 2.6 %collective-permute-done.3.refs_1_ = bf16[512,128]{1,0:T(8,128)(2,1)S(1)} collective-permute-done((bf16[512,128]{1,0:T(8,128)(2,1)S(1)}, bf16[512,128]{1,0:T(8,128)(2,1)S(1)}, u32[]{:S(2)}, u32[]{:S(2)}) %collective-permute-start.3) | collective-permute-done | bytes 131104 | tf_op jit(solution)/shard_map/ppermute | solution.py:44
  24.8 1.2 %copy-done = bf16[2,256,1024]{2,1,0:T(8,128)(2,1)S(1)} copy-done((bf16[2,256,1024]{2,1,0:T(8,128)(2,1)S(1)}, bf16[2,256,1024]{2,1,0:T(8,128)(2,1)}, u32[]{:S(2)}) %copy-start) | copy-done | bytes 1048600
  26.1 0.9 %copy-done.1 = bf16[1024,128]{1,0:T(8,128)(2,1)S(1)} copy-done((bf16[1024,128]{1,0:T(8,128)(2,1)S(1)}, bf16[1024,128]{1,0:T(8,128)(2,1)}, u32[]{:S(2)}) %copy-start.1) | copy-done | bytes 262168
  27.0 0.8 %pg.1.refs_5_ = bf16[128,256]{1,0:T(8,128)(2,1)S(1)} custom-call(bf16[2,256,1024]{2,1,0:T(8,128)(2,1)S(1)} %copy-done, bf16[1024,128]{1,0:T(8,128)(2,1)S(1)} %copy-done.1), custom_call_target="tpu_custom_call" | custom-call | flops 134217728 | bytes 1048576 | tf_op jit(solution)/shard_map/pg/pallas_call | solution.py:249
  27.8 0.9 %copy-done.2 = bf16[512,128]{1,0:T(8,128)(2,1)S(1)} copy-done((bf16[512,128]{1,0:T(8,128)(2,1)S(1)}, bf16[512,128]{1,0:T(8,128)(2,1)}, u32[]{:S(2)}) %copy-start.2) | copy-done | bytes 131096
  28.7 2.3 %px.3.refs_8_ = f32[2,256,128]{2,1,0:T(8,128)S(1)} custom-call(bf16[2,256,8192]{2,1,0:T(8,128)(2,1)} %acts.5, bf16[512,128]{1,0:T(8,128)(2,1)S(1)} %copy-done.2, bf16[512,128]{1,0:T(8,128)(2,1)S(1)} %collective-permute-done.2.refs_1_, bf16[512,128]{1,0:T(8,128)(2,1)S(1)} %collective-permute-done.5.refs_2_, bf16[512,128]{1,0:T(8,128)(2,1)S(1)} %collective-permute-done.8.refs_3_), custom_call_target="tpu_custom_call" | custom-call | flops 268435456 | bytes 2097152 | tf_op jit(solution)/shard_map/px/pallas_call | solution.py:276
  31.0 3.5 %px.4.refs_4_ = f32[2,256,128]{2,1,0:T(8,128)S(1)} custom-call(bf16[2,256,8192]{2,1,0:T(8,128)(2,1)} %acts.5, bf16[512,128]{1,0:T(8,128)(2,1)S(1)} %collective-permute-done.refs_0_, bf16[512,128]{1,0:T(8,128)(2,1)S(1)} %collective-permute-done.3.refs_1_, bf16[512,128]{1,0:T(8,128)(2,1)S(1)} %collective-permute-done.6.refs_2_, ...), custom_call_target="tpu_custom_call" | custom-call | flops 536870912 | bytes 4194304 | tf_op jit(solution)/shard_map/px/pallas_call | solution.py:276
  34.5 2.3 %px.5.refs_0_ = bf16[512,128]{1,0:T(8,128)(2,1)S(1)} custom-call(bf16[2,256,8192]{2,1,0:T(8,128)(2,1)} %acts.5, bf16[512,128]{1,0:T(8,128)(2,1)S(1)} %collective-permute-done.1.refs_0_, bf16[512,128]{1,0:T(8,128)(2,1)S(1)} %collective-permute-done.4.refs_1_, bf16[512,128]{1,0:T(8,128)(2,1)S(1)} %collective-permute-done.7.refs_2_, ...), custom_call_target="tpu_custom_call" | custom-call | flops 268435456 | bytes 2097152 | tf_op jit(solution)/shard_map/px/pallas_call | solution.py:276
  36.8 1.8 %collective-permute-start.15 = (bf16[512,128]{1,0:T(8,128)(2,1)S(1)}, bf16[512,128]{1,0:T(8,128)(2,1)S(1)}, u32[]{:S(2)}, u32[]{:S(2)}) collective-permute-start(bf16[512,128]{1,0:T(8,128)(2,1)S(1)} %px.5.refs_0_), channel_id=1, source_target_pairs={{0,2},{1,3},{2,0},{3,1},{4,6},{5,7},{6,4},{7,5},{8,10},{9,11},{10,... | collective-permute-start | bytes 393224 | tf_op jit(solution)/shard_map/ppermute | solution.py:44
  38.9 3.9 %collective-permute-done.15.refs_1_ = bf16[512,128]{1,0:T(8,128)(2,1)S(1)} collective-permute-done((bf16[512,128]{1,0:T(8,128)(2,1)S(1)}, bf16[512,128]{1,0:T(8,128)(2,1)S(1)}, u32[]{:S(2)}, u32[]{:S(2)}) %collective-permute-start.15) | collective-permute-done | bytes 131104 | tf_op jit(solution)/shard_map/ppermute | solution.py:44
  42.8 1.3 %collective-permute-done.17.refs_3_ = bf16[512,128]{1,0:T(8,128)(2,1)S(1)} collective-permute-done((bf16[512,128]{1,0:T(8,128)(2,1)S(1)}, bf16[512,128]{1,0:T(8,128)(2,1)S(1)}, u32[]{:S(2)}, u32[]{:S(2)}) %collective-permute-start.17) | collective-permute-done | bytes 131104 | tf_op jit(solution)/shard_map/ppermute | solution.py:44
  44.1 0.9 %grads.1.refs_0_ = bf16[32,2048]{1,0:T(8,128)(2,1)S(1)} custom-call(bf16[512,128]{1,0:T(8,128)(2,1)S(1)} %px.5.refs_0_, bf16[512,128]{1,0:T(8,128)(2,1)S(1)} %collective-permute-done.15.refs_1_, bf16[512,128]{1,0:T(8,128)(2,1)S(1)} %collective-permute-done.16.refs_2_, bf16[512,128]{1,0:T(8,128)(2,1)S(1)} %collective-permute-done.17.refs_3_, ...), custom_call_target="tpu_custom_call" | custom-call | tf_op jit(solution)/shard_map/grads/pallas_call | solution.py:314
  45.1 4.5 %collective-permute-start.20 = (bf16[32,2048]{1,0:T(8,128)(2,1)S(1)}, bf16[32,2048]{1,0:T(8,128)(2,1)S(1)}, u32[]{:S(2)}, u32[]{:S(2)}) collective-permute-start(bf16[32,2048]{1,0:T(8,128)(2,1)S(1)} %grads.1.refs_0_), channel_id=1, source_target_pairs={{0,12},{1,13},{2,14},{3,15},{4,0},{5,1},{6,2},{7,3},{8,4},{9,5},{1... | collective-permute-start | bytes 393224 | tf_op jit(solution)/shard_map/ppermute | solution.py:44
  49.8 0.8 %collective-permute-start.18 = (bf16[32,2048]{1,0:T(8,128)(2,1)S(1)}, bf16[32,2048]{1,0:T(8,128)(2,1)S(1)}, u32[]{:S(2)}, u32[]{:S(2)}) collective-permute-start(bf16[32,2048]{1,0:T(8,128)(2,1)S(1)} %grads.1.refs_0_), channel_id=1, source_target_pairs={{0,4},{1,5},{2,6},{3,7},{4,8},{5,9},{6,10},{7,11},{8,12},{9,13},{1... | collective-permute-start | bytes 393224 | tf_op jit(solution)/shard_map/ppermute | solution.py:44
  50.6 2.9 %collective-permute-done.20.refs_3_ = bf16[32,2048]{1,0:T(8,128)(2,1)S(1)} collective-permute-done((bf16[32,2048]{1,0:T(8,128)(2,1)S(1)}, bf16[32,2048]{1,0:T(8,128)(2,1)S(1)}, u32[]{:S(2)}, u32[]{:S(2)}) %collective-permute-start.20) | collective-permute-done | bytes 131104 | tf_op jit(solution)/shard_map/ppermute | solution.py:44
  53.5 8.2 %collective-permute-done.19.refs_2_ = bf16[32,2048]{1,0:T(8,128)(2,1)S(1)} collective-permute-done((bf16[32,2048]{1,0:T(8,128)(2,1)S(1)}, bf16[32,2048]{1,0:T(8,128)(2,1)S(1)}, u32[]{:S(2)}, u32[]{:S(2)}) %collective-permute-start.19) | collective-permute-done | bytes 131104 | tf_op jit(solution)/shard_map/ppermute | solution.py:44
  61.8 1.6 %collective-permute-start.21 = (bf16[32,2048]{1,0:T(8,128)(2,1)S(1)}, bf16[32,2048]{1,0:T(8,128)(2,1)S(1)}, u32[]{:S(2)}, u32[]{:S(2)}) collective-permute-start(bf16[32,2048]{1,0:T(8,128)(2,1)S(1)} %total.1.refs_0_), channel_id=1, source_target_pairs={{0,2},{1,3},{2,0},{3,1},{4,6},{5,7},{6,4},{7,5},{8,10},{9,11},{10,... | collective-permute-start | bytes 393224 | tf_op jit(solution)/shard_map/ppermute | solution.py:44
  63.4 3.6 %collective-permute-done.21.refs_1_ = bf16[32,2048]{1,0:T(8,128)(2,1)S(1)} collective-permute-done((bf16[32,2048]{1,0:T(8,128)(2,1)S(1)}, bf16[32,2048]{1,0:T(8,128)(2,1)S(1)}, u32[]{:S(2)}, u32[]{:S(2)}) %collective-permute-start.21) | collective-permute-done | bytes 131104 | tf_op jit(solution)/shard_map/ppermute | solution.py:44
  67.1 1.2 %collective-permute-done.23.refs_3_ = bf16[32,2048]{1,0:T(8,128)(2,1)S(1)} collective-permute-done((bf16[32,2048]{1,0:T(8,128)(2,1)S(1)}, bf16[32,2048]{1,0:T(8,128)(2,1)S(1)}, u32[]{:S(2)}, u32[]{:S(2)}) %collective-permute-start.23) | collective-permute-done | bytes 131104 | tf_op jit(solution)/shard_map/ppermute | solution.py:44
  68.4 6.3 %covariance.1 = (bf16[2,8192]{1,0:T(2,128)(2,1)}, f32[3,256,4096]{2,1,0:T(8,128)}) custom-call(bf16[32,2048]{1,0:T(8,128)(2,1)S(1)} %total.1.refs_0_, bf16[32,2048]{1,0:T(8,128)(2,1)S(1)} %collective-permute-done.21.refs_1_, bf16[32,2048]{1,0:T(8,128)(2,1)S(1)} %collective-permute-done.22.refs_2_, bf16[32,2048]{1,0:T(8,128)(2,1)S(1)} %collective-permute-done.23.refs_3_, ...), custom_call_target="tpu_custom_call" | custom-call | tf_op jit(solution)/shard_map/covariance/pallas_call | solution.py:333
  (36 shorter events, 0.7 us)
Async XLA Ops:
  0.6 12.3 %collective-permute-start.8 = (bf16[512,128]{1,0:T(8,128)(2,1)}, bf16[512,128]{1,0:T(8,128)(2,1)S(1)}, u32[]{:S(2)}, u32[]{:S(2)}) collective-permute-start(bf16[512,128]{1,0:T(8,128)(2,1)} %refs_0_.1), channel_id=1, source_target_pairs={{0,8},{1,9},{2,10},{3,11},{4,12},{5,13},{6,14},{7,15},{8,0},{9,1},... | collective-permute-start | bytes 393224 | tf_op jit(solution)/shard_map/ppermute | solution.py:44
  4.7 8.2 %collective-permute-start.5 = (bf16[512,128]{1,0:T(8,128)(2,1)}, bf16[512,128]{1,0:T(8,128)(2,1)S(1)}, u32[]{:S(2)}, u32[]{:S(2)}) collective-permute-start(bf16[512,128]{1,0:T(8,128)(2,1)} %refs_0_.1), channel_id=1, source_target_pairs={{0,12},{1,13},{2,14},{3,15},{4,0},{5,1},{6,2},{7,3},{8,4},{9,5},{1... | collective-permute-start | bytes 393224 | tf_op jit(solution)/shard_map/ppermute | solution.py:44
  6.1 9.2 %collective-permute-start.2 = (bf16[512,128]{1,0:T(8,128)(2,1)}, bf16[512,128]{1,0:T(8,128)(2,1)S(1)}, u32[]{:S(2)}, u32[]{:S(2)}) collective-permute-start(bf16[512,128]{1,0:T(8,128)(2,1)} %refs_0_.1), channel_id=1, source_target_pairs={{0,4},{1,5},{2,6},{3,7},{4,8},{5,9},{6,10},{7,11},{8,12},{9,13},{1... | collective-permute-start | bytes 393224 | tf_op jit(solution)/shard_map/ppermute | solution.py:44
  6.8 8.5 %collective-permute-start = (bf16[512,128]{1,0:T(8,128)(2,1)}, bf16[512,128]{1,0:T(8,128)(2,1)S(1)}, u32[]{:S(2)}, u32[]{:S(2)}) collective-permute-start(bf16[512,128]{1,0:T(8,128)(2,1)} %refs_0_.1), channel_id=1, source_target_pairs={{0,2},{1,3},{2,0},{3,1},{4,6},{5,7},{6,4},{7,5},{8,10},{9,11},{10,... | collective-permute-start | bytes 393224 | tf_op jit(solution)/shard_map/ppermute | solution.py:44
  8.2 8.5 %collective-permute-start.11 = (bf16[512,128]{1,0:T(8,128)(2,1)}, bf16[512,128]{1,0:T(8,128)(2,1)S(1)}, u32[]{:S(2)}, u32[]{:S(2)}) collective-permute-start(bf16[512,128]{1,0:T(8,128)(2,1)} %refs_0_.1), channel_id=1, source_target_pairs={{0,1},{1,0},{2,3},{3,2},{4,5},{5,4},{6,7},{7,6},{8,9},{9,8},{10,11... | collective-permute-start | bytes 393224 | tf_op jit(solution)/shard_map/ppermute | solution.py:44
  12.9 4.4 %collective-permute-start.14 = (bf16[512,128]{1,0:T(8,128)(2,1)S(1)}, bf16[512,128]{1,0:T(8,128)(2,1)S(1)}, u32[]{:S(2)}, u32[]{:S(2)}) collective-permute-start(bf16[512,128]{1,0:T(8,128)(2,1)S(1)} %collective-permute-done.8.refs_3_), channel_id=1, source_target_pairs={{0,1},{1,0},{2,3},{3,2},{4,5},{5,4},{6,7},{7,6},{8,9},{9,8},{10,11... | collective-permute-start | bytes 393224 | tf_op jit(solution)/shard_map/ppermute | solution.py:44
  12.9 6.5 %collective-permute-start.9 = (bf16[512,128]{1,0:T(8,128)(2,1)S(1)}, bf16[512,128]{1,0:T(8,128)(2,1)S(1)}, u32[]{:S(2)}, u32[]{:S(2)}) collective-permute-start(bf16[512,128]{1,0:T(8,128)(2,1)S(1)} %collective-permute-done.8.refs_3_), channel_id=1, source_target_pairs={{0,2},{1,3},{2,0},{3,1},{4,6},{5,7},{6,4},{7,5},{8,10},{9,11},{10,... | collective-permute-start | bytes 393224 | tf_op jit(solution)/shard_map/ppermute | solution.py:44
  15.3 4.1 %collective-permute-start.13 = (bf16[512,128]{1,0:T(8,128)(2,1)S(1)}, bf16[512,128]{1,0:T(8,128)(2,1)S(1)}, u32[]{:S(2)}, u32[]{:S(2)}) collective-permute-start(bf16[512,128]{1,0:T(8,128)(2,1)S(1)} %collective-permute-done.5.refs_2_), channel_id=1, source_target_pairs={{0,1},{1,0},{2,3},{3,2},{4,5},{5,4},{6,7},{7,6},{8,9},{9,8},{10,11... | collective-permute-start | bytes 393224 | tf_op jit(solution)/shard_map/ppermute | solution.py:44
  15.3 6.9 %collective-permute-start.6 = (bf16[512,128]{1,0:T(8,128)(2,1)S(1)}, bf16[512,128]{1,0:T(8,128)(2,1)S(1)}, u32[]{:S(2)}, u32[]{:S(2)}) collective-permute-start(bf16[512,128]{1,0:T(8,128)(2,1)S(1)} %collective-permute-done.5.refs_2_), channel_id=1, source_target_pairs={{0,2},{1,3},{2,0},{3,1},{4,6},{5,7},{6,4},{7,5},{8,10},{9,11},{10,... | collective-permute-start | bytes 393224 | tf_op jit(solution)/shard_map/ppermute | solution.py:44
  16.8 8.0 %collective-permute-start.3 = (bf16[512,128]{1,0:T(8,128)(2,1)S(1)}, bf16[512,128]{1,0:T(8,128)(2,1)S(1)}, u32[]{:S(2)}, u32[]{:S(2)}) collective-permute-start(bf16[512,128]{1,0:T(8,128)(2,1)S(1)} %collective-permute-done.2.refs_1_), channel_id=1, source_target_pairs={{0,2},{1,3},{2,0},{3,1},{4,6},{5,7},{6,4},{7,5},{8,10},{9,11},{10,... | collective-permute-start | bytes 393224 | tf_op jit(solution)/shard_map/ppermute | solution.py:44
  17.3 13.7 %collective-permute-start.12 = (bf16[512,128]{1,0:T(8,128)(2,1)S(1)}, bf16[512,128]{1,0:T(8,128)(2,1)S(1)}, u32[]{:S(2)}, u32[]{:S(2)}) collective-permute-start(bf16[512,128]{1,0:T(8,128)(2,1)S(1)} %collective-permute-done.2.refs_1_), channel_id=1, source_target_pairs={{0,1},{1,0},{2,3},{3,2},{4,5},{5,4},{6,7},{7,6},{8,9},{9,8},{10,11... | collective-permute-start | bytes 393224 | tf_op jit(solution)/shard_map/ppermute | solution.py:44
  19.4 15.1 %collective-permute-start.1 = (bf16[512,128]{1,0:T(8,128)(2,1)S(1)}, bf16[512,128]{1,0:T(8,128)(2,1)S(1)}, u32[]{:S(2)}, u32[]{:S(2)}) collective-permute-start(bf16[512,128]{1,0:T(8,128)(2,1)S(1)} %collective-permute-done.refs_0_), channel_id=1, source_target_pairs={{0,1},{1,0},{2,3},{3,2},{4,5},{5,4},{6,7},{7,6},{8,9},{9,8},{10,11... | collective-permute-start | bytes 393224 | tf_op jit(solution)/shard_map/ppermute | solution.py:44
  19.4 15.1 %collective-permute-start.10 = (bf16[512,128]{1,0:T(8,128)(2,1)S(1)}, bf16[512,128]{1,0:T(8,128)(2,1)S(1)}, u32[]{:S(2)}, u32[]{:S(2)}) collective-permute-start(bf16[512,128]{1,0:T(8,128)(2,1)S(1)} %collective-permute-done.9.refs_3_), channel_id=1, source_target_pairs={{0,1},{1,0},{2,3},{3,2},{4,5},{5,4},{6,7},{7,6},{8,9},{9,8},{10,11... | collective-permute-start | bytes 393224 | tf_op jit(solution)/shard_map/ppermute | solution.py:44
  22.2 12.3 %collective-permute-start.7 = (bf16[512,128]{1,0:T(8,128)(2,1)S(1)}, bf16[512,128]{1,0:T(8,128)(2,1)S(1)}, u32[]{:S(2)}, u32[]{:S(2)}) collective-permute-start(bf16[512,128]{1,0:T(8,128)(2,1)S(1)} %collective-permute-done.6.refs_2_), channel_id=1, source_target_pairs={{0,1},{1,0},{2,3},{3,2},{4,5},{5,4},{6,7},{7,6},{8,9},{9,8},{10,11... | collective-permute-start | bytes 393224 | tf_op jit(solution)/shard_map/ppermute | solution.py:44
  24.8 9.7 %collective-permute-start.4 = (bf16[512,128]{1,0:T(8,128)(2,1)S(1)}, bf16[512,128]{1,0:T(8,128)(2,1)S(1)}, u32[]{:S(2)}, u32[]{:S(2)}) collective-permute-start(bf16[512,128]{1,0:T(8,128)(2,1)S(1)} %collective-permute-done.3.refs_1_), channel_id=1, source_target_pairs={{0,1},{1,0},{2,3},{3,2},{4,5},{5,4},{6,7},{7,6},{8,9},{9,8},{10,11... | collective-permute-start | bytes 393224 | tf_op jit(solution)/shard_map/ppermute | solution.py:44
  24.8 1.2 %copy-start = (bf16[2,256,1024]{2,1,0:T(8,128)(2,1)S(1)}, bf16[2,256,1024]{2,1,0:T(8,128)(2,1)}, u32[]{:S(2)}) copy-start(bf16[2,256,1024]{2,1,0:T(8,128)(2,1)} %cots.1) | copy-start | bytes 3145732
  26.0 0.9 %copy-start.1 = (bf16[1024,128]{1,0:T(8,128)(2,1)S(1)}, bf16[1024,128]{1,0:T(8,128)(2,1)}, u32[]{:S(2)}) copy-start(bf16[1024,128]{1,0:T(8,128)(2,1)} %proj_out.1) | copy-start | bytes 786436
  27.8 0.9 %copy-start.2 = (bf16[512,128]{1,0:T(8,128)(2,1)S(1)}, bf16[512,128]{1,0:T(8,128)(2,1)}, u32[]{:S(2)}) copy-start(bf16[512,128]{1,0:T(8,128)(2,1)} %refs_0_.1) | copy-start | bytes 393220
  28.7 15.4 %copy-start.4 = (s32[1,32]{1,0:T(1,128)S(1)}, s32[1,32]{1,0:T(1,128)}, u32[]{:S(2)}) copy-start(s32[1,32]{1,0:T(1,128)} %refs_4_.1) | copy-start | bytes 388
  31.0 36.0 %copy-start.5 = (s32[3,2]{0,1:T(2,128)S(1)}, s32[3,2]{0,1:T(2,128)}, u32[]{:S(2)}) copy-start(s32[3,2]{0,1:T(2,128)} %param.13) | copy-start | bytes 76
  31.0 37.3 %copy-start.3 = (s32[32]{0:T(128)S(1)}, s32[32]{0:T(128)}, u32[]{:S(2)}) copy-start(s32[32]{0:T(128)} %param.12) | copy-start | bytes 388
  36.8 6.0 %collective-permute-start.15 = (bf16[512,128]{1,0:T(8,128)(2,1)S(1)}, bf16[512,128]{1,0:T(8,128)(2,1)S(1)}, u32[]{:S(2)}, u32[]{:S(2)}) collective-permute-start(bf16[512,128]{1,0:T(8,128)(2,1)S(1)} %px.5.refs_0_), channel_id=1, source_target_pairs={{0,2},{1,3},{2,0},{3,1},{4,6},{5,7},{6,4},{7,5},{8,10},{9,11},{10,... | collective-permute-start | bytes 393224 | tf_op jit(solution)/shard_map/ppermute | solution.py:44
  38.6 4.2 %collective-permute-start.16 = (bf16[512,128]{1,0:T(8,128)(2,1)S(1)}, bf16[512,128]{1,0:T(8,128)(2,1)S(1)}, u32[]{:S(2)}, u32[]{:S(2)}) collective-permute-start(bf16[512,128]{1,0:T(8,128)(2,1)S(1)} %px.5.refs_0_), channel_id=1, source_target_pairs={{0,1},{1,0},{2,3},{3,2},{4,5},{5,4},{6,7},{7,6},{8,9},{9,8},{10,11... | collective-permute-start | bytes 393224 | tf_op jit(solution)/shard_map/ppermute | solution.py:44
  42.8 1.3 %collective-permute-start.17 = (bf16[512,128]{1,0:T(8,128)(2,1)S(1)}, bf16[512,128]{1,0:T(8,128)(2,1)S(1)}, u32[]{:S(2)}, u32[]{:S(2)}) collective-permute-start(bf16[512,128]{1,0:T(8,128)(2,1)S(1)} %collective-permute-done.15.refs_1_), channel_id=1, source_target_pairs={{0,1},{1,0},{2,3},{3,2},{4,5},{5,4},{6,7},{7,6},{8,9},{9,8},{10,11... | collective-permute-start | bytes 393224 | tf_op jit(solution)/shard_map/ppermute | solution.py:44
  45.1 8.5 %collective-permute-start.20 = (bf16[32,2048]{1,0:T(8,128)(2,1)S(1)}, bf16[32,2048]{1,0:T(8,128)(2,1)S(1)}, u32[]{:S(2)}, u32[]{:S(2)}) collective-permute-start(bf16[32,2048]{1,0:T(8,128)(2,1)S(1)} %grads.1.refs_0_), channel_id=1, source_target_pairs={{0,12},{1,13},{2,14},{3,15},{4,0},{5,1},{6,2},{7,3},{8,4},{9,5},{1... | collective-permute-start | bytes 393224 | tf_op jit(solution)/shard_map/ppermute | solution.py:44
  49.6 12.2 %collective-permute-start.19 = (bf16[32,2048]{1,0:T(8,128)(2,1)S(1)}, bf16[32,2048]{1,0:T(8,128)(2,1)S(1)}, u32[]{:S(2)}, u32[]{:S(2)}) collective-permute-start(bf16[32,2048]{1,0:T(8,128)(2,1)S(1)} %grads.1.refs_0_), channel_id=1, source_target_pairs={{0,8},{1,9},{2,10},{3,11},{4,12},{5,13},{6,14},{7,15},{8,0},{9,1},... | collective-permute-start | bytes 393224 | tf_op jit(solution)/shard_map/ppermute | solution.py:44
  49.8 12.0 %collective-permute-start.18 = (bf16[32,2048]{1,0:T(8,128)(2,1)S(1)}, bf16[32,2048]{1,0:T(8,128)(2,1)S(1)}, u32[]{:S(2)}, u32[]{:S(2)}) collective-permute-start(bf16[32,2048]{1,0:T(8,128)(2,1)S(1)} %grads.1.refs_0_), channel_id=1, source_target_pairs={{0,4},{1,5},{2,6},{3,7},{4,8},{5,9},{6,10},{7,11},{8,12},{9,13},{1... | collective-permute-start | bytes 393224 | tf_op jit(solution)/shard_map/ppermute | solution.py:44
  61.8 5.2 %collective-permute-start.21 = (bf16[32,2048]{1,0:T(8,128)(2,1)S(1)}, bf16[32,2048]{1,0:T(8,128)(2,1)S(1)}, u32[]{:S(2)}, u32[]{:S(2)}) collective-permute-start(bf16[32,2048]{1,0:T(8,128)(2,1)S(1)} %total.1.refs_0_), channel_id=1, source_target_pairs={{0,2},{1,3},{2,0},{3,1},{4,6},{5,7},{6,4},{7,5},{8,10},{9,11},{10,... | collective-permute-start | bytes 393224 | tf_op jit(solution)/shard_map/ppermute | solution.py:44
  63.4 3.7 %collective-permute-start.22 = (bf16[32,2048]{1,0:T(8,128)(2,1)S(1)}, bf16[32,2048]{1,0:T(8,128)(2,1)S(1)}, u32[]{:S(2)}, u32[]{:S(2)}) collective-permute-start(bf16[32,2048]{1,0:T(8,128)(2,1)S(1)} %total.1.refs_0_), channel_id=1, source_target_pairs={{0,1},{1,0},{2,3},{3,2},{4,5},{5,4},{6,7},{7,6},{8,9},{9,8},{10,11... | collective-permute-start | bytes 393224 | tf_op jit(solution)/shard_map/ppermute | solution.py:44
  67.0 1.3 %collective-permute-start.23 = (bf16[32,2048]{1,0:T(8,128)(2,1)S(1)}, bf16[32,2048]{1,0:T(8,128)(2,1)S(1)}, u32[]{:S(2)}, u32[]{:S(2)}) collective-permute-start(bf16[32,2048]{1,0:T(8,128)(2,1)S(1)} %collective-permute-done.21.refs_1_), channel_id=1, source_target_pairs={{0,1},{1,0},{2,3},{3,2},{4,5},{5,4},{6,7},{7,6},{8,9},{9,8},{10,11... | collective-permute-start | bytes 393224 | tf_op jit(solution)/shard_map/ppermute | solution.py:44

commit v4 on v3

--- a/solution.py
+++ b/solution.py
@@ -53,42 +53,52 @@
     return [(z * band, (z * line + spot) * band, band) for z in range(deep)]
 
 
-def pg_kernel(cots, proj_out, out, held, weights, sems):
+def load_kernel(acts, cots, proj_in, proj_out, held, own, pg_t, cots_held, weights, sems):
     layers = cots.shape[0]
     width_k = proj_out.shape[1] // layers
-    copies = [pltpu.make_async_copy(proj_out, weights, sems.at[layers])]
-    copies += [pltpu.make_async_copy(cots.at[l], held.at[l], sems.at[l]) for l in range(layers)]
+    pairs = [(proj_out, weights), (cots, cots_held), (proj_in, own), (acts, held)]
+    copies = [pltpu.make_async_copy(a, b, sems.at[i]) for i, (a, b) in enumerate(pairs)]
     for copy in copies:
         copy.start()
     copies[0].wait()
+    copies[1].wait()
     for l in range(layers):
-        copies[1 + l].wait()
-        pg = jnp.dot(held[l], weights[...], preferred_element_type=jnp.float32)
-        out[l * width_k:(l + 1) * width_k, :] = pg.T[l * width_k:(l + 1) * width_k, :].astype(jnp.bfloat16)
-
-
-def px_kernel(devices, shifts, begin, end, acts, *refs):
-    count = len(shifts)
-    blocks, refs = refs[:count], refs[count:]
-    out, held, sems = refs[-3:]
+        pg = jnp.dot(cots_held[l], weights[...], preferred_element_type=jnp.float32)
+        pg_t[l * width_k:(l + 1) * width_k, :] = pg.T[l * width_k:(l + 1) * width_k, :].astype(jnp.bfloat16)
+    copies[2].wait()
+    copies[3].wait()
+
+
+def stack_kernel(count, *refs):
+    out = refs[-1]
+    at = 0
+    for ref in refs[:count]:
+        out[at:at + ref.shape[0], :] = ref[...]
+        at += ref.shape[0]
+
+
+def px_kernel(devices, keys, begin, end, keep, acts, *refs):
+    count = len(keys)
+    arrays, refs = refs[:count], refs[count:]
     layers, rows, _ = acts.shape
-    tall, wide = blocks[0].shape
-    me = lax.axis_index("seq")
-    copies = []
-    for i, shift in enumerate(shifts):
-        at = pl.ds(pl.multiple_of(owner(me, devices, shift) * tall, tall), tall)
-        copies.append(pltpu.make_async_copy(acts.at[:, :, at], held.at[i], sems.at[i]))
-        copies[-1].start()
+    wide = arrays[0].shape[1]
+    me = lax.axis_index("seq")
+    if keep:
+        stack_kernel(count, *arrays, refs[-1])
+        refs = refs[:-1]
     total = [jnp.zeros((rows, wide), jnp.float32) if begin else refs[0][l] for l in range(layers)]
-    for i, copy in enumerate(copies):
-        copy.wait()
-        for l in range(layers):
-            total[l] = total[l] + jnp.dot(held[i, l], blocks[i][...], preferred_element_type=jnp.float32)
+    for array, shifts in zip(arrays, keys):
+        tall = array.shape[0] // len(shifts)
+        for i, shift in enumerate(shifts):
+            at = pl.ds(pl.multiple_of(owner(me, devices, shift) * tall, tall), tall)
+            block = array[i * tall:(i + 1) * tall, :]
+            for l in range(layers):
+                total[l] = total[l] + jnp.dot(acts[l, :, at], block, preferred_element_type=jnp.float32)
     if end:
-        pack(total, refs[-4], out)
+        pack(total, refs[-2], refs[-1])
     else:
         for l in range(layers):
-            out[l] = total[l]
+            refs[-1][l] = total[l]
 
 
 def pack(total, pg_t, out):
@@ -244,52 +254,78 @@
     deep, across, cores = levels(devices)
     line = across * cores
     tall = proj_in.shape[0]
-    params = pltpu.CompilerParams(vmem_limit_bytes=52 * MIB)
-
-    pg_t = pl.pallas_call(
-        pg_kernel,
-        out_shape=jax.ShapeDtypeStruct((wide, rows), jnp.bfloat16),
-        in_specs=[ANY, ANY],
-        out_specs=VMEM,
+    params = pltpu.CompilerParams(vmem_limit_bytes=24 * MIB)
+
+    light = pl.CostEstimate(flops=1, bytes_accessed=1, transcendentals=0)
+    held, own, pg_t = pl.pallas_call(
+        load_kernel,
+        out_shape=(
+            pltpu.VMEM(acts.shape, jnp.bfloat16),
+            pltpu.VMEM(proj_in.shape, jnp.bfloat16),
+            pltpu.VMEM((wide, rows), jnp.bfloat16),
+        ),
+        in_specs=[ANY] * 4,
+        out_specs=(VMEM,) * 3,
         scratch_shapes=[
             pltpu.VMEM(cots.shape, jnp.bfloat16),
             pltpu.VMEM(proj_out.shape, jnp.bfloat16),
-            pltpu.SemaphoreType.DMA((layers + 1,)),
+            pltpu.SemaphoreType.DMA((4,)),
         ],
         compiler_params=params,
-        cost_estimate=pl.CostEstimate(flops=1 << 27, bytes_accessed=cots.size * 2, transcendentals=0),
-        name="pg",
-    )(cots, proj_out)
+        cost_estimate=light,
+        name="load",
+    )(acts, cots, proj_in, proj_out)
+
+    def stack(arrays, after):
+        return pl.pallas_call(
+            functools.partial(stack_kernel, len(arrays)),
+            out_shape=jax.ShapeDtypeStruct((sum(a.shape[0] for a in arrays), wide), jnp.bfloat16),
+            in_specs=[VMEM] * len(arrays) + [ANY] * len(after),
+            out_specs=VMEM,
+            compiler_params=params,
+            cost_estimate=light,
+            name="stack",
+        )(*arrays, *after)
+
+    def px(entries, before=None, end=False, keep=False):
+        more = (() if before is None else (before,)) + ((pg_t,) if end else ())
+        arrays, keys = zip(*entries)
+        count = sum(map(len, keys))
+        sums = feat_type if end else jax.ShapeDtypeStruct((layers, rows, wide), jnp.float32)
+        stacked = [jax.ShapeDtypeStruct((count * tall, wide), jnp.bfloat16)] if keep else []
+        result = pl.pallas_call(
+            functools.partial(px_kernel, devices, keys, before is None, end, keep),
+            out_shape=[sums] + stacked,
+            in_specs=[VMEM] * (1 + len(arrays) + len(more)),
+            out_specs=[VMEM] * (1 + len(stacked)),
+            compiler_params=params,
+            cost_estimate=light,
+            name="px",
+        )(held, *arrays, *more)
+        return result if keep else result[0]
 
     feat_type = jax.ShapeDtypeStruct((2 * rows, wide), jnp.bfloat16)
-    if tall % 128 == 0:
-        spins = sorted(range(deep), key=lambda z: min(z, deep - z))
-        column = {(z, 0, 0): send(proj_in, devices, (z, 0, 0)) if z else proj_in for z in spins}
-        beside = {(k[0], x, 0): send(v, devices, (0, x, 0)) for x in range(1, across) for k, v in column.items()}
-        twin = {(*k[:2], c): send(v, devices, (0, 0, c)) for c in range(1, cores) for k, v in column.items()}
-        last = {(*k[:2], c): send(v, devices, (0, 0, c)) for c in range(1, cores) for k, v in beside.items()}
-        stages = [stage for stage in (column, {**beside, **twin}, last) if stage]
-        value = None
-        for i, stage in enumerate(stages):
-            begin, end = i == 0, i == len(stages) - 1
-            more = (() if begin else (value,)) + ((pg_t,) if end else ())
-            value = pl.pallas_call(
-                functools.partial(px_kernel, devices, tuple(stage), begin, end),
-                out_shape=feat_type if end else jax.ShapeDtypeStruct((layers, rows, wide), jnp.float32),
-                in_specs=[ANY] + [VMEM] * (len(stage) + len(more)),
-                out_specs=VMEM,
-                scratch_shapes=[
-                    pltpu.VMEM((len(stage), layers, rows, tall), jnp.bfloat16),
-                    pltpu.SemaphoreType.DMA((len(stage),)),
-                ],
-                compiler_params=params,
-                cost_estimate=pl.CostEstimate(
-                    flops=2 * acts.size * wide * len(stage) // devices,
-                    bytes_accessed=2 * acts.size * len(stage) // devices,
-                    transcendentals=0,
-                ),
-                name="px",
-            )(acts, *stage.values(), *more)
+    if tall % 128 == 0 and deep > 2 and across == 2 and cores == 2:
+        spins = sorted(range(1, deep), key=lambda z: min(z, deep - z))
+        near, far = spins[:-1], spins[-1]
+        got = [send(proj_in, devices, (z, 0, 0)) for z in near]
+        side = send(proj_in, devices, (0, 1, 0))
+        got_far = send(proj_in, devices, (far, 0, 0))
+        got = stack(got, (pg_t, side))
+        side_near = send(got, devices, (0, 1, 0))
+        value, column = px([(own, [(0, 0, 0)]), (got, [(z, 0, 0) for z in near])], keep=True)
+        twin = send(column, devices, (0, 0, 1))
+        side_far = send(got_far, devices, (0, 1, 0))
+        twin_far = send(got_far, devices, (0, 0, 1))
+        side = stack([side, side_near], (value,))
+        twin_side = send(side, devices, (0, 0, 1))
+        first = [0, *near]
+        value = px([(side, [(z, 1, 0) for z in first]), (got_far, [(far, 0, 0)])], value)
+        twin_side_far = send(side_far, devices, (0, 0, 1))
+        value = px(
+            [(twin, [(z, 0, 1) for z in first]), (twin_far, [(far, 0, 1)]), (side_far, [(far, 1, 0)])], value
+        )
+        value = px([(twin_side, [(z, 1, 1) for z in first]), (twin_side_far, [(far, 1, 1)])], value, end=True)
     else:
         groups = [[z * line + i for z in range(deep)] for i in range(line)]
         column = lax.all_to_all(jnp.tile(proj_in, (deep, 1)), "seq", 0, 0, axis_index_groups=groups, tiled=True)
@@ -303,7 +339,7 @@
             scratch_shapes=[pltpu.VMEM((width, wide), jnp.bfloat16)],
             compiler_params=params,
             name="px",
-        )(acts, *blocks, pg_t)
+        )(held, *blocks, pg_t)
 
     def plane(block):
         held = {(0, x, 0): send(block, devices, (0, x, 0)) if x else block for x in range(across)}

time: 74.9 us -> 65.7 us (0.88)
  starting transfers between devices: 21.5 us -> 15.2 us
  Pallas kernels: 16 us -> 11.5 us
  local copies, waits for them, and re-layouts: 3.18 us -> 6.57 us
  waiting for transfers between devices: 33.1 us -> 31.4 us
    ppermute x24 -> x19, starting transfers between devices: 21.5 us -> 15.2 us  [send(): return lax.ppermute(value, 'seq', perm)]
    pallas_call x4 -> x7, Pallas kernels: 8.8 us -> 4.26 us  [the longest x4 2.87 us: px(): pl.pallas_call(functools.partial(px_kernel, devices, keys, before is None...]
    unnamed x13 -> x17, local copies, waits for them, and re-layouts: 3.18 us -> 6.57 us
    ppermute x24 -> x19, waiting for transfers between devices: 33.1 us -> 31.4 us  [send(): return lax.ppermute(value, 'seq', perm)]
  transfers between devices with their start and end apart: 24 -> 19, of which waited for: 11 -> 9; matrix products, arithmetic and copies ran while one was open for 0% -> 0% of each run, Pallas kernels for 9% -> 5%
where the time goes in v4:
time: 65.7 us; the launch traced here: 65.5 us
  waiting for transfers between devices  31.4 us (48%)
  starting transfers between devices  15.2 us (23%)
  Pallas kernels  11.5 us (18%)
  local copies, waits for them, and re-layouts  6.57 us (10%)
  between operations  0.8 us (1%)
    ppermute x19, waiting for transfers between devices, send(): return lax.ppermute(value, 'seq', perm)  31.4 us
    ppermute x19, starting transfers between devices, send(): return lax.ppermute(value, 'seq', perm)  15.2 us
    unnamed x17, local copies, waits for them, and re-layouts  6.57 us
    pallas_call x1, Pallas kernels, shards(): pl.pallas_call(functools.partial(covariance_kernel, devices, tuple(full))...  6.26 us
    pallas_call x4, Pallas kernels, px(): pl.pallas_call(functools.partial(px_kernel, devices, keys, before is None...  2.87 us
    pallas_call x1, Pallas kernels, shards(): pl.pallas_call(load_kernel, out_shape=(pltpu.VMEM(acts.shape, jnp.bfloat1...  1.35 us
  transfers between devices with their start and end apart: 19, of which 9 were waited for; matrix products, arithmetic and copies ran while one was open for 0% of the time, Pallas kernels for 5%

profile of v4, /device:TPU:0, one launch (start us, length us, event | category | flops | bytes accessed | tf_op | source)
XLA Modules:
  0.0 65.5 jit_solution(14141824390784830862)
XLA Ops:
  0.6 3.1 %collective-permute-start.1 = (bf16[512,128]{1,0:T(8,128)(2,1)}, bf16[512,128]{1,0:T(8,128)(2,1)S(1)}, u32[]{:S(2)}, u32[]{:S(2)}) collective-permute-start(bf16[512,128]{1,0:T(8,128)(2,1)} %proj_in.1), channel_id=1, source_target_pairs={{0,4},{1,5},{2,6},{3,7},{4,8},{5,9},{6,10},{7,11},{8,12},{9,13},{1... | collective-permute-start | bytes 393224 | tf_op jit(solution)/shard_map/ppermute | solution.py:44
  3.7 1.5 %collective-permute-start = (bf16[512,128]{1,0:T(8,128)(2,1)}, bf16[512,128]{1,0:T(8,128)(2,1)S(1)}, u32[]{:S(2)}, u32[]{:S(2)}) collective-permute-start(bf16[512,128]{1,0:T(8,128)(2,1)} %proj_in.1), channel_id=1, source_target_pairs={{0,2},{1,3},{2,0},{3,1},{4,6},{5,7},{6,4},{7,5},{8,10},{9,11},{10,... | collective-permute-start | bytes 393224 | tf_op jit(solution)/shard_map/ppermute | solution.py:44
  5.2 2.2 %collective-permute-start.2 = (bf16[512,128]{1,0:T(8,128)(2,1)}, bf16[512,128]{1,0:T(8,128)(2,1)S(1)}, u32[]{:S(2)}, u32[]{:S(2)}) collective-permute-start(bf16[512,128]{1,0:T(8,128)(2,1)} %proj_in.1), channel_id=1, source_target_pairs={{0,12},{1,13},{2,14},{3,15},{4,0},{5,1},{6,2},{7,3},{8,4},{9,5},{1... | collective-permute-start | bytes 393224 | tf_op jit(solution)/shard_map/ppermute | solution.py:44
  7.4 3.4 %copy-done = bf16[2,256,8192]{2,1,0:T(8,128)(2,1)S(1)} copy-done((bf16[2,256,8192]{2,1,0:T(8,128)(2,1)S(1)}, bf16[2,256,8192]{2,1,0:T(8,128)(2,1)}, u32[]{:S(2)}) %copy-start) | copy-done | bytes 8388632
  10.8 1.2 %copy-done.1 = bf16[2,256,1024]{2,1,0:T(8,128)(2,1)S(1)} copy-done((bf16[2,256,1024]{2,1,0:T(8,128)(2,1)S(1)}, bf16[2,256,1024]{2,1,0:T(8,128)(2,1)}, u32[]{:S(2)}) %copy-start.1) | copy-done | bytes 1048600
  12.1 0.9 %copy-done.2 = bf16[1024,128]{1,0:T(8,128)(2,1)S(1)} copy-done((bf16[1024,128]{1,0:T(8,128)(2,1)S(1)}, bf16[1024,128]{1,0:T(8,128)(2,1)}, u32[]{:S(2)}) %copy-start.2) | copy-done | bytes 262168
  13.0 0.9 %copy-done.3 = bf16[512,128]{1,0:T(8,128)(2,1)S(1)} copy-done((bf16[512,128]{1,0:T(8,128)(2,1)S(1)}, bf16[512,128]{1,0:T(8,128)(2,1)}, u32[]{:S(2)}) %copy-start.3) | copy-done | bytes 131096
  13.9 1.3 %load.1 = (bf16[2,256,8192]{2,1,0:T(8,128)(2,1)S(1)}, bf16[512,128]{1,0:T(8,128)(2,1)S(1)}, bf16[128,256]{1,0:T(8,128)(2,1)S(1)}) custom-call(bf16[2,256,8192]{2,1,0:T(8,128)(2,1)S(1)} %copy-done, bf16[2,256,1024]{2,1,0:T(8,128)(2,1)S(1)} %copy-done.1, bf16[512,128]{1,0:T(8,128)(2,1)S(1)} %copy-done.3, bf16[1024,128]{1,0:T(8,128)(2,1)S(1)} %copy-done.2), custom_call_target="tpu_custom_call" | custom-call | flops 1 | bytes 1 | tf_op jit(solution)/shard_map/load/pallas_call | solution.py:260
  15.3 0.5 collective-permute-start.3
  15.8 0.9 %collective-permute-start.5 = (bf16[512,128]{1,0:T(8,128)(2,1)S(1)}, bf16[512,128]{1,0:T(8,128)(2,1)S(1)}, u32[]{:S(2)}, u32[]{:S(2)}) collective-permute-start(bf16[512,128]{1,0:T(8,128)(2,1)S(1)} %copy-done.4), channel_id=1, source_target_pairs={{0,8},{1,9},{2,10},{3,11},{4,12},{5,13},{6,14},{7,15},{8,0},{9,1},... | collective-permute-start | bytes 393224 | tf_op jit(solution)/shard_map/ppermute | solution.py:44
  16.7 0.6 px.4
  17.4 5.3 %collective-permute-done.3.refs_1_ = bf16[1024,128]{1,0:T(8,128)(2,1)S(1)} collective-permute-done((bf16[1024,128]{1,0:T(8,128)(2,1)S(1)}, bf16[1024,128]{1,0:T(8,128)(2,1)S(1)}, u32[]{:S(2)}, u32[]{:S(2)}) %collective-permute-start.3) | collective-permute-done | bytes 262176 | tf_op jit(solution)/shard_map/ppermute | solution.py:44
  22.8 0.1 collective-permute-done.5.refs_1_
  23.0 1.5 %collective-permute-start.6 = (bf16[512,128]{1,0:T(8,128)(2,1)S(1)}, bf16[512,128]{1,0:T(8,128)(2,1)S(1)}, u32[]{:S(2)}, u32[]{:S(2)}) collective-permute-start(bf16[512,128]{1,0:T(8,128)(2,1)S(1)} %collective-permute-done.5.refs_1_), channel_id=1, source_target_pairs={{0,2},{1,3},{2,0},{3,1},{4,6},{5,7},{6,4},{7,5},{8,10},{9,11},{10,... | collective-permute-start | bytes 393224 | tf_op jit(solution)/shard_map/ppermute | solution.py:44
  24.5 4.3 %collective-permute-done.6.refs_2_ = bf16[512,128]{1,0:T(8,128)(2,1)S(1)} collective-permute-done((bf16[512,128]{1,0:T(8,128)(2,1)S(1)}, bf16[512,128]{1,0:T(8,128)(2,1)S(1)}, u32[]{:S(2)}, u32[]{:S(2)}) %collective-permute-start.6) | collective-permute-done | bytes 131104 | tf_op jit(solution)/shard_map/ppermute | solution.py:44
  28.7 0.7 %px.5.refs_3_ = f32[2,256,128]{2,1,0:T(8,128)S(1)} custom-call(bf16[2,256,8192]{2,1,0:T(8,128)(2,1)S(1)} %get-tuple-element.7.acts, bf16[1536,128]{1,0:T(8,128)(2,1)S(1)} %stack.3.refs_0_, bf16[512,128]{1,0:T(8,128)(2,1)S(1)} %collective-permute-done.5.refs_1_, f32[2,256,128]{2,1,0:T(8,128)S(1)} %get-tuple-element.10.refs_2_), custom_call_target="tpu_custom_call" | custom-call | flops 1 | bytes 1 | tf_op jit(solution)/shard_map/px/pallas_call | solution.py:296
  29.5 0.9 %px.6.refs_2_ = f32[2,256,128]{2,1,0:T(8,128)S(1)} custom-call(bf16[2,256,8192]{2,1,0:T(8,128)(2,1)S(1)} %get-tuple-element.7.acts, bf16[1536,128]{1,0:T(8,128)(2,1)S(1)} %collective-permute-done.8.refs_0_, bf16[512,128]{1,0:T(8,128)(2,1)S(1)} %collective-permute-done.9.refs_1_, bf16[512,128]{1,0:T(8,128)(2,1)S(1)} %collective-permute-done.6.refs_2_, ...), custom_call_target="tpu_custom_call" | custom-call | flops 1 | bytes 1 | tf_op jit(solution)/shard_map/px/pallas_call | solution.py:296
  30.4 0.7 %px.7.refs_0_ = bf16[512,128]{1,0:T(8,128)(2,1)S(1)} custom-call(bf16[2,256,8192]{2,1,0:T(8,128)(2,1)S(1)} %get-tuple-element.7.acts, bf16[1536,128]{1,0:T(8,128)(2,1)S(1)} %collective-permute-done.4.refs_0_, bf16[512,128]{1,0:T(8,128)(2,1)S(1)} %collective-permute-done.7.refs_1_, f32[2,256,128]{2,1,0:T(8,128)S(1)} %px.6.refs_2_, ...), custom_call_target="tpu_custom_call" | custom-call | flops 1 | bytes 1 | tf_op jit(solution)/shard_map/px/pallas_call | solution.py:296
  31.1 0.7 %collective-permute-start.10 = (bf16[512,128]{1,0:T(8,128)(2,1)S(1)}, bf16[512,128]{1,0:T(8,128)(2,1)S(1)}, u32[]{:S(2)}, u32[]{:S(2)}) collective-permute-start(bf16[512,128]{1,0:T(8,128)(2,1)S(1)} %px.7.refs_0_), channel_id=1, source_target_pairs={{0,2},{1,3},{2,0},{3,1},{4,6},{5,7},{6,4},{7,5},{8,10},{9,11},{10,... | collective-permute-start | bytes 393224 | tf_op jit(solution)/shard_map/ppermute | solution.py:44
  31.9 0.2 collective-permute-start.11
  32.1 5.0 %collective-permute-done.10.refs_1_ = bf16[512,128]{1,0:T(8,128)(2,1)S(1)} collective-permute-done((bf16[512,128]{1,0:T(8,128)(2,1)S(1)}, bf16[512,128]{1,0:T(8,128)(2,1)S(1)}, u32[]{:S(2)}, u32[]{:S(2)}) %collective-permute-start.10) | collective-permute-done | bytes 131104 | tf_op jit(solution)/shard_map/ppermute | solution.py:44
  37.1 1.3 %collective-permute-done.12.refs_3_ = bf16[512,128]{1,0:T(8,128)(2,1)S(1)} collective-permute-done((bf16[512,128]{1,0:T(8,128)(2,1)S(1)}, bf16[512,128]{1,0:T(8,128)(2,1)S(1)}, u32[]{:S(2)}, u32[]{:S(2)}) %collective-permute-start.12) | collective-permute-done | bytes 131104 | tf_op jit(solution)/shard_map/ppermute | solution.py:44
  38.4 0.9 %grads.1.refs_0_ = bf16[32,2048]{1,0:T(8,128)(2,1)S(1)} custom-call(bf16[512,128]{1,0:T(8,128)(2,1)S(1)} %px.7.refs_0_, bf16[512,128]{1,0:T(8,128)(2,1)S(1)} %collective-permute-done.10.refs_1_, bf16[512,128]{1,0:T(8,128)(2,1)S(1)} %collective-permute-done.11.refs_2_, bf16[512,128]{1,0:T(8,128)(2,1)S(1)} %collective-permute-done.12.refs_3_, ...), custom_call_target="tpu_custom_call" | custom-call | tf_op jit(solution)/shard_map/grads/pallas_call | solution.py:350
  39.3 1.7 %collective-permute-start.15 = (bf16[32,2048]{1,0:T(8,128)(2,1)S(1)}, bf16[32,2048]{1,0:T(8,128)(2,1)S(1)}, u32[]{:S(2)}, u32[]{:S(2)}) collective-permute-start(bf16[32,2048]{1,0:T(8,128)(2,1)S(1)} %grads.1.refs_0_), channel_id=1, source_target_pairs={{0,12},{1,13},{2,14},{3,15},{4,0},{5,1},{6,2},{7,3},{8,4},{9,5},{1... | collective-permute-start | bytes 393224 | tf_op jit(solution)/shard_map/ppermute | solution.py:44
  41.1 1.0 %collective-permute-start.13 = (bf16[32,2048]{1,0:T(8,128)(2,1)S(1)}, bf16[32,2048]{1,0:T(8,128)(2,1)S(1)}, u32[]{:S(2)}, u32[]{:S(2)}) collective-permute-start(bf16[32,2048]{1,0:T(8,128)(2,1)S(1)} %grads.1.refs_0_), channel_id=1, source_target_pairs={{0,4},{1,5},{2,6},{3,7},{4,8},{5,9},{6,10},{7,11},{8,12},{9,13},{1... | collective-permute-start | bytes 393224 | tf_op jit(solution)/shard_map/ppermute | solution.py:44
  42.1 3.4 %collective-permute-done.15.refs_3_ = bf16[32,2048]{1,0:T(8,128)(2,1)S(1)} collective-permute-done((bf16[32,2048]{1,0:T(8,128)(2,1)S(1)}, bf16[32,2048]{1,0:T(8,128)(2,1)S(1)}, u32[]{:S(2)}, u32[]{:S(2)}) %collective-permute-start.15) | collective-permute-done | bytes 131104 | tf_op jit(solution)/shard_map/ppermute | solution.py:44
  45.5 7.3 %collective-permute-done.14.refs_2_ = bf16[32,2048]{1,0:T(8,128)(2,1)S(1)} collective-permute-done((bf16[32,2048]{1,0:T(8,128)(2,1)S(1)}, bf16[32,2048]{1,0:T(8,128)(2,1)S(1)}, u32[]{:S(2)}, u32[]{:S(2)}) %collective-permute-start.14) | collective-permute-done | bytes 131104 | tf_op jit(solution)/shard_map/ppermute | solution.py:44
  52.8 1.6 %collective-permute-start.16 = (bf16[32,2048]{1,0:T(8,128)(2,1)S(1)}, bf16[32,2048]{1,0:T(8,128)(2,1)S(1)}, u32[]{:S(2)}, u32[]{:S(2)}) collective-permute-start(bf16[32,2048]{1,0:T(8,128)(2,1)S(1)} %total.1.refs_0_), channel_id=1, source_target_pairs={{0,2},{1,3},{2,0},{3,1},{4,6},{5,7},{6,4},{7,5},{8,10},{9,11},{10,... | collective-permute-start | bytes 393224 | tf_op jit(solution)/shard_map/ppermute | solution.py:44
  54.5 3.4 %collective-permute-done.16.refs_1_ = bf16[32,2048]{1,0:T(8,128)(2,1)S(1)} collective-permute-done((bf16[32,2048]{1,0:T(8,128)(2,1)S(1)}, bf16[32,2048]{1,0:T(8,128)(2,1)S(1)}, u32[]{:S(2)}, u32[]{:S(2)}) %collective-permute-start.16) | collective-permute-done | bytes 131104 | tf_op jit(solution)/shard_map/ppermute | solution.py:44
  57.9 0.1 copy.9.refs_5_
  58.0 1.2 %collective-permute-done.18.refs_3_ = bf16[32,2048]{1,0:T(8,128)(2,1)S(1)} collective-permute-done((bf16[32,2048]{1,0:T(8,128)(2,1)S(1)}, bf16[32,2048]{1,0:T(8,128)(2,1)S(1)}, u32[]{:S(2)}, u32[]{:S(2)}) %collective-permute-start.18) | collective-permute-done | bytes 131104 | tf_op jit(solution)/shard_map/ppermute | solution.py:44
  59.2 6.3 %covariance.1 = (bf16[2,8192]{1,0:T(2,128)(2,1)}, f32[3,256,4096]{2,1,0:T(8,128)}) custom-call(bf16[32,2048]{1,0:T(8,128)(2,1)S(1)} %total.1.refs_0_, bf16[32,2048]{1,0:T(8,128)(2,1)S(1)} %collective-permute-done.16.refs_1_, bf16[32,2048]{1,0:T(8,128)(2,1)S(1)} %collective-permute-done.17.refs_2_, bf16[32,2048]{1,0:T(8,128)(2,1)S(1)} %collective-permute-done.18.refs_3_, ...), custom_call_target="tpu_custom_call" | custom-call | tf_op jit(solution)/shard_map/covariance/pallas_call | solution.py:369
  (33 shorter events, 0.3 us)
Async XLA Ops:
  0.6 14.6 %collective-permute-start.1 = (bf16[512,128]{1,0:T(8,128)(2,1)}, bf16[512,128]{1,0:T(8,128)(2,1)S(1)}, u32[]{:S(2)}, u32[]{:S(2)}) collective-permute-start(bf16[512,128]{1,0:T(8,128)(2,1)} %proj_in.1), channel_id=1, source_target_pairs={{0,4},{1,5},{2,6},{3,7},{4,8},{5,9},{6,10},{7,11},{8,12},{9,13},{1... | collective-permute-start | bytes 393224 | tf_op jit(solution)/shard_map/ppermute | solution.py:44
  3.7 11.6 %collective-permute-start = (bf16[512,128]{1,0:T(8,128)(2,1)}, bf16[512,128]{1,0:T(8,128)(2,1)S(1)}, u32[]{:S(2)}, u32[]{:S(2)}) collective-permute-start(bf16[512,128]{1,0:T(8,128)(2,1)} %proj_in.1), channel_id=1, source_target_pairs={{0,2},{1,3},{2,0},{3,1},{4,6},{5,7},{6,4},{7,5},{8,10},{9,11},{10,... | collective-permute-start | bytes 393224 | tf_op jit(solution)/shard_map/ppermute | solution.py:44
  5.2 10.1 %collective-permute-start.2 = (bf16[512,128]{1,0:T(8,128)(2,1)}, bf16[512,128]{1,0:T(8,128)(2,1)S(1)}, u32[]{:S(2)}, u32[]{:S(2)}) collective-permute-start(bf16[512,128]{1,0:T(8,128)(2,1)} %proj_in.1), channel_id=1, source_target_pairs={{0,12},{1,13},{2,14},{3,15},{4,0},{5,1},{6,2},{7,3},{8,4},{9,5},{1... | collective-permute-start | bytes 393224 | tf_op jit(solution)/shard_map/ppermute | solution.py:44
  7.4 3.4 %copy-start = (bf16[2,256,8192]{2,1,0:T(8,128)(2,1)S(1)}, bf16[2,256,8192]{2,1,0:T(8,128)(2,1)}, u32[]{:S(2)}) copy-start(bf16[2,256,8192]{2,1,0:T(8,128)(2,1)} %acts.1) | copy-start | bytes 25165828
  10.8 1.2 %copy-start.1 = (bf16[2,256,1024]{2,1,0:T(8,128)(2,1)S(1)}, bf16[2,256,1024]{2,1,0:T(8,128)(2,1)}, u32[]{:S(2)}) copy-start(bf16[2,256,1024]{2,1,0:T(8,128)(2,1)} %cots.1) | copy-start | bytes 3145732
  12.1 0.9 %copy-start.2 = (bf16[1024,128]{1,0:T(8,128)(2,1)S(1)}, bf16[1024,128]{1,0:T(8,128)(2,1)}, u32[]{:S(2)}) copy-start(bf16[1024,128]{1,0:T(8,128)(2,1)} %proj_out.1) | copy-start | bytes 786436
  13.0 0.9 %copy-start.3 = (bf16[512,128]{1,0:T(8,128)(2,1)S(1)}, bf16[512,128]{1,0:T(8,128)(2,1)}, u32[]{:S(2)}) copy-start(bf16[512,128]{1,0:T(8,128)(2,1)} %proj_in.1) | copy-start | bytes 393220
  13.9 1.9 %copy-start.4 = (bf16[512,128]{1,0:T(8,128)(2,1)S(1)}, bf16[512,128]{1,0:T(8,128)(2,1)}, u32[]{:S(2)}) copy-start(bf16[512,128]{1,0:T(8,128)(2,1)} %proj_in.1) | copy-start | bytes 393220
  15.3 7.4 %collective-permute-start.3 = (bf16[1024,128]{1,0:T(8,128)(2,1)S(1)}, bf16[1024,128]{1,0:T(8,128)(2,1)S(1)}, u32[]{:S(2)}, u32[]{:S(2)}) collective-permute-start(bf16[1024,128]{1,0:T(8,128)(2,1)S(1)} %stack.2.refs_1_), channel_id=1, source_target_pairs={{0,2},{1,3},{2,0},{3,1},{4,6},{5,7},{6,4},{7,5},{8,10},{9,11},{10,... | collective-permute-start | bytes 786440 | tf_op jit(solution)/shard_map/ppermute | solution.py:44
  15.8 7.2 %collective-permute-start.5 = (bf16[512,128]{1,0:T(8,128)(2,1)S(1)}, bf16[512,128]{1,0:T(8,128)(2,1)S(1)}, u32[]{:S(2)}, u32[]{:S(2)}) collective-permute-start(bf16[512,128]{1,0:T(8,128)(2,1)S(1)} %copy-done.4), channel_id=1, source_target_pairs={{0,8},{1,9},{2,10},{3,11},{4,12},{5,13},{6,14},{7,15},{8,0},{9,1},... | collective-permute-start | bytes 393224 | tf_op jit(solution)/shard_map/ppermute | solution.py:44
  17.3 12.2 %collective-permute-start.8 = (bf16[1536,128]{1,0:T(8,128)(2,1)S(1)}, bf16[1536,128]{1,0:T(8,128)(2,1)S(1)}, u32[]{:S(2)}, u32[]{:S(2)}) collective-permute-start(bf16[1536,128]{1,0:T(8,128)(2,1)S(1)} %get-tuple-element.11), channel_id=1, source_target_pairs={{0,1},{1,0},{2,3},{3,2},{4,5},{5,4},{6,7},{7,6},{8,9},{9,8},{10,11... | collective-permute-start | bytes 1179656 | tf_op jit(solution)/shard_map/ppermute | solution.py:44
  22.8 7.6 %collective-permute-start.4 = (bf16[1536,128]{1,0:T(8,128)(2,1)S(1)}, bf16[1536,128]{1,0:T(8,128)(2,1)S(1)}, u32[]{:S(2)}, u32[]{:S(2)}) collective-permute-start(bf16[1536,128]{1,0:T(8,128)(2,1)S(1)} %stack.3.refs_0_), channel_id=1, source_target_pairs={{0,1},{1,0},{2,3},{3,2},{4,5},{5,4},{6,7},{7,6},{8,9},{9,8},{10,11... | collective-permute-start | bytes 1179656 | tf_op jit(solution)/shard_map/ppermute | solution.py:44
  23.0 5.8 %collective-permute-start.6 = (bf16[512,128]{1,0:T(8,128)(2,1)S(1)}, bf16[512,128]{1,0:T(8,128)(2,1)S(1)}, u32[]{:S(2)}, u32[]{:S(2)}) collective-permute-start(bf16[512,128]{1,0:T(8,128)(2,1)S(1)} %collective-permute-done.5.refs_1_), channel_id=1, source_target_pairs={{0,2},{1,3},{2,0},{3,1},{4,6},{5,7},{6,4},{7,5},{8,10},{9,11},{10,... | collective-permute-start | bytes 393224 | tf_op jit(solution)/shard_map/ppermute | solution.py:44
  24.5 5.0 %collective-permute-start.9 = (bf16[512,128]{1,0:T(8,128)(2,1)S(1)}, bf16[512,128]{1,0:T(8,128)(2,1)S(1)}, u32[]{:S(2)}, u32[]{:S(2)}) collective-permute-start(bf16[512,128]{1,0:T(8,128)(2,1)S(1)} %collective-permute-done.5.refs_1_), channel_id=1, source_target_pairs={{0,1},{1,0},{2,3},{3,2},{4,5},{5,4},{6,7},{7,6},{8,9},{9,8},{10,11... | collective-permute-start | bytes 393224 | tf_op jit(solution)/shard_map/ppermute | solution.py:44
  28.7 1.6 %collective-permute-start.7 = (bf16[512,128]{1,0:T(8,128)(2,1)S(1)}, bf16[512,128]{1,0:T(8,128)(2,1)S(1)}, u32[]{:S(2)}, u32[]{:S(2)}) collective-permute-start(bf16[512,128]{1,0:T(8,128)(2,1)S(1)} %collective-permute-done.6.refs_2_), channel_id=1, source_target_pairs={{0,1},{1,0},{2,3},{3,2},{4,5},{5,4},{6,7},{7,6},{8,9},{9,8},{10,11... | collective-permute-start | bytes 393224 | tf_op jit(solution)/shard_map/ppermute | solution.py:44
  29.5 9.0 %copy-start.6 = (s32[1,32]{1,0:T(1,128)S(1)}, s32[1,32]{1,0:T(1,128)}, u32[]{:S(2)}) copy-start(s32[1,32]{1,0:T(1,128)} %refs_4_.1) | copy-start | bytes 388
  29.5 28.4 %copy-start.7 = (s32[3,2]{0,1:T(2,128)S(1)}, s32[3,2]{0,1:T(2,128)}, u32[]{:S(2)}) copy-start(s32[3,2]{0,1:T(2,128)} %param.13) | copy-start | bytes 76
  29.5 29.8 %copy-start.5 = (s32[32]{0:T(128)S(1)}, s32[32]{0:T(128)}, u32[]{:S(2)}) copy-start(s32[32]{0:T(128)} %param.12) | copy-start | bytes 388
  31.1 6.0 %collective-permute-start.10 = (bf16[512,128]{1,0:T(8,128)(2,1)S(1)}, bf16[512,128]{1,0:T(8,128)(2,1)S(1)}, u32[]{:S(2)}, u32[]{:S(2)}) collective-permute-start(bf16[512,128]{1,0:T(8,128)(2,1)S(1)} %px.7.refs_0_), channel_id=1, source_target_pairs={{0,2},{1,3},{2,0},{3,1},{4,6},{5,7},{6,4},{7,5},{8,10},{9,11},{10,... | collective-permute-start | bytes 393224 | tf_op jit(solution)/shard_map/ppermute | solution.py:44
  31.9 5.2 %collective-permute-start.11 = (bf16[512,128]{1,0:T(8,128)(2,1)S(1)}, bf16[512,128]{1,0:T(8,128)(2,1)S(1)}, u32[]{:S(2)}, u32[]{:S(2)}) collective-permute-start(bf16[512,128]{1,0:T(8,128)(2,1)S(1)} %px.7.refs_0_), channel_id=1, source_target_pairs={{0,1},{1,0},{2,3},{3,2},{4,5},{5,4},{6,7},{7,6},{8,9},{9,8},{10,11... | collective-permute-start | bytes 393224 | tf_op jit(solution)/shard_map/ppermute | solution.py:44
  37.1 1.3 %collective-permute-start.12 = (bf16[512,128]{1,0:T(8,128)(2,1)S(1)}, bf16[512,128]{1,0:T(8,128)(2,1)S(1)}, u32[]{:S(2)}, u32[]{:S(2)}) collective-permute-start(bf16[512,128]{1,0:T(8,128)(2,1)S(1)} %collective-permute-done.10.refs_1_), channel_id=1, source_target_pairs={{0,1},{1,0},{2,3},{3,2},{4,5},{5,4},{6,7},{7,6},{8,9},{9,8},{10,11... | collective-permute-start | bytes 393224 | tf_op jit(solution)/shard_map/ppermute | solution.py:44
  39.3 6.1 %collective-permute-start.15 = (bf16[32,2048]{1,0:T(8,128)(2,1)S(1)}, bf16[32,2048]{1,0:T(8,128)(2,1)S(1)}, u32[]{:S(2)}, u32[]{:S(2)}) collective-permute-start(bf16[32,2048]{1,0:T(8,128)(2,1)S(1)} %grads.1.refs_0_), channel_id=1, source_target_pairs={{0,12},{1,13},{2,14},{3,15},{4,0},{5,1},{6,2},{7,3},{8,4},{9,5},{1... | collective-permute-start | bytes 393224 | tf_op jit(solution)/shard_map/ppermute | solution.py:44
  41.1 11.7 %collective-permute-start.14 = (bf16[32,2048]{1,0:T(8,128)(2,1)S(1)}, bf16[32,2048]{1,0:T(8,128)(2,1)S(1)}, u32[]{:S(2)}, u32[]{:S(2)}) collective-permute-start(bf16[32,2048]{1,0:T(8,128)(2,1)S(1)} %grads.1.refs_0_), channel_id=1, source_target_pairs={{0,8},{1,9},{2,10},{3,11},{4,12},{5,13},{6,14},{7,15},{8,0},{9,1},... | collective-permute-start | bytes 393224 | tf_op jit(solution)/shard_map/ppermute | solution.py:44
  41.1 11.7 %collective-permute-start.13 = (bf16[32,2048]{1,0:T(8,128)(2,1)S(1)}, bf16[32,2048]{1,0:T(8,128)(2,1)S(1)}, u32[]{:S(2)}, u32[]{:S(2)}) collective-permute-start(bf16[32,2048]{1,0:T(8,128)(2,1)S(1)} %grads.1.refs_0_), channel_id=1, source_target_pairs={{0,4},{1,5},{2,6},{3,7},{4,8},{5,9},{6,10},{7,11},{8,12},{9,13},{1... | collective-permute-start | bytes 393224 | tf_op jit(solution)/shard_map/ppermute | solution.py:44
  52.8 5.0 %collective-permute-start.16 = (bf16[32,2048]{1,0:T(8,128)(2,1)S(1)}, bf16[32,2048]{1,0:T(8,128)(2,1)S(1)}, u32[]{:S(2)}, u32[]{:S(2)}) collective-permute-start(bf16[32,2048]{1,0:T(8,128)(2,1)S(1)} %total.1.refs_0_), channel_id=1, source_target_pairs={{0,2},{1,3},{2,0},{3,1},{4,6},{5,7},{6,4},{7,5},{8,10},{9,11},{10,... | collective-permute-start | bytes 393224 | tf_op jit(solution)/shard_map/ppermute | solution.py:44
  54.5 3.5 %collective-permute-start.17 = (bf16[32,2048]{1,0:T(8,128)(2,1)S(1)}, bf16[32,2048]{1,0:T(8,128)(2,1)S(1)}, u32[]{:S(2)}, u32[]{:S(2)}) collective-permute-start(bf16[32,2048]{1,0:T(8,128)(2,1)S(1)} %total.1.refs_0_), channel_id=1, source_target_pairs={{0,1},{1,0},{2,3},{3,2},{4,5},{5,4},{6,7},{7,6},{8,9},{9,8},{10,11... | collective-permute-start | bytes 393224 | tf_op jit(solution)/shard_map/ppermute | solution.py:44
  57.9 1.3 %collective-permute-start.18 = (bf16[32,2048]{1,0:T(8,128)(2,1)S(1)}, bf16[32,2048]{1,0:T(8,128)(2,1)S(1)}, u32[]{:S(2)}, u32[]{:S(2)}) collective-permute-start(bf16[32,2048]{1,0:T(8,128)(2,1)S(1)} %collective-permute-done.16.refs_1_), channel_id=1, source_target_pairs={{0,1},{1,0},{2,3},{3,2},{4,5},{5,4},{6,7},{7,6},{8,9},{9,8},{10,11... | collective-permute-start | bytes 393224 | tf_op jit(solution)/shard_map/ppermute | solution.py:44

commit v5 on v4

--- a/solution.py
+++ b/solution.py
@@ -12,6 +12,7 @@
 VMEM = pl.BlockSpec(memory_space=pltpu.VMEM)
 SMEM = pl.BlockSpec(memory_space=pltpu.SMEM)
 ANY = pl.BlockSpec(memory_space=pl.ANY)
+HBM = pl.BlockSpec(memory_space=pltpu.HBM)
 
 
 def levels(devices):
@@ -240,6 +241,53 @@
         copy.wait()
 
 
+def part_kernel(devices, shifts, more, mine, *refs):
+    array, refs = refs[0], refs[1:]
+    if more:
+        rest, slots = refs[:len(more) - 1], refs[len(more) - 1]
+        refs = refs[len(more):]
+    pairs, (side, out, held, sems) = refs[0], refs[-4:]
+    npair, band, _ = held.shape
+    seqs, full = mine.shape
+    deep, across, cores = levels(devices)
+    line = across * cores
+    square = band * devices
+    lanes = square // line
+    layers = full // lanes
+    me = lax.axis_index("seq")
+    scale = jnp.float32(1.0 / seqs)
+    copies = []
+    for p in range(npair):
+        at = pl.multiple_of(pairs[p, 0] * lanes + me // line * band, band)
+        left = mine[:, pl.ds(at, band)]
+        for i, shift in enumerate(shifts):
+            spot = owner(me, devices, shift) % line
+            right = array[i * seqs:(i + 1) * seqs, pl.ds(pl.multiple_of(pairs[p, 1] * lanes, lanes), lanes)]
+            product = lax.dot_general(left, right, (((0,), (0,)), ((), ())), preferred_element_type=jnp.float32)
+            held[p, :, i * lanes:(i + 1) * lanes] = product * scale
+            for here, there, size in chunks(spot, devices, square):
+                to = pl.ds(pl.multiple_of(there, size), size)
+                copies.append(
+                    pltpu.make_async_copy(held.at[p, :, pl.ds(i * lanes + here, size)], out.at[p, :, to], sems.at[len(copies)])
+                )
+                copies[-1].start()
+    if not more:
+        side[...] = jnp.zeros(side.shape, side.dtype)
+    else:
+        own = me * CAP + lax.broadcasted_iota(jnp.int32, (CAP, seqs), 0)
+        picker = (jnp.broadcast_to(slots[...], (CAP, seqs)) == own).astype(jnp.float32).astype(jnp.bfloat16)
+        blocks = [array[i * seqs:(i + 1) * seqs, :] for i in range(len(shifts))] + [ref[...] for ref in (mine, *rest)]
+        for shift, block in zip((*shifts, *more), blocks):
+            spot = owner(me, devices, shift) % line
+            picked = jnp.dot(picker, block, preferred_element_type=jnp.float32).astype(jnp.bfloat16)
+            for here, there, size in chunks(spot, devices, square):
+                for l in range(layers):
+                    to = pl.ds(pl.multiple_of(l * square + there, size), size)
+                    side[:, to] = picked[:, l * lanes + here:l * lanes + here + size]
+    for copy in copies:
+        copy.wait()
+
+
 def shards(acts, cots, proj_in, proj_out, lengths, slots, pairs):
     layers, rows, width = acts.shape
     wide = proj_out.shape[1]
@@ -264,7 +312,7 @@
             pltpu.VMEM(proj_in.shape, jnp.bfloat16),
             pltpu.VMEM((wide, rows), jnp.bfloat16),
         ),
-        in_specs=[ANY] * 4,
+        in_specs=[HBM] * 4,
         out_specs=(VMEM,) * 3,
         scratch_shapes=[
             pltpu.VMEM(cots.shape, jnp.bfloat16),
@@ -274,12 +322,12 @@
         compiler_params=params,
         cost_estimate=light,
         name="load",
-    )(acts, cots, proj_in, proj_out)
+    )(*[pltpu.with_memory_space_constraint(a, pltpu.HBM) for a in (acts, cots, proj_in, proj_out)])
 
     def stack(arrays, after):
         return pl.pallas_call(
             functools.partial(stack_kernel, len(arrays)),
-            out_shape=jax.ShapeDtypeStruct((sum(a.shape[0] for a in arrays), wide), jnp.bfloat16),
+            out_shape=jax.ShapeDtypeStruct((sum(a.shape[0] for a in arrays), arrays[0].shape[1]), jnp.bfloat16),
             in_specs=[VMEM] * len(arrays) + [ANY] * len(after),
             out_specs=VMEM,
             compiler_params=params,
@@ -313,19 +361,16 @@
         got_far = send(proj_in, devices, (far, 0, 0))
         got = stack(got, (pg_t, side))
         side_near = send(got, devices, (0, 1, 0))
-        value, column = px([(own, [(0, 0, 0)]), (got, [(z, 0, 0) for z in near])], keep=True)
+        side_far = send(got_far, devices, (0, 1, 0))
+        value, column = px(
+            [(own, [(0, 0, 0)]), (got, [(z, 0, 0) for z in near]), (got_far, [(far, 0, 0)])], keep=True
+        )
         twin = send(column, devices, (0, 0, 1))
-        side_far = send(got_far, devices, (0, 1, 0))
-        twin_far = send(got_far, devices, (0, 0, 1))
-        side = stack([side, side_near], (value,))
+        side = stack([side, side_near, side_far], (value,))
         twin_side = send(side, devices, (0, 0, 1))
-        first = [0, *near]
-        value = px([(side, [(z, 1, 0) for z in first]), (got_far, [(far, 0, 0)])], value)
-        twin_side_far = send(side_far, devices, (0, 0, 1))
-        value = px(
-            [(twin, [(z, 0, 1) for z in first]), (twin_far, [(far, 0, 1)]), (side_far, [(far, 1, 0)])], value
-        )
-        value = px([(twin_side, [(z, 1, 1) for z in first]), (twin_side_far, [(far, 1, 1)])], value, end=True)
+        order = [0, *near, far]
+        value = px([(side, [(z, 1, 0) for z in order]), (twin, [(z, 0, 1) for z in order])], value)
+        value = px([(twin_side, [(z, 1, 1) for z in order])], value, end=True)
     else:
         groups = [[z * line + i for z in range(deep)] for i in range(line)]
         column = lax.all_to_all(jnp.tile(proj_in, (deep, 1)), "seq", 0, 0, axis_index_groups=groups, tiled=True)
@@ -365,13 +410,55 @@
         compiler_params=params,
         name="total",
     )(*terms)
+    logged_type = jax.ShapeDtypeStruct((CAP, layers * square), jnp.bfloat16)
+    covariance_type = jax.ShapeDtypeStruct((npair, band, square), jnp.float32)
+    if band % 128 == 0 and across == 2 and cores == 2:
+        width = square // line
+        shape = (npair, band, width)
+        covariance = None
+        side = send(total, devices, (0, 1, 0))
+        for shifts in (((0, 0, 0),), ((0, 1, 0),), ((0, 0, 1), (0, 1, 1))):
+            last = len(shifts) > 1
+            arrays = [total, total if covariance is None else send(both, devices, (0, 0, 1)) if last else side]
+            specs = [VMEM] * len(arrays)
+            more = ()
+            if last:
+                more = ((0, 0, 0), (0, 1, 0))
+                arrays += [side, slots.reshape(1, seqs)]
+                specs += [VMEM, VMEM]
+            arrays.append(pairs)
+            specs.append(SMEM)
+            alias = {}
+            if covariance is not None:
+                alias = {len(arrays): 1}
+                arrays.append(covariance)
+                specs.append(ANY)
+            result = pl.pallas_call(
+                functools.partial(part_kernel, devices, shifts, more),
+                out_shape=[logged_type if last else jax.ShapeDtypeStruct((8, 128), jnp.float32), covariance_type],
+                in_specs=specs,
+                out_specs=[VMEM, ANY],
+                scratch_shapes=[
+                    pltpu.VMEM((npair, band, len(shifts) * width), jnp.float32),
+                    pltpu.SemaphoreType.DMA((npair * len(shifts) * deep,)),
+                ],
+                input_output_aliases=alias,
+                compiler_params=params,
+                cost_estimate=pl.CostEstimate(
+                    flops=2 * npair * seqs * band * width * len(shifts),
+                    bytes_accessed=4 * npair * band * width * len(shifts),
+                    transcendentals=0,
+                ),
+                name="covariance",
+            )(*arrays)
+            if covariance is None:
+                both = stack([total, side], (result[0],))
+            covariance = result[1]
+        return result[0], covariance
     full = plane(total)
     return pl.pallas_call(
         functools.partial(covariance_kernel, devices, tuple(full)),
-        out_shape=[
-            jax.ShapeDtypeStruct((CAP, layers * square), jnp.bfloat16),
-            jax.ShapeDtypeStruct((npair, band, square), jnp.float32),
-        ],
+        out_shape=[logged_type, covariance_type],
         in_specs=[VMEM] * (len(full) + 1) + [SMEM],
         out_specs=[VMEM, ANY],
         scratch_shapes=[

time: 65.7 us -> 62.5 us (0.951)
  local copies, waits for them, and re-layouts: 6.57 us -> 0.11 us
  Pallas kernels: 11.5 us -> 17.9 us
  waiting for transfers between devices: 31.4 us -> 26.9 us
  starting transfers between devices: 15.2 us -> 16.6 us
    unnamed x17 -> x7, local copies, waits for them, and re-layouts: 6.57 us -> 0.11 us
    ppermute x19 -> x16, waiting for transfers between devices: 31.4 us -> 26.9 us  [send(): return lax.ppermute(value, 'seq', perm)]
    pallas_call x1 -> x3, Pallas kernels: 6.26 us -> 10.3 us  [shards(): pl.pallas_call(functools.partial(part_kernel, devices, shifts, more), out...]
    pallas_call x1, Pallas kernels: 1.35 us -> 3.87 us  [shards(): pl.pallas_call(load_kernel, out_shape=(pltpu.VMEM(acts.shape, jnp.bfloat1...]
    ppermute x19 -> x16, starting transfers between devices: 15.2 us -> 16.6 us  [send(): return lax.ppermute(value, 'seq', perm)]
    pallas_call x4 -> x3, Pallas kernels: 2.87 us -> 2.72 us  [px(): pl.pallas_call(functools.partial(px_kernel, devices, keys, before is None...]
  transfers between devices with their start and end apart: 19 -> 16, of which waited for: 9 -> 9; matrix products, arithmetic and copies ran while one was open for 0% -> 0% of each run, Pallas kernels for 5% -> 19%
where the time goes in v5:
time: 62.5 us; the launch traced here: 62.3 us
  waiting for transfers between devices  26.9 us (43%)
  Pallas kernels  17.9 us (29%)
  starting transfers between devices  16.6 us (27%)
  between operations  0.78 us (1%)
    ppermute x16, waiting for transfers between devices, send(): return lax.ppermute(value, 'seq', perm)  26.9 us
    ppermute x16, starting transfers between devices, send(): return lax.ppermute(value, 'seq', perm)  16.6 us
    pallas_call x3, Pallas kernels, shards(): pl.pallas_call(functools.partial(part_kernel, devices, shifts, more), out...  10.3 us
    pallas_call x1, Pallas kernels, shards(): pl.pallas_call(load_kernel, out_shape=(pltpu.VMEM(acts.shape, jnp.bfloat1...  3.87 us
    pallas_call x3, Pallas kernels, px(): pl.pallas_call(functools.partial(px_kernel, devices, keys, before is None...  2.72 us
  transfers between devices with their start and end apart: 16, of which 9 were waited for; matrix products, arithmetic and copies ran while one was open for 0% of the time, Pallas kernels for 19%

profile of v5, /device:TPU:0, one launch (start us, length us, event | category | flops | bytes accessed | tf_op | source)
XLA Modules:
  0.0 62.3 jit_solution(8875591967402710752)
XLA Ops:
  0.6 3.1 %collective-permute-start.1 = (bf16[512,128]{1,0:T(8,128)(2,1)}, bf16[512,128]{1,0:T(8,128)(2,1)S(1)}, u32[]{:S(2)}, u32[]{:S(2)}) collective-permute-start(bf16[512,128]{1,0:T(8,128)(2,1)} %proj_in.1), channel_id=1, source_target_pairs={{0,4},{1,5},{2,6},{3,7},{4,8},{5,9},{6,10},{7,11},{8,12},{9,13},{1... | collective-permute-start | bytes 393224 | tf_op jit(solution)/shard_map/ppermute | solution.py:45
  3.7 1.5 %collective-permute-start = (bf16[512,128]{1,0:T(8,128)(2,1)}, bf16[512,128]{1,0:T(8,128)(2,1)S(1)}, u32[]{:S(2)}, u32[]{:S(2)}) collective-permute-start(bf16[512,128]{1,0:T(8,128)(2,1)} %proj_in.1), channel_id=1, source_target_pairs={{0,2},{1,3},{2,0},{3,1},{4,6},{5,7},{6,4},{7,5},{8,10},{9,11},{10,... | collective-permute-start | bytes 393224 | tf_op jit(solution)/shard_map/ppermute | solution.py:45
  5.2 2.2 %collective-permute-start.2 = (bf16[512,128]{1,0:T(8,128)(2,1)}, bf16[512,128]{1,0:T(8,128)(2,1)S(1)}, u32[]{:S(2)}, u32[]{:S(2)}) collective-permute-start(bf16[512,128]{1,0:T(8,128)(2,1)} %proj_in.1), channel_id=1, source_target_pairs={{0,12},{1,13},{2,14},{3,15},{4,0},{5,1},{6,2},{7,3},{8,4},{9,5},{1... | collective-permute-start | bytes 393224 | tf_op jit(solution)/shard_map/ppermute | solution.py:45
  7.4 0.8 %collective-permute-start.4 = (bf16[512,128]{1,0:T(8,128)(2,1)}, bf16[512,128]{1,0:T(8,128)(2,1)S(1)}, u32[]{:S(2)}, u32[]{:S(2)}) collective-permute-start(bf16[512,128]{1,0:T(8,128)(2,1)} %proj_in.1), channel_id=1, source_target_pairs={{0,8},{1,9},{2,10},{3,11},{4,12},{5,13},{6,14},{7,15},{8,0},{9,1},... | collective-permute-start | bytes 393224 | tf_op jit(solution)/shard_map/ppermute | solution.py:45
  8.2 3.9 %load.1 = (bf16[2,256,8192]{2,1,0:T(8,128)(2,1)S(1)}, bf16[512,128]{1,0:T(8,128)(2,1)S(1)}, bf16[128,256]{1,0:T(8,128)(2,1)S(1)}) custom-call(bf16[2,256,8192]{2,1,0:T(8,128)(2,1)} %acts.1, bf16[2,256,1024]{2,1,0:T(8,128)(2,1)} %cots.1, bf16[512,128]{1,0:T(8,128)(2,1)} %proj_in.1, bf16[1024,128]{1,0:T(8,128)(2,1)} %proj_out.1), custom_call_target="tpu_custom_call" | custom-call | flops 1 | bytes 1 | tf_op jit(solution)/shard_map/load/pallas_call | solution.py:308
  12.1 0.1 collective-permute-done.2.refs_1_
  12.3 1.2 %collective-permute-start.3 = (bf16[1024,128]{1,0:T(8,128)(2,1)S(1)}, bf16[1024,128]{1,0:T(8,128)(2,1)S(1)}, u32[]{:S(2)}, u32[]{:S(2)}) collective-permute-start(bf16[1024,128]{1,0:T(8,128)(2,1)S(1)} %stack.3.refs_1_), channel_id=1, source_target_pairs={{0,2},{1,3},{2,0},{3,1},{4,6},{5,7},{6,4},{7,5},{8,10},{9,11},{10,... | collective-permute-start | bytes 786440 | tf_op jit(solution)/shard_map/ppermute | solution.py:45
  13.5 4.3 %collective-permute-done.4.refs_2_ = bf16[512,128]{1,0:T(8,128)(2,1)S(1)} collective-permute-done((bf16[512,128]{1,0:T(8,128)(2,1)}, bf16[512,128]{1,0:T(8,128)(2,1)S(1)}, u32[]{:S(2)}, u32[]{:S(2)}) %collective-permute-start.4) | collective-permute-done | bytes 131104 | tf_op jit(solution)/shard_map/ppermute | solution.py:45
  17.9 1.5 %collective-permute-start.5 = (bf16[512,128]{1,0:T(8,128)(2,1)S(1)}, bf16[512,128]{1,0:T(8,128)(2,1)S(1)}, u32[]{:S(2)}, u32[]{:S(2)}) collective-permute-start(bf16[512,128]{1,0:T(8,128)(2,1)S(1)} %collective-permute-done.4.refs_2_), channel_id=1, source_target_pairs={{0,2},{1,3},{2,0},{3,1},{4,6},{5,7},{6,4},{7,5},{8,10},{9,11},{10,... | collective-permute-start | bytes 393224 | tf_op jit(solution)/shard_map/ppermute | solution.py:45
  19.4 0.7 %px.3 = (f32[2,256,128]{2,1,0:T(8,128)S(1)}, bf16[2048,128]{1,0:T(8,128)(2,1)S(1)}) custom-call(bf16[2,256,8192]{2,1,0:T(8,128)(2,1)S(1)} %get-tuple-element.10.acts, bf16[512,128]{1,0:T(8,128)(2,1)S(1)} %get-tuple-element.12.refs_0_, bf16[1024,128]{1,0:T(8,128)(2,1)S(1)} %stack.3.refs_1_, bf16[512,128]{1,0:T(8,128)(2,1)S(1)} %collective-permute-done.4.refs_2_), custom_call_target="tpu_custom_call" | custom-call | flops 1 | bytes 1 | tf_op jit(solution)/shard_map/px/pallas_call | solution.py:344
  20.1 0.1 collective-permute-start.7
  20.2 3.2 %collective-permute-done.5.refs_2_ = bf16[512,128]{1,0:T(8,128)(2,1)S(1)} collective-permute-done((bf16[512,128]{1,0:T(8,128)(2,1)S(1)}, bf16[512,128]{1,0:T(8,128)(2,1)S(1)}, u32[]{:S(2)}, u32[]{:S(2)}) %collective-permute-start.5) | collective-permute-done | bytes 131104 | tf_op jit(solution)/shard_map/ppermute | solution.py:45
  23.4 0.1 collective-permute-start.6
  23.5 1.3 %px.4.refs_1_ = f32[2,256,128]{2,1,0:T(8,128)S(1)} custom-call(bf16[2,256,8192]{2,1,0:T(8,128)(2,1)S(1)} %get-tuple-element.10.acts, bf16[2048,128]{1,0:T(8,128)(2,1)S(1)} %stack.4.refs_0_, bf16[2048,128]{1,0:T(8,128)(2,1)S(1)} %collective-permute-done.7.refs_1_, f32[2,256,128]{2,1,0:T(8,128)S(1)} %get-tuple-element.13.refs_3_.refs_2_), custom_call_target="tpu_custom_call" | custom-call | flops 1 | bytes 1 | tf_op jit(solution)/shard_map/px/pallas_call | solution.py:344
  24.8 0.6 collective-permute-done.6.refs_0_
  25.4 0.7 %px.5.refs_0_ = bf16[512,128]{1,0:T(8,128)(2,1)S(1)} custom-call(bf16[2,256,8192]{2,1,0:T(8,128)(2,1)S(1)} %get-tuple-element.10.acts, bf16[2048,128]{1,0:T(8,128)(2,1)S(1)} %collective-permute-done.6.refs_0_, f32[2,256,128]{2,1,0:T(8,128)S(1)} %px.4.refs_1_, bf16[128,256]{1,0:T(8,128)(2,1)S(1)} %get-tuple-element.11.refs_2_), custom_call_target="tpu_custom_call" | custom-call | flops 1 | bytes 1 | tf_op jit(solution)/shard_map/px/pallas_call | solution.py:344
  26.1 1.3 %collective-permute-start.8 = (bf16[512,128]{1,0:T(8,128)(2,1)S(1)}, bf16[512,128]{1,0:T(8,128)(2,1)S(1)}, u32[]{:S(2)}, u32[]{:S(2)}) collective-permute-start(bf16[512,128]{1,0:T(8,128)(2,1)S(1)} %px.5.refs_0_), channel_id=1, source_target_pairs={{0,2},{1,3},{2,0},{3,1},{4,6},{5,7},{6,4},{7,5},{8,10},{9,11},{10,... | collective-permute-start | bytes 393224 | tf_op jit(solution)/shard_map/ppermute | solution.py:45
  27.3 4.3 %collective-permute-done.8.refs_1_ = bf16[512,128]{1,0:T(8,128)(2,1)S(1)} collective-permute-done((bf16[512,128]{1,0:T(8,128)(2,1)S(1)}, bf16[512,128]{1,0:T(8,128)(2,1)S(1)}, u32[]{:S(2)}, u32[]{:S(2)}) %collective-permute-start.8) | collective-permute-done | bytes 131104 | tf_op jit(solution)/shard_map/ppermute | solution.py:45
  31.7 1.3 %collective-permute-done.10.refs_3_ = bf16[512,128]{1,0:T(8,128)(2,1)S(1)} collective-permute-done((bf16[512,128]{1,0:T(8,128)(2,1)S(1)}, bf16[512,128]{1,0:T(8,128)(2,1)S(1)}, u32[]{:S(2)}, u32[]{:S(2)}) %collective-permute-start.10) | collective-permute-done | bytes 131104 | tf_op jit(solution)/shard_map/ppermute | solution.py:45
  33.0 0.9 %grads.1.refs_0_ = bf16[32,2048]{1,0:T(8,128)(2,1)S(1)} custom-call(bf16[512,128]{1,0:T(8,128)(2,1)S(1)} %px.5.refs_0_, bf16[512,128]{1,0:T(8,128)(2,1)S(1)} %collective-permute-done.8.refs_1_, bf16[512,128]{1,0:T(8,128)(2,1)S(1)} %collective-permute-done.9.refs_2_, bf16[512,128]{1,0:T(8,128)(2,1)S(1)} %collective-permute-done.10.refs_3_, s32[1,32]{1,0:T(1,128)S(1)} %copy-done.1), custom_call_target="tpu_custom_call" | custom-call | tf_op jit(solution)/shard_map/grads/pallas_call | solution.py:395
  34.0 2.0 %collective-permute-start.13 = (bf16[32,2048]{1,0:T(8,128)(2,1)S(1)}, bf16[32,2048]{1,0:T(8,128)(2,1)S(1)}, u32[]{:S(2)}, u32[]{:S(2)}) collective-permute-start(bf16[32,2048]{1,0:T(8,128)(2,1)S(1)} %grads.1.refs_0_), channel_id=1, source_target_pairs={{0,12},{1,13},{2,14},{3,15},{4,0},{5,1},{6,2},{7,3},{8,4},{9,5},{1... | collective-permute-start | bytes 393224 | tf_op jit(solution)/shard_map/ppermute | solution.py:45
  36.0 1.6 %collective-permute-start.12 = (bf16[32,2048]{1,0:T(8,128)(2,1)S(1)}, bf16[32,2048]{1,0:T(8,128)(2,1)S(1)}, u32[]{:S(2)}, u32[]{:S(2)}) collective-permute-start(bf16[32,2048]{1,0:T(8,128)(2,1)S(1)} %grads.1.refs_0_), channel_id=1, source_target_pairs={{0,8},{1,9},{2,10},{3,11},{4,12},{5,13},{6,14},{7,15},{8,0},{9,1},... | collective-permute-start | bytes 393224 | tf_op jit(solution)/shard_map/ppermute | solution.py:45
  37.5 0.2 collective-permute-start.11
  37.7 2.1 %collective-permute-done.13.refs_3_ = bf16[32,2048]{1,0:T(8,128)(2,1)S(1)} collective-permute-done((bf16[32,2048]{1,0:T(8,128)(2,1)S(1)}, bf16[32,2048]{1,0:T(8,128)(2,1)S(1)}, u32[]{:S(2)}, u32[]{:S(2)}) %collective-permute-start.13) | collective-permute-done | bytes 131104 | tf_op jit(solution)/shard_map/ppermute | solution.py:45
  39.9 9.6 %collective-permute-done.12.refs_2_ = bf16[32,2048]{1,0:T(8,128)(2,1)S(1)} collective-permute-done((bf16[32,2048]{1,0:T(8,128)(2,1)S(1)}, bf16[32,2048]{1,0:T(8,128)(2,1)S(1)}, u32[]{:S(2)}, u32[]{:S(2)}) %collective-permute-start.12) | collective-permute-done | bytes 131104 | tf_op jit(solution)/shard_map/ppermute | solution.py:45
  49.6 1.0 %collective-permute-start.14 = (bf16[32,2048]{1,0:T(8,128)(2,1)S(1)}, bf16[32,2048]{1,0:T(8,128)(2,1)S(1)}, u32[]{:S(2)}, u32[]{:S(2)}) collective-permute-start(bf16[32,2048]{1,0:T(8,128)(2,1)S(1)} %total.1.mine.refs_0_), channel_id=1, source_target_pairs={{0,2},{1,3},{2,0},{3,1},{4,6},{5,7},{6,4},{7,5},{8,10},{9,11},{10,... | collective-permute-start | bytes 393224 | tf_op jit(solution)/shard_map/ppermute | solution.py:45
  50.6 0.1 copy.11.refs_1_.refs_3_
  50.7 2.6 %covariance.3 = (f32[8,128]{1,0:T(8,128)S(1)}, f32[3,256,4096]{2,1,0:T(8,128)}) custom-call(bf16[32,2048]{1,0:T(8,128)(2,1)S(1)} %total.1.mine.refs_0_, bf16[32,2048]{1,0:T(8,128)(2,1)S(1)} %total.1.mine.refs_0_, s32[3,2]{1,0:T(4,128)S(1)} %copy.11.refs_1_.refs_3_), custom_call_target="tpu_custom_call" | custom-call | flops 50331648 | bytes 3145728 | tf_op jit(solution)/shard_map/covariance/pallas_call | solution.py:436
  53.3 1.3 %collective-permute-done.14.refs_1_.refs_0_ = bf16[32,2048]{1,0:T(8,128)(2,1)S(1)} collective-permute-done((bf16[32,2048]{1,0:T(8,128)(2,1)S(1)}, bf16[32,2048]{1,0:T(8,128)(2,1)S(1)}, u32[]{:S(2)}, u32[]{:S(2)}) %collective-permute-start.14) | collective-permute-done | bytes 131104 | tf_op jit(solution)/shard_map/ppermute | solution.py:45
  54.6 0.1 collective-permute-start.15
  54.7 3.3 %covariance.4 = (f32[8,128]{1,0:T(8,128)}, f32[3,256,4096]{2,1,0:T(8,128)}) custom-call(bf16[32,2048]{1,0:T(8,128)(2,1)S(1)} %total.1.mine.refs_0_, bf16[32,2048]{1,0:T(8,128)(2,1)S(1)} %collective-permute-done.14.refs_1_.refs_0_, s32[3,2]{1,0:T(4,128)S(1)} %copy.11.refs_1_.refs_3_, ...), custom_call_target="tpu_custom_call", output_to_operand_aliasing={{1}: (3, {})} | custom-call | flops 50331648 | bytes 3145728 | tf_op jit(solution)/shard_map/covariance/pallas_call | solution.py:436
  58.0 4.4 %covariance.5 = (bf16[2,8192]{1,0:T(2,128)(2,1)}, f32[3,256,4096]{2,1,0:T(8,128)}) custom-call(bf16[32,2048]{1,0:T(8,128)(2,1)S(1)} %total.1.mine.refs_0_, bf16[64,2048]{1,0:T(8,128)(2,1)S(1)} %collective-permute-done.15.refs_0_, bf16[32,2048]{1,0:T(8,128)(2,1)S(1)} %collective-permute-done.14.refs_1_.refs_0_, ...), custom_call_target="tpu_custom_call", output_to_operand_aliasing={{1}: (5, {})} | custom-call | flops 100663296 | bytes 6291456 | tf_op jit(solution)/shard_map/covariance/pallas_call | solution.py:436
  (19 shorter events, 0.2 us)
Async XLA Ops:
  0.6 11.5 %collective-permute-start.1 = (bf16[512,128]{1,0:T(8,128)(2,1)}, bf16[512,128]{1,0:T(8,128)(2,1)S(1)}, u32[]{:S(2)}, u32[]{:S(2)}) collective-permute-start(bf16[512,128]{1,0:T(8,128)(2,1)} %proj_in.1), channel_id=1, source_target_pairs={{0,4},{1,5},{2,6},{3,7},{4,8},{5,9},{6,10},{7,11},{8,12},{9,13},{1... | collective-permute-start | bytes 393224 | tf_op jit(solution)/shard_map/ppermute | solution.py:45
  3.7 8.4 %collective-permute-start = (bf16[512,128]{1,0:T(8,128)(2,1)}, bf16[512,128]{1,0:T(8,128)(2,1)S(1)}, u32[]{:S(2)}, u32[]{:S(2)}) collective-permute-start(bf16[512,128]{1,0:T(8,128)(2,1)} %proj_in.1), channel_id=1, source_target_pairs={{0,2},{1,3},{2,0},{3,1},{4,6},{5,7},{6,4},{7,5},{8,10},{9,11},{10,... | collective-permute-start | bytes 393224 | tf_op jit(solution)/shard_map/ppermute | solution.py:45
  5.2 7.0 %collective-permute-start.2 = (bf16[512,128]{1,0:T(8,128)(2,1)}, bf16[512,128]{1,0:T(8,128)(2,1)S(1)}, u32[]{:S(2)}, u32[]{:S(2)}) collective-permute-start(bf16[512,128]{1,0:T(8,128)(2,1)} %proj_in.1), channel_id=1, source_target_pairs={{0,12},{1,13},{2,14},{3,15},{4,0},{5,1},{6,2},{7,3},{8,4},{9,5},{1... | collective-permute-start | bytes 393224 | tf_op jit(solution)/shard_map/ppermute | solution.py:45
  7.4 10.4 %collective-permute-start.4 = (bf16[512,128]{1,0:T(8,128)(2,1)}, bf16[512,128]{1,0:T(8,128)(2,1)S(1)}, u32[]{:S(2)}, u32[]{:S(2)}) collective-permute-start(bf16[512,128]{1,0:T(8,128)(2,1)} %proj_in.1), channel_id=1, source_target_pairs={{0,8},{1,9},{2,10},{3,11},{4,12},{5,13},{6,14},{7,15},{8,0},{9,1},... | collective-permute-start | bytes 393224 | tf_op jit(solution)/shard_map/ppermute | solution.py:45
  12.3 11.1 %collective-permute-start.3 = (bf16[1024,128]{1,0:T(8,128)(2,1)S(1)}, bf16[1024,128]{1,0:T(8,128)(2,1)S(1)}, u32[]{:S(2)}, u32[]{:S(2)}) collective-permute-start(bf16[1024,128]{1,0:T(8,128)(2,1)S(1)} %stack.3.refs_1_), channel_id=1, source_target_pairs={{0,2},{1,3},{2,0},{3,1},{4,6},{5,7},{6,4},{7,5},{8,10},{9,11},{10,... | collective-permute-start | bytes 786440 | tf_op jit(solution)/shard_map/ppermute | solution.py:45
  17.9 5.5 %collective-permute-start.5 = (bf16[512,128]{1,0:T(8,128)(2,1)S(1)}, bf16[512,128]{1,0:T(8,128)(2,1)S(1)}, u32[]{:S(2)}, u32[]{:S(2)}) collective-permute-start(bf16[512,128]{1,0:T(8,128)(2,1)S(1)} %collective-permute-done.4.refs_2_), channel_id=1, source_target_pairs={{0,2},{1,3},{2,0},{3,1},{4,6},{5,7},{6,4},{7,5},{8,10},{9,11},{10,... | collective-permute-start | bytes 393224 | tf_op jit(solution)/shard_map/ppermute | solution.py:45
  19.4 13.7 %copy-start.1 = (s32[1,32]{1,0:T(1,128)S(1)}, s32[1,32]{1,0:T(1,128)}, u32[]{:S(2)}) copy-start(s32[1,32]{1,0:T(1,128)} %refs_4_.1) | copy-start | bytes 388
  20.1 30.5 %copy-start.2 = (s32[3,2]{0,1:T(2,128)S(1)}, s32[3,2]{0,1:T(2,128)}, u32[]{:S(2)}) copy-start(s32[3,2]{0,1:T(2,128)} %param.13) | copy-start | bytes 76
  20.1 3.4 %collective-permute-start.7 = (bf16[2048,128]{1,0:T(8,128)(2,1)S(1)}, bf16[2048,128]{1,0:T(8,128)(2,1)S(1)}, u32[]{:S(2)}, u32[]{:S(2)}) collective-permute-start(bf16[2048,128]{1,0:T(8,128)(2,1)S(1)} %get-tuple-element.14), channel_id=1, source_target_pairs={{0,1},{1,0},{2,3},{3,2},{4,5},{5,4},{6,7},{7,6},{8,9},{9,8},{10,11... | collective-permute-start | bytes 1572872 | tf_op jit(solution)/shard_map/ppermute | solution.py:45
  23.4 2.0 %collective-permute-start.6 = (bf16[2048,128]{1,0:T(8,128)(2,1)S(1)}, bf16[2048,128]{1,0:T(8,128)(2,1)S(1)}, u32[]{:S(2)}, u32[]{:S(2)}) collective-permute-start(bf16[2048,128]{1,0:T(8,128)(2,1)S(1)} %stack.4.refs_0_), channel_id=1, source_target_pairs={{0,1},{1,0},{2,3},{3,2},{4,5},{5,4},{6,7},{7,6},{8,9},{9,8},{10,11... | collective-permute-start | bytes 1572872 | tf_op jit(solution)/shard_map/ppermute | solution.py:45
  24.8 33.2 %copy-start = (s32[32]{0:T(128)S(1)}, s32[32]{0:T(128)}, u32[]{:S(2)}) copy-start(s32[32]{0:T(128)} %param.12) | copy-start | bytes 388
  26.1 5.6 %collective-permute-start.8 = (bf16[512,128]{1,0:T(8,128)(2,1)S(1)}, bf16[512,128]{1,0:T(8,128)(2,1)S(1)}, u32[]{:S(2)}, u32[]{:S(2)}) collective-permute-start(bf16[512,128]{1,0:T(8,128)(2,1)S(1)} %px.5.refs_0_), channel_id=1, source_target_pairs={{0,2},{1,3},{2,0},{3,1},{4,6},{5,7},{6,4},{7,5},{8,10},{9,11},{10,... | collective-permute-start | bytes 393224 | tf_op jit(solution)/shard_map/ppermute | solution.py:45
  27.3 4.4 %collective-permute-start.9 = (bf16[512,128]{1,0:T(8,128)(2,1)S(1)}, bf16[512,128]{1,0:T(8,128)(2,1)S(1)}, u32[]{:S(2)}, u32[]{:S(2)}) collective-permute-start(bf16[512,128]{1,0:T(8,128)(2,1)S(1)} %px.5.refs_0_), channel_id=1, source_target_pairs={{0,1},{1,0},{2,3},{3,2},{4,5},{5,4},{6,7},{7,6},{8,9},{9,8},{10,11... | collective-permute-start | bytes 393224 | tf_op jit(solution)/shard_map/ppermute | solution.py:45
  31.7 1.3 %collective-permute-start.10 = (bf16[512,128]{1,0:T(8,128)(2,1)S(1)}, bf16[512,128]{1,0:T(8,128)(2,1)S(1)}, u32[]{:S(2)}, u32[]{:S(2)}) collective-permute-start(bf16[512,128]{1,0:T(8,128)(2,1)S(1)} %collective-permute-done.8.refs_1_), channel_id=1, source_target_pairs={{0,1},{1,0},{2,3},{3,2},{4,5},{5,4},{6,7},{7,6},{8,9},{9,8},{10,11... | collective-permute-start | bytes 393224 | tf_op jit(solution)/shard_map/ppermute | solution.py:45
  34.0 5.9 %collective-permute-start.13 = (bf16[32,2048]{1,0:T(8,128)(2,1)S(1)}, bf16[32,2048]{1,0:T(8,128)(2,1)S(1)}, u32[]{:S(2)}, u32[]{:S(2)}) collective-permute-start(bf16[32,2048]{1,0:T(8,128)(2,1)S(1)} %grads.1.refs_0_), channel_id=1, source_target_pairs={{0,12},{1,13},{2,14},{3,15},{4,0},{5,1},{6,2},{7,3},{8,4},{9,5},{1... | collective-permute-start | bytes 393224 | tf_op jit(solution)/shard_map/ppermute | solution.py:45
  36.0 13.5 %collective-permute-start.12 = (bf16[32,2048]{1,0:T(8,128)(2,1)S(1)}, bf16[32,2048]{1,0:T(8,128)(2,1)S(1)}, u32[]{:S(2)}, u32[]{:S(2)}) collective-permute-start(bf16[32,2048]{1,0:T(8,128)(2,1)S(1)} %grads.1.refs_0_), channel_id=1, source_target_pairs={{0,8},{1,9},{2,10},{3,11},{4,12},{5,13},{6,14},{7,15},{8,0},{9,1},... | collective-permute-start | bytes 393224 | tf_op jit(solution)/shard_map/ppermute | solution.py:45
  37.5 12.0 %collective-permute-start.11 = (bf16[32,2048]{1,0:T(8,128)(2,1)S(1)}, bf16[32,2048]{1,0:T(8,128)(2,1)S(1)}, u32[]{:S(2)}, u32[]{:S(2)}) collective-permute-start(bf16[32,2048]{1,0:T(8,128)(2,1)S(1)} %grads.1.refs_0_), channel_id=1, source_target_pairs={{0,4},{1,5},{2,6},{3,7},{4,8},{5,9},{6,10},{7,11},{8,12},{9,13},{1... | collective-permute-start | bytes 393224 | tf_op jit(solution)/shard_map/ppermute | solution.py:45
  49.6 5.0 %collective-permute-start.14 = (bf16[32,2048]{1,0:T(8,128)(2,1)S(1)}, bf16[32,2048]{1,0:T(8,128)(2,1)S(1)}, u32[]{:S(2)}, u32[]{:S(2)}) collective-permute-start(bf16[32,2048]{1,0:T(8,128)(2,1)S(1)} %total.1.mine.refs_0_), channel_id=1, source_target_pairs={{0,2},{1,3},{2,0},{3,1},{4,6},{5,7},{6,4},{7,5},{8,10},{9,11},{10,... | collective-permute-start | bytes 393224 | tf_op jit(solution)/shard_map/ppermute | solution.py:45
  54.6 3.3 %collective-permute-start.15 = (bf16[64,2048]{1,0:T(8,128)(2,1)S(1)}, bf16[64,2048]{1,0:T(8,128)(2,1)S(1)}, u32[]{:S(2)}, u32[]{:S(2)}) collective-permute-start(bf16[64,2048]{1,0:T(8,128)(2,1)S(1)} %stack.5), channel_id=1, source_target_pairs={{0,1},{1,0},{2,3},{3,2},{4,5},{5,4},{6,7},{7,6},{8,9},{9,8},{10,11... | collective-permute-start | bytes 786440 | tf_op jit(solution)/shard_map/ppermute | solution.py:45

commit v6 on v4

--- a/solution.py
+++ b/solution.py
@@ -12,6 +12,7 @@
 VMEM = pl.BlockSpec(memory_space=pltpu.VMEM)
 SMEM = pl.BlockSpec(memory_space=pltpu.SMEM)
 ANY = pl.BlockSpec(memory_space=pl.ANY)
+HBM = pl.BlockSpec(memory_space=pltpu.HBM)
 
 
 def levels(devices):
@@ -42,15 +43,6 @@
         z, x, core = (z + shift[0]) % deep, (x + shift[1]) % wide, (core + shift[2]) % cores
         perm.append((i, (z * wide + x) * cores + core))
     return lax.ppermute(value, "seq", perm)
-
-
-def chunks(spot, devices, square):
-    deep, wide, cores = levels(devices)
-    line = wide * cores
-    band = square // devices
-    if band % 128:
-        return [(0, spot * (square // line), square // line)]
-    return [(z * band, (z * line + spot) * band, band) for z in range(deep)]
 
 
 def load_kernel(acts, cots, proj_in, proj_out, held, own, pg_t, cots_held, weights, sems):
@@ -126,12 +118,12 @@
 
 def grads_kernel(devices, per_part, layers, rows, shifts, *refs):
     count = len(shifts)
-    feats, (lengths, out, spread) = refs[:count], refs[count:]
+    feats, lengths, outs, spread = refs[:count], refs[count], refs[count + 1:-1], refs[-1]
     wide = feats[0].shape[1]
     runs = rows // wide
     width_k = wide // layers
     square = width_k * width_k
-    _, across, cores = levels(devices)
+    deep, across, cores = levels(devices)
     me = lax.axis_index("seq")
     sizes = lengths[pl.ds(me // per_part, 1), :]
     per_row = sizes.shape[1]
@@ -153,24 +145,30 @@
             at = (f * runs + i) * wide
             spread[:, at:at + wide] = feat[rows + i * wide:rows + (i + 1) * wide, :].astype(jnp.float32)
     low = lax.broadcasted_iota(jnp.int32, (per_row, 2 * width_k), 1) < width_k
-    lanes = square // (across * cores)
-    spot = me % (across * cores)
+    line = across * cores
+    spot = me % line
+    if len(outs) == 1:
+        size = square // line
+        homes = [spot]
+    else:
+        size = square // devices
+        homes = [(me // line + k) % deep * line + spot for k in range(deep)]
     for l in range(layers):
         px = []
         for feat in feats:
             own = feat[:rows, l * width_k:(l + 1) * width_k]
             px.append(jnp.concatenate([own, own], axis=1))
         px = jnp.concatenate(px, axis=0)
-        for here, there, size in chunks(spot, devices, square):
+        for home, out in zip(homes, outs):
             terms = []
             for i in range(size // width_k):
-                row = l * width_k + there // width_k + i
+                row = l * width_k + home * (size // width_k) + i
                 terms.append((member * spread[pl.ds(row, 1), :]).astype(jnp.bfloat16))
             sums = jnp.dot(jnp.concatenate(terms, axis=0), px, preferred_element_type=jnp.float32)
             for i in range(0, size // width_k, 2):
                 even = sums[i * per_row:(i + 1) * per_row]
                 odd = sums[(i + 1) * per_row:(i + 2) * per_row]
-                at = l * lanes + here + i * width_k
+                at = l * size + i * width_k
                 out[:, at:at + 2 * width_k] = jnp.where(low, even, odd).astype(jnp.bfloat16)
 
 
@@ -204,10 +202,9 @@
     me = lax.axis_index("seq")
     for shift, block in zip(shifts, blocks):
         spot = owner(me, devices, shift) % (across * cores)
-        for here, there, size in chunks(spot, devices, square):
-            for l in range(layers):
-                at = pl.multiple_of(l * square + there, size)
-                right[:, pl.ds(at, size)] = block[:, l * lanes + here:l * lanes + here + size]
+        for l in range(layers):
+            at = pl.multiple_of(l * square + spot * lanes, lanes)
+            right[:, pl.ds(at, lanes)] = block[:, l * lanes:(l + 1) * lanes]
     scale = jnp.float32(1.0 / seqs)
     cols = min(1024, square)
     steps = square // cols
@@ -240,6 +237,49 @@
         copy.wait()
 
 
+def part_kernel(devices, keys, more, count, mine, *refs):
+    arrays, refs = refs[:len(keys)], refs[len(keys):]
+    pairs, (side, out, held, sems) = refs[count], refs[-4:]
+    _, band, _ = held.shape
+    npair = pairs.shape[0]
+    seqs, full = mine.shape
+    square = band * devices
+    layers = full // band
+    me = lax.axis_index("seq")
+    scale = jnp.float32(1.0 / seqs)
+
+    def pieces(shifts, array):
+        return [(owner(me, devices, shift), array.at[pl.ds(i * seqs, seqs)]) for i, shift in enumerate(shifts)]
+
+    bands = [piece for shifts, array in zip(keys, arrays) for piece in pieces(shifts, array)]
+    copies = []
+    for p in range(npair):
+        at = pl.multiple_of(pairs[p, 0] * band, band)
+        left = mine[:, pl.ds(at, band)].astype(jnp.float32).T.astype(jnp.bfloat16)
+        at = pl.multiple_of(pairs[p, 1] * band, band)
+        for home, piece in bands:
+            i = len(copies)
+            held[i] = jnp.dot(left, piece[:, pl.ds(at, band)], preferred_element_type=jnp.float32) * scale
+            to = pl.ds(pl.multiple_of(home * band, band), band)
+            copies.append(pltpu.make_async_copy(held.at[i], out.at[p, :, to], sems.at[i]))
+            copies[-1].start()
+    if not more:
+        side[...] = jnp.zeros(side.shape, side.dtype)
+    else:
+        rest, slots = refs[0], refs[1]
+        own = me * CAP + lax.broadcasted_iota(jnp.int32, (CAP, seqs), 0)
+        picker = (jnp.broadcast_to(slots[...], (CAP, seqs)) == own).astype(jnp.float32).astype(jnp.bfloat16)
+        bands = bands + pieces(more, rest)
+        values = jnp.concatenate([piece[...] for _, piece in bands], axis=1)
+        picked = jnp.dot(picker, values, preferred_element_type=jnp.float32).astype(jnp.bfloat16)
+        for i, (home, _) in enumerate(bands):
+            for l in range(layers):
+                to = pl.ds(pl.multiple_of(l * square + home * band, band), band)
+                side[:, to] = picked[:, i * full + l * band:i * full + (l + 1) * band]
+    for copy in copies:
+        copy.wait()
+
+
 def shards(acts, cots, proj_in, proj_out, lengths, slots, pairs):
     layers, rows, width = acts.shape
     wide = proj_out.shape[1]
@@ -264,7 +304,7 @@
             pltpu.VMEM(proj_in.shape, jnp.bfloat16),
             pltpu.VMEM((wide, rows), jnp.bfloat16),
         ),
-        in_specs=[ANY] * 4,
+        in_specs=[HBM] * 4,
         out_specs=(VMEM,) * 3,
         scratch_shapes=[
             pltpu.VMEM(cots.shape, jnp.bfloat16),
@@ -274,12 +314,12 @@
         compiler_params=params,
         cost_estimate=light,
         name="load",
-    )(acts, cots, proj_in, proj_out)
+    )(*[pltpu.with_memory_space_constraint(a, pltpu.HBM) for a in (acts, cots, proj_in, proj_out)])
 
     def stack(arrays, after):
         return pl.pallas_call(
             functools.partial(stack_kernel, len(arrays)),
-            out_shape=jax.ShapeDtypeStruct((sum(a.shape[0] for a in arrays), wide), jnp.bfloat16),
+            out_shape=jax.ShapeDtypeStruct((sum(a.shape[0] for a in arrays), arrays[0].shape[1]), jnp.bfloat16),
             in_specs=[VMEM] * len(arrays) + [ANY] * len(after),
             out_specs=VMEM,
             compiler_params=params,
@@ -305,27 +345,25 @@
         return result if keep else result[0]
 
     feat_type = jax.ShapeDtypeStruct((2 * rows, wide), jnp.bfloat16)
-    if tall % 128 == 0 and deep > 2 and across == 2 and cores == 2:
-        spins = sorted(range(1, deep), key=lambda z: min(z, deep - z))
-        near, far = spins[:-1], spins[-1]
+    spins = sorted(range(1, deep), key=lambda z: min(z, deep - z))
+    near, far = spins[:-1], spins[-1]
+    staged = tall % 128 == 0 and deep > 2 and across == 2 and cores == 2
+    if staged:
         got = [send(proj_in, devices, (z, 0, 0)) for z in near]
         side = send(proj_in, devices, (0, 1, 0))
         got_far = send(proj_in, devices, (far, 0, 0))
         got = stack(got, (pg_t, side))
         side_near = send(got, devices, (0, 1, 0))
-        value, column = px([(own, [(0, 0, 0)]), (got, [(z, 0, 0) for z in near])], keep=True)
+        side_far = send(got_far, devices, (0, 1, 0))
+        value, column = px(
+            [(own, [(0, 0, 0)]), (got, [(z, 0, 0) for z in near]), (got_far, [(far, 0, 0)])], keep=True
+        )
         twin = send(column, devices, (0, 0, 1))
-        side_far = send(got_far, devices, (0, 1, 0))
-        twin_far = send(got_far, devices, (0, 0, 1))
-        side = stack([side, side_near], (value,))
+        side = stack([side, side_near, side_far], (value,))
         twin_side = send(side, devices, (0, 0, 1))
-        first = [0, *near]
-        value = px([(side, [(z, 1, 0) for z in first]), (got_far, [(far, 0, 0)])], value)
-        twin_side_far = send(side_far, devices, (0, 0, 1))
-        value = px(
-            [(twin, [(z, 0, 1) for z in first]), (twin_far, [(far, 0, 1)]), (side_far, [(far, 1, 0)])], value
-        )
-        value = px([(twin_side, [(z, 1, 1) for z in first]), (twin_side_far, [(far, 1, 1)])], value, end=True)
+        order = [0, *near, far]
+        value = px([(side, [(z, 1, 0) for z in order]), (twin, [(z, 0, 1) for z in order])], value)
+        value = px([(twin_side, [(z, 1, 1) for z in order])], value, end=True)
     else:
         groups = [[z * line + i for z in range(deep)] for i in range(line)]
         column = lax.all_to_all(jnp.tile(proj_in, (deep, 1)), "seq", 0, 0, axis_index_groups=groups, tiled=True)
@@ -346,32 +384,81 @@
         return {(*k[:2], c): send(v, devices, (0, 0, c)) if c else v for c in range(cores) for k, v in held.items()}
 
     feats = plane(value)
-    lanes = layers * square // line
+    split = staged and band % 128 == 0
+    lanes = layers * band if split else layers * square // line
     sums = pl.pallas_call(
         functools.partial(grads_kernel, devices, per_part, layers, rows, tuple(feats)),
-        out_shape=jax.ShapeDtypeStruct((per_row, lanes), jnp.bfloat16),
+        out_shape=[jax.ShapeDtypeStruct((per_row, lanes), jnp.bfloat16)] * (deep if split else 1),
         in_specs=[VMEM] * (len(feats) + 1),
-        out_specs=VMEM,
+        out_specs=[VMEM] * (deep if split else 1),
         scratch_shapes=[pltpu.VMEM((wide, rows * line), jnp.float32)],
         compiler_params=params,
+        cost_estimate=light,
         name="grads",
     )(*feats.values(), lengths)
-    terms = [send(sums, devices, (z, 0, 0)) if z else sums for z in range(deep)]
+    sums = sums if split else sums * deep
+    terms = [send(sums[z], devices, (z, 0, 0)) if z else sums[z] for z in range(deep)]
     total = pl.pallas_call(
         functools.partial(total_kernel, devices, per_part),
         out_shape=jax.ShapeDtypeStruct((seqs, lanes), jnp.bfloat16),
         in_specs=[VMEM] * deep,
         out_specs=VMEM,
         compiler_params=params,
+        cost_estimate=light,
         name="total",
     )(*terms)
+    logged_type = jax.ShapeDtypeStruct((CAP, layers * square), jnp.bfloat16)
+    covariance_type = jax.ShapeDtypeStruct((npair, band, square), jnp.float32)
+
+    def part(entries, before=None, more=()):
+        arrays, keys = zip(*entries)
+        count = sum(map(len, keys)) * npair
+        extra = [more[0], slots.reshape(1, seqs)] if more else []
+        operands = [total, *arrays, *extra, pairs]
+        specs = [VMEM] * (len(operands) - 1) + [SMEM]
+        alias = {}
+        if before is not None:
+            alias = {len(operands): 1}
+            operands.append(before)
+            specs.append(ANY)
+        return pl.pallas_call(
+            functools.partial(part_kernel, devices, keys, more[1] if more else (), len(extra)),
+            out_shape=[logged_type if more else jax.ShapeDtypeStruct((8, 128), jnp.float32), covariance_type],
+            in_specs=specs,
+            out_specs=[VMEM, ANY],
+            scratch_shapes=[pltpu.VMEM((count, band, band), jnp.float32), pltpu.SemaphoreType.DMA((count,))],
+            input_output_aliases=alias,
+            compiler_params=params,
+            cost_estimate=light,
+            name="covariance",
+        )(*operands)
+
+    if split:
+        got = [send(total, devices, (z, 0, 0)) for z in near]
+        side = send(total, devices, (0, 1, 0))
+        got_far = send(total, devices, (far, 0, 0))
+        got = stack(got, (side,))
+        side_near = send(got, devices, (0, 1, 0))
+        side_far = send(got_far, devices, (0, 1, 0))
+        done, covariance = part(
+            [(total, [(0, 0, 0)]), (got, [(z, 0, 0) for z in near]), (got_far, [(far, 0, 0)])]
+        )
+        both = stack([total, got, got_far, side, side_near, side_far], (done,))
+        twin = send(both, devices, (0, 0, 1))
+        order = [0, *near, far]
+        _, covariance = part(
+            [(side, [(0, 1, 0)]), (side_near, [(z, 1, 0) for z in near]), (side_far, [(far, 1, 0)])], covariance
+        )
+        logged, covariance = part(
+            [(twin, [(z, x, 1) for x in range(2) for z in order])],
+            covariance,
+            (both, [(z, x, 0) for x in range(2) for z in order]),
+        )
+        return logged, covariance
     full = plane(total)
     return pl.pallas_call(
         functools.partial(covariance_kernel, devices, tuple(full)),
-        out_shape=[
-            jax.ShapeDtypeStruct((CAP, layers * square), jnp.bfloat16),
-            jax.ShapeDtypeStruct((npair, band, square), jnp.float32),
-        ],
+        out_shape=[logged_type, covariance_type],
         in_specs=[VMEM] * (len(full) + 1) + [SMEM],
         out_specs=[VMEM, ANY],
         scratch_shapes=[

time: 65.7 us -> 64.5 us (0.982)
  waiting for transfers between devices: 31.4 us -> 21.7 us
  starting transfers between devices: 15.2 us -> 24 us
  local copies, waits for them, and re-layouts: 6.57 us -> 0.11 us
  Pallas kernels: 11.5 us -> 17.7 us
    ppermute x19 -> x21, waiting for transfers between devices: 31.4 us -> 21.7 us  [send(): return lax.ppermute(value, 'seq', perm)]
    ppermute x19 -> x21, starting transfers between devices: 15.2 us -> 24 us  [send(): return lax.ppermute(value, 'seq', perm)]
    unnamed x17 -> x7, local copies, waits for them, and re-layouts: 6.57 us -> 0.11 us
    pallas_call x1 -> x3, Pallas kernels: 6.26 us -> 10.1 us  [part(): pl.pallas_call(functools.partial(part_kernel, devices, keys, more[1] if m...]
    pallas_call x1, Pallas kernels: 1.35 us -> 3.87 us  [shards(): pl.pallas_call(load_kernel, out_shape=(pltpu.VMEM(acts.shape, jnp.bfloat1...]
    pallas_call x4 -> x3, Pallas kernels: 2.87 us -> 2.72 us  [px(): pl.pallas_call(functools.partial(px_kernel, devices, keys, before is None...]
  transfers between devices with their start and end apart: 19 -> 21, of which waited for: 9 -> 10; matrix products, arithmetic and copies ran while one was open for 0% -> 0% of each run, Pallas kernels for 5% -> 18%
where the time goes in v6:
time: 64.5 us; the launch traced here: 64.3 us
  starting transfers between devices  24 us (37%)
  waiting for transfers between devices  21.7 us (34%)
  Pallas kernels  17.7 us (27%)
  between operations  0.81 us (1%)
    ppermute x21, starting transfers between devices, send(): return lax.ppermute(value, 'seq', perm)  24 us
    ppermute x21, waiting for transfers between devices, send(): return lax.ppermute(value, 'seq', perm)  21.7 us
    pallas_call x3, Pallas kernels, part(): pl.pallas_call(functools.partial(part_kernel, devices, keys, more[1] if m...  10.1 us
    pallas_call x1, Pallas kernels, shards(): pl.pallas_call(load_kernel, out_shape=(pltpu.VMEM(acts.shape, jnp.bfloat1...  3.87 us
    pallas_call x3, Pallas kernels, px(): pl.pallas_call(functools.partial(px_kernel, devices, keys, before is None...  2.72 us
  transfers between devices with their start and end apart: 21, of which 10 were waited for; matrix products, arithmetic and copies ran while one was open for 0% of the time, Pallas kernels for 18%

profile of v6, /device:TPU:0, one launch (start us, length us, event | category | flops | bytes accessed | tf_op | source)
XLA Modules:
  0.0 64.3 jit_solution(3587274522895036037)
XLA Ops:
  0.6 3.1 %collective-permute-start.1 = (bf16[512,128]{1,0:T(8,128)(2,1)}, bf16[512,128]{1,0:T(8,128)(2,1)S(1)}, u32[]{:S(2)}, u32[]{:S(2)}) collective-permute-start(bf16[512,128]{1,0:T(8,128)(2,1)} %proj_in.1), channel_id=1, source_target_pairs={{0,4},{1,5},{2,6},{3,7},{4,8},{5,9},{6,10},{7,11},{8,12},{9,13},{1... | collective-permute-start | bytes 393224 | tf_op jit(solution)/shard_map/ppermute | solution.py:45
  3.7 1.5 %collective-permute-start = (bf16[512,128]{1,0:T(8,128)(2,1)}, bf16[512,128]{1,0:T(8,128)(2,1)S(1)}, u32[]{:S(2)}, u32[]{:S(2)}) collective-permute-start(bf16[512,128]{1,0:T(8,128)(2,1)} %proj_in.1), channel_id=1, source_target_pairs={{0,2},{1,3},{2,0},{3,1},{4,6},{5,7},{6,4},{7,5},{8,10},{9,11},{10,... | collective-permute-start | bytes 393224 | tf_op jit(solution)/shard_map/ppermute | solution.py:45
  5.2 2.2 %collective-permute-start.2 = (bf16[512,128]{1,0:T(8,128)(2,1)}, bf16[512,128]{1,0:T(8,128)(2,1)S(1)}, u32[]{:S(2)}, u32[]{:S(2)}) collective-permute-start(bf16[512,128]{1,0:T(8,128)(2,1)} %proj_in.1), channel_id=1, source_target_pairs={{0,12},{1,13},{2,14},{3,15},{4,0},{5,1},{6,2},{7,3},{8,4},{9,5},{1... | collective-permute-start | bytes 393224 | tf_op jit(solution)/shard_map/ppermute | solution.py:45
  7.4 0.8 %collective-permute-start.4 = (bf16[512,128]{1,0:T(8,128)(2,1)}, bf16[512,128]{1,0:T(8,128)(2,1)S(1)}, u32[]{:S(2)}, u32[]{:S(2)}) collective-permute-start(bf16[512,128]{1,0:T(8,128)(2,1)} %proj_in.1), channel_id=1, source_target_pairs={{0,8},{1,9},{2,10},{3,11},{4,12},{5,13},{6,14},{7,15},{8,0},{9,1},... | collective-permute-start | bytes 393224 | tf_op jit(solution)/shard_map/ppermute | solution.py:45
  8.2 3.9 %load.1 = (bf16[2,256,8192]{2,1,0:T(8,128)(2,1)S(1)}, bf16[512,128]{1,0:T(8,128)(2,1)S(1)}, bf16[128,256]{1,0:T(8,128)(2,1)S(1)}) custom-call(bf16[2,256,8192]{2,1,0:T(8,128)(2,1)} %acts.1, bf16[2,256,1024]{2,1,0:T(8,128)(2,1)} %cots.1, bf16[512,128]{1,0:T(8,128)(2,1)} %proj_in.1, bf16[1024,128]{1,0:T(8,128)(2,1)} %proj_out.1), custom_call_target="tpu_custom_call" | custom-call | flops 1 | bytes 1 | tf_op jit(solution)/shard_map/load/pallas_call | solution.py:300
  12.3 1.2 %collective-permute-start.3 = (bf16[1024,128]{1,0:T(8,128)(2,1)S(1)}, bf16[1024,128]{1,0:T(8,128)(2,1)S(1)}, u32[]{:S(2)}, u32[]{:S(2)}) collective-permute-start(bf16[1024,128]{1,0:T(8,128)(2,1)S(1)} %stack.4.refs_1_), channel_id=1, source_target_pairs={{0,2},{1,3},{2,0},{3,1},{4,6},{5,7},{6,4},{7,5},{8,10},{9,11},{10,... | collective-permute-start | bytes 786440 | tf_op jit(solution)/shard_map/ppermute | solution.py:45
  13.5 4.3 %collective-permute-done.4.refs_2_ = bf16[512,128]{1,0:T(8,128)(2,1)S(1)} collective-permute-done((bf16[512,128]{1,0:T(8,128)(2,1)}, bf16[512,128]{1,0:T(8,128)(2,1)S(1)}, u32[]{:S(2)}, u32[]{:S(2)}) %collective-permute-start.4) | collective-permute-done | bytes 131104 | tf_op jit(solution)/shard_map/ppermute | solution.py:45
  17.9 1.5 %collective-permute-start.5 = (bf16[512,128]{1,0:T(8,128)(2,1)S(1)}, bf16[512,128]{1,0:T(8,128)(2,1)S(1)}, u32[]{:S(2)}, u32[]{:S(2)}) collective-permute-start(bf16[512,128]{1,0:T(8,128)(2,1)S(1)} %collective-permute-done.4.refs_2_), channel_id=1, source_target_pairs={{0,2},{1,3},{2,0},{3,1},{4,6},{5,7},{6,4},{7,5},{8,10},{9,11},{10,... | collective-permute-start | bytes 393224 | tf_op jit(solution)/shard_map/ppermute | solution.py:45
  19.4 0.7 %px.3 = (f32[2,256,128]{2,1,0:T(8,128)S(1)}, bf16[2048,128]{1,0:T(8,128)(2,1)S(1)}) custom-call(bf16[2,256,8192]{2,1,0:T(8,128)(2,1)S(1)} %get-tuple-element.14.acts, bf16[512,128]{1,0:T(8,128)(2,1)S(1)} %get-tuple-element.16.refs_0_, bf16[1024,128]{1,0:T(8,128)(2,1)S(1)} %stack.4.refs_1_, bf16[512,128]{1,0:T(8,128)(2,1)S(1)} %collective-permute-done.4.refs_2_), custom_call_target="tpu_custom_call" | custom-call | flops 1 | bytes 1 | tf_op jit(solution)/shard_map/px/pallas_call | solution.py:336
  20.2 3.2 %collective-permute-done.5.refs_2_ = bf16[512,128]{1,0:T(8,128)(2,1)S(1)} collective-permute-done((bf16[512,128]{1,0:T(8,128)(2,1)S(1)}, bf16[512,128]{1,0:T(8,128)(2,1)S(1)}, u32[]{:S(2)}, u32[]{:S(2)}) %collective-permute-start.5) | collective-permute-done | bytes 131104 | tf_op jit(solution)/shard_map/ppermute | solution.py:45
  23.5 1.3 %px.4.refs_1_ = f32[2,256,128]{2,1,0:T(8,128)S(1)} custom-call(bf16[2,256,8192]{2,1,0:T(8,128)(2,1)S(1)} %get-tuple-element.14.acts, bf16[2048,128]{1,0:T(8,128)(2,1)S(1)} %stack.5.refs_0_, bf16[2048,128]{1,0:T(8,128)(2,1)S(1)} %collective-permute-done.7.refs_1_, f32[2,256,128]{2,1,0:T(8,128)S(1)} %get-tuple-element.17.refs_3_.refs_2_), custom_call_target="tpu_custom_call" | custom-call | flops 1 | bytes 1 | tf_op jit(solution)/shard_map/px/pallas_call | solution.py:336
  24.8 0.6 collective-permute-done.6.refs_0_
  25.4 0.7 %px.5.refs_0_ = bf16[512,128]{1,0:T(8,128)(2,1)S(1)} custom-call(bf16[2,256,8192]{2,1,0:T(8,128)(2,1)S(1)} %get-tuple-element.14.acts, bf16[2048,128]{1,0:T(8,128)(2,1)S(1)} %collective-permute-done.6.refs_0_, f32[2,256,128]{2,1,0:T(8,128)S(1)} %px.4.refs_1_, bf16[128,256]{1,0:T(8,128)(2,1)S(1)} %get-tuple-element.15.refs_2_), custom_call_target="tpu_custom_call" | custom-call | flops 1 | bytes 1 | tf_op jit(solution)/shard_map/px/pallas_call | solution.py:336
  26.1 1.3 %collective-permute-start.8 = (bf16[512,128]{1,0:T(8,128)(2,1)S(1)}, bf16[512,128]{1,0:T(8,128)(2,1)S(1)}, u32[]{:S(2)}, u32[]{:S(2)}) collective-permute-start(bf16[512,128]{1,0:T(8,128)(2,1)S(1)} %px.5.refs_0_), channel_id=1, source_target_pairs={{0,2},{1,3},{2,0},{3,1},{4,6},{5,7},{6,4},{7,5},{8,10},{9,11},{10,... | collective-permute-start | bytes 393224 | tf_op jit(solution)/shard_map/ppermute | solution.py:45
  27.3 4.3 %collective-permute-done.8.refs_1_ = bf16[512,128]{1,0:T(8,128)(2,1)S(1)} collective-permute-done((bf16[512,128]{1,0:T(8,128)(2,1)S(1)}, bf16[512,128]{1,0:T(8,128)(2,1)S(1)}, u32[]{:S(2)}, u32[]{:S(2)}) %collective-permute-start.8) | collective-permute-done | bytes 131104 | tf_op jit(solution)/shard_map/ppermute | solution.py:45
  31.7 1.3 %collective-permute-done.10.refs_3_ = bf16[512,128]{1,0:T(8,128)(2,1)S(1)} collective-permute-done((bf16[512,128]{1,0:T(8,128)(2,1)S(1)}, bf16[512,128]{1,0:T(8,128)(2,1)S(1)}, u32[]{:S(2)}, u32[]{:S(2)}) %collective-permute-start.10) | collective-permute-done | bytes 131104 | tf_op jit(solution)/shard_map/ppermute | solution.py:45
  33.0 0.9 %grads.1 = (bf16[32,512]{1,0:T(8,128)(2,1)S(1)}, bf16[32,512]{1,0:T(8,128)(2,1)S(1)}, bf16[32,512]{1,0:T(8,128)(2,1)S(1)}, bf16[32,512]{1,0:T(8,128)(2,1)S(1)}) custom-call(bf16[512,128]{1,0:T(8,128)(2,1)S(1)} %px.5.refs_0_, bf16[512,128]{1,0:T(8,128)(2,1)S(1)} %collective-permute-done.8.refs_1_, bf16[512,128]{1,0:T(8,128)(2,1)S(1)} %collective-permute-done.9.refs_2_, ...), custom_call_target="tpu_custom_call" | custom-call | flops 1 | bytes 1 | tf_op jit(solution)/shard_map/grads/pallas_call | solution.py:389
  34.0 2.1 %collective-permute-start.11 = (bf16[32,512]{1,0:T(8,128)(2,1)S(1)}, bf16[32,512]{1,0:T(8,128)(2,1)S(1)}, u32[]{:S(2)}, u32[]{:S(2)}) collective-permute-start(bf16[32,512]{1,0:T(8,128)(2,1)S(1)} %get-tuple-element.20), channel_id=1, source_target_pairs={{0,4},{1,5},{2,6},{3,7},{4,8},{5,9},{6,10},{7,11},{8,12},{9,13},{1... | collective-permute-start | bytes 98312 | tf_op jit(solution)/shard_map/ppermute | solution.py:45
  36.1 0.5 collective-permute-start.12
  36.5 2.1 %collective-permute-start.13 = (bf16[32,512]{1,0:T(8,128)(2,1)S(1)}, bf16[32,512]{1,0:T(8,128)(2,1)S(1)}, u32[]{:S(2)}, u32[]{:S(2)}) collective-permute-start(bf16[32,512]{1,0:T(8,128)(2,1)S(1)} %get-tuple-element.22), channel_id=1, source_target_pairs={{0,12},{1,13},{2,14},{3,15},{4,0},{5,1},{6,2},{7,3},{8,4},{9,5},{1... | collective-permute-start | bytes 98312 | tf_op jit(solution)/shard_map/ppermute | solution.py:45
  38.6 1.3 %collective-permute-done.11.refs_1_ = bf16[32,512]{1,0:T(8,128)(2,1)S(1)} collective-permute-done((bf16[32,512]{1,0:T(8,128)(2,1)S(1)}, bf16[32,512]{1,0:T(8,128)(2,1)S(1)}, u32[]{:S(2)}, u32[]{:S(2)}) %collective-permute-start.11) | collective-permute-done | bytes 32800 | tf_op jit(solution)/shard_map/ppermute | solution.py:45
  40.0 1.3 %collective-permute-done.12.refs_2_ = bf16[32,512]{1,0:T(8,128)(2,1)S(1)} collective-permute-done((bf16[32,512]{1,0:T(8,128)(2,1)S(1)}, bf16[32,512]{1,0:T(8,128)(2,1)S(1)}, u32[]{:S(2)}, u32[]{:S(2)}) %collective-permute-start.12) | collective-permute-done | bytes 32800 | tf_op jit(solution)/shard_map/ppermute | solution.py:45
  41.3 1.3 %collective-permute-start.16 = (bf16[32,512]{1,0:T(8,128)(2,1)S(1)}, bf16[32,512]{1,0:T(8,128)(2,1)S(1)}, u32[]{:S(2)}, u32[]{:S(2)}) collective-permute-start(bf16[32,512]{1,0:T(8,128)(2,1)S(1)} %total.1.mine.refs_0_), channel_id=1, source_target_pairs={{0,2},{1,3},{2,0},{3,1},{4,6},{5,7},{6,4},{7,5},{8,10},{9,11},{10,... | collective-permute-start | bytes 98312 | tf_op jit(solution)/shard_map/ppermute | solution.py:45
  42.6 3.6 %collective-permute-start.15 = (bf16[32,512]{1,0:T(8,128)(2,1)S(1)}, bf16[32,512]{1,0:T(8,128)(2,1)S(1)}, u32[]{:S(2)}, u32[]{:S(2)}) collective-permute-start(bf16[32,512]{1,0:T(8,128)(2,1)S(1)} %total.1.mine.refs_0_), channel_id=1, source_target_pairs={{0,12},{1,13},{2,14},{3,15},{4,0},{5,1},{6,2},{7,3},{8,4},{9,5},{1... | collective-permute-start | bytes 98312 | tf_op jit(solution)/shard_map/ppermute | solution.py:45
  46.2 0.6 collective-permute-start.17
  46.7 1.0 %collective-permute-done.15.refs_1_ = bf16[32,512]{1,0:T(8,128)(2,1)S(1)} collective-permute-done((bf16[32,512]{1,0:T(8,128)(2,1)S(1)}, bf16[32,512]{1,0:T(8,128)(2,1)S(1)}, u32[]{:S(2)}, u32[]{:S(2)}) %collective-permute-start.15) | collective-permute-done | bytes 32800 | tf_op jit(solution)/shard_map/ppermute | solution.py:45
  47.8 4.1 %collective-permute-done.14.refs_0_ = bf16[32,512]{1,0:T(8,128)(2,1)S(1)} collective-permute-done((bf16[32,512]{1,0:T(8,128)(2,1)S(1)}, bf16[32,512]{1,0:T(8,128)(2,1)S(1)}, u32[]{:S(2)}, u32[]{:S(2)}) %collective-permute-start.14) | collective-permute-done | bytes 32800 | tf_op jit(solution)/shard_map/ppermute | solution.py:45
  51.9 0.3 collective-permute-start.18
  52.2 1.7 %collective-permute-start.19 = (bf16[32,512]{1,0:T(8,128)(2,1)S(1)}, bf16[32,512]{1,0:T(8,128)(2,1)S(1)}, u32[]{:S(2)}, u32[]{:S(2)}) collective-permute-start(bf16[32,512]{1,0:T(8,128)(2,1)S(1)} %collective-permute-done.17.refs_2_), channel_id=1, source_target_pairs={{0,2},{1,3},{2,0},{3,1},{4,6},{5,7},{6,4},{7,5},{8,10},{9,11},{10,... | collective-permute-start | bytes 98312 | tf_op jit(solution)/shard_map/ppermute | solution.py:45
  54.0 2.6 %covariance.3 = (f32[8,128]{1,0:T(8,128)S(1)}, f32[3,256,4096]{2,1,0:T(8,128)}) custom-call(bf16[32,512]{1,0:T(8,128)(2,1)S(1)} %total.1.mine.refs_0_, bf16[32,512]{1,0:T(8,128)(2,1)S(1)} %total.1.mine.refs_0_, bf16[64,512]{1,0:T(8,128)(2,1)S(1)} %stack.6.refs_1_, bf16[32,512]{1,0:T(8,128)(2,1)S(1)} %collective-permute-done.17.refs_2_, s32[3,2]{1,0:T(4,128)S(1)} %copy.11.refs_3_), custom_call_target="tpu_custom_call" | custom-call | flops 1 | bytes 1 | tf_op jit(solution)/shard_map/covariance/pallas_call | solution.py:424
  56.8 3.2 %covariance.4 = (f32[8,128]{1,0:T(8,128)}, f32[3,256,4096]{2,1,0:T(8,128)}) custom-call(bf16[32,512]{1,0:T(8,128)(2,1)S(1)} %total.1.mine.refs_0_, bf16[32,512]{1,0:T(8,128)(2,1)S(1)} %collective-permute-done.16.refs_2_.refs_3_.refs_0_, bf16[64,512]{1,0:T(8,128)(2,1)S(1)} %collective-permute-done.18.refs_4_.refs_1_, ...), custom_call_target="tpu_custom_call", output_to_operand_aliasing={{1}: (5, {})} | custom-call | flops 1 | bytes 1 | tf_op jit(solution)/shard_map/covariance/pallas_call | solution.py:424
  60.0 4.3 %covariance.5 = (bf16[2,8192]{1,0:T(2,128)(2,1)}, f32[3,256,4096]{2,1,0:T(8,128)}) custom-call(bf16[32,512]{1,0:T(8,128)(2,1)S(1)} %total.1.mine.refs_0_, bf16[256,512]{1,0:T(8,128)(2,1)S(1)} %collective-permute-done.20.refs_0_, bf16[256,512]{1,0:T(8,128)(2,1)S(1)} %stack.7.refs_1_, s32[1,32]{1,0:T(1,128)S(1)} %bitcast.1, ...), custom_call_target="tpu_custom_call", output_to_operand_aliasing={{1}: (5, {})} | custom-call | flops 1 | bytes 1 | tf_op jit(solution)/shard_map/covariance/pallas_call | solution.py:424
  (30 shorter events, 0.6 us)
Async XLA Ops:
  0.6 11.5 %collective-permute-start.1 = (bf16[512,128]{1,0:T(8,128)(2,1)}, bf16[512,128]{1,0:T(8,128)(2,1)S(1)}, u32[]{:S(2)}, u32[]{:S(2)}) collective-permute-start(bf16[512,128]{1,0:T(8,128)(2,1)} %proj_in.1), channel_id=1, source_target_pairs={{0,4},{1,5},{2,6},{3,7},{4,8},{5,9},{6,10},{7,11},{8,12},{9,13},{1... | collective-permute-start | bytes 393224 | tf_op jit(solution)/shard_map/ppermute | solution.py:45
  3.7 8.4 %collective-permute-start = (bf16[512,128]{1,0:T(8,128)(2,1)}, bf16[512,128]{1,0:T(8,128)(2,1)S(1)}, u32[]{:S(2)}, u32[]{:S(2)}) collective-permute-start(bf16[512,128]{1,0:T(8,128)(2,1)} %proj_in.1), channel_id=1, source_target_pairs={{0,2},{1,3},{2,0},{3,1},{4,6},{5,7},{6,4},{7,5},{8,10},{9,11},{10,... | collective-permute-start | bytes 393224 | tf_op jit(solution)/shard_map/ppermute | solution.py:45
  5.2 7.0 %collective-permute-start.2 = (bf16[512,128]{1,0:T(8,128)(2,1)}, bf16[512,128]{1,0:T(8,128)(2,1)S(1)}, u32[]{:S(2)}, u32[]{:S(2)}) collective-permute-start(bf16[512,128]{1,0:T(8,128)(2,1)} %proj_in.1), channel_id=1, source_target_pairs={{0,12},{1,13},{2,14},{3,15},{4,0},{5,1},{6,2},{7,3},{8,4},{9,5},{1... | collective-permute-start | bytes 393224 | tf_op jit(solution)/shard_map/ppermute | solution.py:45
  7.4 10.4 %collective-permute-start.4 = (bf16[512,128]{1,0:T(8,128)(2,1)}, bf16[512,128]{1,0:T(8,128)(2,1)S(1)}, u32[]{:S(2)}, u32[]{:S(2)}) collective-permute-start(bf16[512,128]{1,0:T(8,128)(2,1)} %proj_in.1), channel_id=1, source_target_pairs={{0,8},{1,9},{2,10},{3,11},{4,12},{5,13},{6,14},{7,15},{8,0},{9,1},... | collective-permute-start | bytes 393224 | tf_op jit(solution)/shard_map/ppermute | solution.py:45
  12.3 11.1 %collective-permute-start.3 = (bf16[1024,128]{1,0:T(8,128)(2,1)S(1)}, bf16[1024,128]{1,0:T(8,128)(2,1)S(1)}, u32[]{:S(2)}, u32[]{:S(2)}) collective-permute-start(bf16[1024,128]{1,0:T(8,128)(2,1)S(1)} %stack.4.refs_1_), channel_id=1, source_target_pairs={{0,2},{1,3},{2,0},{3,1},{4,6},{5,7},{6,4},{7,5},{8,10},{9,11},{10,... | collective-permute-start | bytes 786440 | tf_op jit(solution)/shard_map/ppermute | solution.py:45
  17.9 5.5 %collective-permute-start.5 = (bf16[512,128]{1,0:T(8,128)(2,1)S(1)}, bf16[512,128]{1,0:T(8,128)(2,1)S(1)}, u32[]{:S(2)}, u32[]{:S(2)}) collective-permute-start(bf16[512,128]{1,0:T(8,128)(2,1)S(1)} %collective-permute-done.4.refs_2_), channel_id=1, source_target_pairs={{0,2},{1,3},{2,0},{3,1},{4,6},{5,7},{6,4},{7,5},{8,10},{9,11},{10,... | collective-permute-start | bytes 393224 | tf_op jit(solution)/shard_map/ppermute | solution.py:45
  19.4 13.7 %copy-start = (s32[1,32]{1,0:T(1,128)S(1)}, s32[1,32]{1,0:T(1,128)}, u32[]{:S(2)}) copy-start(s32[1,32]{1,0:T(1,128)} %refs_4_.1) | copy-start | bytes 388
  20.1 33.8 %copy-start.2 = (s32[3,2]{0,1:T(2,128)S(1)}, s32[3,2]{0,1:T(2,128)}, u32[]{:S(2)}) copy-start(s32[3,2]{0,1:T(2,128)} %param.13) | copy-start | bytes 76
  20.1 3.4 %collective-permute-start.7 = (bf16[2048,128]{1,0:T(8,128)(2,1)S(1)}, bf16[2048,128]{1,0:T(8,128)(2,1)S(1)}, u32[]{:S(2)}, u32[]{:S(2)}) collective-permute-start(bf16[2048,128]{1,0:T(8,128)(2,1)S(1)} %get-tuple-element.18), channel_id=1, source_target_pairs={{0,1},{1,0},{2,3},{3,2},{4,5},{5,4},{6,7},{7,6},{8,9},{9,8},{10,11... | collective-permute-start | bytes 1572872 | tf_op jit(solution)/shard_map/ppermute | solution.py:45
  23.4 2.0 %collective-permute-start.6 = (bf16[2048,128]{1,0:T(8,128)(2,1)S(1)}, bf16[2048,128]{1,0:T(8,128)(2,1)S(1)}, u32[]{:S(2)}, u32[]{:S(2)}) collective-permute-start(bf16[2048,128]{1,0:T(8,128)(2,1)S(1)} %stack.5.refs_0_), channel_id=1, source_target_pairs={{0,1},{1,0},{2,3},{3,2},{4,5},{5,4},{6,7},{7,6},{8,9},{9,8},{10,11... | collective-permute-start | bytes 1572872 | tf_op jit(solution)/shard_map/ppermute | solution.py:45
  24.8 35.2 %copy-start.1 = (s32[32]{0:T(128)S(1)}, s32[32]{0:T(128)}, u32[]{:S(2)}) copy-start(s32[32]{0:T(128)} %param.12) | copy-start | bytes 388
  26.1 5.6 %collective-permute-start.8 = (bf16[512,128]{1,0:T(8,128)(2,1)S(1)}, bf16[512,128]{1,0:T(8,128)(2,1)S(1)}, u32[]{:S(2)}, u32[]{:S(2)}) collective-permute-start(bf16[512,128]{1,0:T(8,128)(2,1)S(1)} %px.5.refs_0_), channel_id=1, source_target_pairs={{0,2},{1,3},{2,0},{3,1},{4,6},{5,7},{6,4},{7,5},{8,10},{9,11},{10,... | collective-permute-start | bytes 393224 | tf_op jit(solution)/shard_map/ppermute | solution.py:45
  27.3 4.4 %collective-permute-start.9 = (bf16[512,128]{1,0:T(8,128)(2,1)S(1)}, bf16[512,128]{1,0:T(8,128)(2,1)S(1)}, u32[]{:S(2)}, u32[]{:S(2)}) collective-permute-start(bf16[512,128]{1,0:T(8,128)(2,1)S(1)} %px.5.refs_0_), channel_id=1, source_target_pairs={{0,1},{1,0},{2,3},{3,2},{4,5},{5,4},{6,7},{7,6},{8,9},{9,8},{10,11... | collective-permute-start | bytes 393224 | tf_op jit(solution)/shard_map/ppermute | solution.py:45
  31.7 1.3 %collective-permute-start.10 = (bf16[512,128]{1,0:T(8,128)(2,1)S(1)}, bf16[512,128]{1,0:T(8,128)(2,1)S(1)}, u32[]{:S(2)}, u32[]{:S(2)}) collective-permute-start(bf16[512,128]{1,0:T(8,128)(2,1)S(1)} %collective-permute-done.8.refs_1_), channel_id=1, source_target_pairs={{0,1},{1,0},{2,3},{3,2},{4,5},{5,4},{6,7},{7,6},{8,9},{9,8},{10,11... | collective-permute-start | bytes 393224 | tf_op jit(solution)/shard_map/ppermute | solution.py:45
  34.0 6.0 %collective-permute-start.11 = (bf16[32,512]{1,0:T(8,128)(2,1)S(1)}, bf16[32,512]{1,0:T(8,128)(2,1)S(1)}, u32[]{:S(2)}, u32[]{:S(2)}) collective-permute-start(bf16[32,512]{1,0:T(8,128)(2,1)S(1)} %get-tuple-element.20), channel_id=1, source_target_pairs={{0,4},{1,5},{2,6},{3,7},{4,8},{5,9},{6,10},{7,11},{8,12},{9,13},{1... | collective-permute-start | bytes 98312 | tf_op jit(solution)/shard_map/ppermute | solution.py:45
  36.1 5.2 %collective-permute-start.12 = (bf16[32,512]{1,0:T(8,128)(2,1)S(1)}, bf16[32,512]{1,0:T(8,128)(2,1)S(1)}, u32[]{:S(2)}, u32[]{:S(2)}) collective-permute-start(bf16[32,512]{1,0:T(8,128)(2,1)S(1)} %get-tuple-element.21), channel_id=1, source_target_pairs={{0,8},{1,9},{2,10},{3,11},{4,12},{5,13},{6,14},{7,15},{8,0},{9,1},... | collective-permute-start | bytes 98312 | tf_op jit(solution)/shard_map/ppermute | solution.py:45
  36.5 4.7 %collective-permute-start.13 = (bf16[32,512]{1,0:T(8,128)(2,1)S(1)}, bf16[32,512]{1,0:T(8,128)(2,1)S(1)}, u32[]{:S(2)}, u32[]{:S(2)}) collective-permute-start(bf16[32,512]{1,0:T(8,128)(2,1)S(1)} %get-tuple-element.22), channel_id=1, source_target_pairs={{0,12},{1,13},{2,14},{3,15},{4,0},{5,1},{6,2},{7,3},{8,4},{9,5},{1... | collective-permute-start | bytes 98312 | tf_op jit(solution)/shard_map/ppermute | solution.py:45
  41.3 5.5 %collective-permute-start.16 = (bf16[32,512]{1,0:T(8,128)(2,1)S(1)}, bf16[32,512]{1,0:T(8,128)(2,1)S(1)}, u32[]{:S(2)}, u32[]{:S(2)}) collective-permute-start(bf16[32,512]{1,0:T(8,128)(2,1)S(1)} %total.1.mine.refs_0_), channel_id=1, source_target_pairs={{0,2},{1,3},{2,0},{3,1},{4,6},{5,7},{6,4},{7,5},{8,10},{9,11},{10,... | collective-permute-start | bytes 98312 | tf_op jit(solution)/shard_map/ppermute | solution.py:45
  42.6 5.2 %collective-permute-start.15 = (bf16[32,512]{1,0:T(8,128)(2,1)S(1)}, bf16[32,512]{1,0:T(8,128)(2,1)S(1)}, u32[]{:S(2)}, u32[]{:S(2)}) collective-permute-start(bf16[32,512]{1,0:T(8,128)(2,1)S(1)} %total.1.mine.refs_0_), channel_id=1, source_target_pairs={{0,12},{1,13},{2,14},{3,15},{4,0},{5,1},{6,2},{7,3},{8,4},{9,5},{1... | collective-permute-start | bytes 98312 | tf_op jit(solution)/shard_map/ppermute | solution.py:45
  46.2 5.7 %collective-permute-start.14 = (bf16[32,512]{1,0:T(8,128)(2,1)S(1)}, bf16[32,512]{1,0:T(8,128)(2,1)S(1)}, u32[]{:S(2)}, u32[]{:S(2)}) collective-permute-start(bf16[32,512]{1,0:T(8,128)(2,1)S(1)} %total.1.mine.refs_0_), channel_id=1, source_target_pairs={{0,4},{1,5},{2,6},{3,7},{4,8},{5,9},{6,10},{7,11},{8,12},{9,13},{1... | collective-permute-start | bytes 98312 | tf_op jit(solution)/shard_map/ppermute | solution.py:45
  46.2 6.0 %collective-permute-start.17 = (bf16[32,512]{1,0:T(8,128)(2,1)S(1)}, bf16[32,512]{1,0:T(8,128)(2,1)S(1)}, u32[]{:S(2)}, u32[]{:S(2)}) collective-permute-start(bf16[32,512]{1,0:T(8,128)(2,1)S(1)} %total.1.mine.refs_0_), channel_id=1, source_target_pairs={{0,8},{1,9},{2,10},{3,11},{4,12},{5,13},{6,14},{7,15},{8,0},{9,1},... | collective-permute-start | bytes 98312 | tf_op jit(solution)/shard_map/ppermute | solution.py:45
  51.9 4.7 %collective-permute-start.18 = (bf16[64,512]{1,0:T(8,128)(2,1)S(1)}, bf16[64,512]{1,0:T(8,128)(2,1)S(1)}, u32[]{:S(2)}, u32[]{:S(2)}) collective-permute-start(bf16[64,512]{1,0:T(8,128)(2,1)S(1)} %stack.6.refs_1_), channel_id=1, source_target_pairs={{0,2},{1,3},{2,0},{3,1},{4,6},{5,7},{6,4},{7,5},{8,10},{9,11},{10,... | collective-permute-start | bytes 196616 | tf_op jit(solution)/shard_map/ppermute | solution.py:45
  52.2 4.4 %collective-permute-start.19 = (bf16[32,512]{1,0:T(8,128)(2,1)S(1)}, bf16[32,512]{1,0:T(8,128)(2,1)S(1)}, u32[]{:S(2)}, u32[]{:S(2)}) collective-permute-start(bf16[32,512]{1,0:T(8,128)(2,1)S(1)} %collective-permute-done.17.refs_2_), channel_id=1, source_target_pairs={{0,2},{1,3},{2,0},{3,1},{4,6},{5,7},{6,4},{7,5},{8,10},{9,11},{10,... | collective-permute-start | bytes 98312 | tf_op jit(solution)/shard_map/ppermute | solution.py:45
  56.7 3.3 %collective-permute-start.20 = (bf16[256,512]{1,0:T(8,128)(2,1)S(1)}, bf16[256,512]{1,0:T(8,128)(2,1)S(1)}, u32[]{:S(2)}, u32[]{:S(2)}) collective-permute-start(bf16[256,512]{1,0:T(8,128)(2,1)S(1)} %stack.7.refs_1_), channel_id=1, source_target_pairs={{0,1},{1,0},{2,3},{3,2},{4,5},{5,4},{6,7},{7,6},{8,9},{9,8},{10,11... | collective-permute-start | bytes 786440 | tf_op jit(solution)/shard_map/ppermute | solution.py:45

commit v7 on v5

--- a/solution.py
+++ b/solution.py
@@ -54,10 +54,21 @@
     return [(z * band, (z * line + spot) * band, band) for z in range(deep)]
 
 
-def load_kernel(acts, cots, proj_in, proj_out, held, own, pg_t, cots_held, weights, sems):
+def load_kernel(devices, staged, acts, cots, proj_in, proj_out, *refs):
+    own, pg_t, cots_held, weights, sems = refs[-5:]
     layers = cots.shape[0]
     width_k = proj_out.shape[1] // layers
-    pairs = [(proj_out, weights), (cots, cots_held), (proj_in, own), (acts, held)]
+    pairs = [(proj_out, weights), (cots, cots_held), (proj_in, own)]
+    if staged:
+        tall = proj_in.shape[0]
+        me = lax.axis_index("seq")
+        slots = [(held, b) for held in refs[1:-5] for b in range(held.shape[0])]
+        slots = [*zip(slots, staged, [1] * len(staged)), *zip([(refs[0], b) for b in range(len(staged))], staged, [0] * len(staged))]
+        for (held, b), shift, core in slots:
+            at = pl.ds(pl.multiple_of(owner(me, devices, (*shift[:2], core)) * tall, tall), tall)
+            pairs.append((acts.at[:, :, at], held.at[b]))
+    else:
+        pairs.append((acts, refs[0]))
     copies = [pltpu.make_async_copy(a, b, sems.at[i]) for i, (a, b) in enumerate(pairs)]
     for copy in copies:
         copy.start()
@@ -66,8 +77,8 @@
     for l in range(layers):
         pg = jnp.dot(cots_held[l], weights[...], preferred_element_type=jnp.float32)
         pg_t[l * width_k:(l + 1) * width_k, :] = pg.T[l * width_k:(l + 1) * width_k, :].astype(jnp.bfloat16)
-    copies[2].wait()
-    copies[3].wait()
+    for copy in copies[2:]:
+        copy.wait()
 
 
 def stack_kernel(count, *refs):
@@ -78,43 +89,70 @@
         at += ref.shape[0]
 
 
-def px_kernel(devices, keys, begin, end, keep, acts, *refs):
+def joined(total):
+    width_k = total[0].shape[1] // len(total)
+    return jnp.concatenate([value[:, l * width_k:(l + 1) * width_k] for l, value in enumerate(total)], axis=1)
+
+
+def px_kernel(devices, first, keys, begin, cuts, held, *refs):
     count = len(keys)
-    arrays, refs = refs[:count], refs[count:]
-    layers, rows, _ = acts.shape
-    wide = arrays[0].shape[1]
+    given, refs = refs[:cuts], refs[cuts:]
+    arrays, out = refs[:count], refs[-1]
+    _, layers, rows, _ = held.shape
+    wide = out.shape[1]
+    kept = [(held, first + i) for i in range(sum(map(len, keys)))]
+    for half, acts in enumerate((kept, [(array, i) for array in given for i in range(array.shape[0])])):
+        spots = iter(acts)
+        total = [jnp.zeros((rows, wide), jnp.float32) for _ in range(layers)]
+        for array, shifts in zip(arrays, keys):
+            tall = array.shape[0] // len(shifts)
+            for i in range(len(shifts)):
+                from_, at = next(spots)
+                block = array[i * tall:(i + 1) * tall, :]
+                for l in range(layers):
+                    total[l] = total[l] + jnp.dot(from_[at, l], block, preferred_element_type=jnp.float32)
+        value = joined(total)
+        where = slice(half * rows, (half + 1) * rows)
+        out[where, :] = value if begin else refs[count][where, :] + value
+
+
+def pack_kernel(mine, theirs, pg, px, feat):
+    rows = mine.shape[0] // 2
+    for half in range(2):
+        here, there = slice(half * rows, (half + 1) * rows), slice((1 - half) * rows, (2 - half) * rows)
+        value = (mine[here, :] + theirs[there, :]).astype(jnp.bfloat16)
+        px[here, :] = value
+        feat[here, :] = value
+    feat[2 * rows:, :] = pg[...]
+
+
+def pg_kernel(devices, layers, planes, shifts, *refs):
+    count = len(refs) - 1 - len(shifts)
+    pgs, outs, spread = refs[:count], refs[count:-1], refs[-1]
+    wide, rows = pgs[0].shape
+    _, across, cores = levels(devices)
+    line = across * cores
+    width_k = wide // layers
+    size = width_k // (planes * line)
+    for i, pg in enumerate(pgs):
+        spread[:, i * rows:(i + 1) * rows] = pg[...].astype(jnp.float32)
     me = lax.axis_index("seq")
-    if keep:
-        stack_kernel(count, *arrays, refs[-1])
-        refs = refs[:-1]
-    total = [jnp.zeros((rows, wide), jnp.float32) if begin else refs[0][l] for l in range(layers)]
-    for array, shifts in zip(arrays, keys):
-        tall = array.shape[0] // len(shifts)
-        for i, shift in enumerate(shifts):
-            at = pl.ds(pl.multiple_of(owner(me, devices, shift) * tall, tall), tall)
-            block = array[i * tall:(i + 1) * tall, :]
-            for l in range(layers):
-                total[l] = total[l] + jnp.dot(acts[l, :, at], block, preferred_element_type=jnp.float32)
-    if end:
-        pack(total, refs[-2], refs[-1])
-    else:
-        for l in range(layers):
-            refs[-1][l] = total[l]
-
-
-def pack(total, pg_t, out):
-    layers = len(total)
-    rows, wide = total[0].shape
-    width_k = wide // layers
-    for l in range(layers):
-        at = slice(l * width_k, (l + 1) * width_k)
-        out[:rows, at] = total[l][:, at].astype(jnp.bfloat16)
-    for i in range(rows // wide):
-        out[rows + i * wide:rows + (i + 1) * wide, :] = pg_t[:, i * wide:(i + 1) * wide]
+    for shift, out in zip(shifts, outs):
+        spot = owner(me, devices, shift) % line
+        picked = [
+            spread[pl.ds(l * width_k + (z * line + spot) * size + i, 1), :]
+            for l in range(layers)
+            for z in range(planes)
+            for i in range(size)
+        ]
+        picked = jnp.concatenate(picked, axis=0).astype(jnp.bfloat16)
+        tall, lanes = picked.shape[0], out.shape[1]
+        for i in range(picked.shape[1] // lanes):
+            out[i * tall:(i + 1) * tall, :] = picked[:, i * lanes:(i + 1) * lanes]
 
 
 def whole_kernel(devices, acts, *refs):
-    blocks, (pg_t, out, weights) = refs[:-3], refs[-3:]
+    blocks, (out, weights) = refs[:-2], refs[-2:]
     deep, wide, cores = levels(devices)
     me = lax.axis_index("seq")
     tall = blocks[0].shape[0] // deep
@@ -122,16 +160,14 @@
         for z in range(deep):
             at = owner(me, devices, (0, i // cores, i % cores)) % (wide * cores) + z * wide * cores
             weights[pl.ds(pl.multiple_of(at * tall, tall), tall), :] = block[z * tall:(z + 1) * tall, :]
-    pack([jnp.dot(acts[l], weights[...], preferred_element_type=jnp.float32) for l in range(acts.shape[0])], pg_t, out)
-
-
-def grads_kernel(devices, per_part, layers, rows, shifts, *refs):
-    count = len(shifts)
-    feats, (lengths, out, spread) = refs[:count], refs[count:]
+    total = [jnp.dot(acts[l], weights[...], preferred_element_type=jnp.float32) for l in range(acts.shape[0])]
+    out[...] = joined(total).astype(jnp.bfloat16)
+
+
+def grads_kernel(devices, per_part, layers, rows, planes, shifts, packed, *refs):
+    feats, (pg, lengths, out, spread) = refs[:-4], refs[-4:]
     wide = feats[0].shape[1]
-    runs = rows // wide
     width_k = wide // layers
-    square = width_k * width_k
     _, across, cores = levels(devices)
     me = lax.axis_index("seq")
     sizes = lengths[pl.ds(me // per_part, 1), :]
@@ -144,34 +180,35 @@
     member = []
     for shift in shifts:
         first = (owner(me, devices, shift) % per_part) * rows
-        position = first + lax.broadcasted_iota(jnp.int32, (per_row, wide), 1)
-        for i in range(runs):
-            now = position + i * wide
-            member.append(((now >= starts) & (now < ends)).astype(jnp.float32))
+        position = first + lax.broadcasted_iota(jnp.int32, (per_row, rows), 1)
+        member.append(((position >= starts) & (position < ends)).astype(jnp.float32))
     member = jnp.concatenate(member, axis=1)
-    for f, feat in enumerate(feats):
-        for i in range(runs):
-            at = (f * runs + i) * wide
-            spread[:, at:at + wide] = feat[rows + i * wide:rows + (i + 1) * wide, :].astype(jnp.float32)
+    tall, near = pg.shape
+    spread[:, :near] = pg[...].astype(jnp.float32)
+    if packed:
+        far = feats[1][2 * rows:, :].astype(jnp.float32)
+        for i in range(far.shape[0] // tall):
+            at = near + i * wide
+            spread[:, at:at + wide] = far[i * tall:(i + 1) * tall]
+        px = [feats[0][...], feats[1][:2 * rows, :]]
+    else:
+        px = [feat[...] for feat in feats]
+    px = jnp.concatenate(px, axis=0)
     low = lax.broadcasted_iota(jnp.int32, (per_row, 2 * width_k), 1) < width_k
-    lanes = square // (across * cores)
-    spot = me % (across * cores)
+    size = tall // layers
     for l in range(layers):
-        px = []
-        for feat in feats:
-            own = feat[:rows, l * width_k:(l + 1) * width_k]
-            px.append(jnp.concatenate([own, own], axis=1))
-        px = jnp.concatenate(px, axis=0)
-        for here, there, size in chunks(spot, devices, square):
-            terms = []
-            for i in range(size // width_k):
-                row = l * width_k + there // width_k + i
-                terms.append((member * spread[pl.ds(row, 1), :]).astype(jnp.bfloat16))
-            sums = jnp.dot(jnp.concatenate(terms, axis=0), px, preferred_element_type=jnp.float32)
-            for i in range(0, size // width_k, 2):
+        own = px[:, l * width_k:(l + 1) * width_k]
+        own = jnp.concatenate([own, own], axis=1)
+        for z in range(planes):
+            first = l * size + z * (size // planes)
+            terms = [
+                (member * spread[first + i:first + i + 1, :]).astype(jnp.bfloat16) for i in range(size // planes)
+            ]
+            sums = jnp.dot(jnp.concatenate(terms, axis=0), own, preferred_element_type=jnp.float32)
+            for i in range(0, size // planes, 2):
                 even = sums[i * per_row:(i + 1) * per_row]
                 odd = sums[(i + 1) * per_row:(i + 2) * per_row]
-                at = l * lanes + here + i * width_k
+                at = (first + i) * width_k
                 out[:, at:at + 2 * width_k] = jnp.where(low, even, odd).astype(jnp.bfloat16)
 
 
@@ -305,24 +342,43 @@
     params = pltpu.CompilerParams(vmem_limit_bytes=24 * MIB)
 
     light = pl.CostEstimate(flops=1, bytes_accessed=1, transcendentals=0)
-    held, own, pg_t = pl.pallas_call(
-        load_kernel,
-        out_shape=(
-            pltpu.VMEM(acts.shape, jnp.bfloat16),
-            pltpu.VMEM(proj_in.shape, jnp.bfloat16),
-            pltpu.VMEM((wide, rows), jnp.bfloat16),
-        ),
+    spins = sorted(range(1, deep), key=lambda z: min(z, deep - z))
+    staged = tall % 128 == 0 and band % 128 == 0 and deep > 2 and across == 2 and cores == 2
+    order = [(z, x, 0) for x in range(across) for z in (0, *spins)] if staged else []
+    cuts = 2
+    kept = [pltpu.VMEM(acts.shape, jnp.bfloat16)]
+    if staged:
+        kept = [pltpu.VMEM((count, layers, rows, tall), jnp.bfloat16) for count in (len(order), *[len(order) // cuts] * cuts)]
+    *held, own, pg_t = pl.pallas_call(
+        functools.partial(load_kernel, devices, order),
+        out_shape=(*kept, pltpu.VMEM(proj_in.shape, jnp.bfloat16), pltpu.VMEM((wide, rows), jnp.bfloat16)),
         in_specs=[HBM] * 4,
-        out_specs=(VMEM,) * 3,
+        out_specs=(VMEM,) * (2 + len(kept)),
         scratch_shapes=[
             pltpu.VMEM(cots.shape, jnp.bfloat16),
             pltpu.VMEM(proj_out.shape, jnp.bfloat16),
-            pltpu.SemaphoreType.DMA((4,)),
+            pltpu.SemaphoreType.DMA((3 + (devices if staged else 1),)),
         ],
         compiler_params=params,
         cost_estimate=light,
         name="load",
     )(*[pltpu.with_memory_space_constraint(a, pltpu.HBM) for a in (acts, cots, proj_in, proj_out)])
+
+    def call(kernel, name, types, arrays, after=(), scratch=()):
+        return pl.pallas_call(
+            kernel,
+            out_shape=types,
+            in_specs=[VMEM] * len(arrays) + [ANY] * len(after),
+            out_specs=[VMEM] * len(types),
+            scratch_shapes=list(scratch),
+            compiler_params=params,
+            cost_estimate=light,
+            name=name,
+        )(*arrays, *after)
+
+    def plane(block):
+        got = {(0, x, 0): send(block, devices, (0, x, 0)) if x else block for x in range(across)}
+        return {(*k[:2], c): send(v, devices, (0, 0, c)) if c else v for c in range(cores) for k, v in got.items()}
 
     def stack(arrays, after):
         return pl.pallas_call(
@@ -335,42 +391,49 @@
             name="stack",
         )(*arrays, *after)
 
-    def px(entries, before=None, end=False, keep=False):
-        more = (() if before is None else (before,)) + ((pg_t,) if end else ())
-        arrays, keys = zip(*entries)
-        count = sum(map(len, keys))
-        sums = feat_type if end else jax.ShapeDtypeStruct((layers, rows, wide), jnp.float32)
-        stacked = [jax.ShapeDtypeStruct((count * tall, wide), jnp.bfloat16)] if keep else []
-        result = pl.pallas_call(
-            functools.partial(px_kernel, devices, keys, before is None, end, keep),
-            out_shape=[sums] + stacked,
-            in_specs=[VMEM] * (1 + len(arrays) + len(more)),
-            out_specs=[VMEM] * (1 + len(stacked)),
-            compiler_params=params,
-            cost_estimate=light,
-            name="px",
-        )(held, *arrays, *more)
-        return result if keep else result[0]
-
-    feat_type = jax.ShapeDtypeStruct((2 * rows, wide), jnp.bfloat16)
-    if tall % 128 == 0 and deep > 2 and across == 2 and cores == 2:
-        spins = sorted(range(1, deep), key=lambda z: min(z, deep - z))
+    planes = deep if staged else 1
+    quarter = layers * width_k // line
+    if staged:
         near, far = spins[:-1], spins[-1]
+        given = [send(array, devices, (0, 0, 1)) for array in held[1:]]
         got = [send(proj_in, devices, (z, 0, 0)) for z in near]
         side = send(proj_in, devices, (0, 1, 0))
         got_far = send(proj_in, devices, (far, 0, 0))
         got = stack(got, (pg_t, side))
         side_near = send(got, devices, (0, 1, 0))
         side_far = send(got_far, devices, (0, 1, 0))
-        value, column = px(
-            [(own, [(0, 0, 0)]), (got, [(z, 0, 0) for z in near]), (got_far, [(far, 0, 0)])], keep=True
+        pg, pg_side = call(
+            functools.partial(pg_kernel, devices, layers, planes, ((0, 0, 0), (0, 1, 0))),
+            "pg",
+            [
+                jax.ShapeDtypeStruct((quarter, 2 * rows), jnp.bfloat16),
+                jax.ShapeDtypeStruct((quarter * 2 * rows // wide, wide), jnp.bfloat16),
+            ],
+            [pg_t, send(pg_t, devices, (0, 0, 1))],
+            scratch=[pltpu.VMEM((wide, 2 * rows), jnp.float32)],
         )
-        twin = send(column, devices, (0, 0, 1))
-        side = stack([side, side_near, side_far], (value,))
-        twin_side = send(side, devices, (0, 0, 1))
-        order = [0, *near, far]
-        value = px([(side, [(z, 1, 0) for z in order]), (twin, [(z, 0, 1) for z in order])], value)
-        value = px([(twin_side, [(z, 1, 1) for z in order])], value, end=True)
+        partial_type = jax.ShapeDtypeStruct((2 * rows, wide), jnp.float32)
+        value = None
+        for x, arrays in enumerate(([own, got, got_far], [side, side_near, side_far])):
+            keys = ([(0, x, 0)], [(z, x, 0) for z in near], [(far, x, 0)])
+            value = call(
+                functools.partial(px_kernel, devices, x * deep, keys, x == 0, cuts // 2),
+                "px",
+                [partial_type],
+                [held[0], *given[x * cuts // 2:(x + 1) * cuts // 2], *arrays] + ([] if x == 0 else [value]),
+                after=[pg_side] if x == 0 else (),
+            )[0]
+        px, feat = call(
+            pack_kernel,
+            "pack",
+            [
+                jax.ShapeDtypeStruct((2 * rows, wide), jnp.bfloat16),
+                jax.ShapeDtypeStruct((2 * rows + pg_side.shape[0], wide), jnp.bfloat16),
+            ],
+            [value, send(value, devices, (0, 0, 1)), pg_side],
+        )
+        feats = [px, send(feat, devices, (0, 1, 0))]
+        shifts = ((0, 0, 0), (0, 0, 1), (0, 1, 0), (0, 1, 1))
     else:
         groups = [[z * line + i for z in range(deep)] for i in range(line)]
         column = lax.all_to_all(jnp.tile(proj_in, (deep, 1)), "seq", 0, 0, axis_index_groups=groups, tiled=True)
@@ -378,29 +441,32 @@
         blocks = [block if c == 0 else send(block, devices, (0, 0, c)) for block in blocks for c in range(cores)]
         value = pl.pallas_call(
             functools.partial(whole_kernel, devices),
-            out_shape=feat_type,
-            in_specs=[VMEM] * (2 + len(blocks)),
+            out_shape=jax.ShapeDtypeStruct((rows, wide), jnp.bfloat16),
+            in_specs=[VMEM] * (1 + len(blocks)),
             out_specs=VMEM,
             scratch_shapes=[pltpu.VMEM((width, wide), jnp.bfloat16)],
             compiler_params=params,
             name="px",
-        )(held, *blocks, pg_t)
-
-    def plane(block):
-        held = {(0, x, 0): send(block, devices, (0, x, 0)) if x else block for x in range(across)}
-        return {(*k[:2], c): send(v, devices, (0, 0, c)) if c else v for c in range(cores) for k, v in held.items()}
-
-    feats = plane(value)
+        )(*held, *blocks)
+        feats = plane(value)
+        shifts = tuple(feats)
+        feats = list(feats.values())
+        pg = call(
+            functools.partial(pg_kernel, devices, layers, planes, ((0, 0, 0),)),
+            "pg",
+            [jax.ShapeDtypeStruct((quarter, line * rows), jnp.bfloat16)],
+            list(plane(pg_t).values()),
+            scratch=[pltpu.VMEM((wide, line * rows), jnp.float32)],
+        )[0]
+
     lanes = layers * square // line
-    sums = pl.pallas_call(
-        functools.partial(grads_kernel, devices, per_part, layers, rows, tuple(feats)),
-        out_shape=jax.ShapeDtypeStruct((per_row, lanes), jnp.bfloat16),
-        in_specs=[VMEM] * (len(feats) + 1),
-        out_specs=VMEM,
-        scratch_shapes=[pltpu.VMEM((wide, rows * line), jnp.float32)],
-        compiler_params=params,
-        name="grads",
-    )(*feats.values(), lengths)
+    sums = call(
+        functools.partial(grads_kernel, devices, per_part, layers, rows, planes, shifts, staged),
+        "grads",
+        [jax.ShapeDtypeStruct((per_row, lanes), jnp.bfloat16)],
+        [*feats, pg, lengths],
+        scratch=[pltpu.VMEM((quarter, rows * line), jnp.float32)],
+    )[0]
     terms = [send(sums, devices, (z, 0, 0)) if z else sums for z in range(deep)]
     total = pl.pallas_call(
         functools.partial(total_kernel, devices, per_part),
@@ -412,7 +478,7 @@
     )(*terms)
     logged_type = jax.ShapeDtypeStruct((CAP, layers * square), jnp.bfloat16)
     covariance_type = jax.ShapeDtypeStruct((npair, band, square), jnp.float32)
-    if band % 128 == 0 and across == 2 and cores == 2:
+    if staged:
         width = square // line
         shape = (npair, band, width)
         covariance = None

time: 62.5 us -> 65.8 us (1.053)
  starting transfers between devices: 16.6 us -> 20.3 us
    ppermute x16, starting transfers between devices: 16.6 us -> 20.3 us  [send(): return lax.ppermute(value, 'seq', perm)]
    pallas_call x5 -> x6, Pallas kernels: 7.51 us -> 7.62 us  [the longest x1 4.06 us: shards(): pl.pallas_call(functools.partial(load_kernel, devices, order), out_shape=...]
  transfers between devices with their start and end apart: 16 -> 16, of which waited for: 9 -> 10; matrix products, arithmetic and copies ran while one was open for 0% -> 0% of each run, Pallas kernels for 19% -> 11%
where the time goes in v7:
time: 65.8 us; the launch traced here: 65.7 us
  waiting for transfers between devices  26.5 us (40%)
  starting transfers between devices  20.3 us (31%)
  Pallas kernels  18 us (27%)
  between operations  0.79 us (1%)
    ppermute x16, waiting for transfers between devices, send(): return lax.ppermute(value, 'seq', perm)  26.5 us
    ppermute x16, starting transfers between devices, send(): return lax.ppermute(value, 'seq', perm)  20.3 us
    pallas_call x3, Pallas kernels, shards(): pl.pallas_call(functools.partial(part_kernel, devices, shifts, more), out...  10.3 us
    pallas_call x1, Pallas kernels, shards(): pl.pallas_call(functools.partial(load_kernel, devices, order), out_shape=...  4.06 us
    pallas_call x5, Pallas kernels, call(): pl.pallas_call(kernel, out_shape=types, in_specs=[VMEM] * len(arrays) + [...  3.56 us
  transfers between devices with their start and end apart: 16, of which 10 were waited for; matrix products, arithmetic and copies ran while one was open for 0% of the time, Pallas kernels for 11%

profile of v7, /device:TPU:0, one launch (start us, length us, event | category | flops | bytes accessed | tf_op | source)
XLA Modules:
  0.0 65.7 jit_solution(16959225588596305446)
XLA Ops:
  0.6 4.1 %load.1 = (bf16[8,2,256,512]{3,2,1,0:T(8,128)(2,1)S(1)}, bf16[4,2,256,512]{3,2,1,0:T(8,128)(2,1)S(1)}, bf16[4,2,256,512]{3,2,1,0:T(8,128)(2,1)S(1)}, bf16[512,128]{1,0:T(8,128)(2,1)S(1)}, bf16[128,256]{1,0:T(8,128)(2,1)S(1)}) custom-call(bf16[2,256,8192]{2,1,0:T(8,128)(2,1)} %acts.1, bf16[2,256,1024]{2,1,0:T(8,128)(2,1)} %cots.1, bf16[512,128]{1,0:T(8,128)(2,1)} %proj_in.1, ...), custom_call_target="tpu_custom_call" | custom-call | flops 1 | bytes 1 | tf_op jit(solution)/shard_map/load/pallas_call | solution.py:352
  4.7 0.5 collective-permute-start.7
  5.2 0.1 collective-permute-start
  5.3 3.0 %collective-permute-start.2 = (bf16[512,128]{1,0:T(8,128)(2,1)S(1)}, bf16[512,128]{1,0:T(8,128)(2,1)S(1)}, u32[]{:S(2)}, u32[]{:S(2)}) collective-permute-start(bf16[512,128]{1,0:T(8,128)(2,1)S(1)} %copy-done.2), channel_id=1, source_target_pairs={{0,4},{1,5},{2,6},{3,7},{4,8},{5,9},{6,10},{7,11},{8,12},{9,13},{1... | collective-permute-start | bytes 393224 | tf_op jit(solution)/shard_map/ppermute | solution.py:45
  8.3 1.5 %collective-permute-start.1 = (bf16[512,128]{1,0:T(8,128)(2,1)S(1)}, bf16[512,128]{1,0:T(8,128)(2,1)S(1)}, u32[]{:S(2)}, u32[]{:S(2)}) collective-permute-start(bf16[512,128]{1,0:T(8,128)(2,1)S(1)} %copy-done.2), channel_id=1, source_target_pairs={{0,2},{1,3},{2,0},{3,1},{4,6},{5,7},{6,4},{7,5},{8,10},{9,11},{10,... | collective-permute-start | bytes 393224 | tf_op jit(solution)/shard_map/ppermute | solution.py:45
  9.8 2.2 %collective-permute-start.3 = (bf16[512,128]{1,0:T(8,128)(2,1)S(1)}, bf16[512,128]{1,0:T(8,128)(2,1)S(1)}, u32[]{:S(2)}, u32[]{:S(2)}) collective-permute-start(bf16[512,128]{1,0:T(8,128)(2,1)S(1)} %copy-done.2), channel_id=1, source_target_pairs={{0,12},{1,13},{2,14},{3,15},{4,0},{5,1},{6,2},{7,3},{8,4},{9,5},{1... | collective-permute-start | bytes 393224 | tf_op jit(solution)/shard_map/ppermute | solution.py:45
  12.1 2.2 %collective-permute-done.2.refs_0_ = bf16[512,128]{1,0:T(8,128)(2,1)S(1)} collective-permute-done((bf16[512,128]{1,0:T(8,128)(2,1)S(1)}, bf16[512,128]{1,0:T(8,128)(2,1)S(1)}, u32[]{:S(2)}, u32[]{:S(2)}) %collective-permute-start.2) | collective-permute-done | bytes 131104 | tf_op jit(solution)/shard_map/ppermute | solution.py:45
  14.2 0.6 collective-permute-start.5
  14.8 2.1 %collective-permute-done.3.refs_1_ = bf16[512,128]{1,0:T(8,128)(2,1)S(1)} collective-permute-done((bf16[512,128]{1,0:T(8,128)(2,1)S(1)}, bf16[512,128]{1,0:T(8,128)(2,1)S(1)}, u32[]{:S(2)}, u32[]{:S(2)}) %collective-permute-start.3) | collective-permute-done | bytes 131104 | tf_op jit(solution)/shard_map/ppermute | solution.py:45
  16.9 3.7 %collective-permute-start.4 = (bf16[1024,128]{1,0:T(8,128)(2,1)S(1)}, bf16[1024,128]{1,0:T(8,128)(2,1)S(1)}, u32[]{:S(2)}, u32[]{:S(2)}) collective-permute-start(bf16[1024,128]{1,0:T(8,128)(2,1)S(1)} %stack.2.refs_2_), channel_id=1, source_target_pairs={{0,2},{1,3},{2,0},{3,1},{4,6},{5,7},{6,4},{7,5},{8,10},{9,11},{10,... | collective-permute-start | bytes 786440 | tf_op jit(solution)/shard_map/ppermute | solution.py:45
  20.6 1.9 %collective-permute-done.5.refs_3_ = bf16[512,128]{1,0:T(8,128)(2,1)S(1)} collective-permute-done((bf16[512,128]{1,0:T(8,128)(2,1)S(1)}, bf16[512,128]{1,0:T(8,128)(2,1)S(1)}, u32[]{:S(2)}, u32[]{:S(2)}) %collective-permute-start.5) | collective-permute-done | bytes 131104 | tf_op jit(solution)/shard_map/ppermute | solution.py:45
  22.5 2.0 %collective-permute-start.6 = (bf16[512,128]{1,0:T(8,128)(2,1)S(1)}, bf16[512,128]{1,0:T(8,128)(2,1)S(1)}, u32[]{:S(2)}, u32[]{:S(2)}) collective-permute-start(bf16[512,128]{1,0:T(8,128)(2,1)S(1)} %collective-permute-done.5.refs_3_), channel_id=1, source_target_pairs={{0,2},{1,3},{2,0},{3,1},{4,6},{5,7},{6,4},{7,5},{8,10},{9,11},{10,... | collective-permute-start | bytes 393224 | tf_op jit(solution)/shard_map/ppermute | solution.py:45
  24.5 1.3 %collective-permute-done.8.refs_1_ = bf16[128,256]{1,0:T(8,128)(2,1)S(1)} collective-permute-done((bf16[128,256]{1,0:T(8,128)(2,1)S(1)}, bf16[128,256]{1,0:T(8,128)(2,1)S(1)}, u32[]{:S(2)}, u32[]{:S(2)}) %collective-permute-start.8) | collective-permute-done | bytes 65568 | tf_op jit(solution)/shard_map/ppermute | solution.py:45
  25.7 0.1 pg.1
  25.9 1.2 %px.2.refs_4_ = f32[512,128]{1,0:T(8,128)S(1)} custom-call(bf16[8,2,256,512]{3,2,1,0:T(8,128)(2,1)S(1)} %get-tuple-element.14.held, bf16[4,2,256,512]{3,2,1,0:T(8,128)(2,1)S(1)} %collective-permute-done.7.refs_0_, bf16[512,128]{1,0:T(8,128)(2,1)S(1)} %get-tuple-element.18.refs_1_, bf16[1024,128]{1,0:T(8,128)(2,1)S(1)} %stack.2.refs_2_, ...), custom_call_target="tpu_custom_call" | custom-call | flops 1 | bytes 1 | tf_op jit(solution)/shard_map/px/pallas_call | solution.py:368
  27.2 0.9 %collective-permute-done.6.refs_3_ = bf16[512,128]{1,0:T(8,128)(2,1)S(1)} collective-permute-done((bf16[512,128]{1,0:T(8,128)(2,1)S(1)}, bf16[512,128]{1,0:T(8,128)(2,1)S(1)}, u32[]{:S(2)}, u32[]{:S(2)}) %collective-permute-start.6) | collective-permute-done | bytes 131104 | tf_op jit(solution)/shard_map/ppermute | solution.py:45
  28.0 1.2 %px.3.mine = f32[512,128]{1,0:T(8,128)S(1)} custom-call(bf16[8,2,256,512]{3,2,1,0:T(8,128)(2,1)S(1)} %get-tuple-element.14.held, bf16[4,2,256,512]{3,2,1,0:T(8,128)(2,1)S(1)} %collective-permute-done.refs_0_, bf16[512,128]{1,0:T(8,128)(2,1)S(1)} %collective-permute-done.1.refs_3_.refs_1_, bf16[1024,128]{1,0:T(8,128)(2,1)S(1)} %collective-permute-done.4.refs_2_, ...), custom_call_target="tpu_custom_call" | custom-call | flops 1 | bytes 1 | tf_op jit(solution)/shard_map/px/pallas_call | solution.py:368
  29.3 1.5 %collective-permute-done.9.theirs = f32[512,128]{1,0:T(8,128)S(1)} collective-permute-done((f32[512,128]{1,0:T(8,128)S(1)}, f32[512,128]{1,0:T(8,128)S(1)}, u32[]{:S(2)}, u32[]{:S(2)}) %collective-permute-start.9) | collective-permute-done | bytes 262176 | tf_op jit(solution)/shard_map/ppermute | solution.py:45
  30.9 1.8 %collective-permute-start.10 = (bf16[640,128]{1,0:T(8,128)(2,1)S(1)}, bf16[640,128]{1,0:T(8,128)(2,1)S(1)}, u32[]{:S(2)}, u32[]{:S(2)}) collective-permute-start(bf16[640,128]{1,0:T(8,128)(2,1)S(1)} %get-tuple-element.21), channel_id=1, source_target_pairs={{0,2},{1,3},{2,0},{3,1},{4,6},{5,7},{6,4},{7,5},{8,10},{9,11},{10,... | collective-permute-start | bytes 491528 | tf_op jit(solution)/shard_map/ppermute | solution.py:45
  32.7 4.5 %collective-permute-done.10.refs_1_ = bf16[640,128]{1,0:T(8,128)(2,1)S(1)} collective-permute-done((bf16[640,128]{1,0:T(8,128)(2,1)S(1)}, bf16[640,128]{1,0:T(8,128)(2,1)S(1)}, u32[]{:S(2)}, u32[]{:S(2)}) %collective-permute-start.10) | collective-permute-done | bytes 163872 | tf_op jit(solution)/shard_map/ppermute | solution.py:45
  37.2 0.9 %grads.1.refs_0_ = bf16[32,2048]{1,0:T(8,128)(2,1)S(1)} custom-call(bf16[512,128]{1,0:T(8,128)(2,1)S(1)} %get-tuple-element.20.refs_0_, bf16[640,128]{1,0:T(8,128)(2,1)S(1)} %collective-permute-done.10.refs_1_, bf16[32,512]{1,0:T(8,128)(2,1)S(1)} %get-tuple-element.22.refs_2_, s32[1,32]{1,0:T(1,128)S(1)} %copy-done.1), custom_call_target="tpu_custom_call" | custom-call | flops 1 | bytes 1 | tf_op jit(solution)/shard_map/grads/pallas_call | solution.py:368
  38.2 2.6 %collective-permute-start.13 = (bf16[32,2048]{1,0:T(8,128)(2,1)S(1)}, bf16[32,2048]{1,0:T(8,128)(2,1)S(1)}, u32[]{:S(2)}, u32[]{:S(2)}) collective-permute-start(bf16[32,2048]{1,0:T(8,128)(2,1)S(1)} %grads.1.refs_0_), channel_id=1, source_target_pairs={{0,12},{1,13},{2,14},{3,15},{4,0},{5,1},{6,2},{7,3},{8,4},{9,5},{1... | collective-permute-start | bytes 393224 | tf_op jit(solution)/shard_map/ppermute | solution.py:45
  40.8 0.7 %collective-permute-start.12 = (bf16[32,2048]{1,0:T(8,128)(2,1)S(1)}, bf16[32,2048]{1,0:T(8,128)(2,1)S(1)}, u32[]{:S(2)}, u32[]{:S(2)}) collective-permute-start(bf16[32,2048]{1,0:T(8,128)(2,1)S(1)} %grads.1.refs_0_), channel_id=1, source_target_pairs={{0,8},{1,9},{2,10},{3,11},{4,12},{5,13},{6,14},{7,15},{8,0},{9,1},... | collective-permute-start | bytes 393224 | tf_op jit(solution)/shard_map/ppermute | solution.py:45
  41.5 0.4 collective-permute-start.11
  41.9 2.8 %collective-permute-done.13.refs_3_ = bf16[32,2048]{1,0:T(8,128)(2,1)S(1)} collective-permute-done((bf16[32,2048]{1,0:T(8,128)(2,1)S(1)}, bf16[32,2048]{1,0:T(8,128)(2,1)S(1)}, u32[]{:S(2)}, u32[]{:S(2)}) %collective-permute-start.13) | collective-permute-done | bytes 131104 | tf_op jit(solution)/shard_map/ppermute | solution.py:45
  44.7 8.1 %collective-permute-done.12.refs_2_ = bf16[32,2048]{1,0:T(8,128)(2,1)S(1)} collective-permute-done((bf16[32,2048]{1,0:T(8,128)(2,1)S(1)}, bf16[32,2048]{1,0:T(8,128)(2,1)S(1)}, u32[]{:S(2)}, u32[]{:S(2)}) %collective-permute-start.12) | collective-permute-done | bytes 131104 | tf_op jit(solution)/shard_map/ppermute | solution.py:45
  52.9 1.0 %collective-permute-start.14 = (bf16[32,2048]{1,0:T(8,128)(2,1)S(1)}, bf16[32,2048]{1,0:T(8,128)(2,1)S(1)}, u32[]{:S(2)}, u32[]{:S(2)}) collective-permute-start(bf16[32,2048]{1,0:T(8,128)(2,1)S(1)} %total.1.mine.refs_0_), channel_id=1, source_target_pairs={{0,2},{1,3},{2,0},{3,1},{4,6},{5,7},{6,4},{7,5},{8,10},{9,11},{10,... | collective-permute-start | bytes 393224 | tf_op jit(solution)/shard_map/ppermute | solution.py:45
  53.9 0.1 copy.11.refs_1_.refs_3_
  54.0 2.7 %covariance.3 = (f32[8,128]{1,0:T(8,128)S(1)}, f32[3,256,4096]{2,1,0:T(8,128)}) custom-call(bf16[32,2048]{1,0:T(8,128)(2,1)S(1)} %total.1.mine.refs_0_, bf16[32,2048]{1,0:T(8,128)(2,1)S(1)} %total.1.mine.refs_0_, s32[3,2]{1,0:T(4,128)S(1)} %copy.11.refs_1_.refs_3_), custom_call_target="tpu_custom_call" | custom-call | flops 50331648 | bytes 3145728 | tf_op jit(solution)/shard_map/covariance/pallas_call | solution.py:502
  56.6 1.3 %collective-permute-done.14.refs_1_.refs_0_ = bf16[32,2048]{1,0:T(8,128)(2,1)S(1)} collective-permute-done((bf16[32,2048]{1,0:T(8,128)(2,1)S(1)}, bf16[32,2048]{1,0:T(8,128)(2,1)S(1)}, u32[]{:S(2)}, u32[]{:S(2)}) %collective-permute-start.14) | collective-permute-done | bytes 131104 | tf_op jit(solution)/shard_map/ppermute | solution.py:45
  58.0 3.3 %covariance.4 = (f32[8,128]{1,0:T(8,128)}, f32[3,256,4096]{2,1,0:T(8,128)}) custom-call(bf16[32,2048]{1,0:T(8,128)(2,1)S(1)} %total.1.mine.refs_0_, bf16[32,2048]{1,0:T(8,128)(2,1)S(1)} %collective-permute-done.14.refs_1_.refs_0_, s32[3,2]{1,0:T(4,128)S(1)} %copy.11.refs_1_.refs_3_, ...), custom_call_target="tpu_custom_call", output_to_operand_aliasing={{1}: (3, {})} | custom-call | flops 50331648 | bytes 3145728 | tf_op jit(solution)/shard_map/covariance/pallas_call | solution.py:502
  61.3 4.4 %covariance.5 = (bf16[2,8192]{1,0:T(2,128)(2,1)}, f32[3,256,4096]{2,1,0:T(8,128)}) custom-call(bf16[32,2048]{1,0:T(8,128)(2,1)S(1)} %total.1.mine.refs_0_, bf16[64,2048]{1,0:T(8,128)(2,1)S(1)} %collective-permute-done.15.refs_0_, bf16[32,2048]{1,0:T(8,128)(2,1)S(1)} %collective-permute-done.14.refs_1_.refs_0_, ...), custom_call_target="tpu_custom_call", output_to_operand_aliasing={{1}: (5, {})} | custom-call | flops 100663296 | bytes 6291456 | tf_op jit(solution)/shard_map/covariance/pallas_call | solution.py:502
  (21 shorter events, 0.3 us)
Async XLA Ops:
  0.6 4.7 %copy-start.2 = (bf16[512,128]{1,0:T(8,128)(2,1)S(1)}, bf16[512,128]{1,0:T(8,128)(2,1)}, u32[]{:S(2)}) copy-start(bf16[512,128]{1,0:T(8,128)(2,1)} %proj_in.1) | copy-start | bytes 393220
  4.7 21.2 %collective-permute-start.7 = (bf16[4,2,256,512]{3,2,1,0:T(8,128)(2,1)S(1)}, bf16[4,2,256,512]{3,2,1,0:T(8,128)(2,1)S(1)}, u32[]{:S(2)}, u32[]{:S(2)}) collective-permute-start(bf16[4,2,256,512]{3,2,1,0:T(8,128)(2,1)S(1)} %get-tuple-element.17), channel_id=1, source_target_pairs={{0,1},{1,0},{2,3},{3,2},{4,5},{5,4},{6,7},{7,6},{8,9},{9,8},{10,11... | collective-permute-start | bytes 6291464 | tf_op jit(solution)/shard_map/ppermute | solution.py:45
  5.2 22.8 %collective-permute-start = (bf16[4,2,256,512]{3,2,1,0:T(8,128)(2,1)S(1)}, bf16[4,2,256,512]{3,2,1,0:T(8,128)(2,1)S(1)}, u32[]{:S(2)}, u32[]{:S(2)}) collective-permute-start(bf16[4,2,256,512]{3,2,1,0:T(8,128)(2,1)S(1)} %get-tuple-element.15), channel_id=1, source_target_pairs={{0,1},{1,0},{2,3},{3,2},{4,5},{5,4},{6,7},{7,6},{8,9},{9,8},{10,11... | collective-permute-start | bytes 6291464 | tf_op jit(solution)/shard_map/ppermute | solution.py:45
  5.3 8.9 %collective-permute-start.2 = (bf16[512,128]{1,0:T(8,128)(2,1)S(1)}, bf16[512,128]{1,0:T(8,128)(2,1)S(1)}, u32[]{:S(2)}, u32[]{:S(2)}) collective-permute-start(bf16[512,128]{1,0:T(8,128)(2,1)S(1)} %copy-done.2), channel_id=1, source_target_pairs={{0,4},{1,5},{2,6},{3,7},{4,8},{5,9},{6,10},{7,11},{8,12},{9,13},{1... | collective-permute-start | bytes 393224 | tf_op jit(solution)/shard_map/ppermute | solution.py:45
  8.3 6.5 %collective-permute-start.1 = (bf16[512,128]{1,0:T(8,128)(2,1)S(1)}, bf16[512,128]{1,0:T(8,128)(2,1)S(1)}, u32[]{:S(2)}, u32[]{:S(2)}) collective-permute-start(bf16[512,128]{1,0:T(8,128)(2,1)S(1)} %copy-done.2), channel_id=1, source_target_pairs={{0,2},{1,3},{2,0},{3,1},{4,6},{5,7},{6,4},{7,5},{8,10},{9,11},{10,... | collective-permute-start | bytes 393224 | tf_op jit(solution)/shard_map/ppermute | solution.py:45
  9.8 7.1 %collective-permute-start.3 = (bf16[512,128]{1,0:T(8,128)(2,1)S(1)}, bf16[512,128]{1,0:T(8,128)(2,1)S(1)}, u32[]{:S(2)}, u32[]{:S(2)}) collective-permute-start(bf16[512,128]{1,0:T(8,128)(2,1)S(1)} %copy-done.2), channel_id=1, source_target_pairs={{0,12},{1,13},{2,14},{3,15},{4,0},{5,1},{6,2},{7,3},{8,4},{9,5},{1... | collective-permute-start | bytes 393224 | tf_op jit(solution)/shard_map/ppermute | solution.py:45
  14.2 8.3 %collective-permute-start.5 = (bf16[512,128]{1,0:T(8,128)(2,1)S(1)}, bf16[512,128]{1,0:T(8,128)(2,1)S(1)}, u32[]{:S(2)}, u32[]{:S(2)}) collective-permute-start(bf16[512,128]{1,0:T(8,128)(2,1)S(1)} %copy-done.2), channel_id=1, source_target_pairs={{0,8},{1,9},{2,10},{3,11},{4,12},{5,13},{6,14},{7,15},{8,0},{9,1},... | collective-permute-start | bytes 393224 | tf_op jit(solution)/shard_map/ppermute | solution.py:45
  16.9 11.1 %collective-permute-start.4 = (bf16[1024,128]{1,0:T(8,128)(2,1)S(1)}, bf16[1024,128]{1,0:T(8,128)(2,1)S(1)}, u32[]{:S(2)}, u32[]{:S(2)}) collective-permute-start(bf16[1024,128]{1,0:T(8,128)(2,1)S(1)} %stack.2.refs_2_), channel_id=1, source_target_pairs={{0,2},{1,3},{2,0},{3,1},{4,6},{5,7},{6,4},{7,5},{8,10},{9,11},{10,... | collective-permute-start | bytes 786440 | tf_op jit(solution)/shard_map/ppermute | solution.py:45
  22.5 5.5 %collective-permute-start.6 = (bf16[512,128]{1,0:T(8,128)(2,1)S(1)}, bf16[512,128]{1,0:T(8,128)(2,1)S(1)}, u32[]{:S(2)}, u32[]{:S(2)}) collective-permute-start(bf16[512,128]{1,0:T(8,128)(2,1)S(1)} %collective-permute-done.5.refs_3_), channel_id=1, source_target_pairs={{0,2},{1,3},{2,0},{3,1},{4,6},{5,7},{6,4},{7,5},{8,10},{9,11},{10,... | collective-permute-start | bytes 393224 | tf_op jit(solution)/shard_map/ppermute | solution.py:45
  24.5 1.3 %collective-permute-start.8 = (bf16[128,256]{1,0:T(8,128)(2,1)S(1)}, bf16[128,256]{1,0:T(8,128)(2,1)S(1)}, u32[]{:S(2)}, u32[]{:S(2)}) collective-permute-start(bf16[128,256]{1,0:T(8,128)(2,1)S(1)} %get-tuple-element.16.refs_2_.refs_0_), channel_id=1, source_target_pairs={{0,1},{1,0},{2,3},{3,2},{4,5},{5,4},{6,7},{7,6},{8,9},{9,8},{10,11... | collective-permute-start | bytes 196616 | tf_op jit(solution)/shard_map/ppermute | solution.py:45
  27.1 10.1 %copy-start.1 = (s32[1,32]{1,0:T(1,128)S(1)}, s32[1,32]{1,0:T(1,128)}, u32[]{:S(2)}) copy-start(s32[1,32]{1,0:T(1,128)} %refs_3_.2) | copy-start | bytes 388
  27.1 26.8 %copy-start.3 = (s32[3,2]{0,1:T(2,128)S(1)}, s32[3,2]{0,1:T(2,128)}, u32[]{:S(2)}) copy-start(s32[3,2]{0,1:T(2,128)} %param.13) | copy-start | bytes 76
  29.3 1.6 %collective-permute-start.9 = (f32[512,128]{1,0:T(8,128)S(1)}, f32[512,128]{1,0:T(8,128)S(1)}, u32[]{:S(2)}, u32[]{:S(2)}) collective-permute-start(f32[512,128]{1,0:T(8,128)S(1)} %px.3.mine), channel_id=1, source_target_pairs={{0,1},{1,0},{2,3},{3,2},{4,5},{5,4},{6,7},{7,6},{8,9},{9,8},{10,11... | collective-permute-start | bytes 786440 | tf_op jit(solution)/shard_map/ppermute | solution.py:45
  30.9 6.3 %collective-permute-start.10 = (bf16[640,128]{1,0:T(8,128)(2,1)S(1)}, bf16[640,128]{1,0:T(8,128)(2,1)S(1)}, u32[]{:S(2)}, u32[]{:S(2)}) collective-permute-start(bf16[640,128]{1,0:T(8,128)(2,1)S(1)} %get-tuple-element.21), channel_id=1, source_target_pairs={{0,2},{1,3},{2,0},{3,1},{4,6},{5,7},{6,4},{7,5},{8,10},{9,11},{10,... | collective-permute-start | bytes 491528 | tf_op jit(solution)/shard_map/ppermute | solution.py:45
  38.2 6.6 %collective-permute-start.13 = (bf16[32,2048]{1,0:T(8,128)(2,1)S(1)}, bf16[32,2048]{1,0:T(8,128)(2,1)S(1)}, u32[]{:S(2)}, u32[]{:S(2)}) collective-permute-start(bf16[32,2048]{1,0:T(8,128)(2,1)S(1)} %grads.1.refs_0_), channel_id=1, source_target_pairs={{0,12},{1,13},{2,14},{3,15},{4,0},{5,1},{6,2},{7,3},{8,4},{9,5},{1... | collective-permute-start | bytes 393224 | tf_op jit(solution)/shard_map/ppermute | solution.py:45
  40.8 12.0 %collective-permute-start.12 = (bf16[32,2048]{1,0:T(8,128)(2,1)S(1)}, bf16[32,2048]{1,0:T(8,128)(2,1)S(1)}, u32[]{:S(2)}, u32[]{:S(2)}) collective-permute-start(bf16[32,2048]{1,0:T(8,128)(2,1)S(1)} %grads.1.refs_0_), channel_id=1, source_target_pairs={{0,8},{1,9},{2,10},{3,11},{4,12},{5,13},{6,14},{7,15},{8,0},{9,1},... | collective-permute-start | bytes 393224 | tf_op jit(solution)/shard_map/ppermute | solution.py:45
  41.5 11.3 %collective-permute-start.11 = (bf16[32,2048]{1,0:T(8,128)(2,1)S(1)}, bf16[32,2048]{1,0:T(8,128)(2,1)S(1)}, u32[]{:S(2)}, u32[]{:S(2)}) collective-permute-start(bf16[32,2048]{1,0:T(8,128)(2,1)S(1)} %grads.1.refs_0_), channel_id=1, source_target_pairs={{0,4},{1,5},{2,6},{3,7},{4,8},{5,9},{6,10},{7,11},{8,12},{9,13},{1... | collective-permute-start | bytes 393224 | tf_op jit(solution)/shard_map/ppermute | solution.py:45
  52.9 5.0 %collective-permute-start.14 = (bf16[32,2048]{1,0:T(8,128)(2,1)S(1)}, bf16[32,2048]{1,0:T(8,128)(2,1)S(1)}, u32[]{:S(2)}, u32[]{:S(2)}) collective-permute-start(bf16[32,2048]{1,0:T(8,128)(2,1)S(1)} %total.1.mine.refs_0_), channel_id=1, source_target_pairs={{0,2},{1,3},{2,0},{3,1},{4,6},{5,7},{6,4},{7,5},{8,10},{9,11},{10,... | collective-permute-start | bytes 393224 | tf_op jit(solution)/shard_map/ppermute | solution.py:45
  57.9 3.4 %collective-permute-start.15 = (bf16[64,2048]{1,0:T(8,128)(2,1)S(1)}, bf16[64,2048]{1,0:T(8,128)(2,1)S(1)}, u32[]{:S(2)}, u32[]{:S(2)}) collective-permute-start(bf16[64,2048]{1,0:T(8,128)(2,1)S(1)} %stack.3), channel_id=1, source_target_pairs={{0,1},{1,0},{2,3},{3,2},{4,5},{5,4},{6,7},{7,6},{8,9},{9,8},{10,11... | collective-permute-start | bytes 786440 | tf_op jit(solution)/shard_map/ppermute | solution.py:45
  58.0 3.3 %copy-start = (s32[32]{0:T(128)S(1)}, s32[32]{0:T(128)}, u32[]{:S(2)}) copy-start(s32[32]{0:T(128)} %param.12) | copy-start | bytes 388

commit v8 on v5

--- a/solution.py
+++ b/solution.py
@@ -29,7 +29,7 @@
 def owner(me, devices, shift):
     deep, wide, cores = levels(devices)
     z, x, core = place(me, devices)
-    z = (z + (deep - shift[0])) % deep
+    z = z ^ shift[0] if deep & (deep - 1) == 0 else (z + (deep - shift[0])) % deep
     x = (x + (wide - shift[1])) % wide
     core = (core + (cores - shift[2])) % cores
     return (z * wide + x) * cores + core
@@ -40,7 +40,8 @@
     perm = []
     for i in range(devices):
         z, x, core = place(i, devices)
-        z, x, core = (z + shift[0]) % deep, (x + shift[1]) % wide, (core + shift[2]) % cores
+        z = z ^ shift[0] if deep & (deep - 1) == 0 else (z + shift[0]) % deep
+        x, core = (x + shift[1]) % wide, (core + shift[2]) % cores
         perm.append((i, (z * wide + x) * cores + core))
     return lax.ppermute(value, "seq", perm)
 
@@ -354,21 +355,21 @@
 
     feat_type = jax.ShapeDtypeStruct((2 * rows, wide), jnp.bfloat16)
     if tall % 128 == 0 and deep > 2 and across == 2 and cores == 2:
-        spins = sorted(range(1, deep), key=lambda z: min(z, deep - z))
-        near, far = spins[:-1], spins[-1]
-        got = [send(proj_in, devices, (z, 0, 0)) for z in near]
+        got = send(proj_in, devices, (1, 0, 0))
         side = send(proj_in, devices, (0, 1, 0))
-        got_far = send(proj_in, devices, (far, 0, 0))
-        got = stack(got, (pg_t, side))
+        far = range(2, deep)
+        got_far = [send(proj_in, devices, (z, 0, 0)) for z in far]
+        got = stack([got], (side,))
         side_near = send(got, devices, (0, 1, 0))
+        got_far = stack(got_far, (pg_t, side_near))
         side_far = send(got_far, devices, (0, 1, 0))
         value, column = px(
-            [(own, [(0, 0, 0)]), (got, [(z, 0, 0) for z in near]), (got_far, [(far, 0, 0)])], keep=True
+            [(own, [(0, 0, 0)]), (got, [(1, 0, 0)]), (got_far, [(z, 0, 0) for z in far])], keep=True
         )
         twin = send(column, devices, (0, 0, 1))
         side = stack([side, side_near, side_far], (value,))
         twin_side = send(side, devices, (0, 0, 1))
-        order = [0, *near, far]
+        order = range(deep)
         value = px([(side, [(z, 1, 0) for z in order]), (twin, [(z, 0, 1) for z in order])], value)
         value = px([(twin_side, [(z, 1, 1) for z in order])], value, end=True)
     else:

time: 62.5 us -> 64 us (1.024)
  waiting for transfers between devices: 26.9 us -> 29.9 us
  starting transfers between devices: 16.6 us -> 15.1 us
    ppermute x16, waiting for transfers between devices: 26.9 us -> 29.9 us  [send(): return lax.ppermute(value, 'seq', perm)]
    ppermute x16, starting transfers between devices: 16.6 us -> 15.1 us  [send(): return lax.ppermute(value, 'seq', perm)]
where the time goes in v8:
time: 64 us; the launch traced here: 63.8 us
  waiting for transfers between devices  29.9 us (47%)
  Pallas kernels  17.9 us (28%)
  starting transfers between devices  15.1 us (24%)
  between operations  0.78 us (1%)
    ppermute x16, waiting for transfers between devices, send(): return lax.ppermute(value, 'seq', perm)  29.9 us
    ppermute x16, starting transfers between devices, send(): return lax.ppermute(value, 'seq', perm)  15.1 us
    pallas_call x3, Pallas kernels, shards(): pl.pallas_call(functools.partial(part_kernel, devices, shifts, more), out...  10.3 us
    pallas_call x1, Pallas kernels, shards(): pl.pallas_call(load_kernel, out_shape=(pltpu.VMEM(acts.shape, jnp.bfloat1...  3.87 us
    pallas_call x3, Pallas kernels, px(): pl.pallas_call(functools.partial(px_kernel, devices, keys, before is None...  2.72 us
  transfers between devices with their start and end apart: 16, of which 9 were waited for; matrix products, arithmetic and copies ran while one was open for 0% of the time, Pallas kernels for 19%

profile of v8, /device:TPU:0, one launch (start us, length us, event | category | flops | bytes accessed | tf_op | source)
XLA Modules:
  0.0 63.8 jit_solution(614664522960841252)
XLA Ops:
  0.6 3.1 %collective-permute-start.1 = (bf16[512,128]{1,0:T(8,128)(2,1)}, bf16[512,128]{1,0:T(8,128)(2,1)S(1)}, u32[]{:S(2)}, u32[]{:S(2)}) collective-permute-start(bf16[512,128]{1,0:T(8,128)(2,1)} %proj_in.1), channel_id=1, source_target_pairs={{0,4},{1,5},{2,6},{3,7},{4,0},{5,1},{6,2},{7,3},{8,12},{9,13},{10,... | collective-permute-start | bytes 393224 | tf_op jit(solution)/shard_map/ppermute | solution.py:46
  3.7 1.5 %collective-permute-start = (bf16[512,128]{1,0:T(8,128)(2,1)}, bf16[512,128]{1,0:T(8,128)(2,1)S(1)}, u32[]{:S(2)}, u32[]{:S(2)}) collective-permute-start(bf16[512,128]{1,0:T(8,128)(2,1)} %proj_in.1), channel_id=1, source_target_pairs={{0,2},{1,3},{2,0},{3,1},{4,6},{5,7},{6,4},{7,5},{8,10},{9,11},{10,... | collective-permute-start | bytes 393224 | tf_op jit(solution)/shard_map/ppermute | solution.py:46
  5.2 2.5 %collective-permute-start.4 = (bf16[512,128]{1,0:T(8,128)(2,1)}, bf16[512,128]{1,0:T(8,128)(2,1)S(1)}, u32[]{:S(2)}, u32[]{:S(2)}) collective-permute-start(bf16[512,128]{1,0:T(8,128)(2,1)} %proj_in.1), channel_id=1, source_target_pairs={{0,12},{1,13},{2,14},{3,15},{4,8},{5,9},{6,10},{7,11},{8,4},{9,5},... | collective-permute-start | bytes 393224 | tf_op jit(solution)/shard_map/ppermute | solution.py:46
  7.7 0.1 collective-permute-start.3
  7.8 1.1 %collective-permute-done.refs_1_.refs_0_ = bf16[512,128]{1,0:T(8,128)(2,1)S(1)} collective-permute-done((bf16[512,128]{1,0:T(8,128)(2,1)}, bf16[512,128]{1,0:T(8,128)(2,1)S(1)}, u32[]{:S(2)}, u32[]{:S(2)}) %collective-permute-start) | collective-permute-done | bytes 131104 | tf_op jit(solution)/shard_map/ppermute | solution.py:46
  8.9 1.6 %collective-permute-start.2 = (bf16[512,128]{1,0:T(8,128)(2,1)S(1)}, bf16[512,128]{1,0:T(8,128)(2,1)S(1)}, u32[]{:S(2)}, u32[]{:S(2)}) collective-permute-start(bf16[512,128]{1,0:T(8,128)(2,1)S(1)} %stack.4.refs_1_), channel_id=1, source_target_pairs={{0,2},{1,3},{2,0},{3,1},{4,6},{5,7},{6,4},{7,5},{8,10},{9,11},{10,... | collective-permute-start | bytes 393224 | tf_op jit(solution)/shard_map/ppermute | solution.py:46
  10.5 3.9 %load.1 = (bf16[2,256,8192]{2,1,0:T(8,128)(2,1)S(1)}, bf16[512,128]{1,0:T(8,128)(2,1)S(1)}, bf16[128,256]{1,0:T(8,128)(2,1)S(1)}) custom-call(bf16[2,256,8192]{2,1,0:T(8,128)(2,1)} %acts.1, bf16[2,256,1024]{2,1,0:T(8,128)(2,1)} %cots.1, bf16[512,128]{1,0:T(8,128)(2,1)} %proj_in.1, bf16[1024,128]{1,0:T(8,128)(2,1)} %proj_out.1), custom_call_target="tpu_custom_call" | custom-call | flops 1 | bytes 1 | tf_op jit(solution)/shard_map/load/pallas_call | solution.py:309
  14.4 5.0 %collective-permute-done.3.refs_0_ = bf16[512,128]{1,0:T(8,128)(2,1)S(1)} collective-permute-done((bf16[512,128]{1,0:T(8,128)(2,1)}, bf16[512,128]{1,0:T(8,128)(2,1)S(1)}, u32[]{:S(2)}, u32[]{:S(2)}) %collective-permute-start.3) | collective-permute-done | bytes 131104 | tf_op jit(solution)/shard_map/ppermute | solution.py:46
  19.4 0.6 collective-permute-start.5
  20.0 0.7 %px.3 = (f32[2,256,128]{2,1,0:T(8,128)S(1)}, bf16[2048,128]{1,0:T(8,128)(2,1)S(1)}) custom-call(bf16[2,256,8192]{2,1,0:T(8,128)(2,1)S(1)} %get-tuple-element.10.acts, bf16[512,128]{1,0:T(8,128)(2,1)S(1)} %get-tuple-element.12.refs_0_, bf16[512,128]{1,0:T(8,128)(2,1)S(1)} %stack.4.refs_1_, bf16[1024,128]{1,0:T(8,128)(2,1)S(1)} %stack.5.refs_2_), custom_call_target="tpu_custom_call" | custom-call | flops 1 | bytes 1 | tf_op jit(solution)/shard_map/px/pallas_call | solution.py:345
  20.8 0.1 collective-permute-start.7
  20.9 5.7 %collective-permute-done.5.refs_2_ = bf16[1024,128]{1,0:T(8,128)(2,1)S(1)} collective-permute-done((bf16[1024,128]{1,0:T(8,128)(2,1)S(1)}, bf16[1024,128]{1,0:T(8,128)(2,1)S(1)}, u32[]{:S(2)}, u32[]{:S(2)}) %collective-permute-start.5) | collective-permute-done | bytes 262176 | tf_op jit(solution)/shard_map/ppermute | solution.py:46
  26.6 0.1 collective-permute-start.6
  26.7 1.3 %px.4.refs_1_ = f32[2,256,128]{2,1,0:T(8,128)S(1)} custom-call(bf16[2,256,8192]{2,1,0:T(8,128)(2,1)S(1)} %get-tuple-element.10.acts, bf16[2048,128]{1,0:T(8,128)(2,1)S(1)} %stack.6.refs_0_, bf16[2048,128]{1,0:T(8,128)(2,1)S(1)} %collective-permute-done.7.refs_1_, f32[2,256,128]{2,1,0:T(8,128)S(1)} %get-tuple-element.13.refs_3_.refs_2_), custom_call_target="tpu_custom_call" | custom-call | flops 1 | bytes 1 | tf_op jit(solution)/shard_map/px/pallas_call | solution.py:345
  28.0 0.6 collective-permute-done.6.refs_0_
  28.6 0.7 %px.5.refs_0_ = bf16[512,128]{1,0:T(8,128)(2,1)S(1)} custom-call(bf16[2,256,8192]{2,1,0:T(8,128)(2,1)S(1)} %get-tuple-element.10.acts, bf16[2048,128]{1,0:T(8,128)(2,1)S(1)} %collective-permute-done.6.refs_0_, f32[2,256,128]{2,1,0:T(8,128)S(1)} %px.4.refs_1_, bf16[128,256]{1,0:T(8,128)(2,1)S(1)} %get-tuple-element.11.refs_2_), custom_call_target="tpu_custom_call" | custom-call | flops 1 | bytes 1 | tf_op jit(solution)/shard_map/px/pallas_call | solution.py:345
  29.3 0.8 %collective-permute-start.8 = (bf16[512,128]{1,0:T(8,128)(2,1)S(1)}, bf16[512,128]{1,0:T(8,128)(2,1)S(1)}, u32[]{:S(2)}, u32[]{:S(2)}) collective-permute-start(bf16[512,128]{1,0:T(8,128)(2,1)S(1)} %px.5.refs_0_), channel_id=1, source_target_pairs={{0,2},{1,3},{2,0},{3,1},{4,6},{5,7},{6,4},{7,5},{8,10},{9,11},{10,... | collective-permute-start | bytes 393224 | tf_op jit(solution)/shard_map/ppermute | solution.py:46
  30.1 4.8 %collective-permute-done.8.refs_1_ = bf16[512,128]{1,0:T(8,128)(2,1)S(1)} collective-permute-done((bf16[512,128]{1,0:T(8,128)(2,1)S(1)}, bf16[512,128]{1,0:T(8,128)(2,1)S(1)}, u32[]{:S(2)}, u32[]{:S(2)}) %collective-permute-start.8) | collective-permute-done | bytes 131104 | tf_op jit(solution)/shard_map/ppermute | solution.py:46
  34.9 1.3 %collective-permute-done.10.refs_3_ = bf16[512,128]{1,0:T(8,128)(2,1)S(1)} collective-permute-done((bf16[512,128]{1,0:T(8,128)(2,1)S(1)}, bf16[512,128]{1,0:T(8,128)(2,1)S(1)}, u32[]{:S(2)}, u32[]{:S(2)}) %collective-permute-start.10) | collective-permute-done | bytes 131104 | tf_op jit(solution)/shard_map/ppermute | solution.py:46
  36.3 0.9 %grads.1.refs_0_ = bf16[32,2048]{1,0:T(8,128)(2,1)S(1)} custom-call(bf16[512,128]{1,0:T(8,128)(2,1)S(1)} %px.5.refs_0_, bf16[512,128]{1,0:T(8,128)(2,1)S(1)} %collective-permute-done.8.refs_1_, bf16[512,128]{1,0:T(8,128)(2,1)S(1)} %collective-permute-done.9.refs_2_, bf16[512,128]{1,0:T(8,128)(2,1)S(1)} %collective-permute-done.10.refs_3_, s32[1,32]{1,0:T(1,128)S(1)} %copy-done.1), custom_call_target="tpu_custom_call" | custom-call | tf_op jit(solution)/shard_map/grads/pallas_call | solution.py:396
  37.2 3.0 %collective-permute-start.13 = (bf16[32,2048]{1,0:T(8,128)(2,1)S(1)}, bf16[32,2048]{1,0:T(8,128)(2,1)S(1)}, u32[]{:S(2)}, u32[]{:S(2)}) collective-permute-start(bf16[32,2048]{1,0:T(8,128)(2,1)S(1)} %grads.1.refs_0_), channel_id=1, source_target_pairs={{0,12},{1,13},{2,14},{3,15},{4,8},{5,9},{6,10},{7,11},{8,4},{9,5},... | collective-permute-start | bytes 393224 | tf_op jit(solution)/shard_map/ppermute | solution.py:46
  40.1 1.5 %collective-permute-start.11 = (bf16[32,2048]{1,0:T(8,128)(2,1)S(1)}, bf16[32,2048]{1,0:T(8,128)(2,1)S(1)}, u32[]{:S(2)}, u32[]{:S(2)}) collective-permute-start(bf16[32,2048]{1,0:T(8,128)(2,1)S(1)} %grads.1.refs_0_), channel_id=1, source_target_pairs={{0,4},{1,5},{2,6},{3,7},{4,0},{5,1},{6,2},{7,3},{8,12},{9,13},{10,... | collective-permute-start | bytes 393224 | tf_op jit(solution)/shard_map/ppermute | solution.py:46
  41.6 3.9 %collective-permute-done.13.refs_3_ = bf16[32,2048]{1,0:T(8,128)(2,1)S(1)} collective-permute-done((bf16[32,2048]{1,0:T(8,128)(2,1)S(1)}, bf16[32,2048]{1,0:T(8,128)(2,1)S(1)}, u32[]{:S(2)}, u32[]{:S(2)}) %collective-permute-start.13) | collective-permute-done | bytes 131104 | tf_op jit(solution)/shard_map/ppermute | solution.py:46
  45.5 5.4 %collective-permute-done.12.refs_2_ = bf16[32,2048]{1,0:T(8,128)(2,1)S(1)} collective-permute-done((bf16[32,2048]{1,0:T(8,128)(2,1)S(1)}, bf16[32,2048]{1,0:T(8,128)(2,1)S(1)}, u32[]{:S(2)}, u32[]{:S(2)}) %collective-permute-start.12) | collective-permute-done | bytes 131104 | tf_op jit(solution)/shard_map/ppermute | solution.py:46
  50.9 0.1 total.1.mine.refs_0_
  50.9 0.3 collective-permute-start.14
  51.3 0.1 copy.11.refs_1_.refs_3_
  51.4 2.6 %covariance.3 = (f32[8,128]{1,0:T(8,128)S(1)}, f32[3,256,4096]{2,1,0:T(8,128)}) custom-call(bf16[32,2048]{1,0:T(8,128)(2,1)S(1)} %total.1.mine.refs_0_, bf16[32,2048]{1,0:T(8,128)(2,1)S(1)} %total.1.mine.refs_0_, s32[3,2]{1,0:T(4,128)S(1)} %copy.11.refs_1_.refs_3_), custom_call_target="tpu_custom_call" | custom-call | flops 50331648 | bytes 3145728 | tf_op jit(solution)/shard_map/covariance/pallas_call | solution.py:437
  54.0 2.0 %collective-permute-done.14.refs_1_.refs_0_ = bf16[32,2048]{1,0:T(8,128)(2,1)S(1)} collective-permute-done((bf16[32,2048]{1,0:T(8,128)(2,1)S(1)}, bf16[32,2048]{1,0:T(8,128)(2,1)S(1)}, u32[]{:S(2)}, u32[]{:S(2)}) %collective-permute-start.14) | collective-permute-done | bytes 131104 | tf_op jit(solution)/shard_map/ppermute | solution.py:46
  56.1 0.1 collective-permute-start.15
  56.1 3.2 %covariance.4 = (f32[8,128]{1,0:T(8,128)}, f32[3,256,4096]{2,1,0:T(8,128)}) custom-call(bf16[32,2048]{1,0:T(8,128)(2,1)S(1)} %total.1.mine.refs_0_, bf16[32,2048]{1,0:T(8,128)(2,1)S(1)} %collective-permute-done.14.refs_1_.refs_0_, s32[3,2]{1,0:T(4,128)S(1)} %copy.11.refs_1_.refs_3_, ...), custom_call_target="tpu_custom_call", output_to_operand_aliasing={{1}: (3, {})} | custom-call | flops 50331648 | bytes 3145728 | tf_op jit(solution)/shard_map/covariance/pallas_call | solution.py:437
  59.4 4.4 %covariance.5 = (bf16[2,8192]{1,0:T(2,128)(2,1)}, f32[3,256,4096]{2,1,0:T(8,128)}) custom-call(bf16[32,2048]{1,0:T(8,128)(2,1)S(1)} %total.1.mine.refs_0_, bf16[64,2048]{1,0:T(8,128)(2,1)S(1)} %collective-permute-done.15.refs_0_, bf16[32,2048]{1,0:T(8,128)(2,1)S(1)} %collective-permute-done.14.refs_1_.refs_0_, ...), custom_call_target="tpu_custom_call", output_to_operand_aliasing={{1}: (5, {})} | custom-call | flops 100663296 | bytes 6291456 | tf_op jit(solution)/shard_map/covariance/pallas_call | solution.py:437
  (20 shorter events, 0.1 us)
Async XLA Ops:
  0.6 7.2 %collective-permute-start.1 = (bf16[512,128]{1,0:T(8,128)(2,1)}, bf16[512,128]{1,0:T(8,128)(2,1)S(1)}, u32[]{:S(2)}, u32[]{:S(2)}) collective-permute-start(bf16[512,128]{1,0:T(8,128)(2,1)} %proj_in.1), channel_id=1, source_target_pairs={{0,4},{1,5},{2,6},{3,7},{4,0},{5,1},{6,2},{7,3},{8,12},{9,13},{10,... | collective-permute-start | bytes 393224 | tf_op jit(solution)/shard_map/ppermute | solution.py:46
  3.7 5.2 %collective-permute-start = (bf16[512,128]{1,0:T(8,128)(2,1)}, bf16[512,128]{1,0:T(8,128)(2,1)S(1)}, u32[]{:S(2)}, u32[]{:S(2)}) collective-permute-start(bf16[512,128]{1,0:T(8,128)(2,1)} %proj_in.1), channel_id=1, source_target_pairs={{0,2},{1,3},{2,0},{3,1},{4,6},{5,7},{6,4},{7,5},{8,10},{9,11},{10,... | collective-permute-start | bytes 393224 | tf_op jit(solution)/shard_map/ppermute | solution.py:46
  5.2 9.1 %collective-permute-start.4 = (bf16[512,128]{1,0:T(8,128)(2,1)}, bf16[512,128]{1,0:T(8,128)(2,1)S(1)}, u32[]{:S(2)}, u32[]{:S(2)}) collective-permute-start(bf16[512,128]{1,0:T(8,128)(2,1)} %proj_in.1), channel_id=1, source_target_pairs={{0,12},{1,13},{2,14},{3,15},{4,8},{5,9},{6,10},{7,11},{8,4},{9,5},... | collective-permute-start | bytes 393224 | tf_op jit(solution)/shard_map/ppermute | solution.py:46
  7.7 11.7 %collective-permute-start.3 = (bf16[512,128]{1,0:T(8,128)(2,1)}, bf16[512,128]{1,0:T(8,128)(2,1)S(1)}, u32[]{:S(2)}, u32[]{:S(2)}) collective-permute-start(bf16[512,128]{1,0:T(8,128)(2,1)} %proj_in.1), channel_id=1, source_target_pairs={{0,8},{1,9},{2,10},{3,11},{4,12},{5,13},{6,14},{7,15},{8,0},{9,1},... | collective-permute-start | bytes 393224 | tf_op jit(solution)/shard_map/ppermute | solution.py:46
  8.9 10.5 %collective-permute-start.2 = (bf16[512,128]{1,0:T(8,128)(2,1)S(1)}, bf16[512,128]{1,0:T(8,128)(2,1)S(1)}, u32[]{:S(2)}, u32[]{:S(2)}) collective-permute-start(bf16[512,128]{1,0:T(8,128)(2,1)S(1)} %stack.4.refs_1_), channel_id=1, source_target_pairs={{0,2},{1,3},{2,0},{3,1},{4,6},{5,7},{6,4},{7,5},{8,10},{9,11},{10,... | collective-permute-start | bytes 393224 | tf_op jit(solution)/shard_map/ppermute | solution.py:46
  19.4 7.2 %collective-permute-start.5 = (bf16[1024,128]{1,0:T(8,128)(2,1)S(1)}, bf16[1024,128]{1,0:T(8,128)(2,1)S(1)}, u32[]{:S(2)}, u32[]{:S(2)}) collective-permute-start(bf16[1024,128]{1,0:T(8,128)(2,1)S(1)} %stack.5.refs_2_), channel_id=1, source_target_pairs={{0,2},{1,3},{2,0},{3,1},{4,6},{5,7},{6,4},{7,5},{8,10},{9,11},{10,... | collective-permute-start | bytes 786440 | tf_op jit(solution)/shard_map/ppermute | solution.py:46
  20.0 16.2 %copy-start.1 = (s32[1,32]{1,0:T(1,128)S(1)}, s32[1,32]{1,0:T(1,128)}, u32[]{:S(2)}) copy-start(s32[1,32]{1,0:T(1,128)} %refs_4_.1) | copy-start | bytes 388
  20.8 30.5 %copy-start.2 = (s32[3,2]{0,1:T(2,128)S(1)}, s32[3,2]{0,1:T(2,128)}, u32[]{:S(2)}) copy-start(s32[3,2]{0,1:T(2,128)} %param.13) | copy-start | bytes 76
  20.8 5.9 %collective-permute-start.7 = (bf16[2048,128]{1,0:T(8,128)(2,1)S(1)}, bf16[2048,128]{1,0:T(8,128)(2,1)S(1)}, u32[]{:S(2)}, u32[]{:S(2)}) collective-permute-start(bf16[2048,128]{1,0:T(8,128)(2,1)S(1)} %get-tuple-element.14), channel_id=1, source_target_pairs={{0,1},{1,0},{2,3},{3,2},{4,5},{5,4},{6,7},{7,6},{8,9},{9,8},{10,11... | collective-permute-start | bytes 1572872 | tf_op jit(solution)/shard_map/ppermute | solution.py:46
  26.6 2.0 %collective-permute-start.6 = (bf16[2048,128]{1,0:T(8,128)(2,1)S(1)}, bf16[2048,128]{1,0:T(8,128)(2,1)S(1)}, u32[]{:S(2)}, u32[]{:S(2)}) collective-permute-start(bf16[2048,128]{1,0:T(8,128)(2,1)S(1)} %stack.6.refs_0_), channel_id=1, source_target_pairs={{0,1},{1,0},{2,3},{3,2},{4,5},{5,4},{6,7},{7,6},{8,9},{9,8},{10,11... | collective-permute-start | bytes 1572872 | tf_op jit(solution)/shard_map/ppermute | solution.py:46
  28.0 31.4 %copy-start = (s32[32]{0:T(128)S(1)}, s32[32]{0:T(128)}, u32[]{:S(2)}) copy-start(s32[32]{0:T(128)} %param.12) | copy-start | bytes 388
  29.3 5.6 %collective-permute-start.8 = (bf16[512,128]{1,0:T(8,128)(2,1)S(1)}, bf16[512,128]{1,0:T(8,128)(2,1)S(1)}, u32[]{:S(2)}, u32[]{:S(2)}) collective-permute-start(bf16[512,128]{1,0:T(8,128)(2,1)S(1)} %px.5.refs_0_), channel_id=1, source_target_pairs={{0,2},{1,3},{2,0},{3,1},{4,6},{5,7},{6,4},{7,5},{8,10},{9,11},{10,... | collective-permute-start | bytes 393224 | tf_op jit(solution)/shard_map/ppermute | solution.py:46
  30.1 4.8 %collective-permute-start.9 = (bf16[512,128]{1,0:T(8,128)(2,1)S(1)}, bf16[512,128]{1,0:T(8,128)(2,1)S(1)}, u32[]{:S(2)}, u32[]{:S(2)}) collective-permute-start(bf16[512,128]{1,0:T(8,128)(2,1)S(1)} %px.5.refs_0_), channel_id=1, source_target_pairs={{0,1},{1,0},{2,3},{3,2},{4,5},{5,4},{6,7},{7,6},{8,9},{9,8},{10,11... | collective-permute-start | bytes 393224 | tf_op jit(solution)/shard_map/ppermute | solution.py:46
  34.9 1.3 %collective-permute-start.10 = (bf16[512,128]{1,0:T(8,128)(2,1)S(1)}, bf16[512,128]{1,0:T(8,128)(2,1)S(1)}, u32[]{:S(2)}, u32[]{:S(2)}) collective-permute-start(bf16[512,128]{1,0:T(8,128)(2,1)S(1)} %collective-permute-done.8.refs_1_), channel_id=1, source_target_pairs={{0,1},{1,0},{2,3},{3,2},{4,5},{5,4},{6,7},{7,6},{8,9},{9,8},{10,11... | collective-permute-start | bytes 393224 | tf_op jit(solution)/shard_map/ppermute | solution.py:46
  37.2 8.3 %collective-permute-start.13 = (bf16[32,2048]{1,0:T(8,128)(2,1)S(1)}, bf16[32,2048]{1,0:T(8,128)(2,1)S(1)}, u32[]{:S(2)}, u32[]{:S(2)}) collective-permute-start(bf16[32,2048]{1,0:T(8,128)(2,1)S(1)} %grads.1.refs_0_), channel_id=1, source_target_pairs={{0,12},{1,13},{2,14},{3,15},{4,8},{5,9},{6,10},{7,11},{8,4},{9,5},... | collective-permute-start | bytes 393224 | tf_op jit(solution)/shard_map/ppermute | solution.py:46
  40.1 10.7 %collective-permute-start.12 = (bf16[32,2048]{1,0:T(8,128)(2,1)S(1)}, bf16[32,2048]{1,0:T(8,128)(2,1)S(1)}, u32[]{:S(2)}, u32[]{:S(2)}) collective-permute-start(bf16[32,2048]{1,0:T(8,128)(2,1)S(1)} %grads.1.refs_0_), channel_id=1, source_target_pairs={{0,8},{1,9},{2,10},{3,11},{4,12},{5,13},{6,14},{7,15},{8,0},{9,1},... | collective-permute-start | bytes 393224 | tf_op jit(solution)/shard_map/ppermute | solution.py:46
  40.1 10.7 %collective-permute-start.11 = (bf16[32,2048]{1,0:T(8,128)(2,1)S(1)}, bf16[32,2048]{1,0:T(8,128)(2,1)S(1)}, u32[]{:S(2)}, u32[]{:S(2)}) collective-permute-start(bf16[32,2048]{1,0:T(8,128)(2,1)S(1)} %grads.1.refs_0_), channel_id=1, source_target_pairs={{0,4},{1,5},{2,6},{3,7},{4,0},{5,1},{6,2},{7,3},{8,12},{9,13},{10,... | collective-permute-start | bytes 393224 | tf_op jit(solution)/shard_map/ppermute | solution.py:46
  50.9 5.1 %collective-permute-start.14 = (bf16[32,2048]{1,0:T(8,128)(2,1)S(1)}, bf16[32,2048]{1,0:T(8,128)(2,1)S(1)}, u32[]{:S(2)}, u32[]{:S(2)}) collective-permute-start(bf16[32,2048]{1,0:T(8,128)(2,1)S(1)} %total.1.mine.refs_0_), channel_id=1, source_target_pairs={{0,2},{1,3},{2,0},{3,1},{4,6},{5,7},{6,4},{7,5},{8,10},{9,11},{10,... | collective-permute-start | bytes 393224 | tf_op jit(solution)/shard_map/ppermute | solution.py:46
  56.1 3.3 %collective-permute-start.15 = (bf16[64,2048]{1,0:T(8,128)(2,1)S(1)}, bf16[64,2048]{1,0:T(8,128)(2,1)S(1)}, u32[]{:S(2)}, u32[]{:S(2)}) collective-permute-start(bf16[64,2048]{1,0:T(8,128)(2,1)S(1)} %stack.7), channel_id=1, source_target_pairs={{0,1},{1,0},{2,3},{3,2},{4,5},{5,4},{6,7},{7,6},{8,9},{9,8},{10,11... | collective-permute-start | bytes 786440 | tf_op jit(solution)/shard_map/ppermute | solution.py:46

commit v9 on v4

--- a/solution.py
+++ b/solution.py
@@ -12,6 +12,7 @@
 VMEM = pl.BlockSpec(memory_space=pltpu.VMEM)
 SMEM = pl.BlockSpec(memory_space=pltpu.SMEM)
 ANY = pl.BlockSpec(memory_space=pl.ANY)
+HBM = pl.BlockSpec(memory_space=pltpu.HBM)
 
 
 def levels(devices):
@@ -28,7 +29,7 @@
 def owner(me, devices, shift):
     deep, wide, cores = levels(devices)
     z, x, core = place(me, devices)
-    z = (z + (deep - shift[0])) % deep
+    z = z ^ shift[0] if deep & (deep - 1) == 0 else (z + (deep - shift[0])) % deep
     x = (x + (wide - shift[1])) % wide
     core = (core + (cores - shift[2])) % cores
     return (z * wide + x) * cores + core
@@ -39,7 +40,8 @@
     perm = []
     for i in range(devices):
         z, x, core = place(i, devices)
-        z, x, core = (z + shift[0]) % deep, (x + shift[1]) % wide, (core + shift[2]) % cores
+        z = z ^ shift[0] if deep & (deep - 1) == 0 else (z + shift[0]) % deep
+        x, core = (x + shift[1]) % wide, (core + shift[2]) % cores
         perm.append((i, (z * wide + x) * cores + core))
     return lax.ppermute(value, "seq", perm)
 
@@ -240,6 +242,70 @@
         copy.wait()
 
 
+def own_kernel(devices, mine, pairs, token, out, held, sems):
+    npair, band, lanes = held.shape
+    seqs, full = mine.shape
+    _, across, cores = levels(devices)
+    line = across * cores
+    me = lax.axis_index("seq")
+    scale = jnp.float32(1.0 / seqs)
+    copies = []
+    for p in range(npair):
+        at = pl.multiple_of(pairs[p, 0] * lanes + me // line * band, band)
+        right = mine[:, pl.ds(pl.multiple_of(pairs[p, 1] * lanes, lanes), lanes)]
+        product = lax.dot_general(
+            mine[:, pl.ds(at, band)], right, (((0,), (0,)), ((), ())), preferred_element_type=jnp.float32
+        )
+        held[p] = product * scale
+        for here, there, size in chunks(me % line, devices, band * devices):
+            to = pl.ds(pl.multiple_of(there, size), size)
+            copies.append(pltpu.make_async_copy(held.at[p, :, pl.ds(here, size)], out.at[p, :, to], sems.at[len(copies)]))
+            copies[-1].start()
+    token[...] = jnp.zeros(token.shape, token.dtype)
+    for copy in copies:
+        copy.wait()
+
+
+def rest_kernel(devices, keys, *refs):
+    arrays, (slots, pairs, _, logged, out, held, right, sems) = refs[:len(keys)], refs[len(keys):]
+    npair, band, lanes = held.shape
+    seqs, full = right.shape
+    deep, across, cores = levels(devices)
+    line = across * cores
+    square = band * devices
+    layers = full // square
+    me = lax.axis_index("seq")
+    spot = me % line
+    for array, shifts in zip(arrays, keys):
+        for i, shift in enumerate(shifts):
+            for here, there, size in chunks(owner(me, devices, shift) % line, devices, square):
+                for l in range(layers):
+                    at = l * (square // line) + here
+                    to = pl.ds(pl.multiple_of(l * square + there, size), size)
+                    right[:, to] = array[i * seqs:(i + 1) * seqs, at:at + size]
+    runs = [(z * line + spot + 1, line - 1) for z in range(deep - 1)]
+    runs += [((devices - line + spot + 1 + i) % devices, 1) for i in range(line - 1)]
+    scale = jnp.float32(1.0 / seqs)
+    copies = []
+    for p in range(npair):
+        left = right[:, pl.ds(pl.multiple_of(pairs[p, 0] * square + me * band, band), band)]
+        here = 0
+        for first, count in runs:
+            size = count * band
+            value = right[:, pl.ds(pl.multiple_of(pairs[p, 1] * square + first * band, band), size)]
+            product = lax.dot_general(left, value, (((0,), (0,)), ((), ())), preferred_element_type=jnp.float32)
+            held[p, :, here:here + size] = product * scale
+            to = pl.ds(pl.multiple_of(first * band, band), size)
+            copies.append(pltpu.make_async_copy(held.at[p, :, pl.ds(here, size)], out.at[p, :, to], sems.at[len(copies)]))
+            copies[-1].start()
+            here += size
+    own = me * CAP + lax.broadcasted_iota(jnp.int32, (CAP, seqs), 0)
+    picker = (jnp.broadcast_to(slots[...], (CAP, seqs)) == own).astype(jnp.float32).astype(jnp.bfloat16)
+    logged[...] = jnp.dot(picker, right[...], preferred_element_type=jnp.float32).astype(jnp.bfloat16)
+    for copy in copies:
+        copy.wait()
+
+
 def shards(acts, cots, proj_in, proj_out, lengths, slots, pairs):
     layers, rows, width = acts.shape
     wide = proj_out.shape[1]
@@ -264,7 +330,7 @@
             pltpu.VMEM(proj_in.shape, jnp.bfloat16),
             pltpu.VMEM((wide, rows), jnp.bfloat16),
         ),
-        in_specs=[ANY] * 4,
+        in_specs=[HBM] * 4,
         out_specs=(VMEM,) * 3,
         scratch_shapes=[
             pltpu.VMEM(cots.shape, jnp.bfloat16),
@@ -274,12 +340,12 @@
         compiler_params=params,
         cost_estimate=light,
         name="load",
-    )(acts, cots, proj_in, proj_out)
+    )(*[pltpu.with_memory_space_constraint(a, pltpu.HBM) for a in (acts, cots, proj_in, proj_out)])
 
     def stack(arrays, after):
         return pl.pallas_call(
             functools.partial(stack_kernel, len(arrays)),
-            out_shape=jax.ShapeDtypeStruct((sum(a.shape[0] for a in arrays), wide), jnp.bfloat16),
+            out_shape=jax.ShapeDtypeStruct((sum(a.shape[0] for a in arrays), arrays[0].shape[1]), jnp.bfloat16),
             in_specs=[VMEM] * len(arrays) + [ANY] * len(after),
             out_specs=VMEM,
             compiler_params=params,
@@ -306,26 +372,22 @@
 
     feat_type = jax.ShapeDtypeStruct((2 * rows, wide), jnp.bfloat16)
     if tall % 128 == 0 and deep > 2 and across == 2 and cores == 2:
-        spins = sorted(range(1, deep), key=lambda z: min(z, deep - z))
-        near, far = spins[:-1], spins[-1]
+        *near, far = range(1, deep)
         got = [send(proj_in, devices, (z, 0, 0)) for z in near]
         side = send(proj_in, devices, (0, 1, 0))
         got_far = send(proj_in, devices, (far, 0, 0))
         got = stack(got, (pg_t, side))
         side_near = send(got, devices, (0, 1, 0))
-        value, column = px([(own, [(0, 0, 0)]), (got, [(z, 0, 0) for z in near])], keep=True)
+        side_far = send(got_far, devices, (0, 1, 0))
+        value, column = px(
+            [(own, [(0, 0, 0)]), (got, [(z, 0, 0) for z in near]), (got_far, [(far, 0, 0)])], keep=True
+        )
         twin = send(column, devices, (0, 0, 1))
-        side_far = send(got_far, devices, (0, 1, 0))
-        twin_far = send(got_far, devices, (0, 0, 1))
-        side = stack([side, side_near], (value,))
+        side = stack([side, side_near, side_far], (value,))
         twin_side = send(side, devices, (0, 0, 1))
-        first = [0, *near]
-        value = px([(side, [(z, 1, 0) for z in first]), (got_far, [(far, 0, 0)])], value)
-        twin_side_far = send(side_far, devices, (0, 0, 1))
-        value = px(
-            [(twin, [(z, 0, 1) for z in first]), (twin_far, [(far, 0, 1)]), (side_far, [(far, 1, 0)])], value
-        )
-        value = px([(twin_side, [(z, 1, 1) for z in first]), (twin_side_far, [(far, 1, 1)])], value, end=True)
+        order = [0, *near, far]
+        value = px([(side, [(z, 1, 0) for z in order]), (twin, [(z, 0, 1) for z in order])], value)
+        value = px([(twin_side, [(z, 1, 1) for z in order])], value, end=True)
     else:
         groups = [[z * line + i for z in range(deep)] for i in range(line)]
         column = lax.all_to_all(jnp.tile(proj_in, (deep, 1)), "seq", 0, 0, axis_index_groups=groups, tiled=True)
@@ -365,13 +427,46 @@
         compiler_params=params,
         name="total",
     )(*terms)
+    logged_type = jax.ShapeDtypeStruct((CAP, layers * square), jnp.bfloat16)
+    covariance_type = jax.ShapeDtypeStruct((npair, band, square), jnp.float32)
+    if band % 128 == 0 and across == 2 and cores == 2:
+        width = square // line
+        side = send(total, devices, (0, 1, 0))
+        token, covariance = pl.pallas_call(
+            functools.partial(own_kernel, devices),
+            out_shape=[jax.ShapeDtypeStruct((8, 128), jnp.float32), covariance_type],
+            in_specs=[VMEM, SMEM],
+            out_specs=[VMEM, ANY],
+            scratch_shapes=[
+                pltpu.VMEM((npair, band, width), jnp.float32),
+                pltpu.SemaphoreType.DMA((npair * deep,)),
+            ],
+            compiler_params=params,
+            cost_estimate=pl.CostEstimate(
+                flops=2 * npair * seqs * band * width, bytes_accessed=4 * npair * band * width, transcendentals=0
+            ),
+            name="own",
+        )(total, pairs)
+        both = stack([total, side], (token,))
+        twin = send(both, devices, (0, 0, 1))
+        return pl.pallas_call(
+            functools.partial(rest_kernel, devices, [[(0, x, c) for x in range(across)] for c in range(cores)]),
+            out_shape=[logged_type, covariance_type],
+            in_specs=[VMEM, VMEM, VMEM, SMEM, ANY],
+            out_specs=[VMEM, ANY],
+            scratch_shapes=[
+                pltpu.VMEM((npair, band, square - width), jnp.float32),
+                pltpu.VMEM((seqs, layers * square), jnp.bfloat16),
+                pltpu.SemaphoreType.DMA((npair * (deep + line - 2),)),
+            ],
+            input_output_aliases={4: 1},
+            compiler_params=params,
+            name="rest",
+        )(both, twin, slots.reshape(1, seqs), pairs, covariance)
     full = plane(total)
     return pl.pallas_call(
         functools.partial(covariance_kernel, devices, tuple(full)),
-        out_shape=[
-            jax.ShapeDtypeStruct((CAP, layers * square), jnp.bfloat16),
-            jax.ShapeDtypeStruct((npair, band, square), jnp.float32),
-        ],
+        out_shape=[logged_type, covariance_type],
         in_specs=[VMEM] * (len(full) + 1) + [SMEM],
         out_specs=[VMEM, ANY],
         scratch_shapes=[

time: 65.7 us -> 63.4 us (0.965)
  local copies, waits for them, and re-layouts: 6.57 us -> 0.11 us
  Pallas kernels: 11.5 us -> 15.7 us
    unnamed x17 -> x7, local copies, waits for them, and re-layouts: 6.57 us -> 0.11 us
    pallas_call x1, Pallas kernels: 1.35 us -> 3.87 us  [shards(): pl.pallas_call(load_kernel, out_shape=(pltpu.VMEM(acts.shape, jnp.bfloat1...]
    pallas_call x1 -> x2, Pallas kernels: 6.26 us -> 8.01 us  [the longest x1 5.35 us: shards(): pl.pallas_call(functools.partial(rest_kernel, devices, [[(0, x, c) for x...]
    pallas_call x4 -> x3, Pallas kernels: 2.87 us -> 2.72 us  [px(): pl.pallas_call(functools.partial(px_kernel, devices, keys, before is None...]
    ppermute x19 -> x16, starting transfers between devices: 15.2 us -> 15.3 us  [send(): return lax.ppermute(value, 'seq', perm)]
    ppermute x19 -> x16, waiting for transfers between devices: 31.4 us -> 31.4 us  [send(): return lax.ppermute(value, 'seq', perm)]
  transfers between devices with their start and end apart: 19 -> 16, of which waited for: 9 -> 9; matrix products, arithmetic and copies ran while one was open for 0% -> 0% of each run, Pallas kernels for 5% -> 14%
where the time goes in v9:
time: 63.4 us; the launch traced here: 63.3 us
  waiting for transfers between devices  31.4 us (50%)
  Pallas kernels  15.7 us (25%)
  starting transfers between devices  15.3 us (24%)
  between operations  0.76 us (1%)
    ppermute x16, waiting for transfers between devices, send(): return lax.ppermute(value, 'seq', perm)  31.4 us
    ppermute x16, starting transfers between devices, send(): return lax.ppermute(value, 'seq', perm)  15.3 us
    pallas_call x1, Pallas kernels, shards(): pl.pallas_call(functools.partial(rest_kernel, devices, [[(0, x, c) for x...  5.35 us
    pallas_call x1, Pallas kernels, shards(): pl.pallas_call(load_kernel, out_shape=(pltpu.VMEM(acts.shape, jnp.bfloat1...  3.87 us
    pallas_call x3, Pallas kernels, px(): pl.pallas_call(functools.partial(px_kernel, devices, keys, before is None...  2.72 us
    pallas_call x1, Pallas kernels, shards(): pl.pallas_call(functools.partial(own_kernel, devices), out_shape=[jax.Sha...  2.66 us
  transfers between devices with their start and end apart: 16, of which 9 were waited for; matrix products, arithmetic and copies ran while one was open for 0% of the time, Pallas kernels for 14%

profile of v9, /device:TPU:0, one launch (start us, length us, event | category | flops | bytes accessed | tf_op | source)
XLA Modules:
  0.0 63.3 jit_solution(18042312854588138561)
XLA Ops:
  0.6 3.1 %collective-permute-start.1 = (bf16[512,128]{1,0:T(8,128)(2,1)}, bf16[512,128]{1,0:T(8,128)(2,1)S(1)}, u32[]{:S(2)}, u32[]{:S(2)}) collective-permute-start(bf16[512,128]{1,0:T(8,128)(2,1)} %proj_in.1), channel_id=1, source_target_pairs={{0,4},{1,5},{2,6},{3,7},{4,0},{5,1},{6,2},{7,3},{8,12},{9,13},{10,... | collective-permute-start | bytes 393224 | tf_op jit(solution)/shard_map/ppermute | solution.py:46
  3.7 1.5 %collective-permute-start = (bf16[512,128]{1,0:T(8,128)(2,1)}, bf16[512,128]{1,0:T(8,128)(2,1)S(1)}, u32[]{:S(2)}, u32[]{:S(2)}) collective-permute-start(bf16[512,128]{1,0:T(8,128)(2,1)} %proj_in.1), channel_id=1, source_target_pairs={{0,2},{1,3},{2,0},{3,1},{4,6},{5,7},{6,4},{7,5},{8,10},{9,11},{10,... | collective-permute-start | bytes 393224 | tf_op jit(solution)/shard_map/ppermute | solution.py:46
  5.2 2.6 %collective-permute-start.2 = (bf16[512,128]{1,0:T(8,128)(2,1)}, bf16[512,128]{1,0:T(8,128)(2,1)S(1)}, u32[]{:S(2)}, u32[]{:S(2)}) collective-permute-start(bf16[512,128]{1,0:T(8,128)(2,1)} %proj_in.1), channel_id=1, source_target_pairs={{0,8},{1,9},{2,10},{3,11},{4,12},{5,13},{6,14},{7,15},{8,0},{9,1},... | collective-permute-start | bytes 393224 | tf_op jit(solution)/shard_map/ppermute | solution.py:46
  7.8 0.2 collective-permute-start.4
  8.0 3.9 %load.1 = (bf16[2,256,8192]{2,1,0:T(8,128)(2,1)S(1)}, bf16[512,128]{1,0:T(8,128)(2,1)S(1)}, bf16[128,256]{1,0:T(8,128)(2,1)S(1)}) custom-call(bf16[2,256,8192]{2,1,0:T(8,128)(2,1)} %acts.1, bf16[2,256,1024]{2,1,0:T(8,128)(2,1)} %cots.1, bf16[512,128]{1,0:T(8,128)(2,1)} %proj_in.1, bf16[1024,128]{1,0:T(8,128)(2,1)} %proj_out.1), custom_call_target="tpu_custom_call" | custom-call | flops 1 | bytes 1 | tf_op jit(solution)/shard_map/load/pallas_call | solution.py:326
  11.9 5.7 %collective-permute-done.2.refs_1_ = bf16[512,128]{1,0:T(8,128)(2,1)S(1)} collective-permute-done((bf16[512,128]{1,0:T(8,128)(2,1)}, bf16[512,128]{1,0:T(8,128)(2,1)S(1)}, u32[]{:S(2)}, u32[]{:S(2)}) %collective-permute-start.2) | collective-permute-done | bytes 131104 | tf_op jit(solution)/shard_map/ppermute | solution.py:46
  17.7 1.0 %collective-permute-start.3 = (bf16[1024,128]{1,0:T(8,128)(2,1)S(1)}, bf16[1024,128]{1,0:T(8,128)(2,1)S(1)}, u32[]{:S(2)}, u32[]{:S(2)}) collective-permute-start(bf16[1024,128]{1,0:T(8,128)(2,1)S(1)} %stack.3.refs_1_), channel_id=1, source_target_pairs={{0,2},{1,3},{2,0},{3,1},{4,6},{5,7},{6,4},{7,5},{8,10},{9,11},{10,... | collective-permute-start | bytes 786440 | tf_op jit(solution)/shard_map/ppermute | solution.py:46
  18.7 1.1 %collective-permute-start.5 = (bf16[512,128]{1,0:T(8,128)(2,1)S(1)}, bf16[512,128]{1,0:T(8,128)(2,1)S(1)}, u32[]{:S(2)}, u32[]{:S(2)}) collective-permute-start(bf16[512,128]{1,0:T(8,128)(2,1)S(1)} %collective-permute-done.4.refs_2_), channel_id=1, source_target_pairs={{0,2},{1,3},{2,0},{3,1},{4,6},{5,7},{6,4},{7,5},{8,10},{9,11},{10,... | collective-permute-start | bytes 393224 | tf_op jit(solution)/shard_map/ppermute | solution.py:46
  19.8 0.7 %px.3 = (f32[2,256,128]{2,1,0:T(8,128)S(1)}, bf16[2048,128]{1,0:T(8,128)(2,1)S(1)}) custom-call(bf16[2,256,8192]{2,1,0:T(8,128)(2,1)S(1)} %get-tuple-element.9.acts, bf16[512,128]{1,0:T(8,128)(2,1)S(1)} %get-tuple-element.11.refs_0_, bf16[1024,128]{1,0:T(8,128)(2,1)S(1)} %stack.3.refs_1_, bf16[512,128]{1,0:T(8,128)(2,1)S(1)} %collective-permute-done.4.refs_2_), custom_call_target="tpu_custom_call" | custom-call | flops 1 | bytes 1 | tf_op jit(solution)/shard_map/px/pallas_call | solution.py:362
  20.5 0.0 copy-start
  20.6 0.1 collective-permute-start.7
  20.6 6.2 %collective-permute-done.5.refs_2_ = bf16[512,128]{1,0:T(8,128)(2,1)S(1)} collective-permute-done((bf16[512,128]{1,0:T(8,128)(2,1)S(1)}, bf16[512,128]{1,0:T(8,128)(2,1)S(1)}, u32[]{:S(2)}, u32[]{:S(2)}) %collective-permute-start.5) | collective-permute-done | bytes 131104 | tf_op jit(solution)/shard_map/ppermute | solution.py:46
  26.9 0.1 collective-permute-start.6
  27.0 1.3 %px.4.refs_1_ = f32[2,256,128]{2,1,0:T(8,128)S(1)} custom-call(bf16[2,256,8192]{2,1,0:T(8,128)(2,1)S(1)} %get-tuple-element.9.acts, bf16[2048,128]{1,0:T(8,128)(2,1)S(1)} %stack.4.refs_0_, bf16[2048,128]{1,0:T(8,128)(2,1)S(1)} %collective-permute-done.7.refs_1_, f32[2,256,128]{2,1,0:T(8,128)S(1)} %get-tuple-element.12.refs_3_.refs_2_), custom_call_target="tpu_custom_call" | custom-call | flops 1 | bytes 1 | tf_op jit(solution)/shard_map/px/pallas_call | solution.py:362
  28.2 0.6 collective-permute-done.6.refs_0_
  28.8 0.7 %px.5.refs_0_ = bf16[512,128]{1,0:T(8,128)(2,1)S(1)} custom-call(bf16[2,256,8192]{2,1,0:T(8,128)(2,1)S(1)} %get-tuple-element.9.acts, bf16[2048,128]{1,0:T(8,128)(2,1)S(1)} %collective-permute-done.6.refs_0_, f32[2,256,128]{2,1,0:T(8,128)S(1)} %px.4.refs_1_, bf16[128,256]{1,0:T(8,128)(2,1)S(1)} %get-tuple-element.10.refs_2_), custom_call_target="tpu_custom_call" | custom-call | flops 1 | bytes 1 | tf_op jit(solution)/shard_map/px/pallas_call | solution.py:362
  29.6 0.4 collective-permute-start.8
  29.9 5.2 %collective-permute-done.8.refs_1_ = bf16[512,128]{1,0:T(8,128)(2,1)S(1)} collective-permute-done((bf16[512,128]{1,0:T(8,128)(2,1)S(1)}, bf16[512,128]{1,0:T(8,128)(2,1)S(1)}, u32[]{:S(2)}, u32[]{:S(2)}) %collective-permute-start.8) | collective-permute-done | bytes 131104 | tf_op jit(solution)/shard_map/ppermute | solution.py:46
  35.2 1.3 %collective-permute-done.10.refs_3_ = bf16[512,128]{1,0:T(8,128)(2,1)S(1)} collective-permute-done((bf16[512,128]{1,0:T(8,128)(2,1)S(1)}, bf16[512,128]{1,0:T(8,128)(2,1)S(1)}, u32[]{:S(2)}, u32[]{:S(2)}) %collective-permute-start.10) | collective-permute-done | bytes 131104 | tf_op jit(solution)/shard_map/ppermute | solution.py:46
  36.5 0.9 %grads.1.refs_0_ = bf16[32,2048]{1,0:T(8,128)(2,1)S(1)} custom-call(bf16[512,128]{1,0:T(8,128)(2,1)S(1)} %px.5.refs_0_, bf16[512,128]{1,0:T(8,128)(2,1)S(1)} %collective-permute-done.8.refs_1_, bf16[512,128]{1,0:T(8,128)(2,1)S(1)} %collective-permute-done.9.refs_2_, bf16[512,128]{1,0:T(8,128)(2,1)S(1)} %collective-permute-done.10.refs_3_, s32[1,32]{1,0:T(1,128)S(1)} %copy-done.1), custom_call_target="tpu_custom_call" | custom-call | tf_op jit(solution)/shard_map/grads/pallas_call | solution.py:412
  37.4 2.5 %collective-permute-start.13 = (bf16[32,2048]{1,0:T(8,128)(2,1)S(1)}, bf16[32,2048]{1,0:T(8,128)(2,1)S(1)}, u32[]{:S(2)}, u32[]{:S(2)}) collective-permute-start(bf16[32,2048]{1,0:T(8,128)(2,1)S(1)} %grads.1.refs_0_), channel_id=1, source_target_pairs={{0,12},{1,13},{2,14},{3,15},{4,8},{5,9},{6,10},{7,11},{8,4},{9,5},... | collective-permute-start | bytes 393224 | tf_op jit(solution)/shard_map/ppermute | solution.py:46
  39.9 2.0 %collective-permute-start.11 = (bf16[32,2048]{1,0:T(8,128)(2,1)S(1)}, bf16[32,2048]{1,0:T(8,128)(2,1)S(1)}, u32[]{:S(2)}, u32[]{:S(2)}) collective-permute-start(bf16[32,2048]{1,0:T(8,128)(2,1)S(1)} %grads.1.refs_0_), channel_id=1, source_target_pairs={{0,4},{1,5},{2,6},{3,7},{4,0},{5,1},{6,2},{7,3},{8,12},{9,13},{10,... | collective-permute-start | bytes 393224 | tf_op jit(solution)/shard_map/ppermute | solution.py:46
  41.9 3.9 %collective-permute-done.13.refs_3_ = bf16[32,2048]{1,0:T(8,128)(2,1)S(1)} collective-permute-done((bf16[32,2048]{1,0:T(8,128)(2,1)S(1)}, bf16[32,2048]{1,0:T(8,128)(2,1)S(1)}, u32[]{:S(2)}, u32[]{:S(2)}) %collective-permute-start.13) | collective-permute-done | bytes 131104 | tf_op jit(solution)/shard_map/ppermute | solution.py:46
  45.8 5.1 %collective-permute-done.12.refs_2_ = bf16[32,2048]{1,0:T(8,128)(2,1)S(1)} collective-permute-done((bf16[32,2048]{1,0:T(8,128)(2,1)S(1)}, bf16[32,2048]{1,0:T(8,128)(2,1)S(1)}, u32[]{:S(2)}, u32[]{:S(2)}) %collective-permute-start.12) | collective-permute-done | bytes 131104 | tf_op jit(solution)/shard_map/ppermute | solution.py:46
  50.9 0.1 total.1.mine.refs_0_
  51.0 0.8 %collective-permute-start.14 = (bf16[32,2048]{1,0:T(8,128)(2,1)S(1)}, bf16[32,2048]{1,0:T(8,128)(2,1)S(1)}, u32[]{:S(2)}, u32[]{:S(2)}) collective-permute-start(bf16[32,2048]{1,0:T(8,128)(2,1)S(1)} %total.1.mine.refs_0_), channel_id=1, source_target_pairs={{0,2},{1,3},{2,0},{3,1},{4,6},{5,7},{6,4},{7,5},{8,10},{9,11},{10,... | collective-permute-start | bytes 393224 | tf_op jit(solution)/shard_map/ppermute | solution.py:46
  51.8 0.1 copy.10.pairs.refs_3_
  51.9 2.7 %own.1 = (f32[8,128]{1,0:T(8,128)S(1)}, f32[3,256,4096]{2,1,0:T(8,128)}) custom-call(bf16[32,2048]{1,0:T(8,128)(2,1)S(1)} %total.1.mine.refs_0_, s32[3,2]{1,0:T(4,128)S(1)} %copy.10.pairs.refs_3_), custom_call_target="tpu_custom_call" | custom-call | flops 50331648 | bytes 3145728 | tf_op jit(solution)/shard_map/own/pallas_call | solution.py:435
  54.6 1.7 %collective-permute-done.14.refs_1_ = bf16[32,2048]{1,0:T(8,128)(2,1)S(1)} collective-permute-done((bf16[32,2048]{1,0:T(8,128)(2,1)S(1)}, bf16[32,2048]{1,0:T(8,128)(2,1)S(1)}, u32[]{:S(2)}, u32[]{:S(2)}) %collective-permute-start.14) | collective-permute-done | bytes 131104 | tf_op jit(solution)/shard_map/ppermute | solution.py:46
  56.3 0.1 collective-permute-start.15
  56.4 1.5 %collective-permute-done.15.refs_1_ = bf16[64,2048]{1,0:T(8,128)(2,1)S(1)} collective-permute-done((bf16[64,2048]{1,0:T(8,128)(2,1)S(1)}, bf16[64,2048]{1,0:T(8,128)(2,1)S(1)}, u32[]{:S(2)}, u32[]{:S(2)}) %collective-permute-start.15) | collective-permute-done | bytes 262176 | tf_op jit(solution)/shard_map/ppermute | solution.py:46
  57.9 5.4 %rest.1 = (bf16[2,8192]{1,0:T(2,128)(2,1)}, f32[3,256,4096]{2,1,0:T(8,128)}) custom-call(bf16[64,2048]{1,0:T(8,128)(2,1)S(1)} %stack.5.refs_0_, bf16[64,2048]{1,0:T(8,128)(2,1)S(1)} %collective-permute-done.15.refs_1_, s32[1,32]{1,0:T(1,128)S(1)} %bitcast.1, s32[3,2]{1,0:T(4,128)S(1)} %copy.10.pairs.refs_3_, ...), custom_call_target="tpu_custom_call", output_to_operand_aliasing={{1}: (4, {})} | custom-call | tf_op jit(solution)/shard_map/rest/pallas_call | solution.py:452
  (18 shorter events, 0.1 us)
Async XLA Ops:
  0.6 11.3 %collective-permute-start.1 = (bf16[512,128]{1,0:T(8,128)(2,1)}, bf16[512,128]{1,0:T(8,128)(2,1)S(1)}, u32[]{:S(2)}, u32[]{:S(2)}) collective-permute-start(bf16[512,128]{1,0:T(8,128)(2,1)} %proj_in.1), channel_id=1, source_target_pairs={{0,4},{1,5},{2,6},{3,7},{4,0},{5,1},{6,2},{7,3},{8,12},{9,13},{10,... | collective-permute-start | bytes 393224 | tf_op jit(solution)/shard_map/ppermute | solution.py:46
  3.7 8.2 %collective-permute-start = (bf16[512,128]{1,0:T(8,128)(2,1)}, bf16[512,128]{1,0:T(8,128)(2,1)S(1)}, u32[]{:S(2)}, u32[]{:S(2)}) collective-permute-start(bf16[512,128]{1,0:T(8,128)(2,1)} %proj_in.1), channel_id=1, source_target_pairs={{0,2},{1,3},{2,0},{3,1},{4,6},{5,7},{6,4},{7,5},{8,10},{9,11},{10,... | collective-permute-start | bytes 393224 | tf_op jit(solution)/shard_map/ppermute | solution.py:46
  5.2 12.5 %collective-permute-start.2 = (bf16[512,128]{1,0:T(8,128)(2,1)}, bf16[512,128]{1,0:T(8,128)(2,1)S(1)}, u32[]{:S(2)}, u32[]{:S(2)}) collective-permute-start(bf16[512,128]{1,0:T(8,128)(2,1)} %proj_in.1), channel_id=1, source_target_pairs={{0,8},{1,9},{2,10},{3,11},{4,12},{5,13},{6,14},{7,15},{8,0},{9,1},... | collective-permute-start | bytes 393224 | tf_op jit(solution)/shard_map/ppermute | solution.py:46
  7.8 10.9 %collective-permute-start.4 = (bf16[512,128]{1,0:T(8,128)(2,1)}, bf16[512,128]{1,0:T(8,128)(2,1)S(1)}, u32[]{:S(2)}, u32[]{:S(2)}) collective-permute-start(bf16[512,128]{1,0:T(8,128)(2,1)} %proj_in.1), channel_id=1, source_target_pairs={{0,12},{1,13},{2,14},{3,15},{4,8},{5,9},{6,10},{7,11},{8,4},{9,5},... | collective-permute-start | bytes 393224 | tf_op jit(solution)/shard_map/ppermute | solution.py:46
  17.7 9.1 %collective-permute-start.3 = (bf16[1024,128]{1,0:T(8,128)(2,1)S(1)}, bf16[1024,128]{1,0:T(8,128)(2,1)S(1)}, u32[]{:S(2)}, u32[]{:S(2)}) collective-permute-start(bf16[1024,128]{1,0:T(8,128)(2,1)S(1)} %stack.3.refs_1_), channel_id=1, source_target_pairs={{0,2},{1,3},{2,0},{3,1},{4,6},{5,7},{6,4},{7,5},{8,10},{9,11},{10,... | collective-permute-start | bytes 786440 | tf_op jit(solution)/shard_map/ppermute | solution.py:46
  18.7 8.1 %collective-permute-start.5 = (bf16[512,128]{1,0:T(8,128)(2,1)S(1)}, bf16[512,128]{1,0:T(8,128)(2,1)S(1)}, u32[]{:S(2)}, u32[]{:S(2)}) collective-permute-start(bf16[512,128]{1,0:T(8,128)(2,1)S(1)} %collective-permute-done.4.refs_2_), channel_id=1, source_target_pairs={{0,2},{1,3},{2,0},{3,1},{4,6},{5,7},{6,4},{7,5},{8,10},{9,11},{10,... | collective-permute-start | bytes 393224 | tf_op jit(solution)/shard_map/ppermute | solution.py:46
  19.8 16.7 %copy-start.1 = (s32[1,32]{1,0:T(1,128)S(1)}, s32[1,32]{1,0:T(1,128)}, u32[]{:S(2)}) copy-start(s32[1,32]{1,0:T(1,128)} %refs_4_.1) | copy-start | bytes 388
  20.5 31.3 %copy-start.2 = (s32[3,2]{0,1:T(2,128)S(1)}, s32[3,2]{0,1:T(2,128)}, u32[]{:S(2)}) copy-start(s32[3,2]{0,1:T(2,128)} %param.13) | copy-start | bytes 76
  20.5 37.4 %copy-start = (s32[32]{0:T(128)S(1)}, s32[32]{0:T(128)}, u32[]{:S(2)}) copy-start(s32[32]{0:T(128)} %param.12) | copy-start | bytes 388
  20.6 6.4 %collective-permute-start.7 = (bf16[2048,128]{1,0:T(8,128)(2,1)S(1)}, bf16[2048,128]{1,0:T(8,128)(2,1)S(1)}, u32[]{:S(2)}, u32[]{:S(2)}) collective-permute-start(bf16[2048,128]{1,0:T(8,128)(2,1)S(1)} %get-tuple-element.13), channel_id=1, source_target_pairs={{0,1},{1,0},{2,3},{3,2},{4,5},{5,4},{6,7},{7,6},{8,9},{9,8},{10,11... | collective-permute-start | bytes 1572872 | tf_op jit(solution)/shard_map/ppermute | solution.py:46
  26.9 2.0 %collective-permute-start.6 = (bf16[2048,128]{1,0:T(8,128)(2,1)S(1)}, bf16[2048,128]{1,0:T(8,128)(2,1)S(1)}, u32[]{:S(2)}, u32[]{:S(2)}) collective-permute-start(bf16[2048,128]{1,0:T(8,128)(2,1)S(1)} %stack.4.refs_0_), channel_id=1, source_target_pairs={{0,1},{1,0},{2,3},{3,2},{4,5},{5,4},{6,7},{7,6},{8,9},{9,8},{10,11... | collective-permute-start | bytes 1572872 | tf_op jit(solution)/shard_map/ppermute | solution.py:46
  29.6 5.6 %collective-permute-start.8 = (bf16[512,128]{1,0:T(8,128)(2,1)S(1)}, bf16[512,128]{1,0:T(8,128)(2,1)S(1)}, u32[]{:S(2)}, u32[]{:S(2)}) collective-permute-start(bf16[512,128]{1,0:T(8,128)(2,1)S(1)} %px.5.refs_0_), channel_id=1, source_target_pairs={{0,2},{1,3},{2,0},{3,1},{4,6},{5,7},{6,4},{7,5},{8,10},{9,11},{10,... | collective-permute-start | bytes 393224 | tf_op jit(solution)/shard_map/ppermute | solution.py:46
  29.9 5.2 %collective-permute-start.9 = (bf16[512,128]{1,0:T(8,128)(2,1)S(1)}, bf16[512,128]{1,0:T(8,128)(2,1)S(1)}, u32[]{:S(2)}, u32[]{:S(2)}) collective-permute-start(bf16[512,128]{1,0:T(8,128)(2,1)S(1)} %px.5.refs_0_), channel_id=1, source_target_pairs={{0,1},{1,0},{2,3},{3,2},{4,5},{5,4},{6,7},{7,6},{8,9},{9,8},{10,11... | collective-permute-start | bytes 393224 | tf_op jit(solution)/shard_map/ppermute | solution.py:46
  35.1 1.3 %collective-permute-start.10 = (bf16[512,128]{1,0:T(8,128)(2,1)S(1)}, bf16[512,128]{1,0:T(8,128)(2,1)S(1)}, u32[]{:S(2)}, u32[]{:S(2)}) collective-permute-start(bf16[512,128]{1,0:T(8,128)(2,1)S(1)} %collective-permute-done.8.refs_1_), channel_id=1, source_target_pairs={{0,1},{1,0},{2,3},{3,2},{4,5},{5,4},{6,7},{7,6},{8,9},{9,8},{10,11... | collective-permute-start | bytes 393224 | tf_op jit(solution)/shard_map/ppermute | solution.py:46
  37.4 8.3 %collective-permute-start.13 = (bf16[32,2048]{1,0:T(8,128)(2,1)S(1)}, bf16[32,2048]{1,0:T(8,128)(2,1)S(1)}, u32[]{:S(2)}, u32[]{:S(2)}) collective-permute-start(bf16[32,2048]{1,0:T(8,128)(2,1)S(1)} %grads.1.refs_0_), channel_id=1, source_target_pairs={{0,12},{1,13},{2,14},{3,15},{4,8},{5,9},{6,10},{7,11},{8,4},{9,5},... | collective-permute-start | bytes 393224 | tf_op jit(solution)/shard_map/ppermute | solution.py:46
  39.9 11.0 %collective-permute-start.12 = (bf16[32,2048]{1,0:T(8,128)(2,1)S(1)}, bf16[32,2048]{1,0:T(8,128)(2,1)S(1)}, u32[]{:S(2)}, u32[]{:S(2)}) collective-permute-start(bf16[32,2048]{1,0:T(8,128)(2,1)S(1)} %grads.1.refs_0_), channel_id=1, source_target_pairs={{0,8},{1,9},{2,10},{3,11},{4,12},{5,13},{6,14},{7,15},{8,0},{9,1},... | collective-permute-start | bytes 393224 | tf_op jit(solution)/shard_map/ppermute | solution.py:46
  39.9 11.0 %collective-permute-start.11 = (bf16[32,2048]{1,0:T(8,128)(2,1)S(1)}, bf16[32,2048]{1,0:T(8,128)(2,1)S(1)}, u32[]{:S(2)}, u32[]{:S(2)}) collective-permute-start(bf16[32,2048]{1,0:T(8,128)(2,1)S(1)} %grads.1.refs_0_), channel_id=1, source_target_pairs={{0,4},{1,5},{2,6},{3,7},{4,0},{5,1},{6,2},{7,3},{8,12},{9,13},{10,... | collective-permute-start | bytes 393224 | tf_op jit(solution)/shard_map/ppermute | solution.py:46
  51.0 5.3 %collective-permute-start.14 = (bf16[32,2048]{1,0:T(8,128)(2,1)S(1)}, bf16[32,2048]{1,0:T(8,128)(2,1)S(1)}, u32[]{:S(2)}, u32[]{:S(2)}) collective-permute-start(bf16[32,2048]{1,0:T(8,128)(2,1)S(1)} %total.1.mine.refs_0_), channel_id=1, source_target_pairs={{0,2},{1,3},{2,0},{3,1},{4,6},{5,7},{6,4},{7,5},{8,10},{9,11},{10,... | collective-permute-start | bytes 393224 | tf_op jit(solution)/shard_map/ppermute | solution.py:46
  56.3 1.6 %collective-permute-start.15 = (bf16[64,2048]{1,0:T(8,128)(2,1)S(1)}, bf16[64,2048]{1,0:T(8,128)(2,1)S(1)}, u32[]{:S(2)}, u32[]{:S(2)}) collective-permute-start(bf16[64,2048]{1,0:T(8,128)(2,1)S(1)} %stack.5.refs_0_), channel_id=1, source_target_pairs={{0,1},{1,0},{2,3},{3,2},{4,5},{5,4},{6,7},{7,6},{8,9},{9,8},{10,11... | collective-permute-start | bytes 786440 | tf_op jit(solution)/shard_map/ppermute | solution.py:46

commit v10 on v9

--- a/solution.py
+++ b/solution.py
@@ -29,7 +29,7 @@
 def owner(me, devices, shift):
     deep, wide, cores = levels(devices)
     z, x, core = place(me, devices)
-    z = z ^ shift[0] if deep & (deep - 1) == 0 else (z + (deep - shift[0])) % deep
+    z = (z + (deep - shift[0])) % deep
     x = (x + (wide - shift[1])) % wide
     core = (core + (cores - shift[2])) % cores
     return (z * wide + x) * cores + core
@@ -40,8 +40,7 @@
     perm = []
     for i in range(devices):
         z, x, core = place(i, devices)
-        z = z ^ shift[0] if deep & (deep - 1) == 0 else (z + shift[0]) % deep
-        x, core = (x + shift[1]) % wide, (core + shift[2]) % cores
+        z, x, core = (z + shift[0]) % deep, (x + shift[1]) % wide, (core + shift[2]) % cores
         perm.append((i, (z * wide + x) * cores + core))
     return lax.ppermute(value, "seq", perm)
 
@@ -372,7 +371,7 @@
 
     feat_type = jax.ShapeDtypeStruct((2 * rows, wide), jnp.bfloat16)
     if tall % 128 == 0 and deep > 2 and across == 2 and cores == 2:
-        *near, far = range(1, deep)
+        *near, far = sorted(range(1, deep), key=lambda z: min(z, deep - z))
         got = [send(proj_in, devices, (z, 0, 0)) for z in near]
         side = send(proj_in, devices, (0, 1, 0))
         got_far = send(proj_in, devices, (far, 0, 0))

time: 63.4 us -> 61.7 us (0.973)
  waiting for transfers between devices: 31.4 us -> 28.4 us
  starting transfers between devices: 15.3 us -> 16.6 us
    ppermute x16, waiting for transfers between devices: 31.4 us -> 28.4 us  [send(): return lax.ppermute(value, 'seq', perm)]
    ppermute x16, starting transfers between devices: 15.3 us -> 16.6 us  [send(): return lax.ppermute(value, 'seq', perm)]
  transfers between devices with their start and end apart: 16 -> 16, of which waited for: 9 -> 10; matrix products, arithmetic and copies ran while one was open for 0% -> 0% of each run, Pallas kernels for 14% -> 14%
where the time goes in v10:
time: 61.7 us; the launch traced here: 61.6 us
  waiting for transfers between devices  28.4 us (46%)
  starting transfers between devices  16.6 us (27%)
  Pallas kernels  15.6 us (25%)
  between operations  0.76 us (1%)
    ppermute x16, waiting for transfers between devices, send(): return lax.ppermute(value, 'seq', perm)  28.4 us
    ppermute x16, starting transfers between devices, send(): return lax.ppermute(value, 'seq', perm)  16.6 us
    pallas_call x1, Pallas kernels, shards(): pl.pallas_call(functools.partial(rest_kernel, devices, [[(0, x, c) for x...  5.35 us
    pallas_call x1, Pallas kernels, shards(): pl.pallas_call(load_kernel, out_shape=(pltpu.VMEM(acts.shape, jnp.bfloat1...  3.87 us
    pallas_call x3, Pallas kernels, px(): pl.pallas_call(functools.partial(px_kernel, devices, keys, before is None...  2.72 us
    pallas_call x1, Pallas kernels, shards(): pl.pallas_call(functools.partial(own_kernel, devices), out_shape=[jax.Sha...  2.65 us
  transfers between devices with their start and end apart: 16, of which 10 were waited for; matrix products, arithmetic and copies ran while one was open for 0% of the time, Pallas kernels for 14%

profile of v10, /device:TPU:0, one launch (start us, length us, event | category | flops | bytes accessed | tf_op | source)
XLA Modules:
  0.0 61.6 jit_solution(14289971320920497051)
XLA Ops:
  0.6 3.1 %collective-permute-start.1 = (bf16[512,128]{1,0:T(8,128)(2,1)}, bf16[512,128]{1,0:T(8,128)(2,1)S(1)}, u32[]{:S(2)}, u32[]{:S(2)}) collective-permute-start(bf16[512,128]{1,0:T(8,128)(2,1)} %proj_in.1), channel_id=1, source_target_pairs={{0,4},{1,5},{2,6},{3,7},{4,8},{5,9},{6,10},{7,11},{8,12},{9,13},{1... | collective-permute-start | bytes 393224 | tf_op jit(solution)/shard_map/ppermute | solution.py:45
  3.7 1.5 %collective-permute-start = (bf16[512,128]{1,0:T(8,128)(2,1)}, bf16[512,128]{1,0:T(8,128)(2,1)S(1)}, u32[]{:S(2)}, u32[]{:S(2)}) collective-permute-start(bf16[512,128]{1,0:T(8,128)(2,1)} %proj_in.1), channel_id=1, source_target_pairs={{0,2},{1,3},{2,0},{3,1},{4,6},{5,7},{6,4},{7,5},{8,10},{9,11},{10,... | collective-permute-start | bytes 393224 | tf_op jit(solution)/shard_map/ppermute | solution.py:45
  5.2 2.2 %collective-permute-start.2 = (bf16[512,128]{1,0:T(8,128)(2,1)}, bf16[512,128]{1,0:T(8,128)(2,1)S(1)}, u32[]{:S(2)}, u32[]{:S(2)}) collective-permute-start(bf16[512,128]{1,0:T(8,128)(2,1)} %proj_in.1), channel_id=1, source_target_pairs={{0,12},{1,13},{2,14},{3,15},{4,0},{5,1},{6,2},{7,3},{8,4},{9,5},{1... | collective-permute-start | bytes 393224 | tf_op jit(solution)/shard_map/ppermute | solution.py:45
  7.4 0.8 %collective-permute-start.4 = (bf16[512,128]{1,0:T(8,128)(2,1)}, bf16[512,128]{1,0:T(8,128)(2,1)S(1)}, u32[]{:S(2)}, u32[]{:S(2)}) collective-permute-start(bf16[512,128]{1,0:T(8,128)(2,1)} %proj_in.1), channel_id=1, source_target_pairs={{0,8},{1,9},{2,10},{3,11},{4,12},{5,13},{6,14},{7,15},{8,0},{9,1},... | collective-permute-start | bytes 393224 | tf_op jit(solution)/shard_map/ppermute | solution.py:45
  8.2 3.9 %load.1 = (bf16[2,256,8192]{2,1,0:T(8,128)(2,1)S(1)}, bf16[512,128]{1,0:T(8,128)(2,1)S(1)}, bf16[128,256]{1,0:T(8,128)(2,1)S(1)}) custom-call(bf16[2,256,8192]{2,1,0:T(8,128)(2,1)} %acts.1, bf16[2,256,1024]{2,1,0:T(8,128)(2,1)} %cots.1, bf16[512,128]{1,0:T(8,128)(2,1)} %proj_in.1, bf16[1024,128]{1,0:T(8,128)(2,1)} %proj_out.1), custom_call_target="tpu_custom_call" | custom-call | flops 1 | bytes 1 | tf_op jit(solution)/shard_map/load/pallas_call | solution.py:325
  12.1 0.1 collective-permute-done.2.refs_1_
  12.3 1.2 %collective-permute-start.3 = (bf16[1024,128]{1,0:T(8,128)(2,1)S(1)}, bf16[1024,128]{1,0:T(8,128)(2,1)S(1)}, u32[]{:S(2)}, u32[]{:S(2)}) collective-permute-start(bf16[1024,128]{1,0:T(8,128)(2,1)S(1)} %stack.3.refs_1_), channel_id=1, source_target_pairs={{0,2},{1,3},{2,0},{3,1},{4,6},{5,7},{6,4},{7,5},{8,10},{9,11},{10,... | collective-permute-start | bytes 786440 | tf_op jit(solution)/shard_map/ppermute | solution.py:45
  13.5 4.3 %collective-permute-done.4.refs_2_ = bf16[512,128]{1,0:T(8,128)(2,1)S(1)} collective-permute-done((bf16[512,128]{1,0:T(8,128)(2,1)}, bf16[512,128]{1,0:T(8,128)(2,1)S(1)}, u32[]{:S(2)}, u32[]{:S(2)}) %collective-permute-start.4) | collective-permute-done | bytes 131104 | tf_op jit(solution)/shard_map/ppermute | solution.py:45
  17.9 1.5 %collective-permute-start.5 = (bf16[512,128]{1,0:T(8,128)(2,1)S(1)}, bf16[512,128]{1,0:T(8,128)(2,1)S(1)}, u32[]{:S(2)}, u32[]{:S(2)}) collective-permute-start(bf16[512,128]{1,0:T(8,128)(2,1)S(1)} %collective-permute-done.4.refs_2_), channel_id=1, source_target_pairs={{0,2},{1,3},{2,0},{3,1},{4,6},{5,7},{6,4},{7,5},{8,10},{9,11},{10,... | collective-permute-start | bytes 393224 | tf_op jit(solution)/shard_map/ppermute | solution.py:45
  19.4 0.7 %px.3 = (f32[2,256,128]{2,1,0:T(8,128)S(1)}, bf16[2048,128]{1,0:T(8,128)(2,1)S(1)}) custom-call(bf16[2,256,8192]{2,1,0:T(8,128)(2,1)S(1)} %get-tuple-element.9.acts, bf16[512,128]{1,0:T(8,128)(2,1)S(1)} %get-tuple-element.11.refs_0_, bf16[1024,128]{1,0:T(8,128)(2,1)S(1)} %stack.3.refs_1_, bf16[512,128]{1,0:T(8,128)(2,1)S(1)} %collective-permute-done.4.refs_2_), custom_call_target="tpu_custom_call" | custom-call | flops 1 | bytes 1 | tf_op jit(solution)/shard_map/px/pallas_call | solution.py:361
  20.1 0.1 collective-permute-start.7
  20.2 3.2 %collective-permute-done.5.refs_2_ = bf16[512,128]{1,0:T(8,128)(2,1)S(1)} collective-permute-done((bf16[512,128]{1,0:T(8,128)(2,1)S(1)}, bf16[512,128]{1,0:T(8,128)(2,1)S(1)}, u32[]{:S(2)}, u32[]{:S(2)}) %collective-permute-start.5) | collective-permute-done | bytes 131104 | tf_op jit(solution)/shard_map/ppermute | solution.py:45
  23.4 0.1 collective-permute-start.6
  23.5 1.3 %px.4.refs_1_ = f32[2,256,128]{2,1,0:T(8,128)S(1)} custom-call(bf16[2,256,8192]{2,1,0:T(8,128)(2,1)S(1)} %get-tuple-element.9.acts, bf16[2048,128]{1,0:T(8,128)(2,1)S(1)} %stack.4.refs_0_, bf16[2048,128]{1,0:T(8,128)(2,1)S(1)} %collective-permute-done.7.refs_1_, f32[2,256,128]{2,1,0:T(8,128)S(1)} %get-tuple-element.12.refs_3_.refs_2_), custom_call_target="tpu_custom_call" | custom-call | flops 1 | bytes 1 | tf_op jit(solution)/shard_map/px/pallas_call | solution.py:361
  24.8 0.6 collective-permute-done.6.refs_0_
  25.4 0.7 %px.5.refs_0_ = bf16[512,128]{1,0:T(8,128)(2,1)S(1)} custom-call(bf16[2,256,8192]{2,1,0:T(8,128)(2,1)S(1)} %get-tuple-element.9.acts, bf16[2048,128]{1,0:T(8,128)(2,1)S(1)} %collective-permute-done.6.refs_0_, f32[2,256,128]{2,1,0:T(8,128)S(1)} %px.4.refs_1_, bf16[128,256]{1,0:T(8,128)(2,1)S(1)} %get-tuple-element.10.refs_2_), custom_call_target="tpu_custom_call" | custom-call | flops 1 | bytes 1 | tf_op jit(solution)/shard_map/px/pallas_call | solution.py:361
  26.1 1.3 %collective-permute-start.8 = (bf16[512,128]{1,0:T(8,128)(2,1)S(1)}, bf16[512,128]{1,0:T(8,128)(2,1)S(1)}, u32[]{:S(2)}, u32[]{:S(2)}) collective-permute-start(bf16[512,128]{1,0:T(8,128)(2,1)S(1)} %px.5.refs_0_), channel_id=1, source_target_pairs={{0,2},{1,3},{2,0},{3,1},{4,6},{5,7},{6,4},{7,5},{8,10},{9,11},{10,... | collective-permute-start | bytes 393224 | tf_op jit(solution)/shard_map/ppermute | solution.py:45
  27.3 4.3 %collective-permute-done.8.refs_1_ = bf16[512,128]{1,0:T(8,128)(2,1)S(1)} collective-permute-done((bf16[512,128]{1,0:T(8,128)(2,1)S(1)}, bf16[512,128]{1,0:T(8,128)(2,1)S(1)}, u32[]{:S(2)}, u32[]{:S(2)}) %collective-permute-start.8) | collective-permute-done | bytes 131104 | tf_op jit(solution)/shard_map/ppermute | solution.py:45
  31.7 1.3 %collective-permute-done.10.refs_3_ = bf16[512,128]{1,0:T(8,128)(2,1)S(1)} collective-permute-done((bf16[512,128]{1,0:T(8,128)(2,1)S(1)}, bf16[512,128]{1,0:T(8,128)(2,1)S(1)}, u32[]{:S(2)}, u32[]{:S(2)}) %collective-permute-start.10) | collective-permute-done | bytes 131104 | tf_op jit(solution)/shard_map/ppermute | solution.py:45
  33.0 0.9 %grads.1.refs_0_ = bf16[32,2048]{1,0:T(8,128)(2,1)S(1)} custom-call(bf16[512,128]{1,0:T(8,128)(2,1)S(1)} %px.5.refs_0_, bf16[512,128]{1,0:T(8,128)(2,1)S(1)} %collective-permute-done.8.refs_1_, bf16[512,128]{1,0:T(8,128)(2,1)S(1)} %collective-permute-done.9.refs_2_, bf16[512,128]{1,0:T(8,128)(2,1)S(1)} %collective-permute-done.10.refs_3_, s32[1,32]{1,0:T(1,128)S(1)} %copy-done.1), custom_call_target="tpu_custom_call" | custom-call | tf_op jit(solution)/shard_map/grads/pallas_call | solution.py:411
  34.0 2.0 %collective-permute-start.13 = (bf16[32,2048]{1,0:T(8,128)(2,1)S(1)}, bf16[32,2048]{1,0:T(8,128)(2,1)S(1)}, u32[]{:S(2)}, u32[]{:S(2)}) collective-permute-start(bf16[32,2048]{1,0:T(8,128)(2,1)S(1)} %grads.1.refs_0_), channel_id=1, source_target_pairs={{0,12},{1,13},{2,14},{3,15},{4,0},{5,1},{6,2},{7,3},{8,4},{9,5},{1... | collective-permute-start | bytes 393224 | tf_op jit(solution)/shard_map/ppermute | solution.py:45
  36.0 1.6 %collective-permute-start.12 = (bf16[32,2048]{1,0:T(8,128)(2,1)S(1)}, bf16[32,2048]{1,0:T(8,128)(2,1)S(1)}, u32[]{:S(2)}, u32[]{:S(2)}) collective-permute-start(bf16[32,2048]{1,0:T(8,128)(2,1)S(1)} %grads.1.refs_0_), channel_id=1, source_target_pairs={{0,8},{1,9},{2,10},{3,11},{4,12},{5,13},{6,14},{7,15},{8,0},{9,1},... | collective-permute-start | bytes 393224 | tf_op jit(solution)/shard_map/ppermute | solution.py:45
  37.5 0.2 collective-permute-start.11
  37.7 2.1 %collective-permute-done.13.refs_3_ = bf16[32,2048]{1,0:T(8,128)(2,1)S(1)} collective-permute-done((bf16[32,2048]{1,0:T(8,128)(2,1)S(1)}, bf16[32,2048]{1,0:T(8,128)(2,1)S(1)}, u32[]{:S(2)}, u32[]{:S(2)}) %collective-permute-start.13) | collective-permute-done | bytes 131104 | tf_op jit(solution)/shard_map/ppermute | solution.py:45
  39.9 9.6 %collective-permute-done.12.refs_2_ = bf16[32,2048]{1,0:T(8,128)(2,1)S(1)} collective-permute-done((bf16[32,2048]{1,0:T(8,128)(2,1)S(1)}, bf16[32,2048]{1,0:T(8,128)(2,1)S(1)}, u32[]{:S(2)}, u32[]{:S(2)}) %collective-permute-start.12) | collective-permute-done | bytes 131104 | tf_op jit(solution)/shard_map/ppermute | solution.py:45
  49.6 1.0 %collective-permute-start.14 = (bf16[32,2048]{1,0:T(8,128)(2,1)S(1)}, bf16[32,2048]{1,0:T(8,128)(2,1)S(1)}, u32[]{:S(2)}, u32[]{:S(2)}) collective-permute-start(bf16[32,2048]{1,0:T(8,128)(2,1)S(1)} %total.1.mine.refs_0_), channel_id=1, source_target_pairs={{0,2},{1,3},{2,0},{3,1},{4,6},{5,7},{6,4},{7,5},{8,10},{9,11},{10,... | collective-permute-start | bytes 393224 | tf_op jit(solution)/shard_map/ppermute | solution.py:45
  50.6 0.1 copy.10.pairs.refs_3_
  50.7 2.6 %own.1 = (f32[8,128]{1,0:T(8,128)S(1)}, f32[3,256,4096]{2,1,0:T(8,128)}) custom-call(bf16[32,2048]{1,0:T(8,128)(2,1)S(1)} %total.1.mine.refs_0_, s32[3,2]{1,0:T(4,128)S(1)} %copy.10.pairs.refs_3_), custom_call_target="tpu_custom_call" | custom-call | flops 50331648 | bytes 3145728 | tf_op jit(solution)/shard_map/own/pallas_call | solution.py:434
  53.3 1.3 %collective-permute-done.14.refs_1_ = bf16[32,2048]{1,0:T(8,128)(2,1)S(1)} collective-permute-done((bf16[32,2048]{1,0:T(8,128)(2,1)S(1)}, bf16[32,2048]{1,0:T(8,128)(2,1)S(1)}, u32[]{:S(2)}, u32[]{:S(2)}) %collective-permute-start.14) | collective-permute-done | bytes 131104 | tf_op jit(solution)/shard_map/ppermute | solution.py:45
  54.6 0.1 collective-permute-start.15
  54.7 1.5 %collective-permute-done.15.refs_1_ = bf16[64,2048]{1,0:T(8,128)(2,1)S(1)} collective-permute-done((bf16[64,2048]{1,0:T(8,128)(2,1)S(1)}, bf16[64,2048]{1,0:T(8,128)(2,1)S(1)}, u32[]{:S(2)}, u32[]{:S(2)}) %collective-permute-start.15) | collective-permute-done | bytes 262176 | tf_op jit(solution)/shard_map/ppermute | solution.py:45
  56.2 5.3 %rest.1 = (bf16[2,8192]{1,0:T(2,128)(2,1)}, f32[3,256,4096]{2,1,0:T(8,128)}) custom-call(bf16[64,2048]{1,0:T(8,128)(2,1)S(1)} %stack.5.refs_0_, bf16[64,2048]{1,0:T(8,128)(2,1)S(1)} %collective-permute-done.15.refs_1_, s32[1,32]{1,0:T(1,128)S(1)} %bitcast.1, s32[3,2]{1,0:T(4,128)S(1)} %copy.10.pairs.refs_3_, ...), custom_call_target="tpu_custom_call", output_to_operand_aliasing={{1}: (4, {})} | custom-call | tf_op jit(solution)/shard_map/rest/pallas_call | solution.py:451
  (18 shorter events, 0.2 us)
Async XLA Ops:
  0.6 11.5 %collective-permute-start.1 = (bf16[512,128]{1,0:T(8,128)(2,1)}, bf16[512,128]{1,0:T(8,128)(2,1)S(1)}, u32[]{:S(2)}, u32[]{:S(2)}) collective-permute-start(bf16[512,128]{1,0:T(8,128)(2,1)} %proj_in.1), channel_id=1, source_target_pairs={{0,4},{1,5},{2,6},{3,7},{4,8},{5,9},{6,10},{7,11},{8,12},{9,13},{1... | collective-permute-start | bytes 393224 | tf_op jit(solution)/shard_map/ppermute | solution.py:45
  3.7 8.4 %collective-permute-start = (bf16[512,128]{1,0:T(8,128)(2,1)}, bf16[512,128]{1,0:T(8,128)(2,1)S(1)}, u32[]{:S(2)}, u32[]{:S(2)}) collective-permute-start(bf16[512,128]{1,0:T(8,128)(2,1)} %proj_in.1), channel_id=1, source_target_pairs={{0,2},{1,3},{2,0},{3,1},{4,6},{5,7},{6,4},{7,5},{8,10},{9,11},{10,... | collective-permute-start | bytes 393224 | tf_op jit(solution)/shard_map/ppermute | solution.py:45
  5.2 7.0 %collective-permute-start.2 = (bf16[512,128]{1,0:T(8,128)(2,1)}, bf16[512,128]{1,0:T(8,128)(2,1)S(1)}, u32[]{:S(2)}, u32[]{:S(2)}) collective-permute-start(bf16[512,128]{1,0:T(8,128)(2,1)} %proj_in.1), channel_id=1, source_target_pairs={{0,12},{1,13},{2,14},{3,15},{4,0},{5,1},{6,2},{7,3},{8,4},{9,5},{1... | collective-permute-start | bytes 393224 | tf_op jit(solution)/shard_map/ppermute | solution.py:45
  7.4 10.4 %collective-permute-start.4 = (bf16[512,128]{1,0:T(8,128)(2,1)}, bf16[512,128]{1,0:T(8,128)(2,1)S(1)}, u32[]{:S(2)}, u32[]{:S(2)}) collective-permute-start(bf16[512,128]{1,0:T(8,128)(2,1)} %proj_in.1), channel_id=1, source_target_pairs={{0,8},{1,9},{2,10},{3,11},{4,12},{5,13},{6,14},{7,15},{8,0},{9,1},... | collective-permute-start | bytes 393224 | tf_op jit(solution)/shard_map/ppermute | solution.py:45
  12.3 11.1 %collective-permute-start.3 = (bf16[1024,128]{1,0:T(8,128)(2,1)S(1)}, bf16[1024,128]{1,0:T(8,128)(2,1)S(1)}, u32[]{:S(2)}, u32[]{:S(2)}) collective-permute-start(bf16[1024,128]{1,0:T(8,128)(2,1)S(1)} %stack.3.refs_1_), channel_id=1, source_target_pairs={{0,2},{1,3},{2,0},{3,1},{4,6},{5,7},{6,4},{7,5},{8,10},{9,11},{10,... | collective-permute-start | bytes 786440 | tf_op jit(solution)/shard_map/ppermute | solution.py:45
  17.9 5.5 %collective-permute-start.5 = (bf16[512,128]{1,0:T(8,128)(2,1)S(1)}, bf16[512,128]{1,0:T(8,128)(2,1)S(1)}, u32[]{:S(2)}, u32[]{:S(2)}) collective-permute-start(bf16[512,128]{1,0:T(8,128)(2,1)S(1)} %collective-permute-done.4.refs_2_), channel_id=1, source_target_pairs={{0,2},{1,3},{2,0},{3,1},{4,6},{5,7},{6,4},{7,5},{8,10},{9,11},{10,... | collective-permute-start | bytes 393224 | tf_op jit(solution)/shard_map/ppermute | solution.py:45
  19.4 13.7 %copy-start.1 = (s32[1,32]{1,0:T(1,128)S(1)}, s32[1,32]{1,0:T(1,128)}, u32[]{:S(2)}) copy-start(s32[1,32]{1,0:T(1,128)} %refs_4_.1) | copy-start | bytes 388
  20.1 30.5 %copy-start.2 = (s32[3,2]{0,1:T(2,128)S(1)}, s32[3,2]{0,1:T(2,128)}, u32[]{:S(2)}) copy-start(s32[3,2]{0,1:T(2,128)} %param.13) | copy-start | bytes 76
  20.1 36.1 %copy-start = (s32[32]{0:T(128)S(1)}, s32[32]{0:T(128)}, u32[]{:S(2)}) copy-start(s32[32]{0:T(128)} %param.12) | copy-start | bytes 388
  20.1 3.4 %collective-permute-start.7 = (bf16[2048,128]{1,0:T(8,128)(2,1)S(1)}, bf16[2048,128]{1,0:T(8,128)(2,1)S(1)}, u32[]{:S(2)}, u32[]{:S(2)}) collective-permute-start(bf16[2048,128]{1,0:T(8,128)(2,1)S(1)} %get-tuple-element.13), channel_id=1, source_target_pairs={{0,1},{1,0},{2,3},{3,2},{4,5},{5,4},{6,7},{7,6},{8,9},{9,8},{10,11... | collective-permute-start | bytes 1572872 | tf_op jit(solution)/shard_map/ppermute | solution.py:45
  23.4 2.0 %collective-permute-start.6 = (bf16[2048,128]{1,0:T(8,128)(2,1)S(1)}, bf16[2048,128]{1,0:T(8,128)(2,1)S(1)}, u32[]{:S(2)}, u32[]{:S(2)}) collective-permute-start(bf16[2048,128]{1,0:T(8,128)(2,1)S(1)} %stack.4.refs_0_), channel_id=1, source_target_pairs={{0,1},{1,0},{2,3},{3,2},{4,5},{5,4},{6,7},{7,6},{8,9},{9,8},{10,11... | collective-permute-start | bytes 1572872 | tf_op jit(solution)/shard_map/ppermute | solution.py:45
  26.1 5.6 %collective-permute-start.8 = (bf16[512,128]{1,0:T(8,128)(2,1)S(1)}, bf16[512,128]{1,0:T(8,128)(2,1)S(1)}, u32[]{:S(2)}, u32[]{:S(2)}) collective-permute-start(bf16[512,128]{1,0:T(8,128)(2,1)S(1)} %px.5.refs_0_), channel_id=1, source_target_pairs={{0,2},{1,3},{2,0},{3,1},{4,6},{5,7},{6,4},{7,5},{8,10},{9,11},{10,... | collective-permute-start | bytes 393224 | tf_op jit(solution)/shard_map/ppermute | solution.py:45
  27.3 4.4 %collective-permute-start.9 = (bf16[512,128]{1,0:T(8,128)(2,1)S(1)}, bf16[512,128]{1,0:T(8,128)(2,1)S(1)}, u32[]{:S(2)}, u32[]{:S(2)}) collective-permute-start(bf16[512,128]{1,0:T(8,128)(2,1)S(1)} %px.5.refs_0_), channel_id=1, source_target_pairs={{0,1},{1,0},{2,3},{3,2},{4,5},{5,4},{6,7},{7,6},{8,9},{9,8},{10,11... | collective-permute-start | bytes 393224 | tf_op jit(solution)/shard_map/ppermute | solution.py:45
  31.7 1.3 %collective-permute-start.10 = (bf16[512,128]{1,0:T(8,128)(2,1)S(1)}, bf16[512,128]{1,0:T(8,128)(2,1)S(1)}, u32[]{:S(2)}, u32[]{:S(2)}) collective-permute-start(bf16[512,128]{1,0:T(8,128)(2,1)S(1)} %collective-permute-done.8.refs_1_), channel_id=1, source_target_pairs={{0,1},{1,0},{2,3},{3,2},{4,5},{5,4},{6,7},{7,6},{8,9},{9,8},{10,11... | collective-permute-start | bytes 393224 | tf_op jit(solution)/shard_map/ppermute | solution.py:45
  34.0 5.9 %collective-permute-start.13 = (bf16[32,2048]{1,0:T(8,128)(2,1)S(1)}, bf16[32,2048]{1,0:T(8,128)(2,1)S(1)}, u32[]{:S(2)}, u32[]{:S(2)}) collective-permute-start(bf16[32,2048]{1,0:T(8,128)(2,1)S(1)} %grads.1.refs_0_), channel_id=1, source_target_pairs={{0,12},{1,13},{2,14},{3,15},{4,0},{5,1},{6,2},{7,3},{8,4},{9,5},{1... | collective-permute-start | bytes 393224 | tf_op jit(solution)/shard_map/ppermute | solution.py:45
  36.0 13.5 %collective-permute-start.12 = (bf16[32,2048]{1,0:T(8,128)(2,1)S(1)}, bf16[32,2048]{1,0:T(8,128)(2,1)S(1)}, u32[]{:S(2)}, u32[]{:S(2)}) collective-permute-start(bf16[32,2048]{1,0:T(8,128)(2,1)S(1)} %grads.1.refs_0_), channel_id=1, source_target_pairs={{0,8},{1,9},{2,10},{3,11},{4,12},{5,13},{6,14},{7,15},{8,0},{9,1},... | collective-permute-start | bytes 393224 | tf_op jit(solution)/shard_map/ppermute | solution.py:45
  37.5 12.0 %collective-permute-start.11 = (bf16[32,2048]{1,0:T(8,128)(2,1)S(1)}, bf16[32,2048]{1,0:T(8,128)(2,1)S(1)}, u32[]{:S(2)}, u32[]{:S(2)}) collective-permute-start(bf16[32,2048]{1,0:T(8,128)(2,1)S(1)} %grads.1.refs_0_), channel_id=1, source_target_pairs={{0,4},{1,5},{2,6},{3,7},{4,8},{5,9},{6,10},{7,11},{8,12},{9,13},{1... | collective-permute-start | bytes 393224 | tf_op jit(solution)/shard_map/ppermute | solution.py:45
  49.6 5.0 %collective-permute-start.14 = (bf16[32,2048]{1,0:T(8,128)(2,1)S(1)}, bf16[32,2048]{1,0:T(8,128)(2,1)S(1)}, u32[]{:S(2)}, u32[]{:S(2)}) collective-permute-start(bf16[32,2048]{1,0:T(8,128)(2,1)S(1)} %total.1.mine.refs_0_), channel_id=1, source_target_pairs={{0,2},{1,3},{2,0},{3,1},{4,6},{5,7},{6,4},{7,5},{8,10},{9,11},{10,... | collective-permute-start | bytes 393224 | tf_op jit(solution)/shard_map/ppermute | solution.py:45
  54.6 1.6 %collective-permute-start.15 = (bf16[64,2048]{1,0:T(8,128)(2,1)S(1)}, bf16[64,2048]{1,0:T(8,128)(2,1)S(1)}, u32[]{:S(2)}, u32[]{:S(2)}) collective-permute-start(bf16[64,2048]{1,0:T(8,128)(2,1)S(1)} %stack.5.refs_0_), channel_id=1, source_target_pairs={{0,1},{1,0},{2,3},{3,2},{4,5},{5,4},{6,7},{7,6},{8,9},{9,8},{10,11... | collective-permute-start | bytes 786440 | tf_op jit(solution)/shard_map/ppermute | solution.py:45

commit v11 on v10

--- a/solution.py
+++ b/solution.py
@@ -35,12 +35,17 @@
     return (z * wide + x) * cores + core
 
 
-def send(value, devices, shift):
+def flipped(z, shift, deep):
+    return z ^ shift if deep & (deep - 1) == 0 else (z + shift) % deep
+
+
+def send(value, devices, shift, pair=False):
     deep, wide, cores = levels(devices)
     perm = []
     for i in range(devices):
         z, x, core = place(i, devices)
-        z, x, core = (z + shift[0]) % deep, (x + shift[1]) % wide, (core + shift[2]) % cores
+        z = flipped(z, shift[0], deep) if pair else (z + shift[0]) % deep
+        x, core = (x + shift[1]) % wide, (core + shift[2]) % cores
         perm.append((i, (z * wide + x) * cores + core))
     return lax.ppermute(value, "seq", perm)
 
@@ -186,7 +191,10 @@
         out[...] = total.astype(jnp.bfloat16)
         return
     me = lax.axis_index("seq")
-    owned = [owner(me, devices, (shift, 0, 0)) // per_part for shift in range(deep)]
+    line = across * cores
+    power = deep & (deep - 1) == 0
+    homes = [flipped(me // line, shift if power else deep - shift, deep) for shift in range(deep)]
+    owned = [(home * line + me % line) // per_part for home in homes]
     for row in range(out.shape[0] // tall):
         total = jnp.zeros(terms[0].shape, jnp.float32)
         for home, term in zip(owned, terms):
@@ -417,7 +425,7 @@
         compiler_params=params,
         name="grads",
     )(*feats.values(), lengths)
-    terms = [send(sums, devices, (z, 0, 0)) if z else sums for z in range(deep)]
+    terms = [send(sums, devices, (z, 0, 0), pair=True) if z else sums for z in range(deep)]
     total = pl.pallas_call(
         functools.partial(total_kernel, devices, per_part),
         out_shape=jax.ShapeDtypeStruct((seqs, lanes), jnp.bfloat16),

time: 61.7 us -> 61.9 us (level)
  starting transfers between devices: 16.6 us -> 17.3 us
    ppermute x16, starting transfers between devices: 16.6 us -> 17.3 us  [send(): return lax.ppermute(value, 'seq', perm)]
where the time goes in v11:
time: 61.9 us; the launch traced here: 61.7 us
  waiting for transfers between devices  27.9 us (45%)
  starting transfers between devices  17.3 us (28%)
  Pallas kernels  15.6 us (25%)
  between operations  0.76 us (1%)
    ppermute x16, waiting for transfers between devices, send(): return lax.ppermute(value, 'seq', perm)  27.9 us
    ppermute x16, starting transfers between devices, send(): return lax.ppermute(value, 'seq', perm)  17.3 us
    pallas_call x1, Pallas kernels, shards(): pl.pallas_call(functools.partial(rest_kernel, devices, [[(0, x, c) for x...  5.35 us
    pallas_call x1, Pallas kernels, shards(): pl.pallas_call(load_kernel, out_shape=(pltpu.VMEM(acts.shape, jnp.bfloat1...  3.87 us
    pallas_call x3, Pallas kernels, px(): pl.pallas_call(functools.partial(px_kernel, devices, keys, before is None...  2.72 us
    pallas_call x1, Pallas kernels, shards(): pl.pallas_call(functools.partial(own_kernel, devices), out_shape=[jax.Sha...  2.65 us
  transfers between devices with their start and end apart: 16, of which 10 were waited for; matrix products, arithmetic and copies ran while one was open for 0% of the time, Pallas kernels for 14%

profile of v11, /device:TPU:0, one launch (start us, length us, event | category | flops | bytes accessed | tf_op | source)
XLA Modules:
  0.0 61.7 jit_solution(1255337909304401396)
XLA Ops:
  0.6 3.1 %collective-permute-start.1 = (bf16[512,128]{1,0:T(8,128)(2,1)}, bf16[512,128]{1,0:T(8,128)(2,1)S(1)}, u32[]{:S(2)}, u32[]{:S(2)}) collective-permute-start(bf16[512,128]{1,0:T(8,128)(2,1)} %proj_in.1), channel_id=1, source_target_pairs={{0,4},{1,5},{2,6},{3,7},{4,8},{5,9},{6,10},{7,11},{8,12},{9,13},{1... | collective-permute-start | bytes 393224 | tf_op jit(solution)/shard_map/ppermute | solution.py:50
  3.7 1.5 %collective-permute-start = (bf16[512,128]{1,0:T(8,128)(2,1)}, bf16[512,128]{1,0:T(8,128)(2,1)S(1)}, u32[]{:S(2)}, u32[]{:S(2)}) collective-permute-start(bf16[512,128]{1,0:T(8,128)(2,1)} %proj_in.1), channel_id=1, source_target_pairs={{0,2},{1,3},{2,0},{3,1},{4,6},{5,7},{6,4},{7,5},{8,10},{9,11},{10,... | collective-permute-start | bytes 393224 | tf_op jit(solution)/shard_map/ppermute | solution.py:50
  5.2 2.2 %collective-permute-start.2 = (bf16[512,128]{1,0:T(8,128)(2,1)}, bf16[512,128]{1,0:T(8,128)(2,1)S(1)}, u32[]{:S(2)}, u32[]{:S(2)}) collective-permute-start(bf16[512,128]{1,0:T(8,128)(2,1)} %proj_in.1), channel_id=1, source_target_pairs={{0,12},{1,13},{2,14},{3,15},{4,0},{5,1},{6,2},{7,3},{8,4},{9,5},{1... | collective-permute-start | bytes 393224 | tf_op jit(solution)/shard_map/ppermute | solution.py:50
  7.4 0.8 %collective-permute-start.4 = (bf16[512,128]{1,0:T(8,128)(2,1)}, bf16[512,128]{1,0:T(8,128)(2,1)S(1)}, u32[]{:S(2)}, u32[]{:S(2)}) collective-permute-start(bf16[512,128]{1,0:T(8,128)(2,1)} %proj_in.1), channel_id=1, source_target_pairs={{0,8},{1,9},{2,10},{3,11},{4,12},{5,13},{6,14},{7,15},{8,0},{9,1},... | collective-permute-start | bytes 393224 | tf_op jit(solution)/shard_map/ppermute | solution.py:50
  8.2 3.9 %load.1 = (bf16[2,256,8192]{2,1,0:T(8,128)(2,1)S(1)}, bf16[512,128]{1,0:T(8,128)(2,1)S(1)}, bf16[128,256]{1,0:T(8,128)(2,1)S(1)}) custom-call(bf16[2,256,8192]{2,1,0:T(8,128)(2,1)} %acts.1, bf16[2,256,1024]{2,1,0:T(8,128)(2,1)} %cots.1, bf16[512,128]{1,0:T(8,128)(2,1)} %proj_in.1, bf16[1024,128]{1,0:T(8,128)(2,1)} %proj_out.1), custom_call_target="tpu_custom_call" | custom-call | flops 1 | bytes 1 | tf_op jit(solution)/shard_map/load/pallas_call | solution.py:333
  12.1 0.1 collective-permute-done.2.refs_1_
  12.3 1.2 %collective-permute-start.3 = (bf16[1024,128]{1,0:T(8,128)(2,1)S(1)}, bf16[1024,128]{1,0:T(8,128)(2,1)S(1)}, u32[]{:S(2)}, u32[]{:S(2)}) collective-permute-start(bf16[1024,128]{1,0:T(8,128)(2,1)S(1)} %stack.3.refs_1_), channel_id=1, source_target_pairs={{0,2},{1,3},{2,0},{3,1},{4,6},{5,7},{6,4},{7,5},{8,10},{9,11},{10,... | collective-permute-start | bytes 786440 | tf_op jit(solution)/shard_map/ppermute | solution.py:50
  13.5 4.3 %collective-permute-done.4.refs_2_ = bf16[512,128]{1,0:T(8,128)(2,1)S(1)} collective-permute-done((bf16[512,128]{1,0:T(8,128)(2,1)}, bf16[512,128]{1,0:T(8,128)(2,1)S(1)}, u32[]{:S(2)}, u32[]{:S(2)}) %collective-permute-start.4) | collective-permute-done | bytes 131104 | tf_op jit(solution)/shard_map/ppermute | solution.py:50
  17.9 1.5 %collective-permute-start.5 = (bf16[512,128]{1,0:T(8,128)(2,1)S(1)}, bf16[512,128]{1,0:T(8,128)(2,1)S(1)}, u32[]{:S(2)}, u32[]{:S(2)}) collective-permute-start(bf16[512,128]{1,0:T(8,128)(2,1)S(1)} %collective-permute-done.4.refs_2_), channel_id=1, source_target_pairs={{0,2},{1,3},{2,0},{3,1},{4,6},{5,7},{6,4},{7,5},{8,10},{9,11},{10,... | collective-permute-start | bytes 393224 | tf_op jit(solution)/shard_map/ppermute | solution.py:50
  19.4 0.7 %px.3 = (f32[2,256,128]{2,1,0:T(8,128)S(1)}, bf16[2048,128]{1,0:T(8,128)(2,1)S(1)}) custom-call(bf16[2,256,8192]{2,1,0:T(8,128)(2,1)S(1)} %get-tuple-element.9.acts, bf16[512,128]{1,0:T(8,128)(2,1)S(1)} %get-tuple-element.11.refs_0_, bf16[1024,128]{1,0:T(8,128)(2,1)S(1)} %stack.3.refs_1_, bf16[512,128]{1,0:T(8,128)(2,1)S(1)} %collective-permute-done.4.refs_2_), custom_call_target="tpu_custom_call" | custom-call | flops 1 | bytes 1 | tf_op jit(solution)/shard_map/px/pallas_call | solution.py:369
  20.1 0.1 collective-permute-start.7
  20.2 3.2 %collective-permute-done.5.refs_2_ = bf16[512,128]{1,0:T(8,128)(2,1)S(1)} collective-permute-done((bf16[512,128]{1,0:T(8,128)(2,1)S(1)}, bf16[512,128]{1,0:T(8,128)(2,1)S(1)}, u32[]{:S(2)}, u32[]{:S(2)}) %collective-permute-start.5) | collective-permute-done | bytes 131104 | tf_op jit(solution)/shard_map/ppermute | solution.py:50
  23.4 0.1 collective-permute-start.6
  23.5 1.3 %px.4.refs_1_ = f32[2,256,128]{2,1,0:T(8,128)S(1)} custom-call(bf16[2,256,8192]{2,1,0:T(8,128)(2,1)S(1)} %get-tuple-element.9.acts, bf16[2048,128]{1,0:T(8,128)(2,1)S(1)} %stack.4.refs_0_, bf16[2048,128]{1,0:T(8,128)(2,1)S(1)} %collective-permute-done.7.refs_1_, f32[2,256,128]{2,1,0:T(8,128)S(1)} %get-tuple-element.12.refs_3_.refs_2_), custom_call_target="tpu_custom_call" | custom-call | flops 1 | bytes 1 | tf_op jit(solution)/shard_map/px/pallas_call | solution.py:369
  24.8 0.6 collective-permute-done.6.refs_0_
  25.4 0.7 %px.5.refs_0_ = bf16[512,128]{1,0:T(8,128)(2,1)S(1)} custom-call(bf16[2,256,8192]{2,1,0:T(8,128)(2,1)S(1)} %get-tuple-element.9.acts, bf16[2048,128]{1,0:T(8,128)(2,1)S(1)} %collective-permute-done.6.refs_0_, f32[2,256,128]{2,1,0:T(8,128)S(1)} %px.4.refs_1_, bf16[128,256]{1,0:T(8,128)(2,1)S(1)} %get-tuple-element.10.refs_2_), custom_call_target="tpu_custom_call" | custom-call | flops 1 | bytes 1 | tf_op jit(solution)/shard_map/px/pallas_call | solution.py:369
  26.1 1.3 %collective-permute-start.8 = (bf16[512,128]{1,0:T(8,128)(2,1)S(1)}, bf16[512,128]{1,0:T(8,128)(2,1)S(1)}, u32[]{:S(2)}, u32[]{:S(2)}) collective-permute-start(bf16[512,128]{1,0:T(8,128)(2,1)S(1)} %px.5.refs_0_), channel_id=1, source_target_pairs={{0,2},{1,3},{2,0},{3,1},{4,6},{5,7},{6,4},{7,5},{8,10},{9,11},{10,... | collective-permute-start | bytes 393224 | tf_op jit(solution)/shard_map/ppermute | solution.py:50
  27.3 4.3 %collective-permute-done.8.refs_1_ = bf16[512,128]{1,0:T(8,128)(2,1)S(1)} collective-permute-done((bf16[512,128]{1,0:T(8,128)(2,1)S(1)}, bf16[512,128]{1,0:T(8,128)(2,1)S(1)}, u32[]{:S(2)}, u32[]{:S(2)}) %collective-permute-start.8) | collective-permute-done | bytes 131104 | tf_op jit(solution)/shard_map/ppermute | solution.py:50
  31.7 1.3 %collective-permute-done.10.refs_3_ = bf16[512,128]{1,0:T(8,128)(2,1)S(1)} collective-permute-done((bf16[512,128]{1,0:T(8,128)(2,1)S(1)}, bf16[512,128]{1,0:T(8,128)(2,1)S(1)}, u32[]{:S(2)}, u32[]{:S(2)}) %collective-permute-start.10) | collective-permute-done | bytes 131104 | tf_op jit(solution)/shard_map/ppermute | solution.py:50
  33.0 0.9 %grads.1.refs_0_ = bf16[32,2048]{1,0:T(8,128)(2,1)S(1)} custom-call(bf16[512,128]{1,0:T(8,128)(2,1)S(1)} %px.5.refs_0_, bf16[512,128]{1,0:T(8,128)(2,1)S(1)} %collective-permute-done.8.refs_1_, bf16[512,128]{1,0:T(8,128)(2,1)S(1)} %collective-permute-done.9.refs_2_, bf16[512,128]{1,0:T(8,128)(2,1)S(1)} %collective-permute-done.10.refs_3_, s32[1,32]{1,0:T(1,128)S(1)} %copy-done.1), custom_call_target="tpu_custom_call" | custom-call | tf_op jit(solution)/shard_map/grads/pallas_call | solution.py:419
  34.0 2.0 %collective-permute-start.13 = (bf16[32,2048]{1,0:T(8,128)(2,1)S(1)}, bf16[32,2048]{1,0:T(8,128)(2,1)S(1)}, u32[]{:S(2)}, u32[]{:S(2)}) collective-permute-start(bf16[32,2048]{1,0:T(8,128)(2,1)S(1)} %grads.1.refs_0_), channel_id=1, source_target_pairs={{0,12},{1,13},{2,14},{3,15},{4,8},{5,9},{6,10},{7,11},{8,4},{9,5},... | collective-permute-start | bytes 393224 | tf_op jit(solution)/shard_map/ppermute | solution.py:50
  36.0 1.6 %collective-permute-start.12 = (bf16[32,2048]{1,0:T(8,128)(2,1)S(1)}, bf16[32,2048]{1,0:T(8,128)(2,1)S(1)}, u32[]{:S(2)}, u32[]{:S(2)}) collective-permute-start(bf16[32,2048]{1,0:T(8,128)(2,1)S(1)} %grads.1.refs_0_), channel_id=1, source_target_pairs={{0,8},{1,9},{2,10},{3,11},{4,12},{5,13},{6,14},{7,15},{8,0},{9,1},... | collective-permute-start | bytes 393224 | tf_op jit(solution)/shard_map/ppermute | solution.py:50
  37.5 0.9 %collective-permute-start.11 = (bf16[32,2048]{1,0:T(8,128)(2,1)S(1)}, bf16[32,2048]{1,0:T(8,128)(2,1)S(1)}, u32[]{:S(2)}, u32[]{:S(2)}) collective-permute-start(bf16[32,2048]{1,0:T(8,128)(2,1)S(1)} %grads.1.refs_0_), channel_id=1, source_target_pairs={{0,4},{1,5},{2,6},{3,7},{4,0},{5,1},{6,2},{7,3},{8,12},{9,13},{10,... | collective-permute-start | bytes 393224 | tf_op jit(solution)/shard_map/ppermute | solution.py:50
  38.4 3.9 %collective-permute-done.13.refs_3_ = bf16[32,2048]{1,0:T(8,128)(2,1)S(1)} collective-permute-done((bf16[32,2048]{1,0:T(8,128)(2,1)S(1)}, bf16[32,2048]{1,0:T(8,128)(2,1)S(1)}, u32[]{:S(2)}, u32[]{:S(2)}) %collective-permute-start.13) | collective-permute-done | bytes 131104 | tf_op jit(solution)/shard_map/ppermute | solution.py:50
  42.3 7.2 %collective-permute-done.12.refs_2_ = bf16[32,2048]{1,0:T(8,128)(2,1)S(1)} collective-permute-done((bf16[32,2048]{1,0:T(8,128)(2,1)S(1)}, bf16[32,2048]{1,0:T(8,128)(2,1)S(1)}, u32[]{:S(2)}, u32[]{:S(2)}) %collective-permute-start.12) | collective-permute-done | bytes 131104 | tf_op jit(solution)/shard_map/ppermute | solution.py:50
  49.6 1.0 %collective-permute-start.14 = (bf16[32,2048]{1,0:T(8,128)(2,1)S(1)}, bf16[32,2048]{1,0:T(8,128)(2,1)S(1)}, u32[]{:S(2)}, u32[]{:S(2)}) collective-permute-start(bf16[32,2048]{1,0:T(8,128)(2,1)S(1)} %total.1.mine.refs_0_), channel_id=1, source_target_pairs={{0,2},{1,3},{2,0},{3,1},{4,6},{5,7},{6,4},{7,5},{8,10},{9,11},{10,... | collective-permute-start | bytes 393224 | tf_op jit(solution)/shard_map/ppermute | solution.py:50
  50.6 0.1 copy.10.pairs.refs_3_
  50.7 2.7 %own.1 = (f32[8,128]{1,0:T(8,128)S(1)}, f32[3,256,4096]{2,1,0:T(8,128)}) custom-call(bf16[32,2048]{1,0:T(8,128)(2,1)S(1)} %total.1.mine.refs_0_, s32[3,2]{1,0:T(4,128)S(1)} %copy.10.pairs.refs_3_), custom_call_target="tpu_custom_call" | custom-call | flops 50331648 | bytes 3145728 | tf_op jit(solution)/shard_map/own/pallas_call | solution.py:442
  53.3 1.4 %collective-permute-done.14.refs_1_ = bf16[32,2048]{1,0:T(8,128)(2,1)S(1)} collective-permute-done((bf16[32,2048]{1,0:T(8,128)(2,1)S(1)}, bf16[32,2048]{1,0:T(8,128)(2,1)S(1)}, u32[]{:S(2)}, u32[]{:S(2)}) %collective-permute-start.14) | collective-permute-done | bytes 131104 | tf_op jit(solution)/shard_map/ppermute | solution.py:50
  54.8 0.1 collective-permute-start.15
  54.9 1.5 %collective-permute-done.15.refs_1_ = bf16[64,2048]{1,0:T(8,128)(2,1)S(1)} collective-permute-done((bf16[64,2048]{1,0:T(8,128)(2,1)S(1)}, bf16[64,2048]{1,0:T(8,128)(2,1)S(1)}, u32[]{:S(2)}, u32[]{:S(2)}) %collective-permute-start.15) | collective-permute-done | bytes 262176 | tf_op jit(solution)/shard_map/ppermute | solution.py:50
  56.4 5.3 %rest.1 = (bf16[2,8192]{1,0:T(2,128)(2,1)}, f32[3,256,4096]{2,1,0:T(8,128)}) custom-call(bf16[64,2048]{1,0:T(8,128)(2,1)S(1)} %stack.5.refs_0_, bf16[64,2048]{1,0:T(8,128)(2,1)S(1)} %collective-permute-done.15.refs_1_, s32[1,32]{1,0:T(1,128)S(1)} %bitcast.1, s32[3,2]{1,0:T(4,128)S(1)} %copy.10.pairs.refs_3_, ...), custom_call_target="tpu_custom_call", output_to_operand_aliasing={{1}: (4, {})} | custom-call | tf_op jit(solution)/shard_map/rest/pallas_call | solution.py:459
  (18 shorter events, 0.2 us)
Async XLA Ops:
  0.6 11.5 %collective-permute-start.1 = (bf16[512,128]{1,0:T(8,128)(2,1)}, bf16[512,128]{1,0:T(8,128)(2,1)S(1)}, u32[]{:S(2)}, u32[]{:S(2)}) collective-permute-start(bf16[512,128]{1,0:T(8,128)(2,1)} %proj_in.1), channel_id=1, source_target_pairs={{0,4},{1,5},{2,6},{3,7},{4,8},{5,9},{6,10},{7,11},{8,12},{9,13},{1... | collective-permute-start | bytes 393224 | tf_op jit(solution)/shard_map/ppermute | solution.py:50
  3.7 8.4 %collective-permute-start = (bf16[512,128]{1,0:T(8,128)(2,1)}, bf16[512,128]{1,0:T(8,128)(2,1)S(1)}, u32[]{:S(2)}, u32[]{:S(2)}) collective-permute-start(bf16[512,128]{1,0:T(8,128)(2,1)} %proj_in.1), channel_id=1, source_target_pairs={{0,2},{1,3},{2,0},{3,1},{4,6},{5,7},{6,4},{7,5},{8,10},{9,11},{10,... | collective-permute-start | bytes 393224 | tf_op jit(solution)/shard_map/ppermute | solution.py:50
  5.2 7.0 %collective-permute-start.2 = (bf16[512,128]{1,0:T(8,128)(2,1)}, bf16[512,128]{1,0:T(8,128)(2,1)S(1)}, u32[]{:S(2)}, u32[]{:S(2)}) collective-permute-start(bf16[512,128]{1,0:T(8,128)(2,1)} %proj_in.1), channel_id=1, source_target_pairs={{0,12},{1,13},{2,14},{3,15},{4,0},{5,1},{6,2},{7,3},{8,4},{9,5},{1... | collective-permute-start | bytes 393224 | tf_op jit(solution)/shard_map/ppermute | solution.py:50
  7.4 10.4 %collective-permute-start.4 = (bf16[512,128]{1,0:T(8,128)(2,1)}, bf16[512,128]{1,0:T(8,128)(2,1)S(1)}, u32[]{:S(2)}, u32[]{:S(2)}) collective-permute-start(bf16[512,128]{1,0:T(8,128)(2,1)} %proj_in.1), channel_id=1, source_target_pairs={{0,8},{1,9},{2,10},{3,11},{4,12},{5,13},{6,14},{7,15},{8,0},{9,1},... | collective-permute-start | bytes 393224 | tf_op jit(solution)/shard_map/ppermute | solution.py:50
  12.3 11.1 %collective-permute-start.3 = (bf16[1024,128]{1,0:T(8,128)(2,1)S(1)}, bf16[1024,128]{1,0:T(8,128)(2,1)S(1)}, u32[]{:S(2)}, u32[]{:S(2)}) collective-permute-start(bf16[1024,128]{1,0:T(8,128)(2,1)S(1)} %stack.3.refs_1_), channel_id=1, source_target_pairs={{0,2},{1,3},{2,0},{3,1},{4,6},{5,7},{6,4},{7,5},{8,10},{9,11},{10,... | collective-permute-start | bytes 786440 | tf_op jit(solution)/shard_map/ppermute | solution.py:50
  17.9 5.5 %collective-permute-start.5 = (bf16[512,128]{1,0:T(8,128)(2,1)S(1)}, bf16[512,128]{1,0:T(8,128)(2,1)S(1)}, u32[]{:S(2)}, u32[]{:S(2)}) collective-permute-start(bf16[512,128]{1,0:T(8,128)(2,1)S(1)} %collective-permute-done.4.refs_2_), channel_id=1, source_target_pairs={{0,2},{1,3},{2,0},{3,1},{4,6},{5,7},{6,4},{7,5},{8,10},{9,11},{10,... | collective-permute-start | bytes 393224 | tf_op jit(solution)/shard_map/ppermute | solution.py:50
  19.4 13.7 %copy-start.1 = (s32[1,32]{1,0:T(1,128)S(1)}, s32[1,32]{1,0:T(1,128)}, u32[]{:S(2)}) copy-start(s32[1,32]{1,0:T(1,128)} %refs_4_.1) | copy-start | bytes 388
  20.1 30.5 %copy-start.2 = (s32[3,2]{0,1:T(2,128)S(1)}, s32[3,2]{0,1:T(2,128)}, u32[]{:S(2)}) copy-start(s32[3,2]{0,1:T(2,128)} %param.13) | copy-start | bytes 76
  20.1 36.3 %copy-start = (s32[32]{0:T(128)S(1)}, s32[32]{0:T(128)}, u32[]{:S(2)}) copy-start(s32[32]{0:T(128)} %param.12) | copy-start | bytes 388
  20.1 3.4 %collective-permute-start.7 = (bf16[2048,128]{1,0:T(8,128)(2,1)S(1)}, bf16[2048,128]{1,0:T(8,128)(2,1)S(1)}, u32[]{:S(2)}, u32[]{:S(2)}) collective-permute-start(bf16[2048,128]{1,0:T(8,128)(2,1)S(1)} %get-tuple-element.13), channel_id=1, source_target_pairs={{0,1},{1,0},{2,3},{3,2},{4,5},{5,4},{6,7},{7,6},{8,9},{9,8},{10,11... | collective-permute-start | bytes 1572872 | tf_op jit(solution)/shard_map/ppermute | solution.py:50
  23.4 2.0 %collective-permute-start.6 = (bf16[2048,128]{1,0:T(8,128)(2,1)S(1)}, bf16[2048,128]{1,0:T(8,128)(2,1)S(1)}, u32[]{:S(2)}, u32[]{:S(2)}) collective-permute-start(bf16[2048,128]{1,0:T(8,128)(2,1)S(1)} %stack.4.refs_0_), channel_id=1, source_target_pairs={{0,1},{1,0},{2,3},{3,2},{4,5},{5,4},{6,7},{7,6},{8,9},{9,8},{10,11... | collective-permute-start | bytes 1572872 | tf_op jit(solution)/shard_map/ppermute | solution.py:50
  26.1 5.6 %collective-permute-start.8 = (bf16[512,128]{1,0:T(8,128)(2,1)S(1)}, bf16[512,128]{1,0:T(8,128)(2,1)S(1)}, u32[]{:S(2)}, u32[]{:S(2)}) collective-permute-start(bf16[512,128]{1,0:T(8,128)(2,1)S(1)} %px.5.refs_0_), channel_id=1, source_target_pairs={{0,2},{1,3},{2,0},{3,1},{4,6},{5,7},{6,4},{7,5},{8,10},{9,11},{10,... | collective-permute-start | bytes 393224 | tf_op jit(solution)/shard_map/ppermute | solution.py:50
  27.3 4.4 %collective-permute-start.9 = (bf16[512,128]{1,0:T(8,128)(2,1)S(1)}, bf16[512,128]{1,0:T(8,128)(2,1)S(1)}, u32[]{:S(2)}, u32[]{:S(2)}) collective-permute-start(bf16[512,128]{1,0:T(8,128)(2,1)S(1)} %px.5.refs_0_), channel_id=1, source_target_pairs={{0,1},{1,0},{2,3},{3,2},{4,5},{5,4},{6,7},{7,6},{8,9},{9,8},{10,11... | collective-permute-start | bytes 393224 | tf_op jit(solution)/shard_map/ppermute | solution.py:50
  31.7 1.3 %collective-permute-start.10 = (bf16[512,128]{1,0:T(8,128)(2,1)S(1)}, bf16[512,128]{1,0:T(8,128)(2,1)S(1)}, u32[]{:S(2)}, u32[]{:S(2)}) collective-permute-start(bf16[512,128]{1,0:T(8,128)(2,1)S(1)} %collective-permute-done.8.refs_1_), channel_id=1, source_target_pairs={{0,1},{1,0},{2,3},{3,2},{4,5},{5,4},{6,7},{7,6},{8,9},{9,8},{10,11... | collective-permute-start | bytes 393224 | tf_op jit(solution)/shard_map/ppermute | solution.py:50
  34.0 8.3 %collective-permute-start.13 = (bf16[32,2048]{1,0:T(8,128)(2,1)S(1)}, bf16[32,2048]{1,0:T(8,128)(2,1)S(1)}, u32[]{:S(2)}, u32[]{:S(2)}) collective-permute-start(bf16[32,2048]{1,0:T(8,128)(2,1)S(1)} %grads.1.refs_0_), channel_id=1, source_target_pairs={{0,12},{1,13},{2,14},{3,15},{4,8},{5,9},{6,10},{7,11},{8,4},{9,5},... | collective-permute-start | bytes 393224 | tf_op jit(solution)/shard_map/ppermute | solution.py:50
  36.0 13.5 %collective-permute-start.12 = (bf16[32,2048]{1,0:T(8,128)(2,1)S(1)}, bf16[32,2048]{1,0:T(8,128)(2,1)S(1)}, u32[]{:S(2)}, u32[]{:S(2)}) collective-permute-start(bf16[32,2048]{1,0:T(8,128)(2,1)S(1)} %grads.1.refs_0_), channel_id=1, source_target_pairs={{0,8},{1,9},{2,10},{3,11},{4,12},{5,13},{6,14},{7,15},{8,0},{9,1},... | collective-permute-start | bytes 393224 | tf_op jit(solution)/shard_map/ppermute | solution.py:50
  37.5 12.0 %collective-permute-start.11 = (bf16[32,2048]{1,0:T(8,128)(2,1)S(1)}, bf16[32,2048]{1,0:T(8,128)(2,1)S(1)}, u32[]{:S(2)}, u32[]{:S(2)}) collective-permute-start(bf16[32,2048]{1,0:T(8,128)(2,1)S(1)} %grads.1.refs_0_), channel_id=1, source_target_pairs={{0,4},{1,5},{2,6},{3,7},{4,0},{5,1},{6,2},{7,3},{8,12},{9,13},{10,... | collective-permute-start | bytes 393224 | tf_op jit(solution)/shard_map/ppermute | solution.py:50
  49.6 5.2 %collective-permute-start.14 = (bf16[32,2048]{1,0:T(8,128)(2,1)S(1)}, bf16[32,2048]{1,0:T(8,128)(2,1)S(1)}, u32[]{:S(2)}, u32[]{:S(2)}) collective-permute-start(bf16[32,2048]{1,0:T(8,128)(2,1)S(1)} %total.1.mine.refs_0_), channel_id=1, source_target_pairs={{0,2},{1,3},{2,0},{3,1},{4,6},{5,7},{6,4},{7,5},{8,10},{9,11},{10,... | collective-permute-start | bytes 393224 | tf_op jit(solution)/shard_map/ppermute | solution.py:50
  54.8 1.6 %collective-permute-start.15 = (bf16[64,2048]{1,0:T(8,128)(2,1)S(1)}, bf16[64,2048]{1,0:T(8,128)(2,1)S(1)}, u32[]{:S(2)}, u32[]{:S(2)}) collective-permute-start(bf16[64,2048]{1,0:T(8,128)(2,1)S(1)} %stack.5.refs_0_), channel_id=1, source_target_pairs={{0,1},{1,0},{2,3},{3,2},{4,5},{5,4},{6,7},{7,6},{8,9},{9,8},{10,11... | collective-permute-start | bytes 786440 | tf_op jit(solution)/shard_map/ppermute | solution.py:50
